TPU v7x, 32 devices: a whole 2x2x4 slice. The times are simulated.
32 devices in a mesh: col: 8 (over z, x), row: 4 (over y, core).
Axes of the slice: x: 2, y: 2, z: 4, core: 2. Of those that a mesh axis runs over, the one named last changes fastest.
Arguments:
- tiles: bfloat16 [4, 8, 8, 1024, 512], P('row', 'col'), may hold values from -0.15625 to 0.15625
- tile_index: int32 [4, 8, 8, 2], P('row', 'col'), may hold values from 0 to 15, as said below
- tile_count: int32 [4, 8], P('row', 'col'), may hold values from 1 to 8, as said below
- weights: float32 [32], replicated, may hold values from 0.02 to 0.98
- carbon: float32 [8, 8192], P('col', 'row'), may hold values from 0.1 to 2
- completion: float32 [8, 8192], P('col', 'row'), may hold values from 0.1 to 2
- demand: float32 [4, 16384], P('row', 'col'), may hold values from -6 to 6
- row_kind: int32 [4, 16384], P('row', 'col'), may hold values 0 or 1
- primal_start: float32 [32, 8, 8192], P(None, 'col', 'row'), may hold values from 0 to 2
- dual_start: float32 [32, 4, 16384], P(None, 'row', 'col'), may hold values from -6 to 6
Outputs:
- primal_out: float32 [32, 8, 8192], P(None, 'col', 'row')
- dual_out: float32 [32, 4, 16384], P(None, 'row', 'col')
Inputs may be any that keep to these rules, and one draw needn't show every extreme that they name: `tile_index`: column 0 is a local block row below 16, column 1 a local block column below 16; the pairs of one region pair are all different. `tile_count`: at least one region pair holds 8 live tiles in every draw.
All inputs are finite; a program needn't handle non-finite values. No bound on the sum of `row_kind` on one device may be relied on, other than what follows from the above.
Results may differ from a plain program's by a relative error of at most 0.0021.
Values may be sent and summed in bfloat16 or wider, within the bound.
No kernel may reach another device: no remote copies, remote signals or barrier semaphores. Data moves between devices by JAX's collectives and lax.ppermute only.
A program may use at most 64 MiB of HBM per device.

v0:
```python
import jax
import jax.numpy as jnp
from jax import lax
from jax.sharding import PartitionSpec as P

BR_DEV = 16
BC_DEV = 16
ITERS = 2


step_primal = 0.4
step_dual = 0.4


def transpose_sweep(blocks, places, live, dual_region, width):
    rows_tile = blocks.shape[1]
    cols_tile = blocks.shape[2]
    start = jnp.zeros((dual_region.shape[0], width), jnp.float32)

    def transpose_visit(slot, total):
        tile = lax.dynamic_index_in_dim(blocks, slot, 0, keepdims=False)
        rows_at = places[slot, 0] * rows_tile
        cols_at = places[slot, 1] * cols_tile
        piece = lax.dynamic_slice_in_dim(dual_region, rows_at, rows_tile, 1)
        term = jnp.dot(piece, tile, preferred_element_type=jnp.float32)
        prior = lax.dynamic_slice_in_dim(total, cols_at, cols_tile, 1)
        return lax.dynamic_update_slice_in_dim(total, prior + term, cols_at, 1)

    return lax.fori_loop(0, live, transpose_visit, start)


def forward_sweep(blocks, places, live, primal_region, height):
    rows_tile = blocks.shape[1]
    cols_tile = blocks.shape[2]
    start = jnp.zeros((primal_region.shape[0], height), jnp.float32)

    def forward_visit(slot, total):
        tile = lax.dynamic_index_in_dim(blocks, slot, 0, keepdims=False)
        rows_at = places[slot, 0] * rows_tile
        cols_at = places[slot, 1] * cols_tile
        piece = lax.dynamic_slice_in_dim(primal_region, cols_at, cols_tile, 1)
        term = lax.dot_general(
            piece, tile, (((1,), (1,)), ((), ())), preferred_element_type=jnp.float32
        )
        prior = lax.dynamic_slice_in_dim(total, rows_at, rows_tile, 1)
        return lax.dynamic_update_slice_in_dim(total, prior + term, rows_at, 1)

    return lax.fori_loop(0, live, forward_visit, start)


def body(
    tiles,
    tile_index,
    tile_count,
    weights,
    carbon,
    completion,
    demand,
    row_kind,
    primal_start,
    dual_start,
):
    blocks = tiles[0, 0]
    places = tile_index[0, 0]
    live = tile_count[0, 0]
    rows_wide = BR_DEV * blocks.shape[1]
    cols_wide = BC_DEV * blocks.shape[2]
    primal = primal_start[:, 0, :]
    dual = dual_start[:, 0, :]
    share = weights[:, None]
    carbon_part, completion_part = (carbon, completion)
    cost = share * carbon_part + (1.0 - share) * completion_part
    for step in range(ITERS):
        dual_region = lax.all_gather(dual.astype(jnp.bfloat16), "col", axis=1, tiled=True)
        pull = transpose_sweep(blocks, places, live, dual_region, cols_wide)
        pull = lax.psum_scatter(pull, "row", scatter_dimension=1, tiled=True)
        fresh = jnp.maximum(primal - step_primal * (cost - pull), 0.0)
        extra = (2.0 * fresh - primal).astype(jnp.bfloat16)
        primal_region = lax.all_gather(extra, "row", axis=1, tiled=True)
        primal = fresh
        push = forward_sweep(blocks, places, live, primal_region, rows_wide)
        piece_rows = dual.shape[1]
        push = lax.psum(push, "col")
        push = lax.dynamic_slice_in_dim(push, lax.axis_index("col") * piece_rows, piece_rows, 1)
        moved = dual + step_dual * (demand - push)
        dual = jnp.where(row_kind == 1, jnp.maximum(moved, 0.0), moved)
    return (primal[:, None, :], dual[:, None, :])


def solution(mesh):
    placed = (
        P("row", "col", None, None, None),
        P("row", "col", None, None),
        P("row", "col"),
        P(),
        P("col", "row"),
        P("col", "row"),
        P("row", "col"),
        P("row", "col"),
        P(None, "col", "row"),
        P(None, "row", "col"),
    )
    return jax.shard_map(
        body,
        mesh=mesh,
        in_specs=placed,
        out_specs=(P(None, "col", "row"), P(None, "row", "col")),
        check_vma=False,
    )
```

profile of v0, /device:TPU:0, one launch (start us, length us, event | category | flops | bytes accessed | tf_op | source)
XLA Modules:
  0.0 518.7 jit_solution(10362405691772397516)
XLA Ops:
  7.2 1.7 copy.29
  9.0 44.7 %all-gather.3.cloned.1.call-done = bf16[32,16384]{1,0:T(8,128)(2,1)} async-done(((bf16[32,2048]{1,0:T(8,128)(2,1)}), bf16[32,16384]{1,0:T(8,128)(2,1)}) %all-gather.3.cloned.1.call-update) | async-done | bytes 1048592 | tf_op jit(solution)/shard_map/all_gather | solution.py:74
  53.8 10.4 %while.40 = (s32[]{:T(128)}, f32[32,8192]{1,0:T(8,128)S(1)}, s32[]{:T(128)}, s32[8,2]{0,1:T(2,128)}, bf16[32,16384]{1,0:T(8,128)(2,1)}, /*index=5*/bf16[8,1024,5...) while((s32[]{:T(128)}, f32[32,8192]{1,0:T(8,128)S(1)}, ...), condition=%wide.region_1.2_spmd, body=%wide.region_0.1_spmd.sunk | while | flops 33570828 | bytes 1245475 | solution.py:29
  54.5 1.4 constant_dynamic-slice_fusion.12
  57.1 1.5 fusion.37
  59.4 1.4 constant_dynamic-slice_fusion.12
  62.0 1.5 fusion.37
  65.3 52.0 %reduce-scatter.3.cloned.1.call-done = f32[32,2048]{1,0:T(8,128)} async-done(((f32[32,8192]{1,0:T(8,128)}), f32[32,2048]{1,0:T(8,128)}) %reduce-scatter.3.cloned.1.call-update) | async-done | bytes 262160 | tf_op jit(solution)/shard_map/reduce_scatter | solution.py:76
  118.4 6.8 %all_gather.13 = bf16[32,8192]{1,0:T(8,128)(2,1)S(1)} all-gather(bf16[32,2048]{1,0:T(8,128)(2,1)S(1)} %fusion.21), channel_id=1, replica_groups=mesh['col'=8,'row'=4] {'row'}, dimensions={1}, use_global_device_ids=true | all-gather | bytes 655360 | tf_op jit(solution)/shard_map/all_gather | solution.py:79
  125.4 9.3 %while.41 = (s32[]{:T(128)}, f32[32,16384]{1,0:T(8,128)S(1)}, s32[]{:T(128)}, s32[8,2]{0,1:T(2,128)S(1)}, bf16[32,8192]{1,0:T(8,128)(2,1)S(1)}, /*index=5*/bf16[...) while((s32[]{:T(128)}, f32[32,16384]{1,0:T(8,128)S(1)}, ...), condition=%wide.region_4.5_spmd, body=%wide.region_3.4_spmd.sunk | while | flops 33587212 | bytes 1343779 | solution.py:48
  128.1 1.6 fusion.40
  132.4 1.6 fusion.40
  136.2 128.0 %all-reduce.3.cloned.1.call-done = f32[32,16384]{1,0:T(8,128)} async-done(((f32[32,16384]{1,0:T(8,128)}), f32[32,16384]{1,0:T(8,128)}) %all-reduce.3.cloned.1.call-update) | async-done | bytes 2097168 | tf_op jit(solution)/shard_map/psum | solution.py:83
  264.1 1.7 fusion.22
  265.9 41.0 %all-gather.5.cloned.1.call-done = bf16[32,16384]{1,0:T(8,128)(2,1)} async-done(((bf16[32,2048]{1,0:T(8,128)(2,1)}), bf16[32,16384]{1,0:T(8,128)(2,1)}) %all-gather.5.cloned.1.call-update) | async-done | bytes 1048592 | tf_op jit(solution)/shard_map/all_gather | solution.py:74
  307.0 8.7 %while.42 = (s32[]{:T(128)}, f32[32,8192]{1,0:T(8,128)S(1)}, s32[]{:T(128)}, s32[8,2]{0,1:T(2,128)S(1)}, bf16[32,16384]{1,0:T(8,128)(2,1)}, /*index=5*/bf16[8,10...) while((s32[]{:T(128)}, f32[32,8192]{1,0:T(8,128)S(1)}, ...), condition=%wide.region_7.8_spmd, body=%wide.region_6.7_spmd.sunk | while | flops 33570828 | bytes 1245475 | solution.py:29
  309.5 1.5 fusion.43
  313.5 1.5 fusion.43
  316.8 46.9 %reduce-scatter.5.cloned.1.call-done = f32[32,2048]{1,0:T(8,128)} async-done(((f32[32,8192]{1,0:T(8,128)}), f32[32,2048]{1,0:T(8,128)}) %reduce-scatter.5.cloned.1.call-update) | async-done | bytes 262160 | tf_op jit(solution)/shard_map/reduce_scatter | solution.py:76
  364.9 6.8 %all_gather.15 = bf16[32,8192]{1,0:T(8,128)(2,1)S(1)} all-gather(bf16[32,2048]{1,0:T(8,128)(2,1)S(1)} %get-tuple-element.186), channel_id=1, replica_groups=mesh['col'=8,'row'=4] {'row'}, dimensions={1}, use_global_device_ids=true | all-gather | bytes 655360 | tf_op jit(solution)/shard_map/all_gather | solution.py:79
  371.9 9.1 %while.43 = (s32[]{:T(128)}, f32[32,16384]{1,0:T(8,128)S(1)}, s32[]{:T(128)}, s32[8,2]{0,1:T(2,128)S(1)}, bf16[32,8192]{1,0:T(8,128)(2,1)S(1)}, /*index=5*/bf16[...) while((s32[]{:T(128)}, f32[32,16384]{1,0:T(8,128)S(1)}, ...), condition=%wide.region_10.11_spmd, body=%wide.region_9.10_spmd.sunk | while | flops 33587212 | bytes 1343779 | solution.py:48
  374.4 1.6 fusion.46
  378.7 1.6 fusion.46
  383.2 126.5 %all-reduce.5.cloned.1.call-done = f32[32,16384]{1,0:T(8,128)} async-done(((f32[32,16384]{1,0:T(8,128)}), f32[32,16384]{1,0:T(8,128)}) %all-reduce.5.cloned.1.call-update) | async-done | bytes 2097168 | tf_op jit(solution)/shard_map/psum | solution.py:83
  (55 shorter events, 14.4 us)
Async XLA Ops:
  7.2 46.5 %all-gather.3.cloned.1.call-start = ((), (), s32[]{:S(2)}) async-start(), calls=%async_computation.2 | async-start | bytes 1179648 | tf_op jit(solution)/shard_map/all_gather | solution.py:74
  8.9 108.4 %reduce-scatter.3.cloned.1.call-start = ((), (), s32[]{:S(2)}) async-start(), calls=%async_computation.3 | async-start | bytes 1310720 | tf_op jit(solution)/shard_map/reduce_scatter | solution.py:76
  53.8 11.6 %copy-start.12 = (f32[32]{0:T(128)S(1)}, f32[32]{0:T(128)}, u32[]{:S(2)}) copy-start(f32[32]{0:T(128)} %param.21) | copy-start | bytes 388
  53.8 63.6 %copy-start.5 = (f32[32,1,2048]{2,1,0:T(1,128)S(1)}, f32[32,1,2048]{2,1,0:T(1,128)}, u32[]{:S(2)}) copy-start(f32[32,1,2048]{2,1,0:T(1,128)} %param.26) | copy-start | bytes 786436
  53.8 63.6 %copy-start.8 = (f32[1,2048]{1,0:T(1,128)S(1)}, f32[1,2048]{1,0:T(1,128)}, u32[]{:S(2)}) copy-start(f32[1,2048]{1,0:T(1,128)} %param.23) | copy-start | bytes 24580
  53.8 63.5 %copy-start.9 = (f32[1,2048]{1,0:T(1,128)S(1)}, f32[1,2048]{1,0:T(1,128)}, u32[]{:S(2)}) copy-start(f32[1,2048]{1,0:T(1,128)} %param.22) | copy-start | bytes 24580
  64.2 1.0 copy-start.2
  64.2 61.1 %copy-start.7 = (s32[8,2]{0,1:T(2,128)S(1)}, s32[8,2]{0,1:T(2,128)}, u32[]{:S(2)}) copy-start(s32[8,2]{0,1:T(2,128)} %get-tuple-element.542) | copy-start | bytes 196
  65.3 198.9 %all-reduce.3.cloned.1.call-start = ((), (), s32[]{:S(2)}) async-start(), calls=%async_computation.4 | async-start | bytes 4194304 | tf_op jit(solution)/shard_map/psum | solution.py:83
  134.7 1.3 copy-start.1
  134.7 1.4 copy-start.11
  134.8 129.4 %copy-start.4 = (f32[32,1,2048]{2,1,0:T(1,128)S(1)}, f32[32,1,2048]{2,1,0:T(1,128)}, u32[]{:S(2)}) copy-start(f32[32,1,2048]{2,1,0:T(1,128)} %param.27) | copy-start | bytes 786436
  134.8 129.4 %copy-start.10 = (f32[1,2048]{1,0:T(1,128)S(1)}, f32[1,2048]{1,0:T(1,128)}, u32[]{:S(2)}) copy-start(f32[1,2048]{1,0:T(1,128)} %param.24) | copy-start | bytes 24580
  136.1 170.9 %all-gather.5.cloned.1.call-start = ((), (), s32[]{:S(2)}) async-start(), calls=%async_computation.5 | async-start | bytes 1179648 | tf_op jit(solution)/shard_map/all_gather | solution.py:74
  265.9 97.9 %reduce-scatter.5.cloned.1.call-start = ((), (), s32[]{:S(2)}) async-start(), calls=%async_computation.6 | async-start | bytes 1310720 | tf_op jit(solution)/shard_map/reduce_scatter | solution.py:76
  307.0 56.7 %copy-start.6 = (f32[32,2048]{1,0:T(8,128)S(1)}, f32[32,2048]{1,0:T(8,128)}, u32[]{:S(2)}) copy-start(f32[32,2048]{1,0:T(8,128)} %reduce-scatter.3.cloned.1.call-done) | copy-start | bytes 786436
  315.7 1.0 copy-start.3
  316.8 193.0 %all-reduce.5.cloned.1.call-start = ((), (), s32[]{:S(2)}) async-start(), calls=%async_computation.7 | async-start | bytes 4194304 | tf_op jit(solution)/shard_map/psum | solution.py:83
  381.0 1.3 copy-start
Sparse Core Ops, SparseCore 0:
  10.8 42.8 all-gather.2
  65.4 51.9 reduce-scatter.2
  136.2 127.8 all-reduce.2
  267.0 39.9 all-gather.4
  316.9 46.8 reduce-scatter.4
  382.5 127.2 all-reduce.4
where the time goes:
time: 518 us; the launch traced here: 519 us
  waiting for transfers between devices  439 us (85%)
  loops' own time  18.4 us (4%)
  local copies, waits for them, and re-layouts  15 us (3%)
  between operations  14.3 us (3%)
  blocking collectives  13.6 us (3%)
  matrix products  12.7 us (2%)
  other arithmetic  5.25 us (1%)
    psum x2, waiting for transfers between devices, body(): push = lax.psum(push, 'col')  254 us
    reduce_scatter x2, waiting for transfers between devices, body(): pull = lax.psum_scatter(pull, 'row', scatter_dimension=1, tiled=True)  98.9 us
    all_gather x2, waiting for transfers between devices, body(): lax.all_gather(dual.astype(jnp.bfloat16), 'col', axis=1, tiled=True)  85.7 us
    all_gather x2, blocking collectives, body(): primal_region = lax.all_gather(extra, 'row', axis=1, tiled=True)  13.6 us
  transfers between devices with their start and end apart: 6, of which 6 were waited for; matrix products, arithmetic and copies ran while one was open for 0% of the time, Pallas kernels for 0%

commit v1 on v0

v1 whole, which is shorter than its diff:
```python
import functools

import jax
import jax.numpy as jnp
from jax import lax
from jax.experimental import pallas as pl
from jax.experimental.pallas import tpu as pltpu
from jax.sharding import PartitionSpec as P

BR_DEV = 16
BC_DEV = 16
ITERS = 2


step_primal = 0.4
step_dual = 0.4

VMEM_LIMIT = 24 * 1024 * 1024


def sweep_kernel(forward, pieces, outs, per_in, per_out, info, tiles, *refs):
    parts = refs[:pieces]
    results = refs[pieces : pieces + outs]
    held, total, operand, arrived = refs[pieces + outs :]
    slots = tiles.shape[0]
    live = info[2 * slots]
    me_in = info[2 * slots + 1]
    me_out = info[2 * slots + 2]
    span_in = operand.shape[1]
    span_out = total.shape[2]

    def fetch(slot):
        return pltpu.make_async_copy(tiles.at[slot], held.at[slot], arrived.at[slot])

    def start(slot, carry):
        fetch(slot).start()
        return carry

    lax.fori_loop(0, live, start, 0)
    total[...] = jnp.zeros_like(total)

    def visit(slot, carry):
        block_row = info[2 * slot]
        block_col = info[2 * slot + 1]
        block_in = block_col if forward else block_row
        block_out = block_row if forward else block_col
        source = (block_in // per_in) ^ me_in
        place = pl.multiple_of((block_in % per_in) * span_in, span_in)
        for k in range(pieces):

            @pl.when(source == k)
            def _():
                operand[...] = parts[k][:, pl.ds(place, span_in)]

        fetch(slot).wait()
        contract = (((1,), (1,)), ((), ())) if forward else (((1,), (0,)), ((), ()))
        total[block_out] += lax.dot_general(
            operand[...], held[slot], contract, preferred_element_type=jnp.float32
        )
        return carry

    lax.fori_loop(0, live, visit, 0)
    for k in range(outs):
        first = (me_out ^ k) * per_out
        for b in range(per_out):
            results[k][:, b * span_out : (b + 1) * span_out] = total[first + b].astype(
                results[k].dtype
            )


def sweep(forward, tiles, info, parts, outs, per_in, per_out, blocks_out):
    slots, rows_tile, cols_tile = tiles.shape
    width = parts[0].shape[0]
    span_in, span_out = (cols_tile, rows_tile) if forward else (rows_tile, cols_tile)
    pieces = len(parts)
    vmem = pl.BlockSpec(memory_space=pltpu.VMEM)
    return pl.pallas_call(
        functools.partial(sweep_kernel, forward, pieces, outs, per_in, per_out),
        out_shape=[
            jax.ShapeDtypeStruct((width, per_out * span_out), jnp.bfloat16)
        ]
        * outs,
        in_specs=[pl.BlockSpec(memory_space=pltpu.SMEM), pl.BlockSpec(memory_space=pl.ANY)]
        + [vmem] * pieces,
        out_specs=[vmem] * outs,
        scratch_shapes=[
            pltpu.VMEM(tiles.shape, tiles.dtype),
            pltpu.VMEM((blocks_out, width, span_out), jnp.float32),
            pltpu.VMEM((width, span_in), jnp.bfloat16),
            pltpu.SemaphoreType.DMA((slots,)),
        ],
        compiler_params=pltpu.CompilerParams(vmem_limit_bytes=VMEM_LIMIT),
        cost_estimate=pl.CostEstimate(
            flops=2 * slots * width * rows_tile * cols_tile,
            bytes_accessed=tiles.size * 2,
            transcendentals=0,
        ),
        name="forward_sweep" if forward else "transpose_sweep",
    )(info, tiles, *parts)


def swap(value, axis, size, k):
    return lax.ppermute(value, axis, [(i, i ^ k) for i in range(size)])


def gather_pairs(own, axis, size):
    parts = [None] * size
    parts[0] = own
    for k in range(2, size, 2):
        parts[k] = swap(own, axis, size, k)
    for k in range(0, size, 2):
        parts[k + 1] = swap(parts[k], axis, size, 1)
    return parts


def sum_direct(parts, axis, size):
    total = parts[0].astype(jnp.float32)
    for k in range(1, size):
        total = total + swap(parts[k], axis, size, k).astype(jnp.float32)
    return total


def body(
    rows,
    cols,
    tiles,
    tile_index,
    tile_count,
    weights,
    carbon,
    completion,
    demand,
    row_kind,
    primal_start,
    dual_start,
):
    blocks = tiles[0, 0]
    info = jnp.concatenate(
        [
            tile_index.reshape(-1),
            tile_count.reshape(-1),
            lax.axis_index("col")[None],
            lax.axis_index("row")[None],
        ]
    ).astype(jnp.int32)
    info_back = jnp.concatenate([info[:-2], info[-1:], info[-2:-1]])
    primal = primal_start[:, 0, :]
    dual = dual_start[:, 0, :]
    per_row = dual.shape[1] // blocks.shape[1]
    per_col = primal.shape[1] // blocks.shape[2]
    share = weights[:, None]
    cost = share * carbon + (1.0 - share) * completion
    for step in range(ITERS):
        dual_parts = gather_pairs(dual.astype(jnp.bfloat16), "col", cols)
        pull_parts = sweep(
            False, blocks, info, dual_parts, rows, per_row, per_col, BC_DEV
        )
        pull = sum_direct(pull_parts, "row", rows)
        fresh = jnp.maximum(primal - step_primal * (cost - pull), 0.0)
        extra = (2.0 * fresh - primal).astype(jnp.bfloat16)
        primal = fresh
        extra_parts = gather_pairs(extra, "row", rows)
        push_parts = sweep(
            True, blocks, info_back, extra_parts, cols, per_col, per_row, BR_DEV
        )
        push = sum_direct(push_parts, "col", cols)
        moved = dual + step_dual * (demand - push)
        dual = jnp.where(row_kind == 1, jnp.maximum(moved, 0.0), moved)
    return (primal[:, None, :], dual[:, None, :])


def solution(mesh):
    placed = (
        P("row", "col", None, None, None),
        P("row", "col", None, None),
        P("row", "col"),
        P(),
        P("col", "row"),
        P("col", "row"),
        P("row", "col"),
        P("row", "col"),
        P(None, "col", "row"),
        P(None, "row", "col"),
    )
    return jax.shard_map(
        functools.partial(body, mesh.shape["row"], mesh.shape["col"]),
        mesh=mesh,
        in_specs=placed,
        out_specs=(P(None, "col", "row"), P(None, "row", "col")),
        check_vma=False,
    )
```

time: 518 us -> 148 us (0.29)
  waiting for transfers between devices: 439 us -> 70.1 us
  starting transfers between devices: 0.24 us -> 61.1 us
  loops' own time: 18.4 us -> 0 us
  blocking collectives: 13.6 us -> 0 us
  between operations: 14.3 us -> 1.46 us
  matrix products: 12.7 us -> 0 us
  local copies, waits for them, and re-layouts: 15 us -> 7.27 us
    psum x2 -> x0, waiting for transfers between devices: 254 us -> none  [body(): push = lax.psum(push, 'col')]
    reduce_scatter x2 -> x0, waiting for transfers between devices: 98.9 us -> none  [body(): pull = lax.psum_scatter(pull, 'row', scatter_dimension=1, tiled=True)]
    all_gather x2 -> x0, waiting for transfers between devices: 85.7 us -> none  [body(): lax.all_gather(dual.astype(jnp.bfloat16), 'col', axis=1, tiled=True)]
    ppermute x0 -> x40, waiting for transfers between devices: none -> 70.1 us  [swap(): return lax.ppermute(value, axis, [(i, i ^ k) for i in range(size)])]
    ppermute x0 -> x40, starting transfers between devices: none -> 61.1 us  [swap(): return lax.ppermute(value, axis, [(i, i ^ k) for i in range(size)])]
    another operation x4 -> x0, loops' own time: 18.4 us -> none  [the longest x2 9.33 us: forward_sweep(): return lax.fori_loop(0, live, forward_visit, start)]
    all_gather x2 -> x0, blocking collectives: 13.6 us -> none  [body(): primal_region = lax.all_gather(extra, 'row', axis=1, tiled=True)]
    dot_general x8 -> x0, matrix products: 12.7 us -> none  [the longest x4 6.54 us: forward_visit(): lax.dot_general(piece, tile, (((1,), (1,)), ((), ())), preferred_element_...]
  transfers between devices with their start and end apart: 6 -> 40, of which waited for: 6 -> 18; matrix products, arithmetic and copies ran while one was open for 0% -> 1% of each run, Pallas kernels for 0% -> 0%
where the time goes in v1:
time: 148 us; the launch traced here: 146 us
  waiting for transfers between devices  70.1 us (47%)
  starting transfers between devices  61.1 us (41%)
  local copies, waits for them, and re-layouts  7.27 us (5%)
  Pallas kernels  5.08 us (3%)
    ppermute x40, waiting for transfers between devices, swap(): return lax.ppermute(value, axis, [(i, i ^ k) for i in range(size)])  70.1 us
    ppermute x40, starting transfers between devices, swap(): return lax.ppermute(value, axis, [(i, i ^ k) for i in range(size)])  61.1 us
    unnamed x22, local copies, waits for them, and re-layouts  7.19 us
    pallas_call x4, Pallas kernels, sweep(): pl.pallas_call(functools.partial(sweep_kernel, forward, pieces, outs, per...  5.08 us
  transfers between devices with their start and end apart: 40, of which 18 were waited for; matrix products, arithmetic and copies ran while one was open for 1% of the time, Pallas kernels for 0%

profile of v1, /device:TPU:0, one launch (start us, length us, event | category | flops | bytes accessed | tf_op | source)
XLA Modules:
  0.0 146.0 jit_solution(10657443242139039752)
XLA Ops:
  1.7 5.1 %collective-permute-start.5 = (bf16[32,2048]{1,0:T(8,128)(2,1)S(1)}, bf16[32,2048]{1,0:T(8,128)(2,1)S(1)}, u32[]{:S(2)}, u32[]{:S(2)}) collective-permute-start(bf16[32,2048]{1,0:T(8,128)(2,1)S(1)} %bitcast.33), channel_id=1, source_target_pairs={{0,24},{4,28},{8,16},{12,20},{16,8},{20,12},{24,0},{28,4},{1,25},{... | collective-permute-start | bytes 393224 | tf_op jit(solution)/shard_map/ppermute | solution.py:103
  9.1 2.1 %collective-permute-done.5.refs_6_ = bf16[32,2048]{1,0:T(8,128)(2,1)S(1)} collective-permute-done((bf16[32,2048]{1,0:T(8,128)(2,1)S(1)}, bf16[32,2048]{1,0:T(8,128)(2,1)S(1)}, u32[]{:S(2)}, u32[]{:S(2)}) %collective-permute-start.5) | collective-permute-done | bytes 131104 | tf_op jit(solution)/shard_map/ppermute | solution.py:103
  13.0 5.0 %collective-permute-done.3.refs_4_ = bf16[32,2048]{1,0:T(8,128)(2,1)S(1)} collective-permute-done((bf16[32,2048]{1,0:T(8,128)(2,1)S(1)}, bf16[32,2048]{1,0:T(8,128)(2,1)S(1)}, u32[]{:S(2)}, u32[]{:S(2)}) %collective-permute-start.3) | collective-permute-done | bytes 131104 | tf_op jit(solution)/shard_map/ppermute | solution.py:103
  21.6 2.3 %collective-permute-done.4.refs_5_ = bf16[32,2048]{1,0:T(8,128)(2,1)S(1)} collective-permute-done((bf16[32,2048]{1,0:T(8,128)(2,1)S(1)}, bf16[32,2048]{1,0:T(8,128)(2,1)S(1)}, u32[]{:S(2)}, u32[]{:S(2)}) %collective-permute-start.4) | collective-permute-done | bytes 131104 | tf_op jit(solution)/shard_map/ppermute | solution.py:103
  25.3 3.4 %copy-done = bf16[1,1,8,1024,512]{4,3,2,1,0:T(8,128)(2,1)S(1)} copy-done((bf16[1,1,8,1024,512]{4,3,2,1,0:T(8,128)(2,1)S(1)}, bf16[1,1,8,1024,512]{4,3,2,1,0:T(8,128)(2,1)}, u32[]{:S(2)}) %copy-start) | copy-done | bytes 8388632
  29.9 2.7 %collective-permute-start.8 = (bf16[32,2048]{1,0:T(8,128)(2,1)S(1)}, bf16[32,2048]{1,0:T(8,128)(2,1)S(1)}, u32[]{:S(2)}, u32[]{:S(2)}) collective-permute-start(bf16[32,2048]{1,0:T(8,128)(2,1)S(1)} %get-tuple-element.28), channel_id=1, source_target_pairs={{0,2},{1,3},{2,0},{3,1},{4,6},{5,7},{6,4},{7,5},{8,10},{9,11},{10,... | collective-permute-start | bytes 393224 | tf_op jit(solution)/shard_map/ppermute | solution.py:103
  32.7 4.3 %collective-permute-done.8 = bf16[32,2048]{1,0:T(8,128)(2,1)S(1)} collective-permute-done((bf16[32,2048]{1,0:T(8,128)(2,1)S(1)}, bf16[32,2048]{1,0:T(8,128)(2,1)S(1)}, u32[]{:S(2)}, u32[]{:S(2)}) %collective-permute-start.8) | collective-permute-done | bytes 131104 | tf_op jit(solution)/shard_map/ppermute | solution.py:103
  37.0 2.3 %collective-permute-done.9 = bf16[32,2048]{1,0:T(8,128)(2,1)S(1)} collective-permute-done((bf16[32,2048]{1,0:T(8,128)(2,1)S(1)}, bf16[32,2048]{1,0:T(8,128)(2,1)S(1)}, u32[]{:S(2)}, u32[]{:S(2)}) %collective-permute-start.9) | collective-permute-done | bytes 131104 | tf_op jit(solution)/shard_map/ppermute | solution.py:103
  41.2 3.9 %collective-permute-done.11.refs_2_ = bf16[32,2048]{1,0:T(8,128)(2,1)S(1)} collective-permute-done((bf16[32,2048]{1,0:T(8,128)(2,1)S(1)}, bf16[32,2048]{1,0:T(8,128)(2,1)S(1)}, u32[]{:S(2)}, u32[]{:S(2)}) %collective-permute-start.11) | collective-permute-done | bytes 131104 | tf_op jit(solution)/shard_map/ppermute | solution.py:103
  51.4 3.0 %collective-permute-start.16 = (bf16[32,2048]{1,0:T(8,128)(2,1)S(1)}, bf16[32,2048]{1,0:T(8,128)(2,1)S(1)}, u32[]{:S(2)}, u32[]{:S(2)}) collective-permute-start(bf16[32,2048]{1,0:T(8,128)(2,1)S(1)} %get-tuple-element.34), channel_id=1, source_target_pairs={{0,16},{4,20},{8,24},{12,28},{16,0},{20,4},{24,8},{28,12},{1,17},{... | collective-permute-start | bytes 393224 | tf_op jit(solution)/shard_map/ppermute | solution.py:103
  55.8 3.5 %collective-permute-start.18 = (bf16[32,2048]{1,0:T(8,128)(2,1)S(1)}, bf16[32,2048]{1,0:T(8,128)(2,1)S(1)}, u32[]{:S(2)}, u32[]{:S(2)}) collective-permute-start(bf16[32,2048]{1,0:T(8,128)(2,1)S(1)} %get-tuple-element.36), channel_id=1, source_target_pairs={{0,24},{4,28},{8,16},{12,20},{16,8},{20,12},{24,0},{28,4},{1,25},{... | collective-permute-start | bytes 393224 | tf_op jit(solution)/shard_map/ppermute | solution.py:103
  59.3 3.0 %collective-permute-start.19 = (bf16[32,2048]{1,0:T(8,128)(2,1)S(1)}, bf16[32,2048]{1,0:T(8,128)(2,1)S(1)}, u32[]{:S(2)}, u32[]{:S(2)}) collective-permute-start(bf16[32,2048]{1,0:T(8,128)(2,1)S(1)} %get-tuple-element.37), channel_id=1, source_target_pairs={{0,28},{4,24},{8,20},{12,16},{16,12},{20,8},{24,4},{28,0},{1,29},{... | collective-permute-start | bytes 393224 | tf_op jit(solution)/shard_map/ppermute | solution.py:103
  62.4 11.8 %collective-permute-done.17 = bf16[32,2048]{1,0:T(8,128)(2,1)S(1)} collective-permute-done((bf16[32,2048]{1,0:T(8,128)(2,1)S(1)}, bf16[32,2048]{1,0:T(8,128)(2,1)S(1)}, u32[]{:S(2)}, u32[]{:S(2)}) %collective-permute-start.17) | collective-permute-done | bytes 131104 | tf_op jit(solution)/shard_map/ppermute | solution.py:103
  74.5 3.6 %collective-permute-start.25 = (bf16[32,2048]{1,0:T(8,128)(2,1)S(1)}, bf16[32,2048]{1,0:T(8,128)(2,1)S(1)}, u32[]{:S(2)}, u32[]{:S(2)}) collective-permute-start(bf16[32,2048]{1,0:T(8,128)(2,1)S(1)} %get-tuple-element.54.refs_0_), channel_id=1, source_target_pairs={{0,24},{4,28},{8,16},{12,20},{16,8},{20,12},{24,0},{28,4},{1,25},{... | collective-permute-start | bytes 393224 | tf_op jit(solution)/shard_map/ppermute | solution.py:103
  78.1 5.3 %collective-permute-start.23 = (bf16[32,2048]{1,0:T(8,128)(2,1)S(1)}, bf16[32,2048]{1,0:T(8,128)(2,1)S(1)}, u32[]{:S(2)}, u32[]{:S(2)}) collective-permute-start(bf16[32,2048]{1,0:T(8,128)(2,1)S(1)} %get-tuple-element.54.refs_0_), channel_id=1, source_target_pairs={{0,16},{4,20},{8,24},{12,28},{16,0},{20,4},{24,8},{28,12},{1,17},{... | collective-permute-start | bytes 393224 | tf_op jit(solution)/shard_map/ppermute | solution.py:103
  85.3 4.4 %collective-permute-done.23.refs_4_ = bf16[32,2048]{1,0:T(8,128)(2,1)S(1)} collective-permute-done((bf16[32,2048]{1,0:T(8,128)(2,1)S(1)}, bf16[32,2048]{1,0:T(8,128)(2,1)S(1)}, u32[]{:S(2)}, u32[]{:S(2)}) %collective-permute-start.23) | collective-permute-done | bytes 131104 | tf_op jit(solution)/shard_map/ppermute | solution.py:103
  91.8 2.9 %collective-permute-done.24.refs_5_ = bf16[32,2048]{1,0:T(8,128)(2,1)S(1)} collective-permute-done((bf16[32,2048]{1,0:T(8,128)(2,1)S(1)}, bf16[32,2048]{1,0:T(8,128)(2,1)S(1)}, u32[]{:S(2)}, u32[]{:S(2)}) %collective-permute-start.24) | collective-permute-done | bytes 131104 | tf_op jit(solution)/shard_map/ppermute | solution.py:103
  97.3 5.8 %collective-permute-start.28 = (bf16[32,2048]{1,0:T(8,128)(2,1)S(1)}, bf16[32,2048]{1,0:T(8,128)(2,1)S(1)}, u32[]{:S(2)}, u32[]{:S(2)}) collective-permute-start(bf16[32,2048]{1,0:T(8,128)(2,1)S(1)} %get-tuple-element.40), channel_id=1, source_target_pairs={{0,2},{1,3},{2,0},{3,1},{4,6},{5,7},{6,4},{7,5},{8,10},{9,11},{10,... | collective-permute-start | bytes 393224 | tf_op jit(solution)/shard_map/ppermute | solution.py:103
  103.2 4.3 %collective-permute-done.28 = bf16[32,2048]{1,0:T(8,128)(2,1)S(1)} collective-permute-done((bf16[32,2048]{1,0:T(8,128)(2,1)S(1)}, bf16[32,2048]{1,0:T(8,128)(2,1)S(1)}, u32[]{:S(2)}, u32[]{:S(2)}) %collective-permute-start.28) | collective-permute-done | bytes 131104 | tf_op jit(solution)/shard_map/ppermute | solution.py:103
  107.5 2.3 %collective-permute-done.29 = bf16[32,2048]{1,0:T(8,128)(2,1)S(1)} collective-permute-done((bf16[32,2048]{1,0:T(8,128)(2,1)S(1)}, bf16[32,2048]{1,0:T(8,128)(2,1)S(1)}, u32[]{:S(2)}, u32[]{:S(2)}) %collective-permute-start.29) | collective-permute-done | bytes 131104 | tf_op jit(solution)/shard_map/ppermute | solution.py:103
  111.6 3.9 %collective-permute-done.31.refs_2_ = bf16[32,2048]{1,0:T(8,128)(2,1)S(1)} collective-permute-done((bf16[32,2048]{1,0:T(8,128)(2,1)S(1)}, bf16[32,2048]{1,0:T(8,128)(2,1)S(1)}, u32[]{:S(2)}, u32[]{:S(2)}) %collective-permute-start.31) | collective-permute-done | bytes 131104 | tf_op jit(solution)/shard_map/ppermute | solution.py:103
  121.8 3.3 %collective-permute-start.36 = (bf16[32,2048]{1,0:T(8,128)(2,1)S(1)}, bf16[32,2048]{1,0:T(8,128)(2,1)S(1)}, u32[]{:S(2)}, u32[]{:S(2)}) collective-permute-start(bf16[32,2048]{1,0:T(8,128)(2,1)S(1)} %get-tuple-element.46), channel_id=1, source_target_pairs={{0,16},{4,20},{8,24},{12,28},{16,0},{20,4},{24,8},{28,12},{1,17},{... | collective-permute-start | bytes 393224 | tf_op jit(solution)/shard_map/ppermute | solution.py:103
  126.5 2.4 %collective-permute-start.38 = (bf16[32,2048]{1,0:T(8,128)(2,1)S(1)}, bf16[32,2048]{1,0:T(8,128)(2,1)S(1)}, u32[]{:S(2)}, u32[]{:S(2)}) collective-permute-start(bf16[32,2048]{1,0:T(8,128)(2,1)S(1)} %get-tuple-element.48), channel_id=1, source_target_pairs={{0,24},{4,28},{8,16},{12,20},{16,8},{20,12},{24,0},{28,4},{1,25},{... | collective-permute-start | bytes 393224 | tf_op jit(solution)/shard_map/ppermute | solution.py:103
  131.3 13.5 %collective-permute-done.37 = bf16[32,2048]{1,0:T(8,128)(2,1)S(1)} collective-permute-done((bf16[32,2048]{1,0:T(8,128)(2,1)S(1)}, bf16[32,2048]{1,0:T(8,128)(2,1)S(1)}, u32[]{:S(2)}, u32[]{:S(2)}) %collective-permute-start.37) | collective-permute-done | bytes 131104 | tf_op jit(solution)/shard_map/ppermute | solution.py:103
  (90 shorter events, 40.4 us)
Async XLA Ops:
  1.7 9.5 %collective-permute-start.5 = (bf16[32,2048]{1,0:T(8,128)(2,1)S(1)}, bf16[32,2048]{1,0:T(8,128)(2,1)S(1)}, u32[]{:S(2)}, u32[]{:S(2)}) collective-permute-start(bf16[32,2048]{1,0:T(8,128)(2,1)S(1)} %bitcast.33), channel_id=1, source_target_pairs={{0,24},{4,28},{8,16},{12,20},{16,8},{20,12},{24,0},{28,4},{1,25},{... | collective-permute-start | bytes 393224 | tf_op jit(solution)/shard_map/ppermute | solution.py:103
  6.9 11.1 %collective-permute-start.3 = (bf16[32,2048]{1,0:T(8,128)(2,1)S(1)}, bf16[32,2048]{1,0:T(8,128)(2,1)S(1)}, u32[]{:S(2)}, u32[]{:S(2)}) collective-permute-start(bf16[32,2048]{1,0:T(8,128)(2,1)S(1)} %bitcast.34), channel_id=1, source_target_pairs={{0,16},{4,20},{8,24},{12,28},{16,0},{20,4},{24,8},{28,12},{1,17},{... | collective-permute-start | bytes 393224 | tf_op jit(solution)/shard_map/ppermute | solution.py:103
  6.9 12.6 %collective-permute-start.1 = (bf16[32,2048]{1,0:T(8,128)(2,1)S(1)}, bf16[32,2048]{1,0:T(8,128)(2,1)S(1)}, u32[]{:S(2)}, u32[]{:S(2)}) collective-permute-start(bf16[32,2048]{1,0:T(8,128)(2,1)S(1)} %bitcast.35), channel_id=1, source_target_pairs={{0,8},{4,12},{8,0},{12,4},{16,24},{20,28},{24,16},{28,20},{1,9},{5... | collective-permute-start | bytes 393224 | tf_op jit(solution)/shard_map/ppermute | solution.py:103
  7.5 14.0 %collective-permute-start = (bf16[32,2048]{1,0:T(8,128)(2,1)S(1)}, bf16[32,2048]{1,0:T(8,128)(2,1)S(1)}, u32[]{:S(2)}, u32[]{:S(2)}) collective-permute-start(bf16[32,2048]{1,0:T(8,128)(2,1)S(1)} %bitcast.36), channel_id=1, source_target_pairs={{0,4},{4,0},{8,12},{12,8},{16,20},{20,16},{24,28},{28,24},{1,5},{5... | collective-permute-start | bytes 393224 | tf_op jit(solution)/shard_map/ppermute | solution.py:103
  11.3 10.3 %collective-permute-start.6 = (bf16[32,2048]{1,0:T(8,128)(2,1)S(1)}, bf16[32,2048]{1,0:T(8,128)(2,1)S(1)}, u32[]{:S(2)}, u32[]{:S(2)}) collective-permute-start(bf16[32,2048]{1,0:T(8,128)(2,1)S(1)} %collective-permute-done.5.refs_6_), channel_id=1, source_target_pairs={{0,4},{4,0},{8,12},{12,8},{16,20},{20,16},{24,28},{28,24},{1,5},{5... | collective-permute-start | bytes 393224 | tf_op jit(solution)/shard_map/ppermute | solution.py:103
  47.8 8.0 %collective-permute-start.13 = (bf16[32,2048]{1,0:T(8,128)(2,1)S(1)}, bf16[32,2048]{1,0:T(8,128)(2,1)S(1)}, u32[]{:S(2)}, u32[]{:S(2)}) collective-permute-start(bf16[32,2048]{1,0:T(8,128)(2,1)S(1)} %get-tuple-element.31), channel_id=1, source_target_pairs={{0,4},{4,0},{8,12},{12,8},{16,20},{20,16},{24,28},{28,24},{1,5},{5... | collective-permute-start | bytes 393224 | tf_op jit(solution)/shard_map/ppermute | solution.py:103
  49.4 9.9 %collective-permute-start.14 = (bf16[32,2048]{1,0:T(8,128)(2,1)S(1)}, bf16[32,2048]{1,0:T(8,128)(2,1)S(1)}, u32[]{:S(2)}, u32[]{:S(2)}) collective-permute-start(bf16[32,2048]{1,0:T(8,128)(2,1)S(1)} %get-tuple-element.32), channel_id=1, source_target_pairs={{0,8},{4,12},{8,0},{12,4},{16,24},{20,28},{24,16},{28,20},{1,9},{5... | collective-permute-start | bytes 393224 | tf_op jit(solution)/shard_map/ppermute | solution.py:103
  51.2 11.2 %collective-permute-start.15 = (bf16[32,2048]{1,0:T(8,128)(2,1)S(1)}, bf16[32,2048]{1,0:T(8,128)(2,1)S(1)}, u32[]{:S(2)}, u32[]{:S(2)}) collective-permute-start(bf16[32,2048]{1,0:T(8,128)(2,1)S(1)} %get-tuple-element.33), channel_id=1, source_target_pairs={{0,12},{4,8},{8,4},{12,0},{16,28},{20,24},{24,20},{28,16},{1,13},{... | collective-permute-start | bytes 393224 | tf_op jit(solution)/shard_map/ppermute | solution.py:103
  51.4 10.9 %collective-permute-start.16 = (bf16[32,2048]{1,0:T(8,128)(2,1)S(1)}, bf16[32,2048]{1,0:T(8,128)(2,1)S(1)}, u32[]{:S(2)}, u32[]{:S(2)}) collective-permute-start(bf16[32,2048]{1,0:T(8,128)(2,1)S(1)} %get-tuple-element.34), channel_id=1, source_target_pairs={{0,16},{4,20},{8,24},{12,28},{16,0},{20,4},{24,8},{28,12},{1,17},{... | collective-permute-start | bytes 393224 | tf_op jit(solution)/shard_map/ppermute | solution.py:103
  54.4 19.8 %collective-permute-start.17 = (bf16[32,2048]{1,0:T(8,128)(2,1)S(1)}, bf16[32,2048]{1,0:T(8,128)(2,1)S(1)}, u32[]{:S(2)}, u32[]{:S(2)}) collective-permute-start(bf16[32,2048]{1,0:T(8,128)(2,1)S(1)} %get-tuple-element.35), channel_id=1, source_target_pairs={{0,20},{4,16},{8,28},{12,24},{16,4},{20,0},{24,12},{28,8},{1,21},{... | collective-permute-start | bytes 393224 | tf_op jit(solution)/shard_map/ppermute | solution.py:103
  55.8 18.4 %collective-permute-start.18 = (bf16[32,2048]{1,0:T(8,128)(2,1)S(1)}, bf16[32,2048]{1,0:T(8,128)(2,1)S(1)}, u32[]{:S(2)}, u32[]{:S(2)}) collective-permute-start(bf16[32,2048]{1,0:T(8,128)(2,1)S(1)} %get-tuple-element.36), channel_id=1, source_target_pairs={{0,24},{4,28},{8,16},{12,20},{16,8},{20,12},{24,0},{28,4},{1,25},{... | collective-permute-start | bytes 393224 | tf_op jit(solution)/shard_map/ppermute | solution.py:103
  59.3 14.9 %collective-permute-start.19 = (bf16[32,2048]{1,0:T(8,128)(2,1)S(1)}, bf16[32,2048]{1,0:T(8,128)(2,1)S(1)}, u32[]{:S(2)}, u32[]{:S(2)}) collective-permute-start(bf16[32,2048]{1,0:T(8,128)(2,1)S(1)} %get-tuple-element.37), channel_id=1, source_target_pairs={{0,28},{4,24},{8,20},{12,16},{16,12},{20,8},{24,4},{28,0},{1,29},{... | collective-permute-start | bytes 393224 | tf_op jit(solution)/shard_map/ppermute | solution.py:103
  74.5 9.0 %collective-permute-start.25 = (bf16[32,2048]{1,0:T(8,128)(2,1)S(1)}, bf16[32,2048]{1,0:T(8,128)(2,1)S(1)}, u32[]{:S(2)}, u32[]{:S(2)}) collective-permute-start(bf16[32,2048]{1,0:T(8,128)(2,1)S(1)} %get-tuple-element.54.refs_0_), channel_id=1, source_target_pairs={{0,24},{4,28},{8,16},{12,20},{16,8},{20,12},{24,0},{28,4},{1,25},{... | collective-permute-start | bytes 393224 | tf_op jit(solution)/shard_map/ppermute | solution.py:103
  78.1 11.7 %collective-permute-start.23 = (bf16[32,2048]{1,0:T(8,128)(2,1)S(1)}, bf16[32,2048]{1,0:T(8,128)(2,1)S(1)}, u32[]{:S(2)}, u32[]{:S(2)}) collective-permute-start(bf16[32,2048]{1,0:T(8,128)(2,1)S(1)} %get-tuple-element.54.refs_0_), channel_id=1, source_target_pairs={{0,16},{4,20},{8,24},{12,28},{16,0},{20,4},{24,8},{28,12},{1,17},{... | collective-permute-start | bytes 393224 | tf_op jit(solution)/shard_map/ppermute | solution.py:103
  83.3 8.4 %collective-permute-start.20 = (bf16[32,2048]{1,0:T(8,128)(2,1)S(1)}, bf16[32,2048]{1,0:T(8,128)(2,1)S(1)}, u32[]{:S(2)}, u32[]{:S(2)}) collective-permute-start(bf16[32,2048]{1,0:T(8,128)(2,1)S(1)} %get-tuple-element.54.refs_0_), channel_id=1, source_target_pairs={{0,4},{4,0},{8,12},{12,8},{16,20},{20,16},{24,28},{28,24},{1,5},{5... | collective-permute-start | bytes 393224 | tf_op jit(solution)/shard_map/ppermute | solution.py:103
  83.4 8.3 %collective-permute-start.26 = (bf16[32,2048]{1,0:T(8,128)(2,1)S(1)}, bf16[32,2048]{1,0:T(8,128)(2,1)S(1)}, u32[]{:S(2)}, u32[]{:S(2)}) collective-permute-start(bf16[32,2048]{1,0:T(8,128)(2,1)S(1)} %collective-permute-done.25.refs_6_), channel_id=1, source_target_pairs={{0,4},{4,0},{8,12},{12,8},{16,20},{20,16},{24,28},{28,24},{1,5},{5... | collective-permute-start | bytes 393224 | tf_op jit(solution)/shard_map/ppermute | solution.py:103
  97.3 10.1 %collective-permute-start.28 = (bf16[32,2048]{1,0:T(8,128)(2,1)S(1)}, bf16[32,2048]{1,0:T(8,128)(2,1)S(1)}, u32[]{:S(2)}, u32[]{:S(2)}) collective-permute-start(bf16[32,2048]{1,0:T(8,128)(2,1)S(1)} %get-tuple-element.40), channel_id=1, source_target_pairs={{0,2},{1,3},{2,0},{3,1},{4,6},{5,7},{6,4},{7,5},{8,10},{9,11},{10,... | collective-permute-start | bytes 393224 | tf_op jit(solution)/shard_map/ppermute | solution.py:103
  118.3 8.2 %collective-permute-start.33 = (bf16[32,2048]{1,0:T(8,128)(2,1)S(1)}, bf16[32,2048]{1,0:T(8,128)(2,1)S(1)}, u32[]{:S(2)}, u32[]{:S(2)}) collective-permute-start(bf16[32,2048]{1,0:T(8,128)(2,1)S(1)} %get-tuple-element.43), channel_id=1, source_target_pairs={{0,4},{4,0},{8,12},{12,8},{16,20},{20,16},{24,28},{28,24},{1,5},{5... | collective-permute-start | bytes 393224 | tf_op jit(solution)/shard_map/ppermute | solution.py:103
  120.1 10.2 %collective-permute-start.34 = (bf16[32,2048]{1,0:T(8,128)(2,1)S(1)}, bf16[32,2048]{1,0:T(8,128)(2,1)S(1)}, u32[]{:S(2)}, u32[]{:S(2)}) collective-permute-start(bf16[32,2048]{1,0:T(8,128)(2,1)S(1)} %get-tuple-element.44), channel_id=1, source_target_pairs={{0,8},{4,12},{8,0},{12,4},{16,24},{20,28},{24,16},{28,20},{1,9},{5... | collective-permute-start | bytes 393224 | tf_op jit(solution)/shard_map/ppermute | solution.py:103
  121.3 10.0 %collective-permute-start.35 = (bf16[32,2048]{1,0:T(8,128)(2,1)S(1)}, bf16[32,2048]{1,0:T(8,128)(2,1)S(1)}, u32[]{:S(2)}, u32[]{:S(2)}) collective-permute-start(bf16[32,2048]{1,0:T(8,128)(2,1)S(1)} %get-tuple-element.45), channel_id=1, source_target_pairs={{0,12},{4,8},{8,4},{12,0},{16,28},{20,24},{24,20},{28,16},{1,13},{... | collective-permute-start | bytes 393224 | tf_op jit(solution)/shard_map/ppermute | solution.py:103
  121.8 9.5 %collective-permute-start.36 = (bf16[32,2048]{1,0:T(8,128)(2,1)S(1)}, bf16[32,2048]{1,0:T(8,128)(2,1)S(1)}, u32[]{:S(2)}, u32[]{:S(2)}) collective-permute-start(bf16[32,2048]{1,0:T(8,128)(2,1)S(1)} %get-tuple-element.46), channel_id=1, source_target_pairs={{0,16},{4,20},{8,24},{12,28},{16,0},{20,4},{24,8},{28,12},{1,17},{... | collective-permute-start | bytes 393224 | tf_op jit(solution)/shard_map/ppermute | solution.py:103
  125.1 19.7 %collective-permute-start.37 = (bf16[32,2048]{1,0:T(8,128)(2,1)S(1)}, bf16[32,2048]{1,0:T(8,128)(2,1)S(1)}, u32[]{:S(2)}, u32[]{:S(2)}) collective-permute-start(bf16[32,2048]{1,0:T(8,128)(2,1)S(1)} %get-tuple-element.47), channel_id=1, source_target_pairs={{0,20},{4,16},{8,28},{12,24},{16,4},{20,0},{24,12},{28,8},{1,21},{... | collective-permute-start | bytes 393224 | tf_op jit(solution)/shard_map/ppermute | solution.py:103
  126.5 18.4 %collective-permute-start.38 = (bf16[32,2048]{1,0:T(8,128)(2,1)S(1)}, bf16[32,2048]{1,0:T(8,128)(2,1)S(1)}, u32[]{:S(2)}, u32[]{:S(2)}) collective-permute-start(bf16[32,2048]{1,0:T(8,128)(2,1)S(1)} %get-tuple-element.48), channel_id=1, source_target_pairs={{0,24},{4,28},{8,16},{12,20},{16,8},{20,12},{24,0},{28,4},{1,25},{... | collective-permute-start | bytes 393224 | tf_op jit(solution)/shard_map/ppermute | solution.py:103
  130.3 14.5 %collective-permute-start.39 = (bf16[32,2048]{1,0:T(8,128)(2,1)S(1)}, bf16[32,2048]{1,0:T(8,128)(2,1)S(1)}, u32[]{:S(2)}, u32[]{:S(2)}) collective-permute-start(bf16[32,2048]{1,0:T(8,128)(2,1)S(1)} %get-tuple-element.49), channel_id=1, source_target_pairs={{0,28},{4,24},{8,20},{12,16},{16,12},{20,8},{24,4},{28,0},{1,29},{... | collective-permute-start | bytes 393224 | tf_op jit(solution)/shard_map/ppermute | solution.py:103
  (25 other events, 374.4 us)

commit v2 on v1

--- a/solution.py
+++ b/solution.py
@@ -68,19 +68,19 @@
             )
 
 
-def sweep(forward, tiles, info, parts, outs, per_in, per_out, blocks_out):
+def sweep(forward, tiles, info, parts, kinds, per_in, per_out, blocks_out):
     slots, rows_tile, cols_tile = tiles.shape
     width = parts[0].shape[0]
     span_in, span_out = (cols_tile, rows_tile) if forward else (rows_tile, cols_tile)
     pieces = len(parts)
+    outs = len(kinds)
     vmem = pl.BlockSpec(memory_space=pltpu.VMEM)
     return pl.pallas_call(
         functools.partial(sweep_kernel, forward, pieces, outs, per_in, per_out),
         out_shape=[
-            jax.ShapeDtypeStruct((width, per_out * span_out), jnp.bfloat16)
-        ]
-        * outs,
-        in_specs=[pl.BlockSpec(memory_space=pltpu.SMEM), pl.BlockSpec(memory_space=pl.ANY)]
+            jax.ShapeDtypeStruct((width, per_out * span_out), kind) for kind in kinds
+        ],
+        in_specs=[pl.BlockSpec(memory_space=pltpu.SMEM), pl.BlockSpec(memory_space=pltpu.HBM)]
         + [vmem] * pieces,
         out_specs=[vmem] * outs,
         scratch_shapes=[
@@ -111,6 +111,16 @@
     for k in range(0, size, 2):
         parts[k + 1] = swap(parts[k], axis, size, 1)
     return parts
+
+
+def sum_pairs(parts, axis, size):
+    total = None
+    for k in range(size - 2, -1, -2):
+        pair = parts[k] + swap(parts[k + 1], axis, size, 1).astype(jnp.float32)
+        if k:
+            pair = swap(pair.astype(jnp.bfloat16), axis, size, k).astype(jnp.float32)
+        total = pair if total is None else total + pair
+    return total
 
 
 def sum_direct(parts, axis, size):
@@ -149,11 +159,13 @@
     per_row = dual.shape[1] // blocks.shape[1]
     per_col = primal.shape[1] // blocks.shape[2]
     share = weights[:, None]
+    pull_kinds = [jnp.float32] + [jnp.bfloat16] * (rows - 1)
+    push_kinds = [jnp.float32, jnp.bfloat16] * (cols // 2)
     cost = share * carbon + (1.0 - share) * completion
     for step in range(ITERS):
         dual_parts = gather_pairs(dual.astype(jnp.bfloat16), "col", cols)
         pull_parts = sweep(
-            False, blocks, info, dual_parts, rows, per_row, per_col, BC_DEV
+            False, blocks, info, dual_parts, pull_kinds, per_row, per_col, BC_DEV
         )
         pull = sum_direct(pull_parts, "row", rows)
         fresh = jnp.maximum(primal - step_primal * (cost - pull), 0.0)
@@ -161,9 +173,9 @@
         primal = fresh
         extra_parts = gather_pairs(extra, "row", rows)
         push_parts = sweep(
-            True, blocks, info_back, extra_parts, cols, per_col, per_row, BR_DEV
+            True, blocks, info_back, extra_parts, push_kinds, per_col, per_row, BR_DEV
         )
-        push = sum_direct(push_parts, "col", cols)
+        push = sum_pairs(push_parts, "col", cols)
         moved = dual + step_dual * (demand - push)
         dual = jnp.where(row_kind == 1, jnp.maximum(moved, 0.0), moved)
     return (primal[:, None, :], dual[:, None, :])

time: 148 us -> 130 us (0.88)
  waiting for transfers between devices: 70.1 us -> 59 us
  starting transfers between devices: 61.1 us -> 55.3 us
    ppermute x40, waiting for transfers between devices: 70.1 us -> 59 us  [swap(): return lax.ppermute(value, axis, [(i, i ^ k) for i in range(size)])]
    ppermute x40, starting transfers between devices: 61.1 us -> 55.3 us  [swap(): return lax.ppermute(value, axis, [(i, i ^ k) for i in range(size)])]
  transfers between devices with their start and end apart: 40 -> 40, of which waited for: 18 -> 22; matrix products, arithmetic and copies ran while one was open for 1% -> 2% of each run, Pallas kernels for 0% -> 0%
where the time goes in v2:
time: 130 us; the launch traced here: 129 us
  waiting for transfers between devices  59 us (45%)
  starting transfers between devices  55.3 us (43%)
  local copies, waits for them, and re-layouts  7.27 us (6%)
  Pallas kernels  5.12 us (4%)
  between operations  1.47 us (1%)
    ppermute x40, waiting for transfers between devices, swap(): return lax.ppermute(value, axis, [(i, i ^ k) for i in range(size)])  59 us
    ppermute x40, starting transfers between devices, swap(): return lax.ppermute(value, axis, [(i, i ^ k) for i in range(size)])  55.3 us
    unnamed x22, local copies, waits for them, and re-layouts  7.19 us
    pallas_call x4, Pallas kernels, sweep(): pl.pallas_call(functools.partial(sweep_kernel, forward, pieces, outs, per...  5.12 us
  transfers between devices with their start and end apart: 40, of which 22 were waited for; matrix products, arithmetic and copies ran while one was open for 2% of the time, Pallas kernels for 0%

profile of v2, /device:TPU:0, one launch (start us, length us, event | category | flops | bytes accessed | tf_op | source)
XLA Modules:
  0.0 129.2 jit_solution(10011226305958413589)
XLA Ops:
  1.7 5.1 %collective-permute-start.5 = (bf16[32,2048]{1,0:T(8,128)(2,1)S(1)}, bf16[32,2048]{1,0:T(8,128)(2,1)S(1)}, u32[]{:S(2)}, u32[]{:S(2)}) collective-permute-start(bf16[32,2048]{1,0:T(8,128)(2,1)S(1)} %bitcast.33), channel_id=1, source_target_pairs={{0,24},{4,28},{8,16},{12,20},{16,8},{20,12},{24,0},{28,4},{1,25},{... | collective-permute-start | bytes 393224 | tf_op jit(solution)/shard_map/ppermute | solution.py:103
  9.1 2.1 %collective-permute-done.5.refs_6_ = bf16[32,2048]{1,0:T(8,128)(2,1)S(1)} collective-permute-done((bf16[32,2048]{1,0:T(8,128)(2,1)S(1)}, bf16[32,2048]{1,0:T(8,128)(2,1)S(1)}, u32[]{:S(2)}, u32[]{:S(2)}) %collective-permute-start.5) | collective-permute-done | bytes 131104 | tf_op jit(solution)/shard_map/ppermute | solution.py:103
  13.0 5.0 %collective-permute-done.3.refs_4_ = bf16[32,2048]{1,0:T(8,128)(2,1)S(1)} collective-permute-done((bf16[32,2048]{1,0:T(8,128)(2,1)S(1)}, bf16[32,2048]{1,0:T(8,128)(2,1)S(1)}, u32[]{:S(2)}, u32[]{:S(2)}) %collective-permute-start.3) | collective-permute-done | bytes 131104 | tf_op jit(solution)/shard_map/ppermute | solution.py:103
  21.6 2.3 %collective-permute-done.4.refs_5_ = bf16[32,2048]{1,0:T(8,128)(2,1)S(1)} collective-permute-done((bf16[32,2048]{1,0:T(8,128)(2,1)S(1)}, bf16[32,2048]{1,0:T(8,128)(2,1)S(1)}, u32[]{:S(2)}, u32[]{:S(2)}) %collective-permute-start.4) | collective-permute-done | bytes 131104 | tf_op jit(solution)/shard_map/ppermute | solution.py:103
  25.3 3.4 %copy-done = bf16[1,1,8,1024,512]{4,3,2,1,0:T(8,128)(2,1)S(1)} copy-done((bf16[1,1,8,1024,512]{4,3,2,1,0:T(8,128)(2,1)S(1)}, bf16[1,1,8,1024,512]{4,3,2,1,0:T(8,128)(2,1)}, u32[]{:S(2)}) %copy-start) | copy-done | bytes 8388632
  31.8 4.5 %collective-permute-done.8 = bf16[32,2048]{1,0:T(8,128)(2,1)S(1)} collective-permute-done((bf16[32,2048]{1,0:T(8,128)(2,1)S(1)}, bf16[32,2048]{1,0:T(8,128)(2,1)S(1)}, u32[]{:S(2)}, u32[]{:S(2)}) %collective-permute-start.8) | collective-permute-done | bytes 131104 | tf_op jit(solution)/shard_map/ppermute | solution.py:103
  40.0 4.2 %collective-permute-done.11.refs_2_ = bf16[32,2048]{1,0:T(8,128)(2,1)S(1)} collective-permute-done((bf16[32,2048]{1,0:T(8,128)(2,1)S(1)}, bf16[32,2048]{1,0:T(8,128)(2,1)S(1)}, u32[]{:S(2)}, u32[]{:S(2)}) %collective-permute-start.11) | collective-permute-done | bytes 131104 | tf_op jit(solution)/shard_map/ppermute | solution.py:103
  46.9 3.0 %collective-permute-start.13 = (bf16[32,2048]{1,0:T(8,128)(2,1)S(1)}, bf16[32,2048]{1,0:T(8,128)(2,1)S(1)}, u32[]{:S(2)}, u32[]{:S(2)}) collective-permute-start(bf16[32,2048]{1,0:T(8,128)(2,1)S(1)} %get-tuple-element.31), channel_id=1, source_target_pairs={{0,4},{4,0},{8,12},{12,8},{16,20},{20,16},{24,28},{28,24},{1,5},{5... | collective-permute-start | bytes 393224 | tf_op jit(solution)/shard_map/ppermute | solution.py:103
  50.0 2.0 %collective-permute-start.17 = (bf16[32,2048]{1,0:T(8,128)(2,1)S(1)}, bf16[32,2048]{1,0:T(8,128)(2,1)S(1)}, u32[]{:S(2)}, u32[]{:S(2)}) collective-permute-start(bf16[32,2048]{1,0:T(8,128)(2,1)S(1)} %get-tuple-element.35), channel_id=1, source_target_pairs={{0,4},{4,0},{8,12},{12,8},{16,20},{20,16},{24,28},{28,24},{1,5},{5... | collective-permute-start | bytes 393224 | tf_op jit(solution)/shard_map/ppermute | solution.py:103
  52.1 2.2 %collective-permute-done.13 = bf16[32,2048]{1,0:T(8,128)(2,1)S(1)} collective-permute-done((bf16[32,2048]{1,0:T(8,128)(2,1)S(1)}, bf16[32,2048]{1,0:T(8,128)(2,1)S(1)}, u32[]{:S(2)}, u32[]{:S(2)}) %collective-permute-start.13) | collective-permute-done | bytes 131104 | tf_op jit(solution)/shard_map/ppermute | solution.py:103
  54.4 2.2 %collective-permute-start.14 = (bf16[32,2048]{1,0:T(8,128)(2,1)S(1)}, bf16[32,2048]{1,0:T(8,128)(2,1)S(1)}, u32[]{:S(2)}, u32[]{:S(2)}) collective-permute-start(bf16[32,2048]{1,0:T(8,128)(2,1)S(1)} %add_convert_fusion.5), channel_id=1, source_target_pairs={{0,24},{4,28},{8,16},{12,20},{16,8},{20,12},{24,0},{28,4},{1,25},{... | collective-permute-start | bytes 393224 | tf_op jit(solution)/shard_map/ppermute | solution.py:103
  57.2 5.1 %collective-permute-start.16 = (bf16[32,2048]{1,0:T(8,128)(2,1)S(1)}, bf16[32,2048]{1,0:T(8,128)(2,1)S(1)}, u32[]{:S(2)}, u32[]{:S(2)}) collective-permute-start(bf16[32,2048]{1,0:T(8,128)(2,1)S(1)} %add_convert_fusion.4), channel_id=1, source_target_pairs={{0,16},{4,20},{8,24},{12,28},{16,0},{20,4},{24,8},{28,12},{1,17},{... | collective-permute-start | bytes 393224 | tf_op jit(solution)/shard_map/ppermute | solution.py:103
  63.9 4.8 %collective-permute-done.16 = bf16[32,2048]{1,0:T(8,128)(2,1)S(1)} collective-permute-done((bf16[32,2048]{1,0:T(8,128)(2,1)S(1)}, bf16[32,2048]{1,0:T(8,128)(2,1)S(1)}, u32[]{:S(2)}, u32[]{:S(2)}) %collective-permute-start.16) | collective-permute-done | bytes 131104 | tf_op jit(solution)/shard_map/ppermute | solution.py:103
  68.9 3.4 %collective-permute-start.25 = (bf16[32,2048]{1,0:T(8,128)(2,1)S(1)}, bf16[32,2048]{1,0:T(8,128)(2,1)S(1)}, u32[]{:S(2)}, u32[]{:S(2)}) collective-permute-start(bf16[32,2048]{1,0:T(8,128)(2,1)S(1)} %get-tuple-element.54.refs_0_), channel_id=1, source_target_pairs={{0,24},{4,28},{8,16},{12,20},{16,8},{20,12},{24,0},{28,4},{1,25},{... | collective-permute-start | bytes 393224 | tf_op jit(solution)/shard_map/ppermute | solution.py:103
  74.9 2.3 %collective-permute-done.25.refs_6_ = bf16[32,2048]{1,0:T(8,128)(2,1)S(1)} collective-permute-done((bf16[32,2048]{1,0:T(8,128)(2,1)S(1)}, bf16[32,2048]{1,0:T(8,128)(2,1)S(1)}, u32[]{:S(2)}, u32[]{:S(2)}) %collective-permute-start.25) | collective-permute-done | bytes 131104 | tf_op jit(solution)/shard_map/ppermute | solution.py:103
  80.5 2.5 %collective-permute-start.24 = (bf16[32,2048]{1,0:T(8,128)(2,1)S(1)}, bf16[32,2048]{1,0:T(8,128)(2,1)S(1)}, u32[]{:S(2)}, u32[]{:S(2)}) collective-permute-start(bf16[32,2048]{1,0:T(8,128)(2,1)S(1)} %collective-permute-done.23.refs_4_), channel_id=1, source_target_pairs={{0,4},{4,0},{8,12},{12,8},{16,20},{20,16},{24,28},{28,24},{1,5},{5... | collective-permute-start | bytes 393224 | tf_op jit(solution)/shard_map/ppermute | solution.py:103
  83.1 3.9 %collective-permute-done.24.refs_5_ = bf16[32,2048]{1,0:T(8,128)(2,1)S(1)} collective-permute-done((bf16[32,2048]{1,0:T(8,128)(2,1)S(1)}, bf16[32,2048]{1,0:T(8,128)(2,1)S(1)}, u32[]{:S(2)}, u32[]{:S(2)}) %collective-permute-start.24) | collective-permute-done | bytes 131104 | tf_op jit(solution)/shard_map/ppermute | solution.py:103
  91.5 4.5 %collective-permute-done.28 = bf16[32,2048]{1,0:T(8,128)(2,1)S(1)} collective-permute-done((bf16[32,2048]{1,0:T(8,128)(2,1)S(1)}, bf16[32,2048]{1,0:T(8,128)(2,1)S(1)}, u32[]{:S(2)}, u32[]{:S(2)}) %collective-permute-start.28) | collective-permute-done | bytes 131104 | tf_op jit(solution)/shard_map/ppermute | solution.py:103
  98.5 5.3 %collective-permute-done.31.refs_2_ = bf16[32,2048]{1,0:T(8,128)(2,1)S(1)} collective-permute-done((bf16[32,2048]{1,0:T(8,128)(2,1)S(1)}, bf16[32,2048]{1,0:T(8,128)(2,1)S(1)}, u32[]{:S(2)}, u32[]{:S(2)}) %collective-permute-start.31) | collective-permute-done | bytes 131104 | tf_op jit(solution)/shard_map/ppermute | solution.py:103
  106.5 2.7 %collective-permute-start.33 = (bf16[32,2048]{1,0:T(8,128)(2,1)S(1)}, bf16[32,2048]{1,0:T(8,128)(2,1)S(1)}, u32[]{:S(2)}, u32[]{:S(2)}) collective-permute-start(bf16[32,2048]{1,0:T(8,128)(2,1)S(1)} %get-tuple-element.43), channel_id=1, source_target_pairs={{0,4},{4,0},{8,12},{12,8},{16,20},{20,16},{24,28},{28,24},{1,5},{5... | collective-permute-start | bytes 393224 | tf_op jit(solution)/shard_map/ppermute | solution.py:103
  111.3 2.1 %collective-permute-done.33 = bf16[32,2048]{1,0:T(8,128)(2,1)S(1)} collective-permute-done((bf16[32,2048]{1,0:T(8,128)(2,1)S(1)}, bf16[32,2048]{1,0:T(8,128)(2,1)S(1)}, u32[]{:S(2)}, u32[]{:S(2)}) %collective-permute-start.33) | collective-permute-done | bytes 131104 | tf_op jit(solution)/shard_map/ppermute | solution.py:103
  113.5 2.4 %collective-permute-start.34 = (bf16[32,2048]{1,0:T(8,128)(2,1)S(1)}, bf16[32,2048]{1,0:T(8,128)(2,1)S(1)}, u32[]{:S(2)}, u32[]{:S(2)}) collective-permute-start(bf16[32,2048]{1,0:T(8,128)(2,1)S(1)} %add_convert_fusion.2), channel_id=1, source_target_pairs={{0,24},{4,28},{8,16},{12,20},{16,8},{20,12},{24,0},{28,4},{1,25},{... | collective-permute-start | bytes 393224 | tf_op jit(solution)/shard_map/ppermute | solution.py:103
  116.3 5.6 %collective-permute-start.36 = (bf16[32,2048]{1,0:T(8,128)(2,1)S(1)}, bf16[32,2048]{1,0:T(8,128)(2,1)S(1)}, u32[]{:S(2)}, u32[]{:S(2)}) collective-permute-start(bf16[32,2048]{1,0:T(8,128)(2,1)S(1)} %add_convert_fusion.1), channel_id=1, source_target_pairs={{0,16},{4,20},{8,24},{12,28},{16,0},{20,4},{24,8},{28,12},{1,17},{... | collective-permute-start | bytes 393224 | tf_op jit(solution)/shard_map/ppermute | solution.py:103
  124.4 3.7 %collective-permute-done.36 = bf16[32,2048]{1,0:T(8,128)(2,1)S(1)} collective-permute-done((bf16[32,2048]{1,0:T(8,128)(2,1)S(1)}, bf16[32,2048]{1,0:T(8,128)(2,1)S(1)}, u32[]{:S(2)}, u32[]{:S(2)}) %collective-permute-start.36) | collective-permute-done | bytes 131104 | tf_op jit(solution)/shard_map/ppermute | solution.py:103
  (96 shorter events, 43.5 us)
Async XLA Ops:
  1.7 9.5 %collective-permute-start.5 = (bf16[32,2048]{1,0:T(8,128)(2,1)S(1)}, bf16[32,2048]{1,0:T(8,128)(2,1)S(1)}, u32[]{:S(2)}, u32[]{:S(2)}) collective-permute-start(bf16[32,2048]{1,0:T(8,128)(2,1)S(1)} %bitcast.33), channel_id=1, source_target_pairs={{0,24},{4,28},{8,16},{12,20},{16,8},{20,12},{24,0},{28,4},{1,25},{... | collective-permute-start | bytes 393224 | tf_op jit(solution)/shard_map/ppermute | solution.py:103
  6.9 11.1 %collective-permute-start.3 = (bf16[32,2048]{1,0:T(8,128)(2,1)S(1)}, bf16[32,2048]{1,0:T(8,128)(2,1)S(1)}, u32[]{:S(2)}, u32[]{:S(2)}) collective-permute-start(bf16[32,2048]{1,0:T(8,128)(2,1)S(1)} %bitcast.34), channel_id=1, source_target_pairs={{0,16},{4,20},{8,24},{12,28},{16,0},{20,4},{24,8},{28,12},{1,17},{... | collective-permute-start | bytes 393224 | tf_op jit(solution)/shard_map/ppermute | solution.py:103
  6.9 12.6 %collective-permute-start.1 = (bf16[32,2048]{1,0:T(8,128)(2,1)S(1)}, bf16[32,2048]{1,0:T(8,128)(2,1)S(1)}, u32[]{:S(2)}, u32[]{:S(2)}) collective-permute-start(bf16[32,2048]{1,0:T(8,128)(2,1)S(1)} %bitcast.35), channel_id=1, source_target_pairs={{0,8},{4,12},{8,0},{12,4},{16,24},{20,28},{24,16},{28,20},{1,9},{5... | collective-permute-start | bytes 393224 | tf_op jit(solution)/shard_map/ppermute | solution.py:103
  7.5 14.0 %collective-permute-start = (bf16[32,2048]{1,0:T(8,128)(2,1)S(1)}, bf16[32,2048]{1,0:T(8,128)(2,1)S(1)}, u32[]{:S(2)}, u32[]{:S(2)}) collective-permute-start(bf16[32,2048]{1,0:T(8,128)(2,1)S(1)} %bitcast.36), channel_id=1, source_target_pairs={{0,4},{4,0},{8,12},{12,8},{16,20},{20,16},{24,28},{28,24},{1,5},{5... | collective-permute-start | bytes 393224 | tf_op jit(solution)/shard_map/ppermute | solution.py:103
  11.3 10.3 %collective-permute-start.6 = (bf16[32,2048]{1,0:T(8,128)(2,1)S(1)}, bf16[32,2048]{1,0:T(8,128)(2,1)S(1)}, u32[]{:S(2)}, u32[]{:S(2)}) collective-permute-start(bf16[32,2048]{1,0:T(8,128)(2,1)S(1)} %collective-permute-done.5.refs_6_), channel_id=1, source_target_pairs={{0,4},{4,0},{8,12},{12,8},{16,20},{20,16},{24,28},{28,24},{1,5},{5... | collective-permute-start | bytes 393224 | tf_op jit(solution)/shard_map/ppermute | solution.py:103
  31.5 6.7 %collective-permute-start.9 = (bf16[32,2048]{1,0:T(8,128)(2,1)S(1)}, bf16[32,2048]{1,0:T(8,128)(2,1)S(1)}, u32[]{:S(2)}, u32[]{:S(2)}) collective-permute-start(bf16[32,2048]{1,0:T(8,128)(2,1)S(1)} %get-tuple-element.29), channel_id=1, source_target_pairs={{0,3},{1,2},{2,1},{3,0},{4,7},{5,6},{6,5},{7,4},{8,11},{9,10},{10,... | collective-permute-start | bytes 393224 | tf_op jit(solution)/shard_map/ppermute | solution.py:103
  46.9 7.4 %collective-permute-start.13 = (bf16[32,2048]{1,0:T(8,128)(2,1)S(1)}, bf16[32,2048]{1,0:T(8,128)(2,1)S(1)}, u32[]{:S(2)}, u32[]{:S(2)}) collective-permute-start(bf16[32,2048]{1,0:T(8,128)(2,1)S(1)} %get-tuple-element.31), channel_id=1, source_target_pairs={{0,4},{4,0},{8,12},{12,8},{16,20},{20,16},{24,28},{28,24},{1,5},{5... | collective-permute-start | bytes 393224 | tf_op jit(solution)/shard_map/ppermute | solution.py:103
  50.0 7.2 %collective-permute-start.15 = (bf16[32,2048]{1,0:T(8,128)(2,1)S(1)}, bf16[32,2048]{1,0:T(8,128)(2,1)S(1)}, u32[]{:S(2)}, u32[]{:S(2)}) collective-permute-start(bf16[32,2048]{1,0:T(8,128)(2,1)S(1)} %get-tuple-element.33), channel_id=1, source_target_pairs={{0,4},{4,0},{8,12},{12,8},{16,20},{20,16},{24,28},{28,24},{1,5},{5... | collective-permute-start | bytes 393224 | tf_op jit(solution)/shard_map/ppermute | solution.py:103
  50.0 12.2 %collective-permute-start.17 = (bf16[32,2048]{1,0:T(8,128)(2,1)S(1)}, bf16[32,2048]{1,0:T(8,128)(2,1)S(1)}, u32[]{:S(2)}, u32[]{:S(2)}) collective-permute-start(bf16[32,2048]{1,0:T(8,128)(2,1)S(1)} %get-tuple-element.35), channel_id=1, source_target_pairs={{0,4},{4,0},{8,12},{12,8},{16,20},{20,16},{24,28},{28,24},{1,5},{5... | collective-permute-start | bytes 393224 | tf_op jit(solution)/shard_map/ppermute | solution.py:103
  52.0 11.9 %collective-permute-start.19 = (bf16[32,2048]{1,0:T(8,128)(2,1)S(1)}, bf16[32,2048]{1,0:T(8,128)(2,1)S(1)}, u32[]{:S(2)}, u32[]{:S(2)}) collective-permute-start(bf16[32,2048]{1,0:T(8,128)(2,1)S(1)} %get-tuple-element.37), channel_id=1, source_target_pairs={{0,4},{4,0},{8,12},{12,8},{16,20},{20,16},{24,28},{28,24},{1,5},{5... | collective-permute-start | bytes 393224 | tf_op jit(solution)/shard_map/ppermute | solution.py:103
  54.4 9.5 %collective-permute-start.14 = (bf16[32,2048]{1,0:T(8,128)(2,1)S(1)}, bf16[32,2048]{1,0:T(8,128)(2,1)S(1)}, u32[]{:S(2)}, u32[]{:S(2)}) collective-permute-start(bf16[32,2048]{1,0:T(8,128)(2,1)S(1)} %add_convert_fusion.5), channel_id=1, source_target_pairs={{0,24},{4,28},{8,16},{12,20},{16,8},{20,12},{24,0},{28,4},{1,25},{... | collective-permute-start | bytes 393224 | tf_op jit(solution)/shard_map/ppermute | solution.py:103
  57.2 11.5 %collective-permute-start.16 = (bf16[32,2048]{1,0:T(8,128)(2,1)S(1)}, bf16[32,2048]{1,0:T(8,128)(2,1)S(1)}, u32[]{:S(2)}, u32[]{:S(2)}) collective-permute-start(bf16[32,2048]{1,0:T(8,128)(2,1)S(1)} %add_convert_fusion.4), channel_id=1, source_target_pairs={{0,16},{4,20},{8,24},{12,28},{16,0},{20,4},{24,8},{28,12},{1,17},{... | collective-permute-start | bytes 393224 | tf_op jit(solution)/shard_map/ppermute | solution.py:103
  68.9 8.3 %collective-permute-start.25 = (bf16[32,2048]{1,0:T(8,128)(2,1)S(1)}, bf16[32,2048]{1,0:T(8,128)(2,1)S(1)}, u32[]{:S(2)}, u32[]{:S(2)}) collective-permute-start(bf16[32,2048]{1,0:T(8,128)(2,1)S(1)} %get-tuple-element.54.refs_0_), channel_id=1, source_target_pairs={{0,24},{4,28},{8,16},{12,20},{16,8},{20,12},{24,0},{28,4},{1,25},{... | collective-permute-start | bytes 393224 | tf_op jit(solution)/shard_map/ppermute | solution.py:103
  72.3 8.2 %collective-permute-start.23 = (bf16[32,2048]{1,0:T(8,128)(2,1)S(1)}, bf16[32,2048]{1,0:T(8,128)(2,1)S(1)}, u32[]{:S(2)}, u32[]{:S(2)}) collective-permute-start(bf16[32,2048]{1,0:T(8,128)(2,1)S(1)} %get-tuple-element.54.refs_0_), channel_id=1, source_target_pairs={{0,16},{4,20},{8,24},{12,28},{16,0},{20,4},{24,8},{28,12},{1,17},{... | collective-permute-start | bytes 393224 | tf_op jit(solution)/shard_map/ppermute | solution.py:103
  72.3 10.7 %collective-permute-start.21 = (bf16[32,2048]{1,0:T(8,128)(2,1)S(1)}, bf16[32,2048]{1,0:T(8,128)(2,1)S(1)}, u32[]{:S(2)}, u32[]{:S(2)}) collective-permute-start(bf16[32,2048]{1,0:T(8,128)(2,1)S(1)} %get-tuple-element.54.refs_0_), channel_id=1, source_target_pairs={{0,8},{4,12},{8,0},{12,4},{16,24},{20,28},{24,16},{28,20},{1,9},{5... | collective-permute-start | bytes 393224 | tf_op jit(solution)/shard_map/ppermute | solution.py:103
  73.3 9.7 %collective-permute-start.20 = (bf16[32,2048]{1,0:T(8,128)(2,1)S(1)}, bf16[32,2048]{1,0:T(8,128)(2,1)S(1)}, u32[]{:S(2)}, u32[]{:S(2)}) collective-permute-start(bf16[32,2048]{1,0:T(8,128)(2,1)S(1)} %get-tuple-element.54.refs_0_), channel_id=1, source_target_pairs={{0,4},{4,0},{8,12},{12,8},{16,20},{20,16},{24,28},{28,24},{1,5},{5... | collective-permute-start | bytes 393224 | tf_op jit(solution)/shard_map/ppermute | solution.py:103
  80.5 6.5 %collective-permute-start.24 = (bf16[32,2048]{1,0:T(8,128)(2,1)S(1)}, bf16[32,2048]{1,0:T(8,128)(2,1)S(1)}, u32[]{:S(2)}, u32[]{:S(2)}) collective-permute-start(bf16[32,2048]{1,0:T(8,128)(2,1)S(1)} %collective-permute-done.23.refs_4_), channel_id=1, source_target_pairs={{0,4},{4,0},{8,12},{12,8},{16,20},{20,16},{24,28},{28,24},{1,5},{5... | collective-permute-start | bytes 393224 | tf_op jit(solution)/shard_map/ppermute | solution.py:103
  89.9 8.0 %collective-permute-start.29 = (bf16[32,2048]{1,0:T(8,128)(2,1)S(1)}, bf16[32,2048]{1,0:T(8,128)(2,1)S(1)}, u32[]{:S(2)}, u32[]{:S(2)}) collective-permute-start(bf16[32,2048]{1,0:T(8,128)(2,1)S(1)} %get-tuple-element.41), channel_id=1, source_target_pairs={{0,3},{1,2},{2,1},{3,0},{4,7},{5,6},{6,5},{7,4},{8,11},{9,10},{10,... | collective-permute-start | bytes 393224 | tf_op jit(solution)/shard_map/ppermute | solution.py:103
  106.5 6.9 %collective-permute-start.33 = (bf16[32,2048]{1,0:T(8,128)(2,1)S(1)}, bf16[32,2048]{1,0:T(8,128)(2,1)S(1)}, u32[]{:S(2)}, u32[]{:S(2)}) collective-permute-start(bf16[32,2048]{1,0:T(8,128)(2,1)S(1)} %get-tuple-element.43), channel_id=1, source_target_pairs={{0,4},{4,0},{8,12},{12,8},{16,20},{20,16},{24,28},{28,24},{1,5},{5... | collective-permute-start | bytes 393224 | tf_op jit(solution)/shard_map/ppermute | solution.py:103
  109.2 7.0 %collective-permute-start.35 = (bf16[32,2048]{1,0:T(8,128)(2,1)S(1)}, bf16[32,2048]{1,0:T(8,128)(2,1)S(1)}, u32[]{:S(2)}, u32[]{:S(2)}) collective-permute-start(bf16[32,2048]{1,0:T(8,128)(2,1)S(1)} %get-tuple-element.45), channel_id=1, source_target_pairs={{0,4},{4,0},{8,12},{12,8},{16,20},{20,16},{24,28},{28,24},{1,5},{5... | collective-permute-start | bytes 393224 | tf_op jit(solution)/shard_map/ppermute | solution.py:103
  109.3 12.6 %collective-permute-start.37 = (bf16[32,2048]{1,0:T(8,128)(2,1)S(1)}, bf16[32,2048]{1,0:T(8,128)(2,1)S(1)}, u32[]{:S(2)}, u32[]{:S(2)}) collective-permute-start(bf16[32,2048]{1,0:T(8,128)(2,1)S(1)} %get-tuple-element.47), channel_id=1, source_target_pairs={{0,4},{4,0},{8,12},{12,8},{16,20},{20,16},{24,28},{28,24},{1,5},{5... | collective-permute-start | bytes 393224 | tf_op jit(solution)/shard_map/ppermute | solution.py:103
  111.2 13.1 %collective-permute-start.39 = (bf16[32,2048]{1,0:T(8,128)(2,1)S(1)}, bf16[32,2048]{1,0:T(8,128)(2,1)S(1)}, u32[]{:S(2)}, u32[]{:S(2)}) collective-permute-start(bf16[32,2048]{1,0:T(8,128)(2,1)S(1)} %get-tuple-element.49), channel_id=1, source_target_pairs={{0,4},{4,0},{8,12},{12,8},{16,20},{20,16},{24,28},{28,24},{1,5},{5... | collective-permute-start | bytes 393224 | tf_op jit(solution)/shard_map/ppermute | solution.py:103
  113.5 10.9 %collective-permute-start.34 = (bf16[32,2048]{1,0:T(8,128)(2,1)S(1)}, bf16[32,2048]{1,0:T(8,128)(2,1)S(1)}, u32[]{:S(2)}, u32[]{:S(2)}) collective-permute-start(bf16[32,2048]{1,0:T(8,128)(2,1)S(1)} %add_convert_fusion.2), channel_id=1, source_target_pairs={{0,24},{4,28},{8,16},{12,20},{16,8},{20,12},{24,0},{28,4},{1,25},{... | collective-permute-start | bytes 393224 | tf_op jit(solution)/shard_map/ppermute | solution.py:103
  116.3 11.8 %collective-permute-start.36 = (bf16[32,2048]{1,0:T(8,128)(2,1)S(1)}, bf16[32,2048]{1,0:T(8,128)(2,1)S(1)}, u32[]{:S(2)}, u32[]{:S(2)}) collective-permute-start(bf16[32,2048]{1,0:T(8,128)(2,1)S(1)} %add_convert_fusion.1), channel_id=1, source_target_pairs={{0,16},{4,20},{8,24},{12,28},{16,0},{20,4},{24,8},{28,12},{1,17},{... | collective-permute-start | bytes 393224 | tf_op jit(solution)/shard_map/ppermute | solution.py:103
  (25 other events, 355.2 us)

commit v3 on v2

--- a/solution.py
+++ b/solution.py
@@ -16,27 +16,31 @@
 step_dual = 0.4
 
 VMEM_LIMIT = 24 * 1024 * 1024
-
-
-def sweep_kernel(forward, pieces, outs, per_in, per_out, info, tiles, *refs):
-    parts = refs[:pieces]
+FETCH_LIMIT = 46 * 1024 * 1024
+
+
+def sweep_kernel(forward, fetched, pieces, outs, per_in, per_out, info, tiles, *refs):
+    parts = refs[:pieces][::-1]
     results = refs[pieces : pieces + outs]
-    held, total, operand, arrived = refs[pieces + outs :]
+    total, operand = refs[pieces + outs : pieces + outs + 2]
     slots = tiles.shape[0]
     live = info[2 * slots]
     me_in = info[2 * slots + 1]
     me_out = info[2 * slots + 2]
     span_in = operand.shape[1]
     span_out = total.shape[2]
-
-    def fetch(slot):
-        return pltpu.make_async_copy(tiles.at[slot], held.at[slot], arrived.at[slot])
-
-    def start(slot, carry):
-        fetch(slot).start()
-        return carry
-
-    lax.fori_loop(0, live, start, 0)
+    held = tiles
+    if fetched:
+        held, arrived = refs[pieces + outs + 2 :]
+
+        def fetch(slot):
+            return pltpu.make_async_copy(tiles.at[slot], held.at[slot], arrived.at[slot])
+
+        def start(slot, carry):
+            fetch(slot).start()
+            return carry
+
+        lax.fori_loop(0, live, start, 0)
     total[...] = jnp.zeros_like(total)
 
     def visit(slot, carry):
@@ -52,7 +56,8 @@
             def _():
                 operand[...] = parts[k][:, pl.ds(place, span_in)]
 
-        fetch(slot).wait()
+        if fetched:
+            fetch(slot).wait()
         contract = (((1,), (1,)), ((), ())) if forward else (((1,), (0,)), ((), ()))
         total[block_out] += lax.dot_general(
             operand[...], held[slot], contract, preferred_element_type=jnp.float32
@@ -68,35 +73,41 @@
             )
 
 
-def sweep(forward, tiles, info, parts, kinds, per_in, per_out, blocks_out):
+def sweep(forward, fetched, tiles, info, parts, kinds, per_in, per_out, blocks_out):
     slots, rows_tile, cols_tile = tiles.shape
     width = parts[0].shape[0]
     span_in, span_out = (cols_tile, rows_tile) if forward else (rows_tile, cols_tile)
     pieces = len(parts)
     outs = len(kinds)
     vmem = pl.BlockSpec(memory_space=pltpu.VMEM)
+    scratch = [
+        pltpu.VMEM((blocks_out, width, span_out), jnp.float32),
+        pltpu.VMEM((width, span_in), jnp.bfloat16),
+    ]
+    if fetched:
+        scratch += [pltpu.VMEM(tiles.shape, tiles.dtype), pltpu.SemaphoreType.DMA((slots,))]
     return pl.pallas_call(
-        functools.partial(sweep_kernel, forward, pieces, outs, per_in, per_out),
+        functools.partial(sweep_kernel, forward, fetched, pieces, outs, per_in, per_out),
         out_shape=[
             jax.ShapeDtypeStruct((width, per_out * span_out), kind) for kind in kinds
         ],
-        in_specs=[pl.BlockSpec(memory_space=pltpu.SMEM), pl.BlockSpec(memory_space=pltpu.HBM)]
+        in_specs=[
+            pl.BlockSpec(memory_space=pltpu.SMEM),
+            pl.BlockSpec(memory_space=pl.ANY) if fetched else vmem,
+        ]
         + [vmem] * pieces,
         out_specs=[vmem] * outs,
-        scratch_shapes=[
-            pltpu.VMEM(tiles.shape, tiles.dtype),
-            pltpu.VMEM((blocks_out, width, span_out), jnp.float32),
-            pltpu.VMEM((width, span_in), jnp.bfloat16),
-            pltpu.SemaphoreType.DMA((slots,)),
-        ],
-        compiler_params=pltpu.CompilerParams(vmem_limit_bytes=VMEM_LIMIT),
+        scratch_shapes=scratch,
+        compiler_params=pltpu.CompilerParams(
+            vmem_limit_bytes=FETCH_LIMIT if fetched else VMEM_LIMIT
+        ),
         cost_estimate=pl.CostEstimate(
             flops=2 * slots * width * rows_tile * cols_tile,
             bytes_accessed=tiles.size * 2,
             transcendentals=0,
         ),
         name="forward_sweep" if forward else "transpose_sweep",
-    )(info, tiles, *parts)
+    )(info, tiles, *parts[::-1])
 
 
 def swap(value, axis, size, k):
@@ -106,9 +117,9 @@
 def gather_pairs(own, axis, size):
     parts = [None] * size
     parts[0] = own
-    for k in range(2, size, 2):
+    for k in range(size - 2, 0, -2):
         parts[k] = swap(own, axis, size, k)
-    for k in range(0, size, 2):
+    for k in range(size - 2, -1, -2):
         parts[k + 1] = swap(parts[k], axis, size, 1)
     return parts
 
@@ -165,7 +176,7 @@
     for step in range(ITERS):
         dual_parts = gather_pairs(dual.astype(jnp.bfloat16), "col", cols)
         pull_parts = sweep(
-            False, blocks, info, dual_parts, pull_kinds, per_row, per_col, BC_DEV
+            False, step == 0, blocks, info, dual_parts, pull_kinds, per_row, per_col, BC_DEV
         )
         pull = sum_direct(pull_parts, "row", rows)
         fresh = jnp.maximum(primal - step_primal * (cost - pull), 0.0)
@@ -173,7 +184,7 @@
         primal = fresh
         extra_parts = gather_pairs(extra, "row", rows)
         push_parts = sweep(
-            True, blocks, info_back, extra_parts, push_kinds, per_col, per_row, BR_DEV
+            True, False, blocks, info_back, extra_parts, push_kinds, per_col, per_row, BR_DEV
         )
         push = sum_pairs(push_parts, "col", cols)
         moved = dual + step_dual * (demand - push)

time: 130 us -> 126 us (0.969)
  starting transfers between devices: 55.3 us -> 40.5 us
  waiting for transfers between devices: 59 us -> 70.8 us
  Pallas kernels: 5.12 us -> 8.69 us
  local copies, waits for them, and re-layouts: 7.27 us -> 3.89 us
    ppermute x40, starting transfers between devices: 55.3 us -> 40.5 us  [swap(): return lax.ppermute(value, axis, [(i, i ^ k) for i in range(size)])]
    ppermute x40, waiting for transfers between devices: 59 us -> 70.8 us  [swap(): return lax.ppermute(value, axis, [(i, i ^ k) for i in range(size)])]
    pallas_call x4, Pallas kernels: 5.12 us -> 8.69 us  [sweep(): pl.pallas_call(functools.partial(sweep_kernel, forward, fetched, pieces,...]
    unnamed x22 -> x20, local copies, waits for them, and re-layouts: 7.19 us -> 3.8 us
  transfers between devices with their start and end apart: 40 -> 40, of which waited for: 22 -> 25; matrix products, arithmetic and copies ran while one was open for 2% -> 2% of each run, Pallas kernels for 0% -> 0%
where the time goes in v3:
time: 126 us
  waiting for transfers between devices  70.8 us (56%)
  starting transfers between devices  40.5 us (32%)
  Pallas kernels  8.69 us (7%)
  local copies, waits for them, and re-layouts  3.89 us (3%)
  between operations  1.47 us (1%)
    ppermute x40, waiting for transfers between devices, swap(): return lax.ppermute(value, axis, [(i, i ^ k) for i in range(size)])  70.8 us
    ppermute x40, starting transfers between devices, swap(): return lax.ppermute(value, axis, [(i, i ^ k) for i in range(size)])  40.5 us
    pallas_call x4, Pallas kernels, sweep(): pl.pallas_call(functools.partial(sweep_kernel, forward, fetched, pieces,...  8.69 us
    unnamed x20, local copies, waits for them, and re-layouts  3.8 us
  transfers between devices with their start and end apart: 40, of which 25 were waited for; matrix products, arithmetic and copies ran while one was open for 2% of the time, Pallas kernels for 0%

profile of v3, /device:TPU:0, one launch (start us, length us, event | category | flops | bytes accessed | tf_op | source)
XLA Modules:
  0.0 126.4 jit_solution(18115139761032166189)
XLA Ops:
  1.7 3.1 %collective-permute-start.4 = (bf16[32,2048]{1,0:T(8,128)(2,1)S(1)}, bf16[32,2048]{1,0:T(8,128)(2,1)S(1)}, u32[]{:S(2)}, u32[]{:S(2)}) collective-permute-start(bf16[32,2048]{1,0:T(8,128)(2,1)S(1)} %bitcast.33), channel_id=1, source_target_pairs={{0,8},{4,12},{8,0},{12,4},{16,24},{20,28},{24,16},{28,20},{1,9},{5... | collective-permute-start | bytes 393224 | tf_op jit(solution)/shard_map/ppermute | solution.py:114
  4.8 2.6 %collective-permute-start.2 = (bf16[32,2048]{1,0:T(8,128)(2,1)S(1)}, bf16[32,2048]{1,0:T(8,128)(2,1)S(1)}, u32[]{:S(2)}, u32[]{:S(2)}) collective-permute-start(bf16[32,2048]{1,0:T(8,128)(2,1)S(1)} %bitcast.34), channel_id=1, source_target_pairs={{0,16},{4,20},{8,24},{12,28},{16,0},{20,4},{24,8},{28,12},{1,17},{... | collective-permute-start | bytes 393224 | tf_op jit(solution)/shard_map/ppermute | solution.py:114
  11.6 6.2 %collective-permute-done.2.refs_3_ = bf16[32,2048]{1,0:T(8,128)(2,1)S(1)} collective-permute-done((bf16[32,2048]{1,0:T(8,128)(2,1)S(1)}, bf16[32,2048]{1,0:T(8,128)(2,1)S(1)}, u32[]{:S(2)}, u32[]{:S(2)}) %collective-permute-start.2) | collective-permute-done | bytes 131104 | tf_op jit(solution)/shard_map/ppermute | solution.py:114
  24.2 2.8 %transpose_sweep.2 = (f32[32,2048]{1,0:T(8,128)S(1)}, bf16[32,2048]{1,0:T(8,128)(2,1)S(1)}, bf16[32,2048]{1,0:T(8,128)(2,1)S(1)}, bf16[32,2048]{1,0:T(8,128)(2,1)S(1)}) custom-call(s32[19]{0:T(128)S(1)} %get-tuple-element.61.info, bf16[8,1024,512]{2,1,0:T(8,128)(2,1)} %bitcast.29, bf16[32,2048]{1,0:T(8,128)(2,1)S(1)} %collective-permute-done.1.refs_0_, ...), custom_call_target="tpu_custom_call" | custom-call | flops 268435456 | bytes 8388608 | tf_op jit(solution)/shard_map/transpose_sweep/pallas_call | solution.py:89
  29.0 4.5 %collective-permute-done.8 = bf16[32,2048]{1,0:T(8,128)(2,1)S(1)} collective-permute-done((bf16[32,2048]{1,0:T(8,128)(2,1)S(1)}, bf16[32,2048]{1,0:T(8,128)(2,1)S(1)}, u32[]{:S(2)}, u32[]{:S(2)}) %collective-permute-start.8) | collective-permute-done | bytes 131104 | tf_op jit(solution)/shard_map/ppermute | solution.py:114
  33.5 1.9 %collective-permute-done.9 = bf16[32,2048]{1,0:T(8,128)(2,1)S(1)} collective-permute-done((bf16[32,2048]{1,0:T(8,128)(2,1)S(1)}, bf16[32,2048]{1,0:T(8,128)(2,1)S(1)}, u32[]{:S(2)}, u32[]{:S(2)}) %collective-permute-start.9) | collective-permute-done | bytes 131104 | tf_op jit(solution)/shard_map/ppermute | solution.py:114
  36.6 4.8 %collective-permute-done.10.refs_1_ = bf16[32,2048]{1,0:T(8,128)(2,1)S(1)} collective-permute-done((bf16[32,2048]{1,0:T(8,128)(2,1)S(1)}, bf16[32,2048]{1,0:T(8,128)(2,1)S(1)}, u32[]{:S(2)}, u32[]{:S(2)}) %collective-permute-start.10) | collective-permute-done | bytes 131104 | tf_op jit(solution)/shard_map/ppermute | solution.py:114
  42.8 2.1 %forward_sweep.2 = (f32[32,2048]{1,0:T(8,128)S(1)}, bf16[32,2048]{1,0:T(8,128)(2,1)S(1)}, f32[32,2048]{1,0:T(8,128)S(1)}, bf16[32,2048]{1,0:T(8,128)(2,1)S(1)}, ...) custom-call(s32[19]{0:T(128)S(1)} %get-tuple-element.60.info, ...), custom_call_target="tpu_custom_call" | custom-call | flops 268435456 | bytes 8388608 | tf_op jit(solution)/shard_map/forward_sweep/pallas_call | solution.py:89
  44.9 2.2 %collective-permute-start.13 = (bf16[32,2048]{1,0:T(8,128)(2,1)S(1)}, bf16[32,2048]{1,0:T(8,128)(2,1)S(1)}, u32[]{:S(2)}, u32[]{:S(2)}) collective-permute-start(bf16[32,2048]{1,0:T(8,128)(2,1)S(1)} %get-tuple-element.31), channel_id=1, source_target_pairs={{0,4},{4,0},{8,12},{12,8},{16,20},{20,16},{24,28},{28,24},{1,5},{5... | collective-permute-start | bytes 393224 | tf_op jit(solution)/shard_map/ppermute | solution.py:114
  47.1 1.9 %collective-permute-start.17 = (bf16[32,2048]{1,0:T(8,128)(2,1)S(1)}, bf16[32,2048]{1,0:T(8,128)(2,1)S(1)}, u32[]{:S(2)}, u32[]{:S(2)}) collective-permute-start(bf16[32,2048]{1,0:T(8,128)(2,1)S(1)} %get-tuple-element.35), channel_id=1, source_target_pairs={{0,4},{4,0},{8,12},{12,8},{16,20},{20,16},{24,28},{28,24},{1,5},{5... | collective-permute-start | bytes 393224 | tf_op jit(solution)/shard_map/ppermute | solution.py:114
  49.1 2.2 %collective-permute-done.13 = bf16[32,2048]{1,0:T(8,128)(2,1)S(1)} collective-permute-done((bf16[32,2048]{1,0:T(8,128)(2,1)S(1)}, bf16[32,2048]{1,0:T(8,128)(2,1)S(1)}, u32[]{:S(2)}, u32[]{:S(2)}) %collective-permute-start.13) | collective-permute-done | bytes 131104 | tf_op jit(solution)/shard_map/ppermute | solution.py:114
  51.4 2.5 %collective-permute-start.14 = (bf16[32,2048]{1,0:T(8,128)(2,1)S(1)}, bf16[32,2048]{1,0:T(8,128)(2,1)S(1)}, u32[]{:S(2)}, u32[]{:S(2)}) collective-permute-start(bf16[32,2048]{1,0:T(8,128)(2,1)S(1)} %add_convert_fusion.5), channel_id=1, source_target_pairs={{0,24},{4,28},{8,16},{12,20},{16,8},{20,12},{24,0},{28,4},{1,25},{... | collective-permute-start | bytes 393224 | tf_op jit(solution)/shard_map/ppermute | solution.py:114
  59.3 6.9 %collective-permute-done.16 = bf16[32,2048]{1,0:T(8,128)(2,1)S(1)} collective-permute-done((bf16[32,2048]{1,0:T(8,128)(2,1)S(1)}, bf16[32,2048]{1,0:T(8,128)(2,1)S(1)}, u32[]{:S(2)}, u32[]{:S(2)}) %collective-permute-start.16) | collective-permute-done | bytes 131104 | tf_op jit(solution)/shard_map/ppermute | solution.py:114
  67.8 3.1 %collective-permute-start.20 = (bf16[32,2048]{1,0:T(8,128)(2,1)S(1)}, bf16[32,2048]{1,0:T(8,128)(2,1)S(1)}, u32[]{:S(2)}, u32[]{:S(2)}) collective-permute-start(bf16[32,2048]{1,0:T(8,128)(2,1)S(1)} %get-tuple-element.54.refs_7_), channel_id=1, source_target_pairs={{0,24},{4,28},{8,16},{12,20},{16,8},{20,12},{24,0},{28,4},{1,25},{... | collective-permute-start | bytes 393224 | tf_op jit(solution)/shard_map/ppermute | solution.py:114
  71.3 1.9 %collective-permute-done.24.refs_5_ = bf16[32,2048]{1,0:T(8,128)(2,1)S(1)} collective-permute-done((bf16[32,2048]{1,0:T(8,128)(2,1)S(1)}, bf16[32,2048]{1,0:T(8,128)(2,1)S(1)}, u32[]{:S(2)}, u32[]{:S(2)}) %collective-permute-start.24) | collective-permute-done | bytes 131104 | tf_op jit(solution)/shard_map/ppermute | solution.py:114
  73.8 5.7 %collective-permute-done.22.refs_3_ = bf16[32,2048]{1,0:T(8,128)(2,1)S(1)} collective-permute-done((bf16[32,2048]{1,0:T(8,128)(2,1)S(1)}, bf16[32,2048]{1,0:T(8,128)(2,1)S(1)}, u32[]{:S(2)}, u32[]{:S(2)}) %collective-permute-start.22) | collective-permute-done | bytes 131104 | tf_op jit(solution)/shard_map/ppermute | solution.py:114
  81.5 3.1 %collective-permute-done.23.refs_2_ = bf16[32,2048]{1,0:T(8,128)(2,1)S(1)} collective-permute-done((bf16[32,2048]{1,0:T(8,128)(2,1)S(1)}, bf16[32,2048]{1,0:T(8,128)(2,1)S(1)}, u32[]{:S(2)}, u32[]{:S(2)}) %collective-permute-start.23) | collective-permute-done | bytes 131104 | tf_op jit(solution)/shard_map/ppermute | solution.py:114
  89.7 4.5 %collective-permute-done.28 = bf16[32,2048]{1,0:T(8,128)(2,1)S(1)} collective-permute-done((bf16[32,2048]{1,0:T(8,128)(2,1)S(1)}, bf16[32,2048]{1,0:T(8,128)(2,1)S(1)}, u32[]{:S(2)}, u32[]{:S(2)}) %collective-permute-start.28) | collective-permute-done | bytes 131104 | tf_op jit(solution)/shard_map/ppermute | solution.py:114
  94.2 1.9 %collective-permute-done.29 = bf16[32,2048]{1,0:T(8,128)(2,1)S(1)} collective-permute-done((bf16[32,2048]{1,0:T(8,128)(2,1)S(1)}, bf16[32,2048]{1,0:T(8,128)(2,1)S(1)}, u32[]{:S(2)}, u32[]{:S(2)}) %collective-permute-start.29) | collective-permute-done | bytes 131104 | tf_op jit(solution)/shard_map/ppermute | solution.py:114
  96.8 5.2 %collective-permute-done.30.refs_1_ = bf16[32,2048]{1,0:T(8,128)(2,1)S(1)} collective-permute-done((bf16[32,2048]{1,0:T(8,128)(2,1)S(1)}, bf16[32,2048]{1,0:T(8,128)(2,1)S(1)}, u32[]{:S(2)}, u32[]{:S(2)}) %collective-permute-start.30) | collective-permute-done | bytes 131104 | tf_op jit(solution)/shard_map/ppermute | solution.py:114
  103.3 2.1 %forward_sweep.3 = (f32[32,2048]{1,0:T(8,128)S(1)}, bf16[32,2048]{1,0:T(8,128)(2,1)S(1)}, f32[32,2048]{1,0:T(8,128)S(1)}, bf16[32,2048]{1,0:T(8,128)(2,1)S(1)}, ...) custom-call(s32[19]{0:T(128)S(1)} %get-tuple-element.60.info, ...), custom_call_target="tpu_custom_call" | custom-call | flops 268435456 | bytes 8388608 | tf_op jit(solution)/shard_map/forward_sweep/pallas_call | solution.py:89
  109.5 2.3 %collective-permute-done.33 = bf16[32,2048]{1,0:T(8,128)(2,1)S(1)} collective-permute-done((bf16[32,2048]{1,0:T(8,128)(2,1)S(1)}, bf16[32,2048]{1,0:T(8,128)(2,1)S(1)}, u32[]{:S(2)}, u32[]{:S(2)}) %collective-permute-start.33) | collective-permute-done | bytes 131104 | tf_op jit(solution)/shard_map/ppermute | solution.py:114
  115.1 2.4 %collective-permute-done.37 = bf16[32,2048]{1,0:T(8,128)(2,1)S(1)} collective-permute-done((bf16[32,2048]{1,0:T(8,128)(2,1)S(1)}, bf16[32,2048]{1,0:T(8,128)(2,1)S(1)}, u32[]{:S(2)}, u32[]{:S(2)}) %collective-permute-start.37) | collective-permute-done | bytes 131104 | tf_op jit(solution)/shard_map/ppermute | solution.py:114
  120.1 5.2 %collective-permute-done.36 = bf16[32,2048]{1,0:T(8,128)(2,1)S(1)} collective-permute-done((bf16[32,2048]{1,0:T(8,128)(2,1)S(1)}, bf16[32,2048]{1,0:T(8,128)(2,1)S(1)}, u32[]{:S(2)}, u32[]{:S(2)}) %collective-permute-start.36) | collective-permute-done | bytes 131104 | tf_op jit(solution)/shard_map/ppermute | solution.py:114
  (94 shorter events, 43.8 us)
Async XLA Ops:
  1.7 8.1 %collective-permute-start.4 = (bf16[32,2048]{1,0:T(8,128)(2,1)S(1)}, bf16[32,2048]{1,0:T(8,128)(2,1)S(1)}, u32[]{:S(2)}, u32[]{:S(2)}) collective-permute-start(bf16[32,2048]{1,0:T(8,128)(2,1)S(1)} %bitcast.33), channel_id=1, source_target_pairs={{0,8},{4,12},{8,0},{12,4},{16,24},{20,28},{24,16},{28,20},{1,9},{5... | collective-permute-start | bytes 393224 | tf_op jit(solution)/shard_map/ppermute | solution.py:114
  4.8 12.9 %collective-permute-start.2 = (bf16[32,2048]{1,0:T(8,128)(2,1)S(1)}, bf16[32,2048]{1,0:T(8,128)(2,1)S(1)}, u32[]{:S(2)}, u32[]{:S(2)}) collective-permute-start(bf16[32,2048]{1,0:T(8,128)(2,1)S(1)} %bitcast.34), channel_id=1, source_target_pairs={{0,16},{4,20},{8,24},{12,28},{16,0},{20,4},{24,8},{28,12},{1,17},{... | collective-permute-start | bytes 393224 | tf_op jit(solution)/shard_map/ppermute | solution.py:114
  7.4 11.8 %collective-permute-start = (bf16[32,2048]{1,0:T(8,128)(2,1)S(1)}, bf16[32,2048]{1,0:T(8,128)(2,1)S(1)}, u32[]{:S(2)}, u32[]{:S(2)}) collective-permute-start(bf16[32,2048]{1,0:T(8,128)(2,1)S(1)} %bitcast.35), channel_id=1, source_target_pairs={{0,24},{4,28},{8,16},{12,20},{16,8},{20,12},{24,0},{28,4},{1,25},{... | collective-permute-start | bytes 393224 | tf_op jit(solution)/shard_map/ppermute | solution.py:114
  7.4 13.9 %collective-permute-start.6 = (bf16[32,2048]{1,0:T(8,128)(2,1)S(1)}, bf16[32,2048]{1,0:T(8,128)(2,1)S(1)}, u32[]{:S(2)}, u32[]{:S(2)}) collective-permute-start(bf16[32,2048]{1,0:T(8,128)(2,1)S(1)} %bitcast.36), channel_id=1, source_target_pairs={{0,4},{4,0},{8,12},{12,8},{16,20},{20,16},{24,28},{28,24},{1,5},{5... | collective-permute-start | bytes 393224 | tf_op jit(solution)/shard_map/ppermute | solution.py:114
  9.9 11.5 %collective-permute-start.5 = (bf16[32,2048]{1,0:T(8,128)(2,1)S(1)}, bf16[32,2048]{1,0:T(8,128)(2,1)S(1)}, u32[]{:S(2)}, u32[]{:S(2)}) collective-permute-start(bf16[32,2048]{1,0:T(8,128)(2,1)S(1)} %collective-permute-done.4.refs_5_), channel_id=1, source_target_pairs={{0,4},{4,0},{8,12},{12,8},{16,20},{20,16},{24,28},{28,24},{1,5},{5... | collective-permute-start | bytes 393224 | tf_op jit(solution)/shard_map/ppermute | solution.py:114
  28.1 7.3 %collective-permute-start.9 = (bf16[32,2048]{1,0:T(8,128)(2,1)S(1)}, bf16[32,2048]{1,0:T(8,128)(2,1)S(1)}, u32[]{:S(2)}, u32[]{:S(2)}) collective-permute-start(bf16[32,2048]{1,0:T(8,128)(2,1)S(1)} %get-tuple-element.29), channel_id=1, source_target_pairs={{0,3},{1,2},{2,1},{3,0},{4,7},{5,6},{6,5},{7,4},{8,11},{9,10},{10,... | collective-permute-start | bytes 393224 | tf_op jit(solution)/shard_map/ppermute | solution.py:114
  47.0 7.1 %collective-permute-start.15 = (bf16[32,2048]{1,0:T(8,128)(2,1)S(1)}, bf16[32,2048]{1,0:T(8,128)(2,1)S(1)}, u32[]{:S(2)}, u32[]{:S(2)}) collective-permute-start(bf16[32,2048]{1,0:T(8,128)(2,1)S(1)} %get-tuple-element.33), channel_id=1, source_target_pairs={{0,4},{4,0},{8,12},{12,8},{16,20},{20,16},{24,28},{28,24},{1,5},{5... | collective-permute-start | bytes 393224 | tf_op jit(solution)/shard_map/ppermute | solution.py:114
  47.1 9.8 %collective-permute-start.17 = (bf16[32,2048]{1,0:T(8,128)(2,1)S(1)}, bf16[32,2048]{1,0:T(8,128)(2,1)S(1)}, u32[]{:S(2)}, u32[]{:S(2)}) collective-permute-start(bf16[32,2048]{1,0:T(8,128)(2,1)S(1)} %get-tuple-element.35), channel_id=1, source_target_pairs={{0,4},{4,0},{8,12},{12,8},{16,20},{20,16},{24,28},{28,24},{1,5},{5... | collective-permute-start | bytes 393224 | tf_op jit(solution)/shard_map/ppermute | solution.py:114
  49.1 10.2 %collective-permute-start.19 = (bf16[32,2048]{1,0:T(8,128)(2,1)S(1)}, bf16[32,2048]{1,0:T(8,128)(2,1)S(1)}, u32[]{:S(2)}, u32[]{:S(2)}) collective-permute-start(bf16[32,2048]{1,0:T(8,128)(2,1)S(1)} %get-tuple-element.37), channel_id=1, source_target_pairs={{0,4},{4,0},{8,12},{12,8},{16,20},{20,16},{24,28},{28,24},{1,5},{5... | collective-permute-start | bytes 393224 | tf_op jit(solution)/shard_map/ppermute | solution.py:114
  51.4 7.9 %collective-permute-start.14 = (bf16[32,2048]{1,0:T(8,128)(2,1)S(1)}, bf16[32,2048]{1,0:T(8,128)(2,1)S(1)}, u32[]{:S(2)}, u32[]{:S(2)}) collective-permute-start(bf16[32,2048]{1,0:T(8,128)(2,1)S(1)} %add_convert_fusion.5), channel_id=1, source_target_pairs={{0,24},{4,28},{8,16},{12,20},{16,8},{20,12},{24,0},{28,4},{1,25},{... | collective-permute-start | bytes 393224 | tf_op jit(solution)/shard_map/ppermute | solution.py:114
  54.2 12.1 %collective-permute-start.16 = (bf16[32,2048]{1,0:T(8,128)(2,1)S(1)}, bf16[32,2048]{1,0:T(8,128)(2,1)S(1)}, u32[]{:S(2)}, u32[]{:S(2)}) collective-permute-start(bf16[32,2048]{1,0:T(8,128)(2,1)S(1)} %add_convert_fusion.4), channel_id=1, source_target_pairs={{0,16},{4,20},{8,24},{12,28},{16,0},{20,4},{24,8},{28,12},{1,17},{... | collective-permute-start | bytes 393224 | tf_op jit(solution)/shard_map/ppermute | solution.py:114
  57.0 9.3 %collective-permute-start.18 = (bf16[32,2048]{1,0:T(8,128)(2,1)S(1)}, bf16[32,2048]{1,0:T(8,128)(2,1)S(1)}, u32[]{:S(2)}, u32[]{:S(2)}) collective-permute-start(bf16[32,2048]{1,0:T(8,128)(2,1)S(1)} %add_convert_fusion.3), channel_id=1, source_target_pairs={{0,8},{4,12},{8,0},{12,4},{16,24},{20,28},{24,16},{28,20},{1,9},{5... | collective-permute-start | bytes 393224 | tf_op jit(solution)/shard_map/ppermute | solution.py:114
  66.4 6.8 %collective-permute-start.24 = (bf16[32,2048]{1,0:T(8,128)(2,1)S(1)}, bf16[32,2048]{1,0:T(8,128)(2,1)S(1)}, u32[]{:S(2)}, u32[]{:S(2)}) collective-permute-start(bf16[32,2048]{1,0:T(8,128)(2,1)S(1)} %get-tuple-element.54.refs_7_), channel_id=1, source_target_pairs={{0,8},{4,12},{8,0},{12,4},{16,24},{20,28},{24,16},{28,20},{1,9},{5... | collective-permute-start | bytes 393224 | tf_op jit(solution)/shard_map/ppermute | solution.py:114
  66.5 13.0 %collective-permute-start.22 = (bf16[32,2048]{1,0:T(8,128)(2,1)S(1)}, bf16[32,2048]{1,0:T(8,128)(2,1)S(1)}, u32[]{:S(2)}, u32[]{:S(2)}) collective-permute-start(bf16[32,2048]{1,0:T(8,128)(2,1)S(1)} %get-tuple-element.54.refs_7_), channel_id=1, source_target_pairs={{0,16},{4,20},{8,24},{12,28},{16,0},{20,4},{24,8},{28,12},{1,17},{... | collective-permute-start | bytes 393224 | tf_op jit(solution)/shard_map/ppermute | solution.py:114
  67.8 12.1 %collective-permute-start.20 = (bf16[32,2048]{1,0:T(8,128)(2,1)S(1)}, bf16[32,2048]{1,0:T(8,128)(2,1)S(1)}, u32[]{:S(2)}, u32[]{:S(2)}) collective-permute-start(bf16[32,2048]{1,0:T(8,128)(2,1)S(1)} %get-tuple-element.54.refs_7_), channel_id=1, source_target_pairs={{0,24},{4,28},{8,16},{12,20},{16,8},{20,12},{24,0},{28,4},{1,25},{... | collective-permute-start | bytes 393224 | tf_op jit(solution)/shard_map/ppermute | solution.py:114
  70.9 10.6 %collective-permute-start.26 = (bf16[32,2048]{1,0:T(8,128)(2,1)S(1)}, bf16[32,2048]{1,0:T(8,128)(2,1)S(1)}, u32[]{:S(2)}, u32[]{:S(2)}) collective-permute-start(bf16[32,2048]{1,0:T(8,128)(2,1)S(1)} %get-tuple-element.54.refs_7_), channel_id=1, source_target_pairs={{0,4},{4,0},{8,12},{12,8},{16,20},{20,16},{24,28},{28,24},{1,5},{5... | collective-permute-start | bytes 393224 | tf_op jit(solution)/shard_map/ppermute | solution.py:114
  73.3 8.3 %collective-permute-start.25 = (bf16[32,2048]{1,0:T(8,128)(2,1)S(1)}, bf16[32,2048]{1,0:T(8,128)(2,1)S(1)}, u32[]{:S(2)}, u32[]{:S(2)}) collective-permute-start(bf16[32,2048]{1,0:T(8,128)(2,1)S(1)} %collective-permute-done.24.refs_5_), channel_id=1, source_target_pairs={{0,4},{4,0},{8,12},{12,8},{16,20},{20,16},{24,28},{28,24},{1,5},{5... | collective-permute-start | bytes 393224 | tf_op jit(solution)/shard_map/ppermute | solution.py:114
  87.9 8.2 %collective-permute-start.29 = (bf16[32,2048]{1,0:T(8,128)(2,1)S(1)}, bf16[32,2048]{1,0:T(8,128)(2,1)S(1)}, u32[]{:S(2)}, u32[]{:S(2)}) collective-permute-start(bf16[32,2048]{1,0:T(8,128)(2,1)S(1)} %get-tuple-element.41), channel_id=1, source_target_pairs={{0,3},{1,2},{2,1},{3,0},{4,7},{5,6},{6,5},{7,4},{8,11},{9,10},{10,... | collective-permute-start | bytes 393224 | tf_op jit(solution)/shard_map/ppermute | solution.py:114
  107.2 7.4 %collective-permute-start.35 = (bf16[32,2048]{1,0:T(8,128)(2,1)S(1)}, bf16[32,2048]{1,0:T(8,128)(2,1)S(1)}, u32[]{:S(2)}, u32[]{:S(2)}) collective-permute-start(bf16[32,2048]{1,0:T(8,128)(2,1)S(1)} %get-tuple-element.45), channel_id=1, source_target_pairs={{0,4},{4,0},{8,12},{12,8},{16,20},{20,16},{24,28},{28,24},{1,5},{5... | collective-permute-start | bytes 393224 | tf_op jit(solution)/shard_map/ppermute | solution.py:114
  107.5 9.9 %collective-permute-start.37 = (bf16[32,2048]{1,0:T(8,128)(2,1)S(1)}, bf16[32,2048]{1,0:T(8,128)(2,1)S(1)}, u32[]{:S(2)}, u32[]{:S(2)}) collective-permute-start(bf16[32,2048]{1,0:T(8,128)(2,1)S(1)} %get-tuple-element.47), channel_id=1, source_target_pairs={{0,4},{4,0},{8,12},{12,8},{16,20},{20,16},{24,28},{28,24},{1,5},{5... | collective-permute-start | bytes 393224 | tf_op jit(solution)/shard_map/ppermute | solution.py:114
  109.3 10.9 %collective-permute-start.39 = (bf16[32,2048]{1,0:T(8,128)(2,1)S(1)}, bf16[32,2048]{1,0:T(8,128)(2,1)S(1)}, u32[]{:S(2)}, u32[]{:S(2)}) collective-permute-start(bf16[32,2048]{1,0:T(8,128)(2,1)S(1)} %get-tuple-element.49), channel_id=1, source_target_pairs={{0,4},{4,0},{8,12},{12,8},{16,20},{20,16},{24,28},{28,24},{1,5},{5... | collective-permute-start | bytes 393224 | tf_op jit(solution)/shard_map/ppermute | solution.py:114
  111.9 8.3 %collective-permute-start.34 = (bf16[32,2048]{1,0:T(8,128)(2,1)S(1)}, bf16[32,2048]{1,0:T(8,128)(2,1)S(1)}, u32[]{:S(2)}, u32[]{:S(2)}) collective-permute-start(bf16[32,2048]{1,0:T(8,128)(2,1)S(1)} %add_convert_fusion.2), channel_id=1, source_target_pairs={{0,24},{4,28},{8,16},{12,20},{16,8},{20,12},{24,0},{28,4},{1,25},{... | collective-permute-start | bytes 393224 | tf_op jit(solution)/shard_map/ppermute | solution.py:114
  114.7 10.6 %collective-permute-start.36 = (bf16[32,2048]{1,0:T(8,128)(2,1)S(1)}, bf16[32,2048]{1,0:T(8,128)(2,1)S(1)}, u32[]{:S(2)}, u32[]{:S(2)}) collective-permute-start(bf16[32,2048]{1,0:T(8,128)(2,1)S(1)} %add_convert_fusion.1), channel_id=1, source_target_pairs={{0,16},{4,20},{8,24},{12,28},{16,0},{20,4},{24,8},{28,12},{1,17},{... | collective-permute-start | bytes 393224 | tf_op jit(solution)/shard_map/ppermute | solution.py:114
  117.5 7.8 %collective-permute-start.38 = (bf16[32,2048]{1,0:T(8,128)(2,1)S(1)}, bf16[32,2048]{1,0:T(8,128)(2,1)S(1)}, u32[]{:S(2)}, u32[]{:S(2)}) collective-permute-start(bf16[32,2048]{1,0:T(8,128)(2,1)S(1)} %add_convert_fusion), channel_id=1, source_target_pairs={{0,8},{4,12},{8,0},{12,4},{16,24},{20,28},{24,16},{28,20},{1,9},{5... | collective-permute-start | bytes 393224 | tf_op jit(solution)/shard_map/ppermute | solution.py:114
  (24 other events, 347.3 us)

commit v4 on v3

v4 whole, which is shorter than its diff:
```python
import functools

import jax
import jax.numpy as jnp
from jax import lax
from jax.experimental import pallas as pl
from jax.experimental.pallas import tpu as pltpu
from jax.sharding import PartitionSpec as P

BR_DEV = 16
BC_DEV = 16
ITERS = 2


step_primal = 0.4
step_dual = 0.4

VMEM_LIMIT = 24 * 1024 * 1024
FETCH_LIMIT = 46 * 1024 * 1024


def sweep_kernel(forward, fetched, parities, pieces, per_in, info, tiles, *refs):
    parts = refs[:pieces][::-1]
    own = 4 if fetched else 2
    results = refs[pieces:-own]
    scratch = refs[-own:]
    total, operand = scratch[:2]
    slots = tiles.shape[0]
    live = info[2 * slots]
    me_in = info[2 * slots + 1]
    me_out = info[2 * slots + 2]
    span_in = operand.shape[1]
    count, width, span_out = total.shape[1:]
    places = [[] for _ in parities]
    per_parity = len(results) // len(parities)
    for p in range(len(parities)):
        for ref in results[p * per_parity : (p + 1) * per_parity]:
            places[p] += [ref.at[h] for h in range(ref.shape[0])]
    per_out = count // len(places[0])
    held = tiles
    if fetched:
        held, arrived = scratch[2:]

        def fetch(slot):
            return pltpu.make_async_copy(tiles.at[slot], held.at[slot], arrived.at[slot])

        def start(slot, carry):
            fetch(slot).start()
            return carry

        lax.fori_loop(0, live, start, 0)
    total[...] = jnp.zeros_like(total)

    def visit(slot, carry):
        block_row = info[2 * slot]
        block_col = info[2 * slot + 1]
        block_in = block_col if forward else block_row
        block_out = block_row if forward else block_col
        target = (block_out // per_out) ^ me_out

        def add():
            source = (block_in // per_in) ^ me_in
            place = pl.multiple_of((block_in % per_in) * span_in, span_in)
            for k in range(pieces):

                @pl.when(source % pieces == k)
                def _():
                    operand[...] = parts[k][source // pieces, :, pl.ds(place, span_in)]

            contract = (((1,), (1,)), ((), ())) if forward else (((1,), (0,)), ((), ()))
            at = (target // 2) * per_out + block_out % per_out
            side = target % 2 if len(parities) == 2 else 0
            total[side, at] += lax.dot_general(
                operand[...], held[slot], contract, preferred_element_type=jnp.float32
            )

        if fetched:
            fetch(slot).wait()
        if len(parities) == 2:
            add()
        else:
            pl.when(target % 2 == parities[0])(add)
        return carry

    lax.fori_loop(0, live, visit, 0)
    for p in range(len(parities)):
        for h, ref in enumerate(places[p]):
            for b in range(per_out):
                ref[:, b * span_out : (b + 1) * span_out] = total[
                    p, h * per_out + b
                ].astype(ref.dtype)


def sweep(forward, fetched, parities, tiles, info, parts, receivers, stacked, blocks_out):
    slots, rows_tile, cols_tile = tiles.shape
    width = parts[0].shape[1]
    span_in, span_out = (cols_tile, rows_tile) if forward else (rows_tile, cols_tile)
    pieces = len(parts)
    half = receivers // 2
    wide = blocks_out // receivers * span_out
    out_shape = []
    for p in parities:
        kind = jnp.bfloat16 if p else jnp.float32
        if stacked:
            out_shape += [jax.ShapeDtypeStruct((half, width, wide), kind)]
        else:
            out_shape += [jax.ShapeDtypeStruct((1, width, wide), kind)] * half
    vmem = pl.BlockSpec(memory_space=pltpu.VMEM)
    scratch = [
        pltpu.VMEM((len(parities), blocks_out // 2, width, span_out), jnp.float32),
        pltpu.VMEM((width, span_in), jnp.bfloat16),
    ]
    if fetched:
        scratch += [pltpu.VMEM(tiles.shape, tiles.dtype), pltpu.SemaphoreType.DMA((slots,))]
    results = pl.pallas_call(
        functools.partial(
            sweep_kernel, forward, fetched, parities, pieces, parts[0].shape[2] // span_in
        ),
        out_shape=out_shape,
        in_specs=[
            pl.BlockSpec(memory_space=pltpu.SMEM),
            pl.BlockSpec(memory_space=pl.ANY) if fetched else vmem,
        ]
        + [vmem] * pieces,
        out_specs=[vmem] * len(out_shape),
        scratch_shapes=scratch,
        compiler_params=pltpu.CompilerParams(
            vmem_limit_bytes=FETCH_LIMIT if fetched else VMEM_LIMIT
        ),
        cost_estimate=pl.CostEstimate(
            flops=len(parities) * slots * width * rows_tile * cols_tile,
            bytes_accessed=tiles.size * len(parities),
            transcendentals=0,
        ),
        name="forward_sweep" if forward else "transpose_sweep",
    )(info, tiles, *parts[::-1])
    each = len(results) // len(parities)
    return [results[i * each : (i + 1) * each] for i in range(len(parities))]


def swap(value, axis, size, k):
    return lax.ppermute(value, axis, [(i, i ^ k) for i in range(size)])


def gather_pairs(own, axis, size):
    parts = [None] * size
    parts[0] = own
    for k in range(size - 2, 0, -2):
        parts[k] = swap(own, axis, size, k)
    for k in range(size - 2, -1, -2):
        parts[k + 1] = swap(parts[k], axis, size, 1)
    return parts


def sum_pairs(kept, sent, axis, size):
    total = None
    for h in range(size // 2 - 1, -1, -1):
        pair = kept[h] + swap(sent[h], axis, size, 1).astype(jnp.float32)
        if h:
            pair = swap(pair.astype(jnp.bfloat16), axis, size, 2 * h).astype(jnp.float32)
        total = pair if total is None else total + pair
    return total


def sum_halves(kept, sent, axis, size):
    here = kept + swap(sent, axis, size, 1).astype(jnp.float32)
    away = here.astype(jnp.bfloat16)
    total = here
    for t in range(1, size // 2):
        other = swap(away, axis, size, 2 * t)
        order = [h ^ t for h in range(size // 2)]
        total = total + jnp.stack([other[h] for h in order]).astype(jnp.float32)
    return total


def body(
    rows,
    cols,
    tiles,
    tile_index,
    tile_count,
    weights,
    carbon,
    completion,
    demand,
    row_kind,
    primal_start,
    dual_start,
):
    blocks = tiles[0, 0]
    info = jnp.concatenate(
        [
            tile_index.reshape(-1),
            tile_count.reshape(-1),
            lax.axis_index("col")[None],
            lax.axis_index("row")[None],
        ]
    ).astype(jnp.int32)
    info_back = jnp.concatenate([info[:-2], info[-1:], info[-2:-1]])
    dual = dual_start[:, 0, :]
    state = jnp.concatenate([primal_start[:, 0, :], carbon, completion])
    states = [state] + [swap(state, "row", rows, k) for k in range(2, rows, 2)]
    states = jnp.stack(states)
    width = weights.shape[0]
    primal = states[:, :width]
    share = weights[:, None]
    cost = share * states[:, width : width + 1] + (1.0 - share) * states[:, width + 1 :]
    for step in range(ITERS):
        dual_parts = gather_pairs(dual.astype(jnp.bfloat16)[None], "col", cols)
        (kept,), (sent,) = sweep(
            False, step == 0, (0, 1), blocks, info, dual_parts, rows, True, BC_DEV
        )
        pull = sum_halves(kept, sent, "row", rows)
        fresh = jnp.maximum(primal - step_primal * (cost - pull), 0.0)
        extra = (2.0 * fresh - primal).astype(jnp.bfloat16)
        primal = fresh
        extra_parts = [extra, swap(extra, "row", rows, 1)]
        kept, sent = sweep(
            True, False, (0, 1), blocks, info_back, extra_parts, cols, False, BR_DEV
        )
        push = sum_pairs(kept, sent, "col", cols)[0]
        moved = dual + step_dual * (demand - push)
        dual = jnp.where(row_kind == 1, jnp.maximum(moved, 0.0), moved)
    return (primal[0][:, None, :], dual[:, None, :])


def solution(mesh):
    placed = (
        P("row", "col", None, None, None),
        P("row", "col", None, None),
        P("row", "col"),
        P(),
        P("col", "row"),
        P("col", "row"),
        P("row", "col"),
        P("row", "col"),
        P(None, "col", "row"),
        P(None, "row", "col"),
    )
    return jax.shard_map(
        functools.partial(body, mesh.shape["row"], mesh.shape["col"]),
        mesh=mesh,
        in_specs=placed,
        out_specs=(P(None, "col", "row"), P(None, "row", "col")),
        check_vma=False,
    )
```

time: 126 us -> 118 us (0.937); the launches traced: 126 us -> 117 us
  waiting for transfers between devices: 70.8 us -> 51.3 us
  starting transfers between devices: 40.5 us -> 46 us
  Pallas kernels: 8.69 us -> 10.6 us
    ppermute x40 -> x35, waiting for transfers between devices: 70.8 us -> 51.3 us  [swap(): return lax.ppermute(value, axis, [(i, i ^ k) for i in range(size)])]
    ppermute x40 -> x35, starting transfers between devices: 40.5 us -> 46 us  [swap(): return lax.ppermute(value, axis, [(i, i ^ k) for i in range(size)])]
    pallas_call x4, Pallas kernels: 8.69 us -> 10.6 us  [sweep(): pl.pallas_call(functools.partial(sweep_kernel, forward, fetched, parities...]
    unnamed x20 -> x16, local copies, waits for them, and re-layouts: 3.8 us -> 4.82 us
  transfers between devices with their start and end apart: 40 -> 35, of which waited for: 25 -> 20; matrix products, arithmetic and copies ran while one was open for 2% -> 3% of each run, Pallas kernels for 0% -> 3%
where the time goes in v4:
time: 118 us; the launch traced here: 117 us
  waiting for transfers between devices  51.3 us (43%)
  starting transfers between devices  46 us (39%)
  Pallas kernels  10.6 us (9%)
  local copies, waits for them, and re-layouts  4.95 us (4%)
  other arithmetic  2.25 us (2%)
  between operations  1.55 us (1%)
    ppermute x35, waiting for transfers between devices, swap(): return lax.ppermute(value, axis, [(i, i ^ k) for i in range(size)])  51.3 us
    ppermute x35, starting transfers between devices, swap(): return lax.ppermute(value, axis, [(i, i ^ k) for i in range(size)])  46 us
    pallas_call x4, Pallas kernels, sweep(): pl.pallas_call(functools.partial(sweep_kernel, forward, fetched, parities...  10.6 us
    unnamed x16, local copies, waits for them, and re-layouts  4.82 us
  transfers between devices with their start and end apart: 35, of which 20 were waited for; matrix products, arithmetic and copies ran while one was open for 3% of the time, Pallas kernels for 3%

profile of v4, /device:TPU:0, one launch (start us, length us, event | category | flops | bytes accessed | tf_op | source)
XLA Modules:
  0.0 116.7 jit_solution(17008704471664744676)
XLA Ops:
  1.7 3.1 %collective-permute-start.5 = (bf16[1,32,2048]{2,1,0:T(8,128)(2,1)S(1)}, bf16[1,32,2048]{2,1,0:T(8,128)(2,1)S(1)}, u32[]{:S(2)}, u32[]{:S(2)}) collective-permute-start(bf16[1,32,2048]{2,1,0:T(8,128)(2,1)S(1)} %bitcast.44), channel_id=1, source_target_pairs={{0,8},{4,12},{8,0},{12,4},{16,24},{20,28},{24,16},{28,20},{1,9},{5... | collective-permute-start | bytes 393224 | tf_op jit(solution)/shard_map/ppermute | solution.py:142
  4.8 2.6 %collective-permute-start.3 = (bf16[1,32,2048]{2,1,0:T(8,128)(2,1)S(1)}, bf16[1,32,2048]{2,1,0:T(8,128)(2,1)S(1)}, u32[]{:S(2)}, u32[]{:S(2)}) collective-permute-start(bf16[1,32,2048]{2,1,0:T(8,128)(2,1)S(1)} %bitcast.45), channel_id=1, source_target_pairs={{0,16},{4,20},{8,24},{12,28},{16,0},{20,4},{24,8},{28,12},{1,17},{... | collective-permute-start | bytes 393224 | tf_op jit(solution)/shard_map/ppermute | solution.py:142
  7.4 1.7 %collective-permute-start.7 = (bf16[1,32,2048]{2,1,0:T(8,128)(2,1)S(1)}, bf16[1,32,2048]{2,1,0:T(8,128)(2,1)S(1)}, u32[]{:S(2)}, u32[]{:S(2)}) collective-permute-start(bf16[1,32,2048]{2,1,0:T(8,128)(2,1)S(1)} %bitcast.47), channel_id=1, source_target_pairs={{0,4},{4,0},{8,12},{12,8},{16,20},{20,16},{24,28},{28,24},{1,5},{5... | collective-permute-start | bytes 393224 | tf_op jit(solution)/shard_map/ppermute | solution.py:142
  11.5 6.2 %collective-permute-done.3.refs_3_ = bf16[1,32,2048]{2,1,0:T(8,128)(2,1)S(1)} collective-permute-done((bf16[1,32,2048]{2,1,0:T(8,128)(2,1)S(1)}, bf16[1,32,2048]{2,1,0:T(8,128)(2,1)S(1)}, u32[]{:S(2)}, u32[]{:S(2)}) %collective-permute-start.3) | collective-permute-done | bytes 131104 | tf_op jit(solution)/shard_map/ppermute | solution.py:142
  20.5 1.6 %collective-permute-start = (f32[34,2048]{1,0:T(8,128)S(1)}, f32[34,2048]{1,0:T(8,128)S(1)}, u32[]{:S(2)}, u32[]{:S(2)}) collective-permute-start(f32[34,2048]{1,0:T(8,128)S(1)} %get-tuple-element.53), channel_id=1, source_target_pairs={{0,2},{1,3},{2,0},{3,1},{4,6},{5,7},{6,4},{7,5},{8,10},{9,11},{10,... | collective-permute-start | bytes 835592 | tf_op jit(solution)/shard_map/ppermute | solution.py:142
  24.2 3.6 %transpose_sweep.2 = (f32[2,32,2048]{2,1,0:T(8,128)S(1)}, bf16[2,32,2048]{2,1,0:T(8,128)(2,1)S(1)}) custom-call(s32[19]{0:T(128)S(1)} %get-tuple-element.59.info, bf16[8,1024,512]{2,1,0:T(8,128)(2,1)} %bitcast.40, bf16[1,32,2048]{2,1,0:T(8,128)(2,1)S(1)} %collective-permute-done.2.refs_0_, bf16[1,32,2048]{2,1,0:T(8,128)(2,1)S(1)} %collective-permute-done.1.refs_1_, ...), custom_call_target="tpu_custom_call" | custom-call | flops 268435456 | bytes 8388608 | tf_op jit(solution)/shard_map/transpose_sweep/pallas_call | solution.py:115
  30.2 7.7 %collective-permute-done.9 = bf16[2,32,2048]{2,1,0:T(8,128)(2,1)S(1)} collective-permute-done((bf16[2,32,2048]{2,1,0:T(8,128)(2,1)S(1)}, bf16[2,32,2048]{2,1,0:T(8,128)(2,1)S(1)}, u32[]{:S(2)}, u32[]{:S(2)}) %collective-permute-start.9) | collective-permute-done | bytes 262176 | tf_op jit(solution)/shard_map/ppermute | solution.py:142
  39.8 2.5 %forward_sweep.2 = (f32[1,32,2048]{2,1,0:T(8,128)S(1)}, f32[1,32,2048]{2,1,0:T(8,128)S(1)}, f32[1,32,2048]{2,1,0:T(8,128)S(1)}, f32[1,32,2048]{2,1,0:T(8,128)S(1...) custom-call(s32[19]{0:T(128)S(1)} %get-tuple-element.58.info, ...), custom_call_target="tpu_custom_call" | custom-call | flops 268435456 | bytes 8388608 | tf_op jit(solution)/shard_map/forward_sweep/pallas_call | solution.py:115
  46.5 2.3 %collective-permute-done.11 = bf16[1,32,2048]{2,1,0:T(8,128)(2,1)S(1)} collective-permute-done((bf16[1,32,2048]{2,1,0:T(8,128)(2,1)S(1)}, bf16[1,32,2048]{2,1,0:T(8,128)(2,1)S(1)}, u32[]{:S(2)}, u32[]{:S(2)}) %collective-permute-start.11) | collective-permute-done | bytes 131104 | tf_op jit(solution)/shard_map/ppermute | solution.py:142
  48.8 4.6 %collective-permute-start.12 = (bf16[1,32,2048]{2,1,0:T(8,128)(2,1)S(1)}, bf16[1,32,2048]{2,1,0:T(8,128)(2,1)S(1)}, u32[]{:S(2)}, u32[]{:S(2)}) collective-permute-start(bf16[1,32,2048]{2,1,0:T(8,128)(2,1)S(1)} %add_convert_fusion.5), channel_id=1, source_target_pairs={{0,24},{4,28},{8,16},{12,20},{16,8},{20,12},{24,0},{28,4},{1,25},{... | collective-permute-start | bytes 393224 | tf_op jit(solution)/shard_map/ppermute | solution.py:142
  54.5 2.5 %collective-permute-start.16 = (bf16[1,32,2048]{2,1,0:T(8,128)(2,1)S(1)}, bf16[1,32,2048]{2,1,0:T(8,128)(2,1)S(1)}, u32[]{:S(2)}, u32[]{:S(2)}) collective-permute-start(bf16[1,32,2048]{2,1,0:T(8,128)(2,1)S(1)} %add_convert_fusion.3), channel_id=1, source_target_pairs={{0,8},{4,12},{8,0},{12,4},{16,24},{20,28},{24,16},{28,20},{1,9},{5... | collective-permute-start | bytes 393224 | tf_op jit(solution)/shard_map/ppermute | solution.py:142
  57.5 3.4 %collective-permute-done.14 = bf16[1,32,2048]{2,1,0:T(8,128)(2,1)S(1)} collective-permute-done((bf16[1,32,2048]{2,1,0:T(8,128)(2,1)S(1)}, bf16[1,32,2048]{2,1,0:T(8,128)(2,1)S(1)}, u32[]{:S(2)}, u32[]{:S(2)}) %collective-permute-start.14) | collective-permute-done | bytes 131104 | tf_op jit(solution)/shard_map/ppermute | solution.py:142
  62.2 3.0 %collective-permute-start.20 = (bf16[1,32,2048]{2,1,0:T(8,128)(2,1)S(1)}, bf16[1,32,2048]{2,1,0:T(8,128)(2,1)S(1)}, u32[]{:S(2)}, u32[]{:S(2)}) collective-permute-start(bf16[1,32,2048]{2,1,0:T(8,128)(2,1)S(1)} %fusion.3.refs_7_), channel_id=1, source_target_pairs={{0,16},{4,20},{8,24},{12,28},{16,0},{20,4},{24,8},{28,12},{1,17},{... | collective-permute-start | bytes 393224 | tf_op jit(solution)/shard_map/ppermute | solution.py:142
  66.1 3.0 %collective-permute-start.24 = (bf16[1,32,2048]{2,1,0:T(8,128)(2,1)S(1)}, bf16[1,32,2048]{2,1,0:T(8,128)(2,1)S(1)}, u32[]{:S(2)}, u32[]{:S(2)}) collective-permute-start(bf16[1,32,2048]{2,1,0:T(8,128)(2,1)S(1)} %fusion.3.refs_7_), channel_id=1, source_target_pairs={{0,4},{4,0},{8,12},{12,8},{16,20},{20,16},{24,28},{28,24},{1,5},{5... | collective-permute-start | bytes 393224 | tf_op jit(solution)/shard_map/ppermute | solution.py:142
  69.4 4.1 %collective-permute-done.20.refs_3_ = bf16[1,32,2048]{2,1,0:T(8,128)(2,1)S(1)} collective-permute-done((bf16[1,32,2048]{2,1,0:T(8,128)(2,1)S(1)}, bf16[1,32,2048]{2,1,0:T(8,128)(2,1)S(1)}, u32[]{:S(2)}, u32[]{:S(2)}) %collective-permute-start.20) | collective-permute-done | bytes 131104 | tf_op jit(solution)/shard_map/ppermute | solution.py:142
  73.5 2.5 %collective-permute-start.19 = (bf16[1,32,2048]{2,1,0:T(8,128)(2,1)S(1)}, bf16[1,32,2048]{2,1,0:T(8,128)(2,1)S(1)}, u32[]{:S(2)}, u32[]{:S(2)}) collective-permute-start(bf16[1,32,2048]{2,1,0:T(8,128)(2,1)S(1)} %collective-permute-done.18.refs_1_), channel_id=1, source_target_pairs={{0,4},{4,0},{8,12},{12,8},{16,20},{20,16},{24,28},{28,24},{1,5},{5... | collective-permute-start | bytes 393224 | tf_op jit(solution)/shard_map/ppermute | solution.py:142
  76.0 2.4 %collective-permute-done.21.refs_2_ = bf16[1,32,2048]{2,1,0:T(8,128)(2,1)S(1)} collective-permute-done((bf16[1,32,2048]{2,1,0:T(8,128)(2,1)S(1)}, bf16[1,32,2048]{2,1,0:T(8,128)(2,1)S(1)}, u32[]{:S(2)}, u32[]{:S(2)}) %collective-permute-start.21) | collective-permute-done | bytes 131104 | tf_op jit(solution)/shard_map/ppermute | solution.py:142
  79.8 1.9 %transpose_sweep.3 = (f32[2,32,2048]{2,1,0:T(8,128)S(1)}, bf16[2,32,2048]{2,1,0:T(8,128)(2,1)S(1)}) custom-call(s32[19]{0:T(128)S(1)} %get-tuple-element.59.info, bf16[8,1024,512]{2,1,0:T(8,128)(2,1)S(1)} %bitcast.42, bf16[1,32,2048]{2,1,0:T(8,128)(2,1)S(1)} %collective-permute-done.19.refs_0_, bf16[1,32,2048]{2,1,0:T(8,128)(2,1)S(1)} %collective-permute-done.18.refs_1_, ...), custom_call_target="tpu_custom_call" | custom-call | flops 268435456 | bytes 8388608 | tf_op jit(solution)/shard_map/transpose_sweep/pallas_call | solution.py:115
  84.2 7.7 %collective-permute-done.26 = bf16[2,32,2048]{2,1,0:T(8,128)(2,1)S(1)} collective-permute-done((bf16[2,32,2048]{2,1,0:T(8,128)(2,1)S(1)}, bf16[2,32,2048]{2,1,0:T(8,128)(2,1)S(1)}, u32[]{:S(2)}, u32[]{:S(2)}) %collective-permute-start.26) | collective-permute-done | bytes 262176 | tf_op jit(solution)/shard_map/ppermute | solution.py:142
  93.8 2.5 %forward_sweep.3 = (f32[1,32,2048]{2,1,0:T(8,128)S(1)}, f32[1,32,2048]{2,1,0:T(8,128)S(1)}, f32[1,32,2048]{2,1,0:T(8,128)S(1)}, f32[1,32,2048]{2,1,0:T(8,128)S(1...) custom-call(s32[19]{0:T(128)S(1)} %get-tuple-element.58.info, ...), custom_call_target="tpu_custom_call" | custom-call | flops 268435456 | bytes 8388608 | tf_op jit(solution)/shard_map/forward_sweep/pallas_call | solution.py:115
  100.4 2.4 %collective-permute-done.28 = bf16[1,32,2048]{2,1,0:T(8,128)(2,1)S(1)} collective-permute-done((bf16[1,32,2048]{2,1,0:T(8,128)(2,1)S(1)}, bf16[1,32,2048]{2,1,0:T(8,128)(2,1)S(1)}, u32[]{:S(2)}, u32[]{:S(2)}) %collective-permute-start.28) | collective-permute-done | bytes 131104 | tf_op jit(solution)/shard_map/ppermute | solution.py:142
  102.8 4.1 %collective-permute-start.29 = (bf16[1,32,2048]{2,1,0:T(8,128)(2,1)S(1)}, bf16[1,32,2048]{2,1,0:T(8,128)(2,1)S(1)}, u32[]{:S(2)}, u32[]{:S(2)}) collective-permute-start(bf16[1,32,2048]{2,1,0:T(8,128)(2,1)S(1)} %add_convert_fusion.2), channel_id=1, source_target_pairs={{0,24},{4,28},{8,16},{12,20},{16,8},{20,12},{24,0},{28,4},{1,25},{... | collective-permute-start | bytes 393224 | tf_op jit(solution)/shard_map/ppermute | solution.py:142
  108.5 1.9 %collective-permute-start.33 = (bf16[1,32,2048]{2,1,0:T(8,128)(2,1)S(1)}, bf16[1,32,2048]{2,1,0:T(8,128)(2,1)S(1)}, u32[]{:S(2)}, u32[]{:S(2)}) collective-permute-start(bf16[1,32,2048]{2,1,0:T(8,128)(2,1)S(1)} %add_convert_fusion), channel_id=1, source_target_pairs={{0,8},{4,12},{8,0},{12,4},{16,24},{20,28},{24,16},{28,20},{1,9},{5... | collective-permute-start | bytes 393224 | tf_op jit(solution)/shard_map/ppermute | solution.py:142
  111.4 3.3 %collective-permute-done.31 = bf16[1,32,2048]{2,1,0:T(8,128)(2,1)S(1)} collective-permute-done((bf16[1,32,2048]{2,1,0:T(8,128)(2,1)S(1)}, bf16[1,32,2048]{2,1,0:T(8,128)(2,1)S(1)}, u32[]{:S(2)}, u32[]{:S(2)}) %collective-permute-start.31) | collective-permute-done | bytes 131104 | tf_op jit(solution)/shard_map/ppermute | solution.py:142
  (87 shorter events, 34.4 us)
Async XLA Ops:
  1.7 8.4 %collective-permute-start.5 = (bf16[1,32,2048]{2,1,0:T(8,128)(2,1)S(1)}, bf16[1,32,2048]{2,1,0:T(8,128)(2,1)S(1)}, u32[]{:S(2)}, u32[]{:S(2)}) collective-permute-start(bf16[1,32,2048]{2,1,0:T(8,128)(2,1)S(1)} %bitcast.44), channel_id=1, source_target_pairs={{0,8},{4,12},{8,0},{12,4},{16,24},{20,28},{24,16},{28,20},{1,9},{5... | collective-permute-start | bytes 393224 | tf_op jit(solution)/shard_map/ppermute | solution.py:142
  4.8 12.9 %collective-permute-start.3 = (bf16[1,32,2048]{2,1,0:T(8,128)(2,1)S(1)}, bf16[1,32,2048]{2,1,0:T(8,128)(2,1)S(1)}, u32[]{:S(2)}, u32[]{:S(2)}) collective-permute-start(bf16[1,32,2048]{2,1,0:T(8,128)(2,1)S(1)} %bitcast.45), channel_id=1, source_target_pairs={{0,16},{4,20},{8,24},{12,28},{16,0},{20,4},{24,8},{28,12},{1,17},{... | collective-permute-start | bytes 393224 | tf_op jit(solution)/shard_map/ppermute | solution.py:142
  7.4 11.8 %collective-permute-start.1 = (bf16[1,32,2048]{2,1,0:T(8,128)(2,1)S(1)}, bf16[1,32,2048]{2,1,0:T(8,128)(2,1)S(1)}, u32[]{:S(2)}, u32[]{:S(2)}) collective-permute-start(bf16[1,32,2048]{2,1,0:T(8,128)(2,1)S(1)} %bitcast.46), channel_id=1, source_target_pairs={{0,24},{4,28},{8,16},{12,20},{16,8},{20,12},{24,0},{28,4},{1,25},{... | collective-permute-start | bytes 393224 | tf_op jit(solution)/shard_map/ppermute | solution.py:142
  7.4 16.3 %collective-permute-start.7 = (bf16[1,32,2048]{2,1,0:T(8,128)(2,1)S(1)}, bf16[1,32,2048]{2,1,0:T(8,128)(2,1)S(1)}, u32[]{:S(2)}, u32[]{:S(2)}) collective-permute-start(bf16[1,32,2048]{2,1,0:T(8,128)(2,1)S(1)} %bitcast.47), channel_id=1, source_target_pairs={{0,4},{4,0},{8,12},{12,8},{16,20},{20,16},{24,28},{28,24},{1,5},{5... | collective-permute-start | bytes 393224 | tf_op jit(solution)/shard_map/ppermute | solution.py:142
  10.1 13.5 %collective-permute-start.6 = (bf16[1,32,2048]{2,1,0:T(8,128)(2,1)S(1)}, bf16[1,32,2048]{2,1,0:T(8,128)(2,1)S(1)}, u32[]{:S(2)}, u32[]{:S(2)}) collective-permute-start(bf16[1,32,2048]{2,1,0:T(8,128)(2,1)S(1)} %collective-permute-done.5.refs_5_), channel_id=1, source_target_pairs={{0,4},{4,0},{8,12},{12,8},{16,20},{20,16},{24,28},{28,24},{1,5},{5... | collective-permute-start | bytes 393224 | tf_op jit(solution)/shard_map/ppermute | solution.py:142
  20.5 7.4 %collective-permute-start = (f32[34,2048]{1,0:T(8,128)S(1)}, f32[34,2048]{1,0:T(8,128)S(1)}, u32[]{:S(2)}, u32[]{:S(2)}) collective-permute-start(f32[34,2048]{1,0:T(8,128)S(1)} %get-tuple-element.53), channel_id=1, source_target_pairs={{0,2},{1,3},{2,0},{3,1},{4,6},{5,7},{6,4},{7,5},{8,10},{9,11},{10,... | collective-permute-start | bytes 835592 | tf_op jit(solution)/shard_map/ppermute | solution.py:142
  29.5 8.4 %collective-permute-start.9 = (bf16[2,32,2048]{2,1,0:T(8,128)(2,1)S(1)}, bf16[2,32,2048]{2,1,0:T(8,128)(2,1)S(1)}, u32[]{:S(2)}, u32[]{:S(2)}) collective-permute-start(bf16[2,32,2048]{2,1,0:T(8,128)(2,1)S(1)} %fusion.1), channel_id=1, source_target_pairs={{0,2},{1,3},{2,0},{3,1},{4,6},{5,7},{6,4},{7,5},{8,10},{9,11},{10,... | collective-permute-start | bytes 786440 | tf_op jit(solution)/shard_map/ppermute | solution.py:142
  43.0 10.5 %collective-permute-start.13 = (bf16[1,32,2048]{2,1,0:T(8,128)(2,1)S(1)}, bf16[1,32,2048]{2,1,0:T(8,128)(2,1)S(1)}, u32[]{:S(2)}, u32[]{:S(2)}) collective-permute-start(bf16[1,32,2048]{2,1,0:T(8,128)(2,1)S(1)} %get-tuple-element.27), channel_id=1, source_target_pairs={{0,4},{4,0},{8,12},{12,8},{16,20},{20,16},{24,28},{28,24},{1,5},{5... | collective-permute-start | bytes 393224 | tf_op jit(solution)/shard_map/ppermute | solution.py:142
  44.4 10.0 %collective-permute-start.15 = (bf16[1,32,2048]{2,1,0:T(8,128)(2,1)S(1)}, bf16[1,32,2048]{2,1,0:T(8,128)(2,1)S(1)}, u32[]{:S(2)}, u32[]{:S(2)}) collective-permute-start(bf16[1,32,2048]{2,1,0:T(8,128)(2,1)S(1)} %get-tuple-element.29), channel_id=1, source_target_pairs={{0,4},{4,0},{8,12},{12,8},{16,20},{20,16},{24,28},{28,24},{1,5},{5... | collective-permute-start | bytes 393224 | tf_op jit(solution)/shard_map/ppermute | solution.py:142
  45.1 11.9 %collective-permute-start.17 = (bf16[1,32,2048]{2,1,0:T(8,128)(2,1)S(1)}, bf16[1,32,2048]{2,1,0:T(8,128)(2,1)S(1)}, u32[]{:S(2)}, u32[]{:S(2)}) collective-permute-start(bf16[1,32,2048]{2,1,0:T(8,128)(2,1)S(1)} %get-tuple-element.31), channel_id=1, source_target_pairs={{0,4},{4,0},{8,12},{12,8},{16,20},{20,16},{24,28},{28,24},{1,5},{5... | collective-permute-start | bytes 393224 | tf_op jit(solution)/shard_map/ppermute | solution.py:142
  48.8 8.7 %collective-permute-start.12 = (bf16[1,32,2048]{2,1,0:T(8,128)(2,1)S(1)}, bf16[1,32,2048]{2,1,0:T(8,128)(2,1)S(1)}, u32[]{:S(2)}, u32[]{:S(2)}) collective-permute-start(bf16[1,32,2048]{2,1,0:T(8,128)(2,1)S(1)} %add_convert_fusion.5), channel_id=1, source_target_pairs={{0,24},{4,28},{8,16},{12,20},{16,8},{20,12},{24,0},{28,4},{1,25},{... | collective-permute-start | bytes 393224 | tf_op jit(solution)/shard_map/ppermute | solution.py:142
  53.5 7.4 %collective-permute-start.14 = (bf16[1,32,2048]{2,1,0:T(8,128)(2,1)S(1)}, bf16[1,32,2048]{2,1,0:T(8,128)(2,1)S(1)}, u32[]{:S(2)}, u32[]{:S(2)}) collective-permute-start(bf16[1,32,2048]{2,1,0:T(8,128)(2,1)S(1)} %add_convert_fusion.4), channel_id=1, source_target_pairs={{0,16},{4,20},{8,24},{12,28},{16,0},{20,4},{24,8},{28,12},{1,17},{... | collective-permute-start | bytes 393224 | tf_op jit(solution)/shard_map/ppermute | solution.py:142
  54.5 7.0 %collective-permute-start.16 = (bf16[1,32,2048]{2,1,0:T(8,128)(2,1)S(1)}, bf16[1,32,2048]{2,1,0:T(8,128)(2,1)S(1)}, u32[]{:S(2)}, u32[]{:S(2)}) collective-permute-start(bf16[1,32,2048]{2,1,0:T(8,128)(2,1)S(1)} %add_convert_fusion.3), channel_id=1, source_target_pairs={{0,8},{4,12},{8,0},{12,4},{16,24},{20,28},{24,16},{28,20},{1,9},{5... | collective-permute-start | bytes 393224 | tf_op jit(solution)/shard_map/ppermute | solution.py:142
  61.6 7.5 %collective-permute-start.22 = (bf16[1,32,2048]{2,1,0:T(8,128)(2,1)S(1)}, bf16[1,32,2048]{2,1,0:T(8,128)(2,1)S(1)}, u32[]{:S(2)}, u32[]{:S(2)}) collective-permute-start(bf16[1,32,2048]{2,1,0:T(8,128)(2,1)S(1)} %fusion.3.refs_7_), channel_id=1, source_target_pairs={{0,8},{4,12},{8,0},{12,4},{16,24},{20,28},{24,16},{28,20},{1,9},{5... | collective-permute-start | bytes 393224 | tf_op jit(solution)/shard_map/ppermute | solution.py:142
  62.2 11.3 %collective-permute-start.20 = (bf16[1,32,2048]{2,1,0:T(8,128)(2,1)S(1)}, bf16[1,32,2048]{2,1,0:T(8,128)(2,1)S(1)}, u32[]{:S(2)}, u32[]{:S(2)}) collective-permute-start(bf16[1,32,2048]{2,1,0:T(8,128)(2,1)S(1)} %fusion.3.refs_7_), channel_id=1, source_target_pairs={{0,16},{4,20},{8,24},{12,28},{16,0},{20,4},{24,8},{28,12},{1,17},{... | collective-permute-start | bytes 393224 | tf_op jit(solution)/shard_map/ppermute | solution.py:142
  65.2 8.3 %collective-permute-start.18 = (bf16[1,32,2048]{2,1,0:T(8,128)(2,1)S(1)}, bf16[1,32,2048]{2,1,0:T(8,128)(2,1)S(1)}, u32[]{:S(2)}, u32[]{:S(2)}) collective-permute-start(bf16[1,32,2048]{2,1,0:T(8,128)(2,1)S(1)} %fusion.3.refs_7_), channel_id=1, source_target_pairs={{0,24},{4,28},{8,16},{12,20},{16,8},{20,12},{24,0},{28,4},{1,25},{... | collective-permute-start | bytes 393224 | tf_op jit(solution)/shard_map/ppermute | solution.py:142
  66.1 9.9 %collective-permute-start.24 = (bf16[1,32,2048]{2,1,0:T(8,128)(2,1)S(1)}, bf16[1,32,2048]{2,1,0:T(8,128)(2,1)S(1)}, u32[]{:S(2)}, u32[]{:S(2)}) collective-permute-start(bf16[1,32,2048]{2,1,0:T(8,128)(2,1)S(1)} %fusion.3.refs_7_), channel_id=1, source_target_pairs={{0,4},{4,0},{8,12},{12,8},{16,20},{20,16},{24,28},{28,24},{1,5},{5... | collective-permute-start | bytes 393224 | tf_op jit(solution)/shard_map/ppermute | solution.py:142
  83.5 8.4 %collective-permute-start.26 = (bf16[2,32,2048]{2,1,0:T(8,128)(2,1)S(1)}, bf16[2,32,2048]{2,1,0:T(8,128)(2,1)S(1)}, u32[]{:S(2)}, u32[]{:S(2)}) collective-permute-start(bf16[2,32,2048]{2,1,0:T(8,128)(2,1)S(1)} %fusion.2), channel_id=1, source_target_pairs={{0,2},{1,3},{2,0},{3,1},{4,6},{5,7},{6,4},{7,5},{8,10},{9,11},{10,... | collective-permute-start | bytes 786440 | tf_op jit(solution)/shard_map/ppermute | solution.py:142
  96.9 10.0 %collective-permute-start.30 = (bf16[1,32,2048]{2,1,0:T(8,128)(2,1)S(1)}, bf16[1,32,2048]{2,1,0:T(8,128)(2,1)S(1)}, u32[]{:S(2)}, u32[]{:S(2)}) collective-permute-start(bf16[1,32,2048]{2,1,0:T(8,128)(2,1)S(1)} %get-tuple-element.37), channel_id=1, source_target_pairs={{0,4},{4,0},{8,12},{12,8},{16,20},{20,16},{24,28},{28,24},{1,5},{5... | collective-permute-start | bytes 393224 | tf_op jit(solution)/shard_map/ppermute | solution.py:142
  98.4 10.0 %collective-permute-start.32 = (bf16[1,32,2048]{2,1,0:T(8,128)(2,1)S(1)}, bf16[1,32,2048]{2,1,0:T(8,128)(2,1)S(1)}, u32[]{:S(2)}, u32[]{:S(2)}) collective-permute-start(bf16[1,32,2048]{2,1,0:T(8,128)(2,1)S(1)} %get-tuple-element.39), channel_id=1, source_target_pairs={{0,4},{4,0},{8,12},{12,8},{16,20},{20,16},{24,28},{28,24},{1,5},{5... | collective-permute-start | bytes 393224 | tf_op jit(solution)/shard_map/ppermute | solution.py:142
  98.9 12.4 %collective-permute-start.34 = (bf16[1,32,2048]{2,1,0:T(8,128)(2,1)S(1)}, bf16[1,32,2048]{2,1,0:T(8,128)(2,1)S(1)}, u32[]{:S(2)}, u32[]{:S(2)}) collective-permute-start(bf16[1,32,2048]{2,1,0:T(8,128)(2,1)S(1)} %get-tuple-element.41), channel_id=1, source_target_pairs={{0,4},{4,0},{8,12},{12,8},{16,20},{20,16},{24,28},{28,24},{1,5},{5... | collective-permute-start | bytes 393224 | tf_op jit(solution)/shard_map/ppermute | solution.py:142
  102.8 8.5 %collective-permute-start.29 = (bf16[1,32,2048]{2,1,0:T(8,128)(2,1)S(1)}, bf16[1,32,2048]{2,1,0:T(8,128)(2,1)S(1)}, u32[]{:S(2)}, u32[]{:S(2)}) collective-permute-start(bf16[1,32,2048]{2,1,0:T(8,128)(2,1)S(1)} %add_convert_fusion.2), channel_id=1, source_target_pairs={{0,24},{4,28},{8,16},{12,20},{16,8},{20,12},{24,0},{28,4},{1,25},{... | collective-permute-start | bytes 393224 | tf_op jit(solution)/shard_map/ppermute | solution.py:142
  106.9 7.8 %collective-permute-start.31 = (bf16[1,32,2048]{2,1,0:T(8,128)(2,1)S(1)}, bf16[1,32,2048]{2,1,0:T(8,128)(2,1)S(1)}, u32[]{:S(2)}, u32[]{:S(2)}) collective-permute-start(bf16[1,32,2048]{2,1,0:T(8,128)(2,1)S(1)} %add_convert_fusion.1), channel_id=1, source_target_pairs={{0,16},{4,20},{8,24},{12,28},{16,0},{20,4},{24,8},{28,12},{1,17},{... | collective-permute-start | bytes 393224 | tf_op jit(solution)/shard_map/ppermute | solution.py:142
  108.5 6.9 %collective-permute-start.33 = (bf16[1,32,2048]{2,1,0:T(8,128)(2,1)S(1)}, bf16[1,32,2048]{2,1,0:T(8,128)(2,1)S(1)}, u32[]{:S(2)}, u32[]{:S(2)}) collective-permute-start(bf16[1,32,2048]{2,1,0:T(8,128)(2,1)S(1)} %add_convert_fusion), channel_id=1, source_target_pairs={{0,8},{4,12},{8,0},{12,4},{16,24},{20,28},{24,16},{28,20},{1,9},{5... | collective-permute-start | bytes 393224 | tf_op jit(solution)/shard_map/ppermute | solution.py:142
  (16 other events, 188.5 us)

commit v5 on v4

--- a/solution.py
+++ b/solution.py
@@ -19,46 +19,44 @@
 FETCH_LIMIT = 46 * 1024 * 1024
 
 
-def sweep_kernel(forward, fetched, parities, pieces, per_in, info, tiles, *refs):
+def sweep_kernel(forward, fetched, parity, pieces, per_in, info, tiles, *refs):
     parts = refs[:pieces][::-1]
     own = 4 if fetched else 2
-    results = refs[pieces:-own]
-    scratch = refs[-own:]
-    total, operand = scratch[:2]
+    places = [ref.at[h] for ref in refs[pieces:-own] for h in range(ref.shape[0])]
+    total, operand = refs[-own : 2 - own or None]
     slots = tiles.shape[0]
     live = info[2 * slots]
     me_in = info[2 * slots + 1]
     me_out = info[2 * slots + 2]
     span_in = operand.shape[1]
-    count, width, span_out = total.shape[1:]
-    places = [[] for _ in parities]
-    per_parity = len(results) // len(parities)
-    for p in range(len(parities)):
-        for ref in results[p * per_parity : (p + 1) * per_parity]:
-            places[p] += [ref.at[h] for h in range(ref.shape[0])]
-    per_out = count // len(places[0])
+    span_out = total.shape[2]
+    per_out = total.shape[0] // len(places)
     held = tiles
+
+    def target(slot):
+        return (info[2 * slot + (0 if forward else 1)] // per_out) ^ me_out
+
     if fetched:
-        held, arrived = scratch[2:]
+        held, arrived = refs[-2:]
 
         def fetch(slot):
             return pltpu.make_async_copy(tiles.at[slot], held.at[slot], arrived.at[slot])
 
         def start(slot, carry):
-            fetch(slot).start()
+            @pl.when(target(slot) % 2 == parity)
+            def _():
+                fetch(slot).start()
+
             return carry
 
         lax.fori_loop(0, live, start, 0)
     total[...] = jnp.zeros_like(total)
 
     def visit(slot, carry):
-        block_row = info[2 * slot]
-        block_col = info[2 * slot + 1]
-        block_in = block_col if forward else block_row
-        block_out = block_row if forward else block_col
-        target = (block_out // per_out) ^ me_out
-
-        def add():
+        @pl.when(target(slot) % 2 == parity)
+        def _():
+            block_in = info[2 * slot + (1 if forward else 0)]
+            block_out = info[2 * slot + (0 if forward else 1)]
             source = (block_in // per_in) ^ me_in
             place = pl.multiple_of((block_in % per_in) * span_in, span_in)
             for k in range(pieces):
@@ -67,54 +65,45 @@
                 def _():
                     operand[...] = parts[k][source // pieces, :, pl.ds(place, span_in)]
 
+            if fetched:
+                fetch(slot).wait()
             contract = (((1,), (1,)), ((), ())) if forward else (((1,), (0,)), ((), ()))
-            at = (target // 2) * per_out + block_out % per_out
-            side = target % 2 if len(parities) == 2 else 0
-            total[side, at] += lax.dot_general(
+            total[(target(slot) // 2) * per_out + block_out % per_out] += lax.dot_general(
                 operand[...], held[slot], contract, preferred_element_type=jnp.float32
             )
 
-        if fetched:
-            fetch(slot).wait()
-        if len(parities) == 2:
-            add()
-        else:
-            pl.when(target % 2 == parities[0])(add)
         return carry
 
     lax.fori_loop(0, live, visit, 0)
-    for p in range(len(parities)):
-        for h, ref in enumerate(places[p]):
-            for b in range(per_out):
-                ref[:, b * span_out : (b + 1) * span_out] = total[
-                    p, h * per_out + b
-                ].astype(ref.dtype)
-
-
-def sweep(forward, fetched, parities, tiles, info, parts, receivers, stacked, blocks_out):
+    for h, place in enumerate(places):
+        for b in range(per_out):
+            place[:, b * span_out : (b + 1) * span_out] = total[h * per_out + b].astype(
+                place.dtype
+            )
+
+
+def sweep(forward, fetched, parity, tiles, info, parts, receivers, stacked, blocks_out):
     slots, rows_tile, cols_tile = tiles.shape
     width = parts[0].shape[1]
     span_in, span_out = (cols_tile, rows_tile) if forward else (rows_tile, cols_tile)
     pieces = len(parts)
     half = receivers // 2
     wide = blocks_out // receivers * span_out
-    out_shape = []
-    for p in parities:
-        kind = jnp.bfloat16 if p else jnp.float32
-        if stacked:
-            out_shape += [jax.ShapeDtypeStruct((half, width, wide), kind)]
-        else:
-            out_shape += [jax.ShapeDtypeStruct((1, width, wide), kind)] * half
+    kind = jnp.bfloat16 if parity else jnp.float32
+    if stacked:
+        out_shape = [jax.ShapeDtypeStruct((half, width, wide), kind)]
+    else:
+        out_shape = [jax.ShapeDtypeStruct((1, width, wide), kind)] * half
     vmem = pl.BlockSpec(memory_space=pltpu.VMEM)
     scratch = [
-        pltpu.VMEM((len(parities), blocks_out // 2, width, span_out), jnp.float32),
+        pltpu.VMEM((blocks_out // 2, width, span_out), jnp.float32),
         pltpu.VMEM((width, span_in), jnp.bfloat16),
     ]
     if fetched:
         scratch += [pltpu.VMEM(tiles.shape, tiles.dtype), pltpu.SemaphoreType.DMA((slots,))]
-    results = pl.pallas_call(
+    return pl.pallas_call(
         functools.partial(
-            sweep_kernel, forward, fetched, parities, pieces, parts[0].shape[2] // span_in
+            sweep_kernel, forward, fetched, parity, pieces, parts[0].shape[2] // span_in
         ),
         out_shape=out_shape,
         in_specs=[
@@ -128,14 +117,12 @@
             vmem_limit_bytes=FETCH_LIMIT if fetched else VMEM_LIMIT
         ),
         cost_estimate=pl.CostEstimate(
-            flops=len(parities) * slots * width * rows_tile * cols_tile,
-            bytes_accessed=tiles.size * len(parities),
+            flops=slots * width * rows_tile * cols_tile,
+            bytes_accessed=tiles.size,
             transcendentals=0,
         ),
         name="forward_sweep" if forward else "transpose_sweep",
     )(info, tiles, *parts[::-1])
-    each = len(results) // len(parities)
-    return [results[i * each : (i + 1) * each] for i in range(len(parities))]
 
 
 def swap(value, axis, size, k):
@@ -207,17 +194,23 @@
     cost = share * states[:, width : width + 1] + (1.0 - share) * states[:, width + 1 :]
     for step in range(ITERS):
         dual_parts = gather_pairs(dual.astype(jnp.bfloat16)[None], "col", cols)
-        (kept,), (sent,) = sweep(
-            False, step == 0, (0, 1), blocks, info, dual_parts, rows, True, BC_DEV
+        turn = functools.partial(
+            sweep, False, step == 0, tiles=blocks, info=info, parts=dual_parts,
+            receivers=rows, stacked=True, blocks_out=BC_DEV,
         )
+        (sent,) = turn(1)
+        (kept,) = turn(0)
         pull = sum_halves(kept, sent, "row", rows)
         fresh = jnp.maximum(primal - step_primal * (cost - pull), 0.0)
         extra = (2.0 * fresh - primal).astype(jnp.bfloat16)
         primal = fresh
         extra_parts = [extra, swap(extra, "row", rows, 1)]
-        kept, sent = sweep(
-            True, False, (0, 1), blocks, info_back, extra_parts, cols, False, BR_DEV
+        turn = functools.partial(
+            sweep, True, False, tiles=blocks, info=info_back, parts=extra_parts,
+            receivers=cols, stacked=False, blocks_out=BR_DEV,
         )
+        sent = turn(1)
+        kept = turn(0)
         push = sum_pairs(kept, sent, "col", cols)[0]
         moved = dual + step_dual * (demand - push)
         dual = jnp.where(row_kind == 1, jnp.maximum(moved, 0.0), moved)

time: 118 us -> 117 us (level)
  starting transfers between devices: 46 us -> 44.5 us
    ppermute x35, starting transfers between devices: 46 us -> 44.5 us  [swap(): return lax.ppermute(value, axis, [(i, i ^ k) for i in range(size)])]
    pallas_call x4 -> x8, Pallas kernels: 10.6 us -> 11.5 us  [sweep(): pl.pallas_call(functools.partial(sweep_kernel, forward, fetched, parity,...]
    unnamed x16 -> x18, local copies, waits for them, and re-layouts: 4.82 us -> 4.82 us
  transfers between devices with their start and end apart: 35 -> 35, of which waited for: 20 -> 22; matrix products, arithmetic and copies ran while one was open for 3% -> 3% of each run, Pallas kernels for 3% -> 7%
where the time goes in v5:
time: 117 us; the launch traced here: 115 us
  waiting for transfers between devices  50.7 us (43%)
  starting transfers between devices  44.5 us (38%)
  Pallas kernels  11.5 us (10%)
  local copies, waits for them, and re-layouts  4.96 us (4%)
  other arithmetic  2.21 us (2%)
  between operations  1.58 us (1%)
    ppermute x35, waiting for transfers between devices, swap(): return lax.ppermute(value, axis, [(i, i ^ k) for i in range(size)])  50.7 us
    ppermute x35, starting transfers between devices, swap(): return lax.ppermute(value, axis, [(i, i ^ k) for i in range(size)])  44.5 us
    pallas_call x8, Pallas kernels, sweep(): pl.pallas_call(functools.partial(sweep_kernel, forward, fetched, parity,...  11.5 us
    unnamed x18, local copies, waits for them, and re-layouts  4.82 us
  transfers between devices with their start and end apart: 35, of which 22 were waited for; matrix products, arithmetic and copies ran while one was open for 3% of the time, Pallas kernels for 7%

profile of v5, /device:TPU:0, one launch (start us, length us, event | category | flops | bytes accessed | tf_op | source)
XLA Modules:
  0.0 115.5 jit_solution(2592738231341593439)
XLA Ops:
  1.7 3.1 %collective-permute-start.5 = (bf16[1,32,2048]{2,1,0:T(8,128)(2,1)S(1)}, bf16[1,32,2048]{2,1,0:T(8,128)(2,1)S(1)}, u32[]{:S(2)}, u32[]{:S(2)}) collective-permute-start(bf16[1,32,2048]{2,1,0:T(8,128)(2,1)S(1)} %bitcast.50), channel_id=1, source_target_pairs={{0,8},{4,12},{8,0},{12,4},{16,24},{20,28},{24,16},{28,20},{1,9},{5... | collective-permute-start | bytes 393224 | tf_op jit(solution)/shard_map/ppermute | solution.py:129
  4.8 2.6 %collective-permute-start.3 = (bf16[1,32,2048]{2,1,0:T(8,128)(2,1)S(1)}, bf16[1,32,2048]{2,1,0:T(8,128)(2,1)S(1)}, u32[]{:S(2)}, u32[]{:S(2)}) collective-permute-start(bf16[1,32,2048]{2,1,0:T(8,128)(2,1)S(1)} %bitcast.51), channel_id=1, source_target_pairs={{0,16},{4,20},{8,24},{12,28},{16,0},{20,4},{24,8},{28,12},{1,17},{... | collective-permute-start | bytes 393224 | tf_op jit(solution)/shard_map/ppermute | solution.py:129
  7.4 1.7 %collective-permute-start.7 = (bf16[1,32,2048]{2,1,0:T(8,128)(2,1)S(1)}, bf16[1,32,2048]{2,1,0:T(8,128)(2,1)S(1)}, u32[]{:S(2)}, u32[]{:S(2)}) collective-permute-start(bf16[1,32,2048]{2,1,0:T(8,128)(2,1)S(1)} %bitcast.53), channel_id=1, source_target_pairs={{0,4},{4,0},{8,12},{12,8},{16,20},{20,16},{24,28},{28,24},{1,5},{5... | collective-permute-start | bytes 393224 | tf_op jit(solution)/shard_map/ppermute | solution.py:129
  11.5 6.2 %collective-permute-done.3.refs_3_ = bf16[1,32,2048]{2,1,0:T(8,128)(2,1)S(1)} collective-permute-done((bf16[1,32,2048]{2,1,0:T(8,128)(2,1)S(1)}, bf16[1,32,2048]{2,1,0:T(8,128)(2,1)S(1)}, u32[]{:S(2)}, u32[]{:S(2)}) %collective-permute-start.3) | collective-permute-done | bytes 131104 | tf_op jit(solution)/shard_map/ppermute | solution.py:129
  20.5 1.6 %collective-permute-start = (f32[34,2048]{1,0:T(8,128)S(1)}, f32[34,2048]{1,0:T(8,128)S(1)}, u32[]{:S(2)}, u32[]{:S(2)}) collective-permute-start(f32[34,2048]{1,0:T(8,128)S(1)} %get-tuple-element.45), channel_id=1, source_target_pairs={{0,2},{1,3},{2,0},{3,1},{4,6},{5,7},{6,4},{7,5},{8,10},{9,11},{10,... | collective-permute-start | bytes 835592 | tf_op jit(solution)/shard_map/ppermute | solution.py:129
  24.2 2.5 %transpose_sweep.5 = bf16[2,32,2048]{2,1,0:T(8,128)(2,1)S(1)} custom-call(s32[19]{0:T(128)S(1)} %get-tuple-element.51.info, bf16[8,1024,512]{2,1,0:T(8,128)(2,1)} %bitcast.40, bf16[1,32,2048]{2,1,0:T(8,128)(2,1)S(1)} %collective-permute-done.2.refs_0_, bf16[1,32,2048]{2,1,0:T(8,128)(2,1)S(1)} %collective-permute-done.1.refs_1_, ...), custom_call_target="tpu_custom_call" | custom-call | flops 134217728 | bytes 4194304 | tf_op jit(solution)/shard_map/transpose_sweep/pallas_call | solution.py:104
  26.8 2.5 %transpose_sweep.4 = f32[2,32,2048]{2,1,0:T(8,128)S(1)} custom-call(s32[19]{0:T(128)S(1)} %get-tuple-element.51.info, bf16[8,1024,512]{2,1,0:T(8,128)(2,1)} %bitcast.41, bf16[1,32,2048]{2,1,0:T(8,128)(2,1)S(1)} %collective-permute-done.2.refs_0_, bf16[1,32,2048]{2,1,0:T(8,128)(2,1)S(1)} %collective-permute-done.1.refs_1_, ...), custom_call_target="tpu_custom_call" | custom-call | flops 134217728 | bytes 4194304 | tf_op jit(solution)/shard_map/transpose_sweep/pallas_call | solution.py:104
  29.6 7.2 %collective-permute-done.9 = bf16[2,32,2048]{2,1,0:T(8,128)(2,1)S(1)} collective-permute-done((bf16[2,32,2048]{2,1,0:T(8,128)(2,1)S(1)}, bf16[2,32,2048]{2,1,0:T(8,128)(2,1)S(1)}, u32[]{:S(2)}, u32[]{:S(2)}) %collective-permute-start.9) | collective-permute-done | bytes 262176 | tf_op jit(solution)/shard_map/ppermute | solution.py:129
  39.8 4.4 %collective-permute-start.13 = (bf16[1,32,2048]{2,1,0:T(8,128)(2,1)S(1)}, bf16[1,32,2048]{2,1,0:T(8,128)(2,1)S(1)}, u32[]{:S(2)}, u32[]{:S(2)}) collective-permute-start(bf16[1,32,2048]{2,1,0:T(8,128)(2,1)S(1)} %get-tuple-element.21), channel_id=1, source_target_pairs={{0,4},{4,0},{8,12},{12,8},{16,20},{20,16},{24,28},{28,24},{1,5},{5... | collective-permute-start | bytes 393224 | tf_op jit(solution)/shard_map/ppermute | solution.py:129
  44.3 1.9 %collective-permute-start.15 = (bf16[1,32,2048]{2,1,0:T(8,128)(2,1)S(1)}, bf16[1,32,2048]{2,1,0:T(8,128)(2,1)S(1)}, u32[]{:S(2)}, u32[]{:S(2)}) collective-permute-start(bf16[1,32,2048]{2,1,0:T(8,128)(2,1)S(1)} %get-tuple-element.23), channel_id=1, source_target_pairs={{0,4},{4,0},{8,12},{12,8},{16,20},{20,16},{24,28},{28,24},{1,5},{5... | collective-permute-start | bytes 393224 | tf_op jit(solution)/shard_map/ppermute | solution.py:129
  51.4 2.2 %collective-permute-start.12 = (bf16[1,32,2048]{2,1,0:T(8,128)(2,1)S(1)}, bf16[1,32,2048]{2,1,0:T(8,128)(2,1)S(1)}, u32[]{:S(2)}, u32[]{:S(2)}) collective-permute-start(bf16[1,32,2048]{2,1,0:T(8,128)(2,1)S(1)} %add_convert_fusion.5), channel_id=1, source_target_pairs={{0,24},{4,28},{8,16},{12,20},{16,8},{20,12},{24,0},{28,4},{1,25},{... | collective-permute-start | bytes 393224 | tf_op jit(solution)/shard_map/ppermute | solution.py:129
  55.3 4.8 %collective-permute-done.14 = bf16[1,32,2048]{2,1,0:T(8,128)(2,1)S(1)} collective-permute-done((bf16[1,32,2048]{2,1,0:T(8,128)(2,1)S(1)}, bf16[1,32,2048]{2,1,0:T(8,128)(2,1)S(1)}, u32[]{:S(2)}, u32[]{:S(2)}) %collective-permute-start.14) | collective-permute-done | bytes 131104 | tf_op jit(solution)/shard_map/ppermute | solution.py:129
  62.2 2.1 %collective-permute-start.20 = (bf16[1,32,2048]{2,1,0:T(8,128)(2,1)S(1)}, bf16[1,32,2048]{2,1,0:T(8,128)(2,1)S(1)}, u32[]{:S(2)}, u32[]{:S(2)}) collective-permute-start(bf16[1,32,2048]{2,1,0:T(8,128)(2,1)S(1)} %fusion.3.refs_7_), channel_id=1, source_target_pairs={{0,16},{4,20},{8,24},{12,28},{16,0},{20,4},{24,8},{28,12},{1,17},{... | collective-permute-start | bytes 393224 | tf_op jit(solution)/shard_map/ppermute | solution.py:129
  67.0 1.8 %collective-permute-start.23 = (bf16[1,32,2048]{2,1,0:T(8,128)(2,1)S(1)}, bf16[1,32,2048]{2,1,0:T(8,128)(2,1)S(1)}, u32[]{:S(2)}, u32[]{:S(2)}) collective-permute-start(bf16[1,32,2048]{2,1,0:T(8,128)(2,1)S(1)} %collective-permute-done.22.refs_5_), channel_id=1, source_target_pairs={{0,4},{4,0},{8,12},{12,8},{16,20},{20,16},{24,28},{28,24},{1,5},{5... | collective-permute-start | bytes 393224 | tf_op jit(solution)/shard_map/ppermute | solution.py:129
  68.8 5.2 %collective-permute-done.20.refs_3_ = bf16[1,32,2048]{2,1,0:T(8,128)(2,1)S(1)} collective-permute-done((bf16[1,32,2048]{2,1,0:T(8,128)(2,1)S(1)}, bf16[1,32,2048]{2,1,0:T(8,128)(2,1)S(1)}, u32[]{:S(2)}, u32[]{:S(2)}) %collective-permute-start.20) | collective-permute-done | bytes 131104 | tf_op jit(solution)/shard_map/ppermute | solution.py:129
  73.9 1.6 %collective-permute-start.21 = (bf16[1,32,2048]{2,1,0:T(8,128)(2,1)S(1)}, bf16[1,32,2048]{2,1,0:T(8,128)(2,1)S(1)}, u32[]{:S(2)}, u32[]{:S(2)}) collective-permute-start(bf16[1,32,2048]{2,1,0:T(8,128)(2,1)S(1)} %collective-permute-done.20.refs_3_), channel_id=1, source_target_pairs={{0,4},{4,0},{8,12},{12,8},{16,20},{20,16},{24,28},{28,24},{1,5},{5... | collective-permute-start | bytes 393224 | tf_op jit(solution)/shard_map/ppermute | solution.py:129
  76.0 2.9 %collective-permute-done.21.refs_2_ = bf16[1,32,2048]{2,1,0:T(8,128)(2,1)S(1)} collective-permute-done((bf16[1,32,2048]{2,1,0:T(8,128)(2,1)S(1)}, bf16[1,32,2048]{2,1,0:T(8,128)(2,1)S(1)}, u32[]{:S(2)}, u32[]{:S(2)}) %collective-permute-start.21) | collective-permute-done | bytes 131104 | tf_op jit(solution)/shard_map/ppermute | solution.py:129
  78.9 1.6 %collective-permute-done.19.refs_0_ = bf16[1,32,2048]{2,1,0:T(8,128)(2,1)S(1)} collective-permute-done((bf16[1,32,2048]{2,1,0:T(8,128)(2,1)S(1)}, bf16[1,32,2048]{2,1,0:T(8,128)(2,1)S(1)}, u32[]{:S(2)}, u32[]{:S(2)}) %collective-permute-start.19) | collective-permute-done | bytes 131104 | tf_op jit(solution)/shard_map/ppermute | solution.py:129
  83.2 1.6 %collective-permute-start.26 = (bf16[2,32,2048]{2,1,0:T(8,128)(2,1)S(1)}, bf16[2,32,2048]{2,1,0:T(8,128)(2,1)S(1)}, u32[]{:S(2)}, u32[]{:S(2)}) collective-permute-start(bf16[2,32,2048]{2,1,0:T(8,128)(2,1)S(1)} %fusion.2), channel_id=1, source_target_pairs={{0,2},{1,3},{2,0},{3,1},{4,6},{5,7},{6,4},{7,5},{8,10},{9,11},{10,... | collective-permute-start | bytes 786440 | tf_op jit(solution)/shard_map/ppermute | solution.py:129
  84.8 6.8 %collective-permute-done.26 = bf16[2,32,2048]{2,1,0:T(8,128)(2,1)S(1)} collective-permute-done((bf16[2,32,2048]{2,1,0:T(8,128)(2,1)S(1)}, bf16[2,32,2048]{2,1,0:T(8,128)(2,1)S(1)}, u32[]{:S(2)}, u32[]{:S(2)}) %collective-permute-start.26) | collective-permute-done | bytes 262176 | tf_op jit(solution)/shard_map/ppermute | solution.py:129
  94.7 2.8 %collective-permute-start.30 = (bf16[1,32,2048]{2,1,0:T(8,128)(2,1)S(1)}, bf16[1,32,2048]{2,1,0:T(8,128)(2,1)S(1)}, u32[]{:S(2)}, u32[]{:S(2)}) collective-permute-start(bf16[1,32,2048]{2,1,0:T(8,128)(2,1)S(1)} %get-tuple-element.29), channel_id=1, source_target_pairs={{0,4},{4,0},{8,12},{12,8},{16,20},{20,16},{24,28},{28,24},{1,5},{5... | collective-permute-start | bytes 393224 | tf_op jit(solution)/shard_map/ppermute | solution.py:129
  97.5 2.0 %collective-permute-start.32 = (bf16[1,32,2048]{2,1,0:T(8,128)(2,1)S(1)}, bf16[1,32,2048]{2,1,0:T(8,128)(2,1)S(1)}, u32[]{:S(2)}, u32[]{:S(2)}) collective-permute-start(bf16[1,32,2048]{2,1,0:T(8,128)(2,1)S(1)} %get-tuple-element.31), channel_id=1, source_target_pairs={{0,4},{4,0},{8,12},{12,8},{16,20},{20,16},{24,28},{28,24},{1,5},{5... | collective-permute-start | bytes 393224 | tf_op jit(solution)/shard_map/ppermute | solution.py:129
  104.7 1.9 %collective-permute-start.29 = (bf16[1,32,2048]{2,1,0:T(8,128)(2,1)S(1)}, bf16[1,32,2048]{2,1,0:T(8,128)(2,1)S(1)}, u32[]{:S(2)}, u32[]{:S(2)}) collective-permute-start(bf16[1,32,2048]{2,1,0:T(8,128)(2,1)S(1)} %add_convert_fusion.2), channel_id=1, source_target_pairs={{0,24},{4,28},{8,16},{12,20},{16,8},{20,12},{24,0},{28,4},{1,25},{... | collective-permute-start | bytes 393224 | tf_op jit(solution)/shard_map/ppermute | solution.py:129
  109.3 4.1 %collective-permute-done.31 = bf16[1,32,2048]{2,1,0:T(8,128)(2,1)S(1)} collective-permute-done((bf16[1,32,2048]{2,1,0:T(8,128)(2,1)S(1)}, bf16[1,32,2048]{2,1,0:T(8,128)(2,1)S(1)}, u32[]{:S(2)}, u32[]{:S(2)}) %collective-permute-start.31) | collective-permute-done | bytes 131104 | tf_op jit(solution)/shard_map/ppermute | solution.py:129
  (94 shorter events, 38.9 us)
Async XLA Ops:
  1.7 8.4 %collective-permute-start.5 = (bf16[1,32,2048]{2,1,0:T(8,128)(2,1)S(1)}, bf16[1,32,2048]{2,1,0:T(8,128)(2,1)S(1)}, u32[]{:S(2)}, u32[]{:S(2)}) collective-permute-start(bf16[1,32,2048]{2,1,0:T(8,128)(2,1)S(1)} %bitcast.50), channel_id=1, source_target_pairs={{0,8},{4,12},{8,0},{12,4},{16,24},{20,28},{24,16},{28,20},{1,9},{5... | collective-permute-start | bytes 393224 | tf_op jit(solution)/shard_map/ppermute | solution.py:129
  4.8 12.9 %collective-permute-start.3 = (bf16[1,32,2048]{2,1,0:T(8,128)(2,1)S(1)}, bf16[1,32,2048]{2,1,0:T(8,128)(2,1)S(1)}, u32[]{:S(2)}, u32[]{:S(2)}) collective-permute-start(bf16[1,32,2048]{2,1,0:T(8,128)(2,1)S(1)} %bitcast.51), channel_id=1, source_target_pairs={{0,16},{4,20},{8,24},{12,28},{16,0},{20,4},{24,8},{28,12},{1,17},{... | collective-permute-start | bytes 393224 | tf_op jit(solution)/shard_map/ppermute | solution.py:129
  7.4 11.8 %collective-permute-start.1 = (bf16[1,32,2048]{2,1,0:T(8,128)(2,1)S(1)}, bf16[1,32,2048]{2,1,0:T(8,128)(2,1)S(1)}, u32[]{:S(2)}, u32[]{:S(2)}) collective-permute-start(bf16[1,32,2048]{2,1,0:T(8,128)(2,1)S(1)} %bitcast.52), channel_id=1, source_target_pairs={{0,24},{4,28},{8,16},{12,20},{16,8},{20,12},{24,0},{28,4},{1,25},{... | collective-permute-start | bytes 393224 | tf_op jit(solution)/shard_map/ppermute | solution.py:129
  7.4 16.3 %collective-permute-start.7 = (bf16[1,32,2048]{2,1,0:T(8,128)(2,1)S(1)}, bf16[1,32,2048]{2,1,0:T(8,128)(2,1)S(1)}, u32[]{:S(2)}, u32[]{:S(2)}) collective-permute-start(bf16[1,32,2048]{2,1,0:T(8,128)(2,1)S(1)} %bitcast.53), channel_id=1, source_target_pairs={{0,4},{4,0},{8,12},{12,8},{16,20},{20,16},{24,28},{28,24},{1,5},{5... | collective-permute-start | bytes 393224 | tf_op jit(solution)/shard_map/ppermute | solution.py:129
  10.1 13.5 %collective-permute-start.6 = (bf16[1,32,2048]{2,1,0:T(8,128)(2,1)S(1)}, bf16[1,32,2048]{2,1,0:T(8,128)(2,1)S(1)}, u32[]{:S(2)}, u32[]{:S(2)}) collective-permute-start(bf16[1,32,2048]{2,1,0:T(8,128)(2,1)S(1)} %collective-permute-done.5.refs_5_), channel_id=1, source_target_pairs={{0,4},{4,0},{8,12},{12,8},{16,20},{20,16},{24,28},{28,24},{1,5},{5... | collective-permute-start | bytes 393224 | tf_op jit(solution)/shard_map/ppermute | solution.py:129
  20.5 8.7 %collective-permute-start = (f32[34,2048]{1,0:T(8,128)S(1)}, f32[34,2048]{1,0:T(8,128)S(1)}, u32[]{:S(2)}, u32[]{:S(2)}) collective-permute-start(f32[34,2048]{1,0:T(8,128)S(1)} %get-tuple-element.45), channel_id=1, source_target_pairs={{0,2},{1,3},{2,0},{3,1},{4,6},{5,7},{6,4},{7,5},{8,10},{9,11},{10,... | collective-permute-start | bytes 835592 | tf_op jit(solution)/shard_map/ppermute | solution.py:129
  29.3 7.4 %collective-permute-start.9 = (bf16[2,32,2048]{2,1,0:T(8,128)(2,1)S(1)}, bf16[2,32,2048]{2,1,0:T(8,128)(2,1)S(1)}, u32[]{:S(2)}, u32[]{:S(2)}) collective-permute-start(bf16[2,32,2048]{2,1,0:T(8,128)(2,1)S(1)} %fusion.1), channel_id=1, source_target_pairs={{0,2},{1,3},{2,0},{3,1},{4,6},{5,7},{6,4},{7,5},{8,10},{9,11},{10,... | collective-permute-start | bytes 786440 | tf_op jit(solution)/shard_map/ppermute | solution.py:129
  39.8 8.8 %collective-permute-start.13 = (bf16[1,32,2048]{2,1,0:T(8,128)(2,1)S(1)}, bf16[1,32,2048]{2,1,0:T(8,128)(2,1)S(1)}, u32[]{:S(2)}, u32[]{:S(2)}) collective-permute-start(bf16[1,32,2048]{2,1,0:T(8,128)(2,1)S(1)} %get-tuple-element.21), channel_id=1, source_target_pairs={{0,4},{4,0},{8,12},{12,8},{16,20},{20,16},{24,28},{28,24},{1,5},{5... | collective-permute-start | bytes 393224 | tf_op jit(solution)/shard_map/ppermute | solution.py:129
  44.2 7.1 %collective-permute-start.11 = (bf16[1,32,2048]{2,1,0:T(8,128)(2,1)S(1)}, bf16[1,32,2048]{2,1,0:T(8,128)(2,1)S(1)}, u32[]{:S(2)}, u32[]{:S(2)}) collective-permute-start(bf16[1,32,2048]{2,1,0:T(8,128)(2,1)S(1)} %get-tuple-element.19), channel_id=1, source_target_pairs={{0,4},{4,0},{8,12},{12,8},{16,20},{20,16},{24,28},{28,24},{1,5},{5... | collective-permute-start | bytes 393224 | tf_op jit(solution)/shard_map/ppermute | solution.py:129
  44.3 9.6 %collective-permute-start.15 = (bf16[1,32,2048]{2,1,0:T(8,128)(2,1)S(1)}, bf16[1,32,2048]{2,1,0:T(8,128)(2,1)S(1)}, u32[]{:S(2)}, u32[]{:S(2)}) collective-permute-start(bf16[1,32,2048]{2,1,0:T(8,128)(2,1)S(1)} %get-tuple-element.23), channel_id=1, source_target_pairs={{0,4},{4,0},{8,12},{12,8},{16,20},{20,16},{24,28},{28,24},{1,5},{5... | collective-permute-start | bytes 393224 | tf_op jit(solution)/shard_map/ppermute | solution.py:129
  46.2 9.0 %collective-permute-start.17 = (bf16[1,32,2048]{2,1,0:T(8,128)(2,1)S(1)}, bf16[1,32,2048]{2,1,0:T(8,128)(2,1)S(1)}, u32[]{:S(2)}, u32[]{:S(2)}) collective-permute-start(bf16[1,32,2048]{2,1,0:T(8,128)(2,1)S(1)} %get-tuple-element.25), channel_id=1, source_target_pairs={{0,4},{4,0},{8,12},{12,8},{16,20},{20,16},{24,28},{28,24},{1,5},{5... | collective-permute-start | bytes 393224 | tf_op jit(solution)/shard_map/ppermute | solution.py:129
  48.6 11.4 %collective-permute-start.14 = (bf16[1,32,2048]{2,1,0:T(8,128)(2,1)S(1)}, bf16[1,32,2048]{2,1,0:T(8,128)(2,1)S(1)}, u32[]{:S(2)}, u32[]{:S(2)}) collective-permute-start(bf16[1,32,2048]{2,1,0:T(8,128)(2,1)S(1)} %add_convert_fusion.4), channel_id=1, source_target_pairs={{0,16},{4,20},{8,24},{12,28},{16,0},{20,4},{24,8},{28,12},{1,17},{... | collective-permute-start | bytes 393224 | tf_op jit(solution)/shard_map/ppermute | solution.py:129
  51.4 8.6 %collective-permute-start.12 = (bf16[1,32,2048]{2,1,0:T(8,128)(2,1)S(1)}, bf16[1,32,2048]{2,1,0:T(8,128)(2,1)S(1)}, u32[]{:S(2)}, u32[]{:S(2)}) collective-permute-start(bf16[1,32,2048]{2,1,0:T(8,128)(2,1)S(1)} %add_convert_fusion.5), channel_id=1, source_target_pairs={{0,24},{4,28},{8,16},{12,20},{16,8},{20,12},{24,0},{28,4},{1,25},{... | collective-permute-start | bytes 393224 | tf_op jit(solution)/shard_map/ppermute | solution.py:129
  62.2 11.7 %collective-permute-start.20 = (bf16[1,32,2048]{2,1,0:T(8,128)(2,1)S(1)}, bf16[1,32,2048]{2,1,0:T(8,128)(2,1)S(1)}, u32[]{:S(2)}, u32[]{:S(2)}) collective-permute-start(bf16[1,32,2048]{2,1,0:T(8,128)(2,1)S(1)} %fusion.3.refs_7_), channel_id=1, source_target_pairs={{0,16},{4,20},{8,24},{12,28},{16,0},{20,4},{24,8},{28,12},{1,17},{... | collective-permute-start | bytes 393224 | tf_op jit(solution)/shard_map/ppermute | solution.py:129
  64.3 11.3 %collective-permute-start.18 = (bf16[1,32,2048]{2,1,0:T(8,128)(2,1)S(1)}, bf16[1,32,2048]{2,1,0:T(8,128)(2,1)S(1)}, u32[]{:S(2)}, u32[]{:S(2)}) collective-permute-start(bf16[1,32,2048]{2,1,0:T(8,128)(2,1)S(1)} %fusion.3.refs_7_), channel_id=1, source_target_pairs={{0,24},{4,28},{8,16},{12,20},{16,8},{20,12},{24,0},{28,4},{1,25},{... | collective-permute-start | bytes 393224 | tf_op jit(solution)/shard_map/ppermute | solution.py:129
  65.5 10.5 %collective-permute-start.24 = (bf16[1,32,2048]{2,1,0:T(8,128)(2,1)S(1)}, bf16[1,32,2048]{2,1,0:T(8,128)(2,1)S(1)}, u32[]{:S(2)}, u32[]{:S(2)}) collective-permute-start(bf16[1,32,2048]{2,1,0:T(8,128)(2,1)S(1)} %fusion.3.refs_7_), channel_id=1, source_target_pairs={{0,4},{4,0},{8,12},{12,8},{16,20},{20,16},{24,28},{28,24},{1,5},{5... | collective-permute-start | bytes 393224 | tf_op jit(solution)/shard_map/ppermute | solution.py:129
  67.0 9.0 %collective-permute-start.23 = (bf16[1,32,2048]{2,1,0:T(8,128)(2,1)S(1)}, bf16[1,32,2048]{2,1,0:T(8,128)(2,1)S(1)}, u32[]{:S(2)}, u32[]{:S(2)}) collective-permute-start(bf16[1,32,2048]{2,1,0:T(8,128)(2,1)S(1)} %collective-permute-done.22.refs_5_), channel_id=1, source_target_pairs={{0,4},{4,0},{8,12},{12,8},{16,20},{20,16},{24,28},{28,24},{1,5},{5... | collective-permute-start | bytes 393224 | tf_op jit(solution)/shard_map/ppermute | solution.py:129
  83.2 8.4 %collective-permute-start.26 = (bf16[2,32,2048]{2,1,0:T(8,128)(2,1)S(1)}, bf16[2,32,2048]{2,1,0:T(8,128)(2,1)S(1)}, u32[]{:S(2)}, u32[]{:S(2)}) collective-permute-start(bf16[2,32,2048]{2,1,0:T(8,128)(2,1)S(1)} %fusion.2), channel_id=1, source_target_pairs={{0,2},{1,3},{2,0},{3,1},{4,6},{5,7},{6,4},{7,5},{8,10},{9,11},{10,... | collective-permute-start | bytes 786440 | tf_op jit(solution)/shard_map/ppermute | solution.py:129
  94.7 7.2 %collective-permute-start.30 = (bf16[1,32,2048]{2,1,0:T(8,128)(2,1)S(1)}, bf16[1,32,2048]{2,1,0:T(8,128)(2,1)S(1)}, u32[]{:S(2)}, u32[]{:S(2)}) collective-permute-start(bf16[1,32,2048]{2,1,0:T(8,128)(2,1)S(1)} %get-tuple-element.29), channel_id=1, source_target_pairs={{0,4},{4,0},{8,12},{12,8},{16,20},{20,16},{24,28},{28,24},{1,5},{5... | collective-permute-start | bytes 393224 | tf_op jit(solution)/shard_map/ppermute | solution.py:129
  97.5 7.2 %collective-permute-start.28 = (bf16[1,32,2048]{2,1,0:T(8,128)(2,1)S(1)}, bf16[1,32,2048]{2,1,0:T(8,128)(2,1)S(1)}, u32[]{:S(2)}, u32[]{:S(2)}) collective-permute-start(bf16[1,32,2048]{2,1,0:T(8,128)(2,1)S(1)} %get-tuple-element.27), channel_id=1, source_target_pairs={{0,4},{4,0},{8,12},{12,8},{16,20},{20,16},{24,28},{28,24},{1,5},{5... | collective-permute-start | bytes 393224 | tf_op jit(solution)/shard_map/ppermute | solution.py:129
  97.5 9.8 %collective-permute-start.32 = (bf16[1,32,2048]{2,1,0:T(8,128)(2,1)S(1)}, bf16[1,32,2048]{2,1,0:T(8,128)(2,1)S(1)}, u32[]{:S(2)}, u32[]{:S(2)}) collective-permute-start(bf16[1,32,2048]{2,1,0:T(8,128)(2,1)S(1)} %get-tuple-element.31), channel_id=1, source_target_pairs={{0,4},{4,0},{8,12},{12,8},{16,20},{20,16},{24,28},{28,24},{1,5},{5... | collective-permute-start | bytes 393224 | tf_op jit(solution)/shard_map/ppermute | solution.py:129
  99.5 9.8 %collective-permute-start.34 = (bf16[1,32,2048]{2,1,0:T(8,128)(2,1)S(1)}, bf16[1,32,2048]{2,1,0:T(8,128)(2,1)S(1)}, u32[]{:S(2)}, u32[]{:S(2)}) collective-permute-start(bf16[1,32,2048]{2,1,0:T(8,128)(2,1)S(1)} %get-tuple-element.33), channel_id=1, source_target_pairs={{0,4},{4,0},{8,12},{12,8},{16,20},{20,16},{24,28},{28,24},{1,5},{5... | collective-permute-start | bytes 393224 | tf_op jit(solution)/shard_map/ppermute | solution.py:129
  101.9 11.4 %collective-permute-start.31 = (bf16[1,32,2048]{2,1,0:T(8,128)(2,1)S(1)}, bf16[1,32,2048]{2,1,0:T(8,128)(2,1)S(1)}, u32[]{:S(2)}, u32[]{:S(2)}) collective-permute-start(bf16[1,32,2048]{2,1,0:T(8,128)(2,1)S(1)} %add_convert_fusion.1), channel_id=1, source_target_pairs={{0,16},{4,20},{8,24},{12,28},{16,0},{20,4},{24,8},{28,12},{1,17},{... | collective-permute-start | bytes 393224 | tf_op jit(solution)/shard_map/ppermute | solution.py:129
  104.7 8.6 %collective-permute-start.29 = (bf16[1,32,2048]{2,1,0:T(8,128)(2,1)S(1)}, bf16[1,32,2048]{2,1,0:T(8,128)(2,1)S(1)}, u32[]{:S(2)}, u32[]{:S(2)}) collective-permute-start(bf16[1,32,2048]{2,1,0:T(8,128)(2,1)S(1)} %add_convert_fusion.2), channel_id=1, source_target_pairs={{0,24},{4,28},{8,16},{12,20},{16,8},{20,12},{24,0},{28,4},{1,25},{... | collective-permute-start | bytes 393224 | tf_op jit(solution)/shard_map/ppermute | solution.py:129
  (17 other events, 161.4 us)

commit v6 on v5

v6 whole, which is shorter than its diff:
```python
import functools
import typing

import jax
import jax.numpy as jnp
from jax import lax
from jax.experimental import pallas as pl
from jax.experimental.pallas import tpu as pltpu
from jax.sharding import PartitionSpec as P

BR_DEV = 16
BC_DEV = 16
ITERS = 2


step_primal = 0.4
step_dual = 0.4

VMEM_LIMIT = 24 * 1024 * 1024
FETCH_LIMIT = 46 * 1024 * 1024


def sweep_kernel(plan, info, tiles, *refs):
    refs = list(refs)
    parts = [refs.pop(0) for _ in plan.senders]
    begun = [refs.pop(0) for _ in plan.begun]
    results = [[refs.pop(0) for _ in range(out.arrays)] for out in plan.outs]
    operand = refs.pop(0)
    sums = {}
    for out, result in zip(plan.outs, results):
        sums[out.parity] = result[0] if out.direct else refs.pop(0)
    held, arrived = refs if plan.fetched else (tiles, None)
    slots = tiles.shape[0]
    live = info[2 * slots]
    me_in = info[2 * slots + 1]
    me_out = info[2 * slots + 2]
    span_in = operand.shape[1]
    span_out = tiles.shape[1] if plan.forward else tiles.shape[2]
    per_out = next(iter(sums.values())).shape[2] // span_out

    def ends(slot):
        row, col = info[2 * slot], info[2 * slot + 1]
        return (col, row) if plan.forward else (row, col)

    def accepted(slot):
        block_in, block_out = ends(slot)
        return plan.accept((block_in // plan.per_in) ^ me_in, (block_out // per_out) ^ me_out)

    def fetch(slot):
        return pltpu.make_async_copy(tiles.at[slot], held.at[slot], arrived.at[slot])

    if plan.fetched:

        def start(slot, carry):
            @pl.when(accepted(slot))
            def _():
                fetch(slot).start()

            return carry

        lax.fori_loop(0, live, start, 0)
    for p in sums:
        sums[p][...] = begun[p][...] if begun else jnp.zeros_like(sums[p])

    def visit(slot, carry):
        @pl.when(accepted(slot))
        def _():
            block_in, block_out = ends(slot)
            source = (block_in // plan.per_in) ^ me_in
            target = (block_out // per_out) ^ me_out
            place = pl.multiple_of((block_in % plan.per_in) * span_in, span_in)
            for part, ks in zip(parts, plan.senders):

                @pl.when(functools.reduce(jnp.logical_or, [source == k for k in ks]))
                def _():
                    at = source // 2 if len(ks) > 1 else 0
                    operand[...] = part[at, :, pl.ds(place, span_in)]

            if plan.fetched:
                fetch(slot).wait()
            contract = (((1,), (1,)), ((), ())) if plan.forward else (((1,), (0,)), ((), ()))
            term = lax.dot_general(
                operand[...], held[slot], contract, preferred_element_type=jnp.float32
            )
            to = pl.multiple_of((block_out % per_out) * span_out, span_out)
            for p in sums:

                @pl.when(target % 2 == p)
                def _():
                    sums[p][target // 2, :, pl.ds(to, span_out)] += term

        return carry

    lax.fori_loop(0, live, visit, 0)
    for out, result in zip(plan.outs, results):
        if not out.direct:
            each = sums[out.parity].shape[0] // out.arrays
            for i, ref in enumerate(result):
                ref[...] = sums[out.parity][i * each : (i + 1) * each].astype(ref.dtype)


class Out(typing.NamedTuple):
    parity: int
    kind: typing.Any
    arrays: int

    @property
    def direct(self):
        return self.kind == jnp.float32 and self.arrays == 1


class Plan(typing.NamedTuple):
    forward: bool
    fetched: bool
    outs: tuple
    senders: tuple
    accept: typing.Callable
    begun: tuple
    per_in: int


def sweep(plan, tiles, info, parts, begun, half, wide):
    slots, rows_tile, cols_tile = tiles.shape
    width = parts[0].shape[1]
    span_in = cols_tile if plan.forward else rows_tile
    plan = plan._replace(
        begun=tuple(range(len(begun))), per_in=parts[0].shape[2] // span_in
    )
    out_shape = []
    for out in plan.outs:
        shape = (half // out.arrays, width, wide)
        out_shape += [jax.ShapeDtypeStruct(shape, out.kind)] * out.arrays
    vmem = pl.BlockSpec(memory_space=pltpu.VMEM)
    scratch = [pltpu.VMEM((width, span_in), jnp.bfloat16)]
    for out in plan.outs:
        if not out.direct:
            scratch += [pltpu.VMEM((half, width, wide), jnp.float32)]
    if plan.fetched:
        scratch += [pltpu.VMEM(tiles.shape, tiles.dtype), pltpu.SemaphoreType.DMA((slots,))]
    return pl.pallas_call(
        functools.partial(sweep_kernel, plan),
        out_shape=out_shape,
        in_specs=[
            pl.BlockSpec(memory_space=pltpu.SMEM),
            pl.BlockSpec(memory_space=pl.ANY) if plan.fetched else vmem,
        ]
        + [vmem] * (len(parts) + len(begun)),
        out_specs=[vmem] * len(out_shape),
        scratch_shapes=scratch,
        compiler_params=pltpu.CompilerParams(
            vmem_limit_bytes=FETCH_LIMIT if plan.fetched else VMEM_LIMIT
        ),
        cost_estimate=pl.CostEstimate(
            flops=slots * width * rows_tile * cols_tile,
            bytes_accessed=tiles.size,
            transcendentals=0,
        ),
        name="forward_sweep" if plan.forward else "transpose_sweep",
    )(info, tiles, *parts, *begun)


def swap(value, axis, size, k):
    return lax.ppermute(value, axis, [(i, i ^ k) for i in range(size)])


def gather_pairs(own, axis, size):
    parts = [None] * size
    parts[0] = own
    for k in range(size - 2, 0, -2):
        parts[k] = swap(own, axis, size, k)
    for k in range(size - 2, -1, -2):
        parts[k + 1] = swap(parts[k], axis, size, 1)
    return parts


def sum_pairs(kept, sent, axis, size):
    total = None
    for h in range(size // 2 - 1, -1, -1):
        pair = kept[h] + swap(sent[h], axis, size, 1).astype(jnp.float32)
        if h:
            pair = swap(pair.astype(jnp.bfloat16), axis, size, 2 * h).astype(jnp.float32)
        total = pair if total is None else total + pair
    return total


def sum_halves(kept, sent, axis, size):
    here = kept + swap(sent, axis, size, 1).astype(jnp.float32)
    away = here.astype(jnp.bfloat16)
    total = here
    for t in range(1, size // 2):
        other = swap(away, axis, size, 2 * t)
        order = [h ^ t for h in range(size // 2)]
        total = total + jnp.stack([other[h] for h in order]).astype(jnp.float32)
    return total


def body(
    rows,
    cols,
    tiles,
    tile_index,
    tile_count,
    weights,
    carbon,
    completion,
    demand,
    row_kind,
    primal_start,
    dual_start,
):
    blocks = tiles[0, 0]
    info = jnp.concatenate(
        [
            tile_index.reshape(-1),
            tile_count.reshape(-1),
            lax.axis_index("col")[None],
            lax.axis_index("row")[None],
        ]
    ).astype(jnp.int32)
    info_back = jnp.concatenate([info[:-2], info[-1:], info[-2:-1]])
    dual = dual_start[:, 0, :]
    state = jnp.concatenate([primal_start[:, 0, :], carbon, completion])
    states = [state] + [swap(state, "row", rows, k) for k in range(2, rows, 2)]
    states = jnp.stack(states)
    width = weights.shape[0]
    primal = states[:, :width]
    share = weights[:, None]
    cost = share * states[:, width : width + 1] + (1.0 - share) * states[:, width + 1 :]
    late = [k for k in range(5, cols, 2)]
    early = [k for k in range(cols) if k not in late]

    def is_late(source):
        return (source % 2 == 1) & (source > 3)

    whole, rounded = jnp.float32, jnp.bfloat16
    transpose = Plan(False, False, (), (), None, (), 0)
    forward = Plan(
        True, False, (), tuple(tuple(range(p, rows, 2)) for p in (0, 1)), None, (), 0
    )
    for step in range(ITERS):
        dual_parts = gather_pairs(dual.astype(jnp.bfloat16)[None], "col", cols)
        begun = sweep(
            transpose._replace(
                fetched=step == 0,
                outs=(Out(0, whole, 1), Out(1, whole, 1)),
                senders=tuple((k,) for k in early),
                accept=lambda source, target: jnp.logical_not(is_late(source)),
            ),
            blocks, info, [dual_parts[k] for k in early], [], rows // 2, primal.shape[2],
        )
        kept, sent = sweep(
            transpose._replace(
                outs=(Out(0, whole, 1), Out(1, rounded, 1)),
                senders=tuple((k,) for k in late),
                accept=lambda source, target: is_late(source),
            ),
            blocks, info, [dual_parts[k] for k in late], begun, rows // 2, primal.shape[2],
        )
        pull = sum_halves(kept, sent, "row", rows)
        fresh = jnp.maximum(primal - step_primal * (cost - pull), 0.0)
        extra = (2.0 * fresh - primal).astype(jnp.bfloat16)
        primal = fresh
        extra_parts = [extra, swap(extra, "row", rows, 1)]
        sent = sweep(
            forward._replace(
                outs=(Out(1, rounded, cols // 2),),
                accept=lambda source, target: target % 2 == 1,
            ),
            blocks, info_back, extra_parts, [], cols // 2, dual.shape[1],
        )
        kept = sweep(
            forward._replace(
                outs=(Out(0, whole, cols // 2),),
                accept=lambda source, target: target % 2 == 0,
            ),
            blocks, info_back, extra_parts, [], cols // 2, dual.shape[1],
        )
        push = sum_pairs(kept, sent, "col", cols)[0]
        moved = dual + step_dual * (demand - push)
        dual = jnp.where(row_kind == 1, jnp.maximum(moved, 0.0), moved)
    return (primal[0][:, None, :], dual[:, None, :])


def solution(mesh):
    placed = (
        P("row", "col", None, None, None),
        P("row", "col", None, None),
        P("row", "col"),
        P(),
        P("col", "row"),
        P("col", "row"),
        P("row", "col"),
        P("row", "col"),
        P(None, "col", "row"),
        P(None, "row", "col"),
    )
    return jax.shard_map(
        functools.partial(body, mesh.shape["row"], mesh.shape["col"]),
        mesh=mesh,
        in_specs=placed,
        out_specs=(P(None, "col", "row"), P(None, "row", "col")),
        check_vma=False,
    )
```

time: 117 us -> 118 us (level)
  waiting for transfers between devices: 50.7 us -> 52.4 us
  Pallas kernels: 11.5 us -> 10 us
    ppermute x35, waiting for transfers between devices: 50.7 us -> 52.4 us  [swap(): return lax.ppermute(value, axis, [(i, i ^ k) for i in range(size)])]
    pallas_call x8, Pallas kernels: 11.5 us -> 10 us  [sweep(): pl.pallas_call(functools.partial(sweep_kernel, plan), out_shape=out_shape...]
    unnamed x18 -> x16, local copies, waits for them, and re-layouts: 4.82 us -> 5.95 us
  transfers between devices with their start and end apart: 35 -> 35, of which waited for: 22 -> 24; matrix products, arithmetic and copies ran while one was open for 3% -> 3% of each run, Pallas kernels for 7% -> 6%
where the time goes in v6:
time: 118 us; the launch traced here: 116 us
  waiting for transfers between devices  52.4 us (44%)
  starting transfers between devices  43.9 us (37%)
  Pallas kernels  10 us (8%)
  local copies, waits for them, and re-layouts  6.08 us (5%)
  other arithmetic  2.25 us (2%)
  between operations  1.55 us (1%)
    ppermute x35, waiting for transfers between devices, swap(): return lax.ppermute(value, axis, [(i, i ^ k) for i in range(size)])  52.4 us
    ppermute x35, starting transfers between devices, swap(): return lax.ppermute(value, axis, [(i, i ^ k) for i in range(size)])  43.9 us
    pallas_call x8, Pallas kernels, sweep(): pl.pallas_call(functools.partial(sweep_kernel, plan), out_shape=out_shape...  10 us
    unnamed x16, local copies, waits for them, and re-layouts  5.95 us
  transfers between devices with their start and end apart: 35, of which 24 were waited for; matrix products, arithmetic and copies ran while one was open for 3% of the time, Pallas kernels for 6%

profile of v6, /device:TPU:0, one launch (start us, length us, event | category | flops | bytes accessed | tf_op | source)
XLA Modules:
  0.0 116.2 jit_solution(18343030761498380941)
XLA Ops:
  1.7 3.1 %collective-permute-start.6 = (bf16[1,32,2048]{2,1,0:T(8,128)(2,1)S(1)}, bf16[1,32,2048]{2,1,0:T(8,128)(2,1)S(1)}, u32[]{:S(2)}, u32[]{:S(2)}) collective-permute-start(bf16[1,32,2048]{2,1,0:T(8,128)(2,1)S(1)} %bitcast.48), channel_id=1, source_target_pairs={{0,8},{4,12},{8,0},{12,4},{16,24},{20,28},{24,16},{28,20},{1,9},{5... | collective-permute-start | bytes 393224 | tf_op jit(solution)/shard_map/ppermute | solution.py:163
  4.8 2.5 %collective-permute-start.3 = (bf16[1,32,2048]{2,1,0:T(8,128)(2,1)S(1)}, bf16[1,32,2048]{2,1,0:T(8,128)(2,1)S(1)}, u32[]{:S(2)}, u32[]{:S(2)}) collective-permute-start(bf16[1,32,2048]{2,1,0:T(8,128)(2,1)S(1)} %bitcast.49), channel_id=1, source_target_pairs={{0,24},{4,28},{8,16},{12,20},{16,8},{20,12},{24,0},{28,4},{1,25},{... | collective-permute-start | bytes 393224 | tf_op jit(solution)/shard_map/ppermute | solution.py:163
  10.5 4.0 %collective-permute-done.3.refs_5_ = bf16[1,32,2048]{2,1,0:T(8,128)(2,1)S(1)} collective-permute-done((bf16[1,32,2048]{2,1,0:T(8,128)(2,1)S(1)}, bf16[1,32,2048]{2,1,0:T(8,128)(2,1)S(1)}, u32[]{:S(2)}, u32[]{:S(2)}) %collective-permute-start.3) | collective-permute-done | bytes 131104 | tf_op jit(solution)/shard_map/ppermute | solution.py:163
  16.0 3.0 %collective-permute-done.1.refs_4_ = bf16[1,32,2048]{2,1,0:T(8,128)(2,1)S(1)} collective-permute-done((bf16[1,32,2048]{2,1,0:T(8,128)(2,1)S(1)}, bf16[1,32,2048]{2,1,0:T(8,128)(2,1)S(1)}, u32[]{:S(2)}, u32[]{:S(2)}) %collective-permute-start.1) | collective-permute-done | bytes 131104 | tf_op jit(solution)/shard_map/ppermute | solution.py:163
  21.2 1.6 %collective-permute-start = (f32[34,2048]{1,0:T(8,128)S(1)}, f32[34,2048]{1,0:T(8,128)S(1)}, u32[]{:S(2)}, u32[]{:S(2)}) collective-permute-start(f32[34,2048]{1,0:T(8,128)S(1)} %get-tuple-element.61), channel_id=1, source_target_pairs={{0,2},{1,3},{2,0},{3,1},{4,6},{5,7},{6,4},{7,5},{8,10},{9,11},{10,... | collective-permute-start | bytes 835592 | tf_op jit(solution)/shard_map/ppermute | solution.py:163
  24.4 2.4 %transpose_sweep.4 = (f32[2,32,2048]{2,1,0:T(8,128)S(1)}, f32[2,32,2048]{2,1,0:T(8,128)S(1)}) custom-call(s32[19]{0:T(128)S(1)} %get-tuple-element.67.info, bf16[8,1024,512]{2,1,0:T(8,128)(2,1)} %bitcast.40, bf16[1,32,2048]{2,1,0:T(8,128)(2,1)S(1)} %bitcast.52, bf16[1,32,2048]{2,1,0:T(8,128)(2,1)S(1)} %collective-permute-done.5.refs_1_, ...), custom_call_target="tpu_custom_call" | custom-call | flops 134217728 | bytes 4194304 | tf_op jit(solution)/shard_map/transpose_sweep/pallas_call | solution.py:140
  31.6 7.5 %collective-permute-done.9 = bf16[2,32,2048]{2,1,0:T(8,128)(2,1)S(1)} collective-permute-done((bf16[2,32,2048]{2,1,0:T(8,128)(2,1)S(1)}, bf16[2,32,2048]{2,1,0:T(8,128)(2,1)S(1)}, u32[]{:S(2)}, u32[]{:S(2)}) %collective-permute-start.9) | collective-permute-done | bytes 262176 | tf_op jit(solution)/shard_map/ppermute | solution.py:163
  42.3 2.0 %collective-permute-start.11 = (bf16[1,32,2048]{2,1,0:T(8,128)(2,1)S(1)}, bf16[1,32,2048]{2,1,0:T(8,128)(2,1)S(1)}, u32[]{:S(2)}, u32[]{:S(2)}) collective-permute-start(bf16[1,32,2048]{2,1,0:T(8,128)(2,1)S(1)} %get-tuple-element.31), channel_id=1, source_target_pairs={{0,4},{4,0},{8,12},{12,8},{16,20},{20,16},{24,28},{28,24},{1,5},{5... | collective-permute-start | bytes 393224 | tf_op jit(solution)/shard_map/ppermute | solution.py:163
  44.4 1.9 %collective-permute-start.17 = (bf16[1,32,2048]{2,1,0:T(8,128)(2,1)S(1)}, bf16[1,32,2048]{2,1,0:T(8,128)(2,1)S(1)}, u32[]{:S(2)}, u32[]{:S(2)}) collective-permute-start(bf16[1,32,2048]{2,1,0:T(8,128)(2,1)S(1)} %get-tuple-element.37), channel_id=1, source_target_pairs={{0,4},{4,0},{8,12},{12,8},{16,20},{20,16},{24,28},{28,24},{1,5},{5... | collective-permute-start | bytes 393224 | tf_op jit(solution)/shard_map/ppermute | solution.py:163
  51.5 2.6 %collective-permute-start.12 = (bf16[1,32,2048]{2,1,0:T(8,128)(2,1)S(1)}, bf16[1,32,2048]{2,1,0:T(8,128)(2,1)S(1)}, u32[]{:S(2)}, u32[]{:S(2)}) collective-permute-start(bf16[1,32,2048]{2,1,0:T(8,128)(2,1)S(1)} %add_convert_fusion.5), channel_id=1, source_target_pairs={{0,24},{4,28},{8,16},{12,20},{16,8},{20,12},{24,0},{28,4},{1,25},{... | collective-permute-start | bytes 393224 | tf_op jit(solution)/shard_map/ppermute | solution.py:163
  55.7 3.8 %collective-permute-done.14 = bf16[1,32,2048]{2,1,0:T(8,128)(2,1)S(1)} collective-permute-done((bf16[1,32,2048]{2,1,0:T(8,128)(2,1)S(1)}, bf16[1,32,2048]{2,1,0:T(8,128)(2,1)S(1)}, u32[]{:S(2)}, u32[]{:S(2)}) %collective-permute-start.14) | collective-permute-done | bytes 131104 | tf_op jit(solution)/shard_map/ppermute | solution.py:163
  59.6 1.7 %collective-permute-done.16 = bf16[1,32,2048]{2,1,0:T(8,128)(2,1)S(1)} collective-permute-done((bf16[1,32,2048]{2,1,0:T(8,128)(2,1)S(1)}, bf16[1,32,2048]{2,1,0:T(8,128)(2,1)S(1)}, u32[]{:S(2)}, u32[]{:S(2)}) %collective-permute-start.16) | collective-permute-done | bytes 131104 | tf_op jit(solution)/shard_map/ppermute | solution.py:163
  61.7 2.7 %collective-permute-start.20 = (bf16[1,32,2048]{2,1,0:T(8,128)(2,1)S(1)}, bf16[1,32,2048]{2,1,0:T(8,128)(2,1)S(1)}, u32[]{:S(2)}, u32[]{:S(2)}) collective-permute-start(bf16[1,32,2048]{2,1,0:T(8,128)(2,1)S(1)} %fusion.3.refs_0_), channel_id=1, source_target_pairs={{0,24},{4,28},{8,16},{12,20},{16,8},{20,12},{24,0},{28,4},{1,25},{... | collective-permute-start | bytes 393224 | tf_op jit(solution)/shard_map/ppermute | solution.py:163
  66.9 1.7 %collective-permute-start.24 = (bf16[1,32,2048]{2,1,0:T(8,128)(2,1)S(1)}, bf16[1,32,2048]{2,1,0:T(8,128)(2,1)S(1)}, u32[]{:S(2)}, u32[]{:S(2)}) collective-permute-start(bf16[1,32,2048]{2,1,0:T(8,128)(2,1)S(1)} %collective-permute-done.23.refs_2_), channel_id=1, source_target_pairs={{0,4},{4,0},{8,12},{12,8},{16,20},{20,16},{24,28},{28,24},{1,5},{5... | collective-permute-start | bytes 393224 | tf_op jit(solution)/shard_map/ppermute | solution.py:163
  68.6 3.0 %collective-permute-done.20.refs_5_ = bf16[1,32,2048]{2,1,0:T(8,128)(2,1)S(1)} collective-permute-done((bf16[1,32,2048]{2,1,0:T(8,128)(2,1)S(1)}, bf16[1,32,2048]{2,1,0:T(8,128)(2,1)S(1)}, u32[]{:S(2)}, u32[]{:S(2)}) %collective-permute-start.20) | collective-permute-done | bytes 131104 | tf_op jit(solution)/shard_map/ppermute | solution.py:163
  71.6 1.7 %collective-permute-start.21 = (bf16[1,32,2048]{2,1,0:T(8,128)(2,1)S(1)}, bf16[1,32,2048]{2,1,0:T(8,128)(2,1)S(1)}, u32[]{:S(2)}, u32[]{:S(2)}) collective-permute-start(bf16[1,32,2048]{2,1,0:T(8,128)(2,1)S(1)} %collective-permute-done.20.refs_5_), channel_id=1, source_target_pairs={{0,4},{4,0},{8,12},{12,8},{16,20},{20,16},{24,28},{28,24},{1,5},{5... | collective-permute-start | bytes 393224 | tf_op jit(solution)/shard_map/ppermute | solution.py:163
  73.3 2.9 %collective-permute-done.18.refs_4_ = bf16[1,32,2048]{2,1,0:T(8,128)(2,1)S(1)} collective-permute-done((bf16[1,32,2048]{2,1,0:T(8,128)(2,1)S(1)}, bf16[1,32,2048]{2,1,0:T(8,128)(2,1)S(1)}, u32[]{:S(2)}, u32[]{:S(2)}) %collective-permute-start.18) | collective-permute-done | bytes 131104 | tf_op jit(solution)/shard_map/ppermute | solution.py:163
  76.2 1.6 %collective-permute-start.19 = (bf16[1,32,2048]{2,1,0:T(8,128)(2,1)S(1)}, bf16[1,32,2048]{2,1,0:T(8,128)(2,1)S(1)}, u32[]{:S(2)}, u32[]{:S(2)}) collective-permute-start(bf16[1,32,2048]{2,1,0:T(8,128)(2,1)S(1)} %collective-permute-done.18.refs_4_), channel_id=1, source_target_pairs={{0,4},{4,0},{8,12},{12,8},{16,20},{20,16},{24,28},{28,24},{1,5},{5... | collective-permute-start | bytes 393224 | tf_op jit(solution)/shard_map/ppermute | solution.py:163
  78.8 2.3 %collective-permute-done.19.refs_0_ = bf16[1,32,2048]{2,1,0:T(8,128)(2,1)S(1)} collective-permute-done((bf16[1,32,2048]{2,1,0:T(8,128)(2,1)S(1)}, bf16[1,32,2048]{2,1,0:T(8,128)(2,1)S(1)}, u32[]{:S(2)}, u32[]{:S(2)}) %collective-permute-start.19) | collective-permute-done | bytes 131104 | tf_op jit(solution)/shard_map/ppermute | solution.py:163
  83.8 2.0 %collective-permute-start.26 = (bf16[2,32,2048]{2,1,0:T(8,128)(2,1)S(1)}, bf16[2,32,2048]{2,1,0:T(8,128)(2,1)S(1)}, u32[]{:S(2)}, u32[]{:S(2)}) collective-permute-start(bf16[2,32,2048]{2,1,0:T(8,128)(2,1)S(1)} %fusion.2), channel_id=1, source_target_pairs={{0,2},{1,3},{2,0},{3,1},{4,6},{5,7},{6,4},{7,5},{8,10},{9,11},{10,... | collective-permute-start | bytes 786440 | tf_op jit(solution)/shard_map/ppermute | solution.py:163
  85.8 6.6 %collective-permute-done.26 = bf16[2,32,2048]{2,1,0:T(8,128)(2,1)S(1)} collective-permute-done((bf16[2,32,2048]{2,1,0:T(8,128)(2,1)S(1)}, bf16[2,32,2048]{2,1,0:T(8,128)(2,1)S(1)}, u32[]{:S(2)}, u32[]{:S(2)}) %collective-permute-start.26) | collective-permute-done | bytes 262176 | tf_op jit(solution)/shard_map/ppermute | solution.py:163
  101.9 2.0 %collective-permute-start.31 = (bf16[1,32,2048]{2,1,0:T(8,128)(2,1)S(1)}, bf16[1,32,2048]{2,1,0:T(8,128)(2,1)S(1)}, u32[]{:S(2)}, u32[]{:S(2)}) collective-permute-start(bf16[1,32,2048]{2,1,0:T(8,128)(2,1)S(1)} %add_convert_fusion.1), channel_id=1, source_target_pairs={{0,16},{4,20},{8,24},{12,28},{16,0},{20,4},{24,8},{28,12},{1,17},{... | collective-permute-start | bytes 393224 | tf_op jit(solution)/shard_map/ppermute | solution.py:163
  104.7 2.5 %collective-permute-start.29 = (bf16[1,32,2048]{2,1,0:T(8,128)(2,1)S(1)}, bf16[1,32,2048]{2,1,0:T(8,128)(2,1)S(1)}, u32[]{:S(2)}, u32[]{:S(2)}) collective-permute-start(bf16[1,32,2048]{2,1,0:T(8,128)(2,1)S(1)} %add_convert_fusion.2), channel_id=1, source_target_pairs={{0,24},{4,28},{8,16},{12,20},{16,8},{20,12},{24,0},{28,4},{1,25},{... | collective-permute-start | bytes 393224 | tf_op jit(solution)/shard_map/ppermute | solution.py:163
  109.6 3.9 %collective-permute-done.31 = bf16[1,32,2048]{2,1,0:T(8,128)(2,1)S(1)} collective-permute-done((bf16[1,32,2048]{2,1,0:T(8,128)(2,1)S(1)}, bf16[1,32,2048]{2,1,0:T(8,128)(2,1)S(1)}, u32[]{:S(2)}, u32[]{:S(2)}) %collective-permute-start.31) | collective-permute-done | bytes 131104 | tf_op jit(solution)/shard_map/ppermute | solution.py:163
  (91 shorter events, 45.5 us)
Async XLA Ops:
  1.7 8.2 %collective-permute-start.6 = (bf16[1,32,2048]{2,1,0:T(8,128)(2,1)S(1)}, bf16[1,32,2048]{2,1,0:T(8,128)(2,1)S(1)}, u32[]{:S(2)}, u32[]{:S(2)}) collective-permute-start(bf16[1,32,2048]{2,1,0:T(8,128)(2,1)S(1)} %bitcast.48), channel_id=1, source_target_pairs={{0,8},{4,12},{8,0},{12,4},{16,24},{20,28},{24,16},{28,20},{1,9},{5... | collective-permute-start | bytes 393224 | tf_op jit(solution)/shard_map/ppermute | solution.py:163
  4.8 9.7 %collective-permute-start.3 = (bf16[1,32,2048]{2,1,0:T(8,128)(2,1)S(1)}, bf16[1,32,2048]{2,1,0:T(8,128)(2,1)S(1)}, u32[]{:S(2)}, u32[]{:S(2)}) collective-permute-start(bf16[1,32,2048]{2,1,0:T(8,128)(2,1)S(1)} %bitcast.49), channel_id=1, source_target_pairs={{0,24},{4,28},{8,16},{12,20},{16,8},{20,12},{24,0},{28,4},{1,25},{... | collective-permute-start | bytes 393224 | tf_op jit(solution)/shard_map/ppermute | solution.py:163
  7.2 11.8 %collective-permute-start.1 = (bf16[1,32,2048]{2,1,0:T(8,128)(2,1)S(1)}, bf16[1,32,2048]{2,1,0:T(8,128)(2,1)S(1)}, u32[]{:S(2)}, u32[]{:S(2)}) collective-permute-start(bf16[1,32,2048]{2,1,0:T(8,128)(2,1)S(1)} %bitcast.50), channel_id=1, source_target_pairs={{0,16},{4,20},{8,24},{12,28},{16,0},{20,4},{24,8},{28,12},{1,17},{... | collective-permute-start | bytes 393224 | tf_op jit(solution)/shard_map/ppermute | solution.py:163
  7.3 17.1 %collective-permute-start.5 = (bf16[1,32,2048]{2,1,0:T(8,128)(2,1)S(1)}, bf16[1,32,2048]{2,1,0:T(8,128)(2,1)S(1)}, u32[]{:S(2)}, u32[]{:S(2)}) collective-permute-start(bf16[1,32,2048]{2,1,0:T(8,128)(2,1)S(1)} %bitcast.51), channel_id=1, source_target_pairs={{0,4},{4,0},{8,12},{12,8},{16,20},{20,16},{24,28},{28,24},{1,5},{5... | collective-permute-start | bytes 393224 | tf_op jit(solution)/shard_map/ppermute | solution.py:163
  9.9 14.5 %collective-permute-start.7 = (bf16[1,32,2048]{2,1,0:T(8,128)(2,1)S(1)}, bf16[1,32,2048]{2,1,0:T(8,128)(2,1)S(1)}, u32[]{:S(2)}, u32[]{:S(2)}) collective-permute-start(bf16[1,32,2048]{2,1,0:T(8,128)(2,1)S(1)} %collective-permute-done.6.refs_2_), channel_id=1, source_target_pairs={{0,4},{4,0},{8,12},{12,8},{16,20},{20,16},{24,28},{28,24},{1,5},{5... | collective-permute-start | bytes 393224 | tf_op jit(solution)/shard_map/ppermute | solution.py:163
  14.5 12.4 %collective-permute-start.4 = (bf16[1,32,2048]{2,1,0:T(8,128)(2,1)S(1)}, bf16[1,32,2048]{2,1,0:T(8,128)(2,1)S(1)}, u32[]{:S(2)}, u32[]{:S(2)}) collective-permute-start(bf16[1,32,2048]{2,1,0:T(8,128)(2,1)S(1)} %collective-permute-done.3.refs_5_), channel_id=1, source_target_pairs={{0,4},{4,0},{8,12},{12,8},{16,20},{20,16},{24,28},{28,24},{1,5},{5... | collective-permute-start | bytes 393224 | tf_op jit(solution)/shard_map/ppermute | solution.py:163
  19.0 7.9 %collective-permute-start.2 = (bf16[1,32,2048]{2,1,0:T(8,128)(2,1)S(1)}, bf16[1,32,2048]{2,1,0:T(8,128)(2,1)S(1)}, u32[]{:S(2)}, u32[]{:S(2)}) collective-permute-start(bf16[1,32,2048]{2,1,0:T(8,128)(2,1)S(1)} %collective-permute-done.1.refs_4_), channel_id=1, source_target_pairs={{0,4},{4,0},{8,12},{12,8},{16,20},{20,16},{24,28},{28,24},{1,5},{5... | collective-permute-start | bytes 393224 | tf_op jit(solution)/shard_map/ppermute | solution.py:163
  21.2 8.6 %collective-permute-start = (f32[34,2048]{1,0:T(8,128)S(1)}, f32[34,2048]{1,0:T(8,128)S(1)}, u32[]{:S(2)}, u32[]{:S(2)}) collective-permute-start(f32[34,2048]{1,0:T(8,128)S(1)} %get-tuple-element.61), channel_id=1, source_target_pairs={{0,2},{1,3},{2,0},{3,1},{4,6},{5,7},{6,4},{7,5},{8,10},{9,11},{10,... | collective-permute-start | bytes 835592 | tf_op jit(solution)/shard_map/ppermute | solution.py:163
  30.7 8.4 %collective-permute-start.9 = (bf16[2,32,2048]{2,1,0:T(8,128)(2,1)S(1)}, bf16[2,32,2048]{2,1,0:T(8,128)(2,1)S(1)}, u32[]{:S(2)}, u32[]{:S(2)}) collective-permute-start(bf16[2,32,2048]{2,1,0:T(8,128)(2,1)S(1)} %fusion.1), channel_id=1, source_target_pairs={{0,2},{1,3},{2,0},{3,1},{4,6},{5,7},{6,4},{7,5},{8,10},{9,11},{10,... | collective-permute-start | bytes 786440 | tf_op jit(solution)/shard_map/ppermute | solution.py:163
  42.3 9.2 %collective-permute-start.11 = (bf16[1,32,2048]{2,1,0:T(8,128)(2,1)S(1)}, bf16[1,32,2048]{2,1,0:T(8,128)(2,1)S(1)}, u32[]{:S(2)}, u32[]{:S(2)}) collective-permute-start(bf16[1,32,2048]{2,1,0:T(8,128)(2,1)S(1)} %get-tuple-element.31), channel_id=1, source_target_pairs={{0,4},{4,0},{8,12},{12,8},{16,20},{20,16},{24,28},{28,24},{1,5},{5... | collective-permute-start | bytes 393224 | tf_op jit(solution)/shard_map/ppermute | solution.py:163
  44.3 10.0 %collective-permute-start.15 = (bf16[1,32,2048]{2,1,0:T(8,128)(2,1)S(1)}, bf16[1,32,2048]{2,1,0:T(8,128)(2,1)S(1)}, u32[]{:S(2)}, u32[]{:S(2)}) collective-permute-start(bf16[1,32,2048]{2,1,0:T(8,128)(2,1)S(1)} %get-tuple-element.35), channel_id=1, source_target_pairs={{0,4},{4,0},{8,12},{12,8},{16,20},{20,16},{24,28},{28,24},{1,5},{5... | collective-permute-start | bytes 393224 | tf_op jit(solution)/shard_map/ppermute | solution.py:163
  44.4 11.4 %collective-permute-start.17 = (bf16[1,32,2048]{2,1,0:T(8,128)(2,1)S(1)}, bf16[1,32,2048]{2,1,0:T(8,128)(2,1)S(1)}, u32[]{:S(2)}, u32[]{:S(2)}) collective-permute-start(bf16[1,32,2048]{2,1,0:T(8,128)(2,1)S(1)} %get-tuple-element.37), channel_id=1, source_target_pairs={{0,4},{4,0},{8,12},{12,8},{16,20},{20,16},{24,28},{28,24},{1,5},{5... | collective-permute-start | bytes 393224 | tf_op jit(solution)/shard_map/ppermute | solution.py:163
  48.7 10.9 %collective-permute-start.14 = (bf16[1,32,2048]{2,1,0:T(8,128)(2,1)S(1)}, bf16[1,32,2048]{2,1,0:T(8,128)(2,1)S(1)}, u32[]{:S(2)}, u32[]{:S(2)}) collective-permute-start(bf16[1,32,2048]{2,1,0:T(8,128)(2,1)S(1)} %add_convert_fusion.4), channel_id=1, source_target_pairs={{0,16},{4,20},{8,24},{12,28},{16,0},{20,4},{24,8},{28,12},{1,17},{... | collective-permute-start | bytes 393224 | tf_op jit(solution)/shard_map/ppermute | solution.py:163
  51.5 8.1 %collective-permute-start.12 = (bf16[1,32,2048]{2,1,0:T(8,128)(2,1)S(1)}, bf16[1,32,2048]{2,1,0:T(8,128)(2,1)S(1)}, u32[]{:S(2)}, u32[]{:S(2)}) collective-permute-start(bf16[1,32,2048]{2,1,0:T(8,128)(2,1)S(1)} %add_convert_fusion.5), channel_id=1, source_target_pairs={{0,24},{4,28},{8,16},{12,20},{16,8},{20,12},{24,0},{28,4},{1,25},{... | collective-permute-start | bytes 393224 | tf_op jit(solution)/shard_map/ppermute | solution.py:163
  61.7 9.9 %collective-permute-start.20 = (bf16[1,32,2048]{2,1,0:T(8,128)(2,1)S(1)}, bf16[1,32,2048]{2,1,0:T(8,128)(2,1)S(1)}, u32[]{:S(2)}, u32[]{:S(2)}) collective-permute-start(bf16[1,32,2048]{2,1,0:T(8,128)(2,1)S(1)} %fusion.3.refs_0_), channel_id=1, source_target_pairs={{0,24},{4,28},{8,16},{12,20},{16,8},{20,12},{24,0},{28,4},{1,25},{... | collective-permute-start | bytes 393224 | tf_op jit(solution)/shard_map/ppermute | solution.py:163
  64.4 11.8 %collective-permute-start.18 = (bf16[1,32,2048]{2,1,0:T(8,128)(2,1)S(1)}, bf16[1,32,2048]{2,1,0:T(8,128)(2,1)S(1)}, u32[]{:S(2)}, u32[]{:S(2)}) collective-permute-start(bf16[1,32,2048]{2,1,0:T(8,128)(2,1)S(1)} %fusion.3.refs_0_), channel_id=1, source_target_pairs={{0,16},{4,20},{8,24},{12,28},{16,0},{20,4},{24,8},{28,12},{1,17},{... | collective-permute-start | bytes 393224 | tf_op jit(solution)/shard_map/ppermute | solution.py:163
  65.0 12.8 %collective-permute-start.22 = (bf16[1,32,2048]{2,1,0:T(8,128)(2,1)S(1)}, bf16[1,32,2048]{2,1,0:T(8,128)(2,1)S(1)}, u32[]{:S(2)}, u32[]{:S(2)}) collective-permute-start(bf16[1,32,2048]{2,1,0:T(8,128)(2,1)S(1)} %fusion.3.refs_0_), channel_id=1, source_target_pairs={{0,4},{4,0},{8,12},{12,8},{16,20},{20,16},{24,28},{28,24},{1,5},{5... | collective-permute-start | bytes 393224 | tf_op jit(solution)/shard_map/ppermute | solution.py:163
  66.9 10.9 %collective-permute-start.24 = (bf16[1,32,2048]{2,1,0:T(8,128)(2,1)S(1)}, bf16[1,32,2048]{2,1,0:T(8,128)(2,1)S(1)}, u32[]{:S(2)}, u32[]{:S(2)}) collective-permute-start(bf16[1,32,2048]{2,1,0:T(8,128)(2,1)S(1)} %collective-permute-done.23.refs_2_), channel_id=1, source_target_pairs={{0,4},{4,0},{8,12},{12,8},{16,20},{20,16},{24,28},{28,24},{1,5},{5... | collective-permute-start | bytes 393224 | tf_op jit(solution)/shard_map/ppermute | solution.py:163
  83.8 8.6 %collective-permute-start.26 = (bf16[2,32,2048]{2,1,0:T(8,128)(2,1)S(1)}, bf16[2,32,2048]{2,1,0:T(8,128)(2,1)S(1)}, u32[]{:S(2)}, u32[]{:S(2)}) collective-permute-start(bf16[2,32,2048]{2,1,0:T(8,128)(2,1)S(1)} %fusion.2), channel_id=1, source_target_pairs={{0,2},{1,3},{2,0},{3,1},{4,6},{5,7},{6,4},{7,5},{8,10},{9,11},{10,... | collective-permute-start | bytes 786440 | tf_op jit(solution)/shard_map/ppermute | solution.py:163
  96.2 8.5 %collective-permute-start.28 = (bf16[1,32,2048]{2,1,0:T(8,128)(2,1)S(1)}, bf16[1,32,2048]{2,1,0:T(8,128)(2,1)S(1)}, u32[]{:S(2)}, u32[]{:S(2)}) collective-permute-start(bf16[1,32,2048]{2,1,0:T(8,128)(2,1)S(1)} %get-tuple-element.43), channel_id=1, source_target_pairs={{0,4},{4,0},{8,12},{12,8},{16,20},{20,16},{24,28},{28,24},{1,5},{5... | collective-permute-start | bytes 393224 | tf_op jit(solution)/shard_map/ppermute | solution.py:163
  97.6 9.9 %collective-permute-start.32 = (bf16[1,32,2048]{2,1,0:T(8,128)(2,1)S(1)}, bf16[1,32,2048]{2,1,0:T(8,128)(2,1)S(1)}, u32[]{:S(2)}, u32[]{:S(2)}) collective-permute-start(bf16[1,32,2048]{2,1,0:T(8,128)(2,1)S(1)} %get-tuple-element.47), channel_id=1, source_target_pairs={{0,4},{4,0},{8,12},{12,8},{16,20},{20,16},{24,28},{28,24},{1,5},{5... | collective-permute-start | bytes 393224 | tf_op jit(solution)/shard_map/ppermute | solution.py:163
  98.2 11.4 %collective-permute-start.34 = (bf16[1,32,2048]{2,1,0:T(8,128)(2,1)S(1)}, bf16[1,32,2048]{2,1,0:T(8,128)(2,1)S(1)}, u32[]{:S(2)}, u32[]{:S(2)}) collective-permute-start(bf16[1,32,2048]{2,1,0:T(8,128)(2,1)S(1)} %get-tuple-element.49), channel_id=1, source_target_pairs={{0,4},{4,0},{8,12},{12,8},{16,20},{20,16},{24,28},{28,24},{1,5},{5... | collective-permute-start | bytes 393224 | tf_op jit(solution)/shard_map/ppermute | solution.py:163
  101.9 11.6 %collective-permute-start.31 = (bf16[1,32,2048]{2,1,0:T(8,128)(2,1)S(1)}, bf16[1,32,2048]{2,1,0:T(8,128)(2,1)S(1)}, u32[]{:S(2)}, u32[]{:S(2)}) collective-permute-start(bf16[1,32,2048]{2,1,0:T(8,128)(2,1)S(1)} %add_convert_fusion.1), channel_id=1, source_target_pairs={{0,16},{4,20},{8,24},{12,28},{16,0},{20,4},{24,8},{28,12},{1,17},{... | collective-permute-start | bytes 393224 | tf_op jit(solution)/shard_map/ppermute | solution.py:163
  104.7 8.8 %collective-permute-start.29 = (bf16[1,32,2048]{2,1,0:T(8,128)(2,1)S(1)}, bf16[1,32,2048]{2,1,0:T(8,128)(2,1)S(1)}, u32[]{:S(2)}, u32[]{:S(2)}) collective-permute-start(bf16[1,32,2048]{2,1,0:T(8,128)(2,1)S(1)} %add_convert_fusion.2), channel_id=1, source_target_pairs={{0,24},{4,28},{8,16},{12,20},{16,8},{20,12},{24,0},{28,4},{1,25},{... | collective-permute-start | bytes 393224 | tf_op jit(solution)/shard_map/ppermute | solution.py:163
  (16 other events, 114.3 us)

commit v7 on v6

v7 whole, which is shorter than its diff:
```python
import functools
import typing

import jax
import jax.numpy as jnp
from jax import lax
from jax.experimental import pallas as pl
from jax.experimental.pallas import tpu as pltpu
from jax.sharding import PartitionSpec as P

BR_DEV = 16
BC_DEV = 16
ITERS = 2


step_primal = 0.4
step_dual = 0.4

VMEM_LIMIT = 24 * 1024 * 1024
FETCH_LIMIT = 46 * 1024 * 1024


def among(value, ks):
    return functools.reduce(jnp.logical_or, [value == k for k in ks])


def position(value, ks):
    at = 0
    for i, k in enumerate(ks[1:]):
        at = jnp.where(value == k, i + 1, at)
    return at


class Out(typing.NamedTuple):
    ks: tuple
    kind: typing.Any
    stacked: bool

    @property
    def direct(self):
        return self.kind == jnp.float32 and self.stacked


class Plan(typing.NamedTuple):
    forward: bool
    fetched: bool
    senders: tuple
    outs: tuple
    begun: bool


def sweep_kernel(plan, per_in, info, tiles, *refs):
    refs = list(refs)
    parts = [refs.pop(0) for _ in plan.senders]
    begun = [refs.pop(0) for _ in plan.outs] if plan.begun else []
    results = [[refs.pop(0) for _ in (out.ks[:1] if out.stacked else out.ks)] for out in plan.outs]
    operand = refs.pop(0)
    sums = [
        result[0] if out.direct else refs.pop(0) for out, result in zip(plan.outs, results)
    ]
    held, arrived = refs if plan.fetched else (tiles, None)
    slots = tiles.shape[0]
    live = info[2 * slots]
    me_in = info[2 * slots + 1]
    me_out = info[2 * slots + 2]
    span_in = operand.shape[1]
    span_out = tiles.shape[1] if plan.forward else tiles.shape[2]
    per_out = sums[0].shape[2] // span_out

    def ends(slot):
        row, col = info[2 * slot], info[2 * slot + 1]
        return (col, row) if plan.forward else (row, col)

    def accepted(slot):
        block_in, block_out = ends(slot)
        source = (block_in // per_in) ^ me_in
        target = (block_out // per_out) ^ me_out
        return among(source, sum(plan.senders, ())) & among(
            target, sum((out.ks for out in plan.outs), ())
        )

    def fetch(slot):
        return pltpu.make_async_copy(tiles.at[slot], held.at[slot], arrived.at[slot])

    if plan.fetched:

        def start(slot, carry):
            @pl.when(accepted(slot))
            def _():
                fetch(slot).start()

            return carry

        lax.fori_loop(0, live, start, 0)
    for i, total in enumerate(sums):
        total[...] = begun[i][...] if begun else jnp.zeros_like(total)

    def visit(slot, carry):
        @pl.when(accepted(slot))
        def _():
            block_in, block_out = ends(slot)
            source = (block_in // per_in) ^ me_in
            target = (block_out // per_out) ^ me_out
            place = pl.multiple_of((block_in % per_in) * span_in, span_in)
            for part, ks in zip(parts, plan.senders):

                @pl.when(among(source, ks))
                def _():
                    operand[...] = part[position(source, ks), :, pl.ds(place, span_in)]

            if plan.fetched:
                fetch(slot).wait()
            contract = (((1,), (1,)), ((), ())) if plan.forward else (((1,), (0,)), ((), ()))
            term = lax.dot_general(
                operand[...], held[slot], contract, preferred_element_type=jnp.float32
            )
            to = pl.multiple_of((block_out % per_out) * span_out, span_out)
            for total, out in zip(sums, plan.outs):

                @pl.when(among(target, out.ks))
                def _():
                    total[position(target, out.ks), :, pl.ds(to, span_out)] += term

        return carry

    lax.fori_loop(0, live, visit, 0)
    for out, result, total in zip(plan.outs, results, sums):
        if not out.direct:
            each = len(out.ks) // len(result)
            for i, ref in enumerate(result):
                ref[...] = total[i * each : (i + 1) * each].astype(ref.dtype)


def sweep(plan, tiles, info, parts, begun, wide):
    slots, rows_tile, cols_tile = tiles.shape
    width = parts[0].shape[1]
    span_in = cols_tile if plan.forward else rows_tile
    plan = plan._replace(begun=bool(begun))
    out_shape = []
    scratch = [pltpu.VMEM((width, span_in), jnp.bfloat16)]
    for out in plan.outs:
        many = len(out.ks)
        if out.stacked:
            out_shape += [jax.ShapeDtypeStruct((many, width, wide), out.kind)]
        else:
            out_shape += [jax.ShapeDtypeStruct((1, width, wide), out.kind)] * many
        if not out.direct:
            scratch += [pltpu.VMEM((many, width, wide), jnp.float32)]
    if plan.fetched:
        scratch += [pltpu.VMEM(tiles.shape, tiles.dtype), pltpu.SemaphoreType.DMA((slots,))]
    vmem = pl.BlockSpec(memory_space=pltpu.VMEM)
    flat = pl.pallas_call(
        functools.partial(sweep_kernel, plan, parts[0].shape[2] // span_in),
        out_shape=out_shape,
        in_specs=[
            pl.BlockSpec(memory_space=pltpu.SMEM),
            pl.BlockSpec(memory_space=pl.ANY) if plan.fetched else vmem,
        ]
        + [vmem] * (len(parts) + len(begun)),
        out_specs=[vmem] * len(out_shape),
        scratch_shapes=scratch,
        compiler_params=pltpu.CompilerParams(
            vmem_limit_bytes=FETCH_LIMIT if plan.fetched else VMEM_LIMIT
        ),
        cost_estimate=pl.CostEstimate(
            flops=slots * width * rows_tile * cols_tile,
            bytes_accessed=tiles.size,
            transcendentals=0,
        ),
        name="forward_sweep" if plan.forward else "transpose_sweep",
    )(info, tiles, *parts, *begun)
    flat = list(flat)
    return [
        flat.pop(0) if out.stacked else {k: flat.pop(0) for k in out.ks} for out in plan.outs
    ]


def swap(value, axis, size, k):
    return lax.ppermute(value, axis, [(i, i ^ k) for i in range(size)])


def gather_pairs(own, axis, size):
    parts = [None] * size
    parts[0] = own
    for k in range(size - 2, 0, -2):
        parts[k] = swap(own, axis, size, k)
    for k in range(size - 2, -1, -2):
        parts[k + 1] = swap(parts[k], axis, size, 1)
    return parts


def update_kernel(shares, last, *refs):
    parts, (own, demand, kind, dual), outs = refs[:shares], refs[shares : shares + 4], refs[shares + 4 :]
    push = own[0]
    for part in parts:
        push = push + part[0].astype(jnp.float32)
    moved = dual[...] + step_dual * (demand[...] - push)
    moved = jnp.where(kind[...] == 1, jnp.maximum(moved, 0.0), moved)
    if last:
        outs[0][:, 0, :] = moved
    else:
        outs[0][...] = moved
        outs[1][0] = moved.astype(outs[1].dtype)


def update_dual(parts, own, demand, kind, dual, last):
    width, span = dual.shape
    vmem = pl.BlockSpec(memory_space=pltpu.VMEM)
    if last:
        out_shape = [jax.ShapeDtypeStruct((width, 1, span), jnp.float32)]
    else:
        out_shape = [
            jax.ShapeDtypeStruct((width, span), jnp.float32),
            jax.ShapeDtypeStruct((1, width, span), jnp.bfloat16),
        ]
    return pl.pallas_call(
        functools.partial(update_kernel, len(parts), last),
        out_shape=out_shape,
        in_specs=[vmem] * (len(parts) + 4),
        out_specs=[vmem] * len(out_shape),
        compiler_params=pltpu.CompilerParams(vmem_limit_bytes=VMEM_LIMIT),
        cost_estimate=pl.CostEstimate(
            flops=width * span * 16, bytes_accessed=width * span * 16, transcendentals=0
        ),
        name="update_dual",
    )(*parts, own, demand, kind, dual)


def share_pairs(kept, sent, axis, size):
    shares = {}
    for k in range(4, size, 2):
        pair = kept[k] + swap(sent[k + 1], axis, size, 1).astype(jnp.float32)
        shares[k] = swap(pair.astype(jnp.bfloat16), axis, size, k)
    for k in range(1, min(size, 4)):
        shares[k] = swap(sent[k], axis, size, k)
    return list(shares.values())


def sum_halves(kept, sent, axis, size):
    here = kept + swap(sent, axis, size, 1).astype(jnp.float32)
    away = here.astype(jnp.bfloat16)
    total = here
    for t in range(1, size // 2):
        other = swap(away, axis, size, 2 * t)
        order = [h ^ t for h in range(size // 2)]
        total = total + jnp.stack([other[h] for h in order]).astype(jnp.float32)
    return total


def body(
    rows,
    cols,
    tiles,
    tile_index,
    tile_count,
    weights,
    carbon,
    completion,
    demand,
    row_kind,
    primal_start,
    dual_start,
):
    blocks = tiles[0, 0]
    info = jnp.concatenate(
        [
            tile_index.reshape(-1),
            tile_count.reshape(-1),
            lax.axis_index("col")[None],
            lax.axis_index("row")[None],
        ]
    ).astype(jnp.int32)
    info_back = jnp.concatenate([info[:-2], info[-1:], info[-2:-1]])
    dual = dual_start[:, 0, :]
    rounded_dual = [dual.astype(jnp.bfloat16)[None]]
    state = jnp.concatenate([primal_start[:, 0, :], carbon, completion])
    states = [state] + [swap(state, "row", rows, k) for k in range(2, rows, 2)]
    states = jnp.stack(states)
    width = weights.shape[0]
    primal = states[:, :width]
    share = weights[:, None]
    cost = share * states[:, width : width + 1] + (1.0 - share) * states[:, width + 1 :]
    whole, rounded = jnp.float32, jnp.bfloat16
    late = [k for k in range(5, cols, 2)]
    early = [k for k in range(cols) if k not in late]
    mine, other = (tuple(range(p, rows, 2)) for p in (0, 1))
    keep = tuple(k for k in range(cols) if k % 2 == 0 and k != 2)
    send = tuple(k for k in range(cols) if k not in keep)
    for step in range(ITERS):
        dual_parts = gather_pairs(rounded_dual[0], "col", cols)
        begun = sweep(
            Plan(
                False, step == 0, tuple((k,) for k in early),
                (Out(mine, whole, True), Out(other, whole, True)), False,
            ),
            blocks, info, [dual_parts[k] for k in early], [], primal.shape[2],
        )
        kept, sent = sweep(
            Plan(
                False, False, tuple((k,) for k in late),
                (Out(mine, whole, True), Out(other, rounded, True)), True,
            ),
            blocks, info, [dual_parts[k] for k in late], begun, primal.shape[2],
        )
        pull = sum_halves(kept, sent, "row", rows)
        fresh = jnp.maximum(primal - step_primal * (cost - pull), 0.0)
        extra = (2.0 * fresh - primal).astype(jnp.bfloat16)
        primal = fresh
        kept, sent = sweep(
            Plan(
                True, False, (mine,),
                (Out(keep, whole, True), Out(send, whole, True)), False,
            ),
            blocks, info_back, [extra], [], dual.shape[1],
        )
        extra = swap(extra, "row", rows, 1)
        (sent,) = sweep(
            Plan(True, False, (other,), (Out(send, rounded, False),), True),
            blocks, info_back, [extra], [sent], dual.shape[1],
        )
        (kept,) = sweep(
            Plan(True, False, (other,), (Out(keep, whole, False),), True),
            blocks, info_back, [extra], [kept], dual.shape[1],
        )
        shares = share_pairs(kept, sent, "col", cols)
        dual, *rounded_dual = update_dual(
            shares, kept[0], demand, row_kind, dual, step == ITERS - 1
        )
    return (primal[0][:, None, :], dual)


def solution(mesh):
    placed = (
        P("row", "col", None, None, None),
        P("row", "col", None, None),
        P("row", "col"),
        P(),
        P("col", "row"),
        P("col", "row"),
        P("row", "col"),
        P("row", "col"),
        P(None, "col", "row"),
        P(None, "row", "col"),
    )
    return jax.shard_map(
        functools.partial(body, mesh.shape["row"], mesh.shape["col"]),
        mesh=mesh,
        in_specs=placed,
        out_specs=(P(None, "col", "row"), P(None, "row", "col")),
        check_vma=False,
    )
```

time: 118 us -> 120 us (1.017); the launches traced: 116 us -> 120 us
  starting transfers between devices: 43.9 us -> 53.7 us
  waiting for transfers between devices: 52.4 us -> 44.2 us
  Pallas kernels: 10 us -> 14.3 us
  local copies, waits for them, and re-layouts: 6.08 us -> 4.59 us
    ppermute x35, starting transfers between devices: 43.9 us -> 53.7 us  [swap(): return lax.ppermute(value, axis, [(i, i ^ k) for i in range(size)])]
    ppermute x35, waiting for transfers between devices: 52.4 us -> 44.2 us  [swap(): return lax.ppermute(value, axis, [(i, i ^ k) for i in range(size)])]
    pallas_call x8 -> x12, Pallas kernels: 10 us -> 14.3 us  [the longest x10 13.2 us: sweep(): pl.pallas_call(functools.partial(sweep_kernel, plan, parts[0].shape[2] //...]
    unnamed x16 -> x18, local copies, waits for them, and re-layouts: 5.95 us -> 4.46 us
  transfers between devices with their start and end apart: 35 -> 35, of which waited for: 24 -> 16; matrix products, arithmetic and copies ran while one was open for 3% -> 3% of each run, Pallas kernels for 6% -> 9%
where the time goes in v7:
time: 120 us
  starting transfers between devices  53.7 us (45%)
  waiting for transfers between devices  44.2 us (37%)
  Pallas kernels  14.3 us (12%)
  local copies, waits for them, and re-layouts  4.59 us (4%)
  other arithmetic  1.67 us (1%)
  between operations  1.61 us (1%)
    ppermute x35, starting transfers between devices, swap(): return lax.ppermute(value, axis, [(i, i ^ k) for i in range(size)])  53.7 us
    ppermute x35, waiting for transfers between devices, swap(): return lax.ppermute(value, axis, [(i, i ^ k) for i in range(size)])  44.2 us
    pallas_call x10, Pallas kernels, sweep(): pl.pallas_call(functools.partial(sweep_kernel, plan, parts[0].shape[2] //...  13.2 us
    unnamed x18, local copies, waits for them, and re-layouts  4.46 us
  transfers between devices with their start and end apart: 35, of which 16 were waited for; matrix products, arithmetic and copies ran while one was open for 3% of the time, Pallas kernels for 9%

profile of v7, /device:TPU:0, one launch (start us, length us, event | category | flops | bytes accessed | tf_op | source)
XLA Modules:
  0.0 120.0 jit_solution(12449947584441969680)
XLA Ops:
  1.7 4.1 %collective-permute-start.1 = (bf16[1,32,2048]{2,1,0:T(8,128)(2,1)S(1)}, bf16[1,32,2048]{2,1,0:T(8,128)(2,1)S(1)}, u32[]{:S(2)}, u32[]{:S(2)}) collective-permute-start(bf16[1,32,2048]{2,1,0:T(8,128)(2,1)S(1)} %bitcast.36), channel_id=1, source_target_pairs={{0,16},{4,20},{8,24},{12,28},{16,0},{20,4},{24,8},{28,12},{1,17},{... | collective-permute-start | bytes 393224 | tf_op jit(solution)/shard_map/ppermute | solution.py:179
  9.9 5.9 %collective-permute-done.1.refs_4_ = bf16[1,32,2048]{2,1,0:T(8,128)(2,1)S(1)} collective-permute-done((bf16[1,32,2048]{2,1,0:T(8,128)(2,1)S(1)}, bf16[1,32,2048]{2,1,0:T(8,128)(2,1)S(1)}, u32[]{:S(2)}, u32[]{:S(2)}) %collective-permute-start.1) | collective-permute-done | bytes 131104 | tf_op jit(solution)/shard_map/ppermute | solution.py:179
  15.8 1.8 %collective-permute-start.2 = (bf16[1,32,2048]{2,1,0:T(8,128)(2,1)S(1)}, bf16[1,32,2048]{2,1,0:T(8,128)(2,1)S(1)}, u32[]{:S(2)}, u32[]{:S(2)}) collective-permute-start(bf16[1,32,2048]{2,1,0:T(8,128)(2,1)S(1)} %collective-permute-done.1.refs_4_), channel_id=1, source_target_pairs={{0,4},{4,0},{8,12},{12,8},{16,20},{20,16},{24,28},{28,24},{1,5},{5... | collective-permute-start | bytes 393224 | tf_op jit(solution)/shard_map/ppermute | solution.py:179
  17.8 1.8 %collective-permute-start.7 = (bf16[1,32,2048]{2,1,0:T(8,128)(2,1)S(1)}, bf16[1,32,2048]{2,1,0:T(8,128)(2,1)S(1)}, u32[]{:S(2)}, u32[]{:S(2)}) collective-permute-start(bf16[1,32,2048]{2,1,0:T(8,128)(2,1)S(1)} %collective-permute-done.6.refs_2_), channel_id=1, source_target_pairs={{0,4},{4,0},{8,12},{12,8},{16,20},{20,16},{24,28},{28,24},{1,5},{5... | collective-permute-start | bytes 393224 | tf_op jit(solution)/shard_map/ppermute | solution.py:179
  22.9 2.3 %collective-permute-done.7.refs_3_ = bf16[1,32,2048]{2,1,0:T(8,128)(2,1)S(1)} collective-permute-done((bf16[1,32,2048]{2,1,0:T(8,128)(2,1)S(1)}, bf16[1,32,2048]{2,1,0:T(8,128)(2,1)S(1)}, u32[]{:S(2)}, u32[]{:S(2)}) %collective-permute-start.7) | collective-permute-done | bytes 131104 | tf_op jit(solution)/shard_map/ppermute | solution.py:179
  25.2 2.5 %transpose_sweep.4 = (f32[2,32,2048]{2,1,0:T(8,128)S(1)}, f32[2,32,2048]{2,1,0:T(8,128)S(1)}) custom-call(s32[19]{0:T(128)S(1)} %get-tuple-element.79.info, bf16[8,1024,512]{2,1,0:T(8,128)(2,1)} %bitcast.25, bf16[1,32,2048]{2,1,0:T(8,128)(2,1)S(1)} %bitcast.40, bf16[1,32,2048]{2,1,0:T(8,128)(2,1)S(1)} %collective-permute-done.5.refs_1_, ...), custom_call_target="tpu_custom_call" | custom-call | flops 134217728 | bytes 4194304 | tf_op jit(solution)/shard_map/transpose_sweep/pallas_call | solution.py:152
  33.2 7.1 %collective-permute-done.9 = bf16[2,32,2048]{2,1,0:T(8,128)(2,1)S(1)} collective-permute-done((bf16[2,32,2048]{2,1,0:T(8,128)(2,1)S(1)}, bf16[2,32,2048]{2,1,0:T(8,128)(2,1)S(1)}, u32[]{:S(2)}, u32[]{:S(2)}) %collective-permute-start.9) | collective-permute-done | bytes 262176 | tf_op jit(solution)/shard_map/ppermute | solution.py:179
  40.7 2.1 %forward_sweep.6 = (f32[3,32,2048]{2,1,0:T(8,128)S(1)}, f32[5,32,2048]{2,1,0:T(8,128)S(1)}) custom-call(s32[19]{0:T(128)S(1)} %get-tuple-element.78.info, bf16[8,1024,512]{2,1,0:T(8,128)(2,1)S(1)} %bitcast.27, bf16[2,32,2048]{2,1,0:T(8,128)(2,1)S(1)} %get-tuple-element.68.refs_0_), custom_call_target="tpu_custom_call" | custom-call | flops 134217728 | bytes 4194304 | tf_op jit(solution)/shard_map/forward_sweep/pallas_call | solution.py:152
  43.6 1.6 %collective-permute-start.11 = (bf16[1,32,2048]{2,1,0:T(8,128)(2,1)S(1)}, bf16[1,32,2048]{2,1,0:T(8,128)(2,1)S(1)}, u32[]{:S(2)}, u32[]{:S(2)}) collective-permute-start(bf16[1,32,2048]{2,1,0:T(8,128)(2,1)S(1)} %get-tuple-element.39), channel_id=1, source_target_pairs={{0,4},{4,0},{8,12},{12,8},{16,20},{20,16},{24,28},{28,24},{1,5},{5... | collective-permute-start | bytes 393224 | tf_op jit(solution)/shard_map/ppermute | solution.py:179
  50.0 8.5 %collective-permute-start.12 = (bf16[1,32,2048]{2,1,0:T(8,128)(2,1)S(1)}, bf16[1,32,2048]{2,1,0:T(8,128)(2,1)S(1)}, u32[]{:S(2)}, u32[]{:S(2)}) collective-permute-start(bf16[1,32,2048]{2,1,0:T(8,128)(2,1)S(1)} %add_convert_fusion.3), channel_id=1, source_target_pairs={{0,16},{4,20},{8,24},{12,28},{16,0},{20,4},{24,8},{28,12},{1,17},{... | collective-permute-start | bytes 393224 | tf_op jit(solution)/shard_map/ppermute | solution.py:179
  58.6 1.8 %collective-permute-start.14 = (bf16[1,32,2048]{2,1,0:T(8,128)(2,1)S(1)}, bf16[1,32,2048]{2,1,0:T(8,128)(2,1)S(1)}, u32[]{:S(2)}, u32[]{:S(2)}) collective-permute-start(bf16[1,32,2048]{2,1,0:T(8,128)(2,1)S(1)} %add_convert_fusion.2), channel_id=1, source_target_pairs={{0,24},{4,28},{8,16},{12,20},{16,8},{20,12},{24,0},{28,4},{1,25},{... | collective-permute-start | bytes 393224 | tf_op jit(solution)/shard_map/ppermute | solution.py:179
  60.5 3.2 %collective-permute-done.12.refs_0_ = bf16[1,32,2048]{2,1,0:T(8,128)(2,1)S(1)} collective-permute-done((bf16[1,32,2048]{2,1,0:T(8,128)(2,1)S(1)}, bf16[1,32,2048]{2,1,0:T(8,128)(2,1)S(1)}, u32[]{:S(2)}, u32[]{:S(2)}) %collective-permute-start.12) | collective-permute-done | bytes 131104 | tf_op jit(solution)/shard_map/ppermute | solution.py:179
  63.6 2.5 %collective-permute-done.14.refs_1_ = bf16[1,32,2048]{2,1,0:T(8,128)(2,1)S(1)} collective-permute-done((bf16[1,32,2048]{2,1,0:T(8,128)(2,1)S(1)}, bf16[1,32,2048]{2,1,0:T(8,128)(2,1)S(1)}, u32[]{:S(2)}, u32[]{:S(2)}) %collective-permute-start.14) | collective-permute-done | bytes 131104 | tf_op jit(solution)/shard_map/ppermute | solution.py:179
  66.3 4.4 %collective-permute-start.23 = (bf16[1,32,2048]{2,1,0:T(8,128)(2,1)S(1)}, bf16[1,32,2048]{2,1,0:T(8,128)(2,1)S(1)}, u32[]{:S(2)}, u32[]{:S(2)}) collective-permute-start(bf16[1,32,2048]{2,1,0:T(8,128)(2,1)S(1)} %get-tuple-element.46.refs_0_), channel_id=1, source_target_pairs={{0,8},{4,12},{8,0},{12,4},{16,24},{20,28},{24,16},{28,20},{1,9},{5... | collective-permute-start | bytes 393224 | tf_op jit(solution)/shard_map/ppermute | solution.py:179
  75.2 4.2 %collective-permute-done.18.refs_4_ = bf16[1,32,2048]{2,1,0:T(8,128)(2,1)S(1)} collective-permute-done((bf16[1,32,2048]{2,1,0:T(8,128)(2,1)S(1)}, bf16[1,32,2048]{2,1,0:T(8,128)(2,1)S(1)}, u32[]{:S(2)}, u32[]{:S(2)}) %collective-permute-start.18) | collective-permute-done | bytes 131104 | tf_op jit(solution)/shard_map/ppermute | solution.py:179
  79.4 2.0 %collective-permute-start.21 = (bf16[1,32,2048]{2,1,0:T(8,128)(2,1)S(1)}, bf16[1,32,2048]{2,1,0:T(8,128)(2,1)S(1)}, u32[]{:S(2)}, u32[]{:S(2)}) collective-permute-start(bf16[1,32,2048]{2,1,0:T(8,128)(2,1)S(1)} %collective-permute-done.20.refs_5_), channel_id=1, source_target_pairs={{0,4},{4,0},{8,12},{12,8},{16,20},{20,16},{24,28},{28,24},{1,5},{5... | collective-permute-start | bytes 393224 | tf_op jit(solution)/shard_map/ppermute | solution.py:179
  82.4 1.9 %collective-permute-done.19.refs_0_ = bf16[1,32,2048]{2,1,0:T(8,128)(2,1)S(1)} collective-permute-done((bf16[1,32,2048]{2,1,0:T(8,128)(2,1)S(1)}, bf16[1,32,2048]{2,1,0:T(8,128)(2,1)S(1)}, u32[]{:S(2)}, u32[]{:S(2)}) %collective-permute-start.19) | collective-permute-done | bytes 131104 | tf_op jit(solution)/shard_map/ppermute | solution.py:179
  89.6 7.5 %collective-permute-done.26 = bf16[2,32,2048]{2,1,0:T(8,128)(2,1)S(1)} collective-permute-done((bf16[2,32,2048]{2,1,0:T(8,128)(2,1)S(1)}, bf16[2,32,2048]{2,1,0:T(8,128)(2,1)S(1)}, u32[]{:S(2)}, u32[]{:S(2)}) %collective-permute-start.26) | collective-permute-done | bytes 262176 | tf_op jit(solution)/shard_map/ppermute | solution.py:179
  97.5 2.1 %forward_sweep.9 = (f32[3,32,2048]{2,1,0:T(8,128)S(1)}, f32[5,32,2048]{2,1,0:T(8,128)S(1)}) custom-call(s32[19]{0:T(128)S(1)} %get-tuple-element.78.info, bf16[8,1024,512]{2,1,0:T(8,128)(2,1)S(1)} %bitcast.32, bf16[2,32,2048]{2,1,0:T(8,128)(2,1)S(1)} %get-tuple-element.66.refs_0_), custom_call_target="tpu_custom_call" | custom-call | flops 134217728 | bytes 4194304 | tf_op jit(solution)/shard_map/forward_sweep/pallas_call | solution.py:152
  100.9 1.6 %collective-permute-start.30 = (bf16[1,32,2048]{2,1,0:T(8,128)(2,1)S(1)}, bf16[1,32,2048]{2,1,0:T(8,128)(2,1)S(1)}, u32[]{:S(2)}, u32[]{:S(2)}) collective-permute-start(bf16[1,32,2048]{2,1,0:T(8,128)(2,1)S(1)} %get-tuple-element.56), channel_id=1, source_target_pairs={{0,4},{4,0},{8,12},{12,8},{16,20},{20,16},{24,28},{28,24},{1,5},{5... | collective-permute-start | bytes 393224 | tf_op jit(solution)/shard_map/ppermute | solution.py:179
  102.9 3.1 %collective-permute-start.34 = (bf16[1,32,2048]{2,1,0:T(8,128)(2,1)S(1)}, bf16[1,32,2048]{2,1,0:T(8,128)(2,1)S(1)}, u32[]{:S(2)}, u32[]{:S(2)}) collective-permute-start(bf16[1,32,2048]{2,1,0:T(8,128)(2,1)S(1)} %get-tuple-element.59), channel_id=1, source_target_pairs={{0,12},{4,8},{8,4},{12,0},{16,28},{20,24},{24,20},{28,16},{1,13},{... | collective-permute-start | bytes 393224 | tf_op jit(solution)/shard_map/ppermute | solution.py:179
  106.9 4.6 %collective-permute-start.29 = (bf16[1,32,2048]{2,1,0:T(8,128)(2,1)S(1)}, bf16[1,32,2048]{2,1,0:T(8,128)(2,1)S(1)}, u32[]{:S(2)}, u32[]{:S(2)}) collective-permute-start(bf16[1,32,2048]{2,1,0:T(8,128)(2,1)S(1)} %add_convert_fusion.1), channel_id=1, source_target_pairs={{0,16},{4,20},{8,24},{12,28},{16,0},{20,4},{24,8},{28,12},{1,17},{... | collective-permute-start | bytes 393224 | tf_op jit(solution)/shard_map/ppermute | solution.py:179
  111.7 2.2 %collective-permute-start.31 = (bf16[1,32,2048]{2,1,0:T(8,128)(2,1)S(1)}, bf16[1,32,2048]{2,1,0:T(8,128)(2,1)S(1)}, u32[]{:S(2)}, u32[]{:S(2)}) collective-permute-start(bf16[1,32,2048]{2,1,0:T(8,128)(2,1)S(1)} %add_convert_fusion), channel_id=1, source_target_pairs={{0,24},{4,28},{8,16},{12,20},{16,8},{20,12},{24,0},{28,4},{1,25},{... | collective-permute-start | bytes 393224 | tf_op jit(solution)/shard_map/ppermute | solution.py:179
  114.9 4.2 %collective-permute-done.29.refs_0_ = bf16[1,32,2048]{2,1,0:T(8,128)(2,1)S(1)} collective-permute-done((bf16[1,32,2048]{2,1,0:T(8,128)(2,1)S(1)}, bf16[1,32,2048]{2,1,0:T(8,128)(2,1)S(1)}, u32[]{:S(2)}, u32[]{:S(2)}) %collective-permute-start.29) | collective-permute-done | bytes 131104 | tf_op jit(solution)/shard_map/ppermute | solution.py:179
  (92 shorter events, 35.3 us)
Async XLA Ops:
  1.7 14.1 %collective-permute-start.1 = (bf16[1,32,2048]{2,1,0:T(8,128)(2,1)S(1)}, bf16[1,32,2048]{2,1,0:T(8,128)(2,1)S(1)}, u32[]{:S(2)}, u32[]{:S(2)}) collective-permute-start(bf16[1,32,2048]{2,1,0:T(8,128)(2,1)S(1)} %bitcast.36), channel_id=1, source_target_pairs={{0,16},{4,20},{8,24},{12,28},{16,0},{20,4},{24,8},{28,12},{1,17},{... | collective-permute-start | bytes 393224 | tf_op jit(solution)/shard_map/ppermute | solution.py:179
  5.8 11.8 %collective-permute-start.3 = (bf16[1,32,2048]{2,1,0:T(8,128)(2,1)S(1)}, bf16[1,32,2048]{2,1,0:T(8,128)(2,1)S(1)}, u32[]{:S(2)}, u32[]{:S(2)}) collective-permute-start(bf16[1,32,2048]{2,1,0:T(8,128)(2,1)S(1)} %bitcast.37), channel_id=1, source_target_pairs={{0,24},{4,28},{8,16},{12,20},{16,8},{20,12},{24,0},{28,4},{1,25},{... | collective-permute-start | bytes 393224 | tf_op jit(solution)/shard_map/ppermute | solution.py:179
  7.1 10.7 %collective-permute-start.6 = (bf16[1,32,2048]{2,1,0:T(8,128)(2,1)S(1)}, bf16[1,32,2048]{2,1,0:T(8,128)(2,1)S(1)}, u32[]{:S(2)}, u32[]{:S(2)}) collective-permute-start(bf16[1,32,2048]{2,1,0:T(8,128)(2,1)S(1)} %bitcast.38), channel_id=1, source_target_pairs={{0,8},{4,12},{8,0},{12,4},{16,24},{20,28},{24,16},{28,20},{1,9},{5... | collective-permute-start | bytes 393224 | tf_op jit(solution)/shard_map/ppermute | solution.py:179
  7.4 15.5 %collective-permute-start.5 = (bf16[1,32,2048]{2,1,0:T(8,128)(2,1)S(1)}, bf16[1,32,2048]{2,1,0:T(8,128)(2,1)S(1)}, u32[]{:S(2)}, u32[]{:S(2)}) collective-permute-start(bf16[1,32,2048]{2,1,0:T(8,128)(2,1)S(1)} %bitcast.39), channel_id=1, source_target_pairs={{0,4},{4,0},{8,12},{12,8},{16,20},{20,16},{24,28},{28,24},{1,5},{5... | collective-permute-start | bytes 393224 | tf_op jit(solution)/shard_map/ppermute | solution.py:179
  15.8 11.9 %collective-permute-start.2 = (bf16[1,32,2048]{2,1,0:T(8,128)(2,1)S(1)}, bf16[1,32,2048]{2,1,0:T(8,128)(2,1)S(1)}, u32[]{:S(2)}, u32[]{:S(2)}) collective-permute-start(bf16[1,32,2048]{2,1,0:T(8,128)(2,1)S(1)} %collective-permute-done.1.refs_4_), channel_id=1, source_target_pairs={{0,4},{4,0},{8,12},{12,8},{16,20},{20,16},{24,28},{28,24},{1,5},{5... | collective-permute-start | bytes 393224 | tf_op jit(solution)/shard_map/ppermute | solution.py:179
  17.6 10.1 %collective-permute-start.4 = (bf16[1,32,2048]{2,1,0:T(8,128)(2,1)S(1)}, bf16[1,32,2048]{2,1,0:T(8,128)(2,1)S(1)}, u32[]{:S(2)}, u32[]{:S(2)}) collective-permute-start(bf16[1,32,2048]{2,1,0:T(8,128)(2,1)S(1)} %collective-permute-done.3.refs_5_), channel_id=1, source_target_pairs={{0,4},{4,0},{8,12},{12,8},{16,20},{20,16},{24,28},{28,24},{1,5},{5... | collective-permute-start | bytes 393224 | tf_op jit(solution)/shard_map/ppermute | solution.py:179
  20.4 9.9 %collective-permute-start = (f32[34,2048]{1,0:T(8,128)S(1)}, f32[34,2048]{1,0:T(8,128)S(1)}, u32[]{:S(2)}, u32[]{:S(2)}) collective-permute-start(f32[34,2048]{1,0:T(8,128)S(1)} %get-tuple-element.73), channel_id=1, source_target_pairs={{0,2},{1,3},{2,0},{3,1},{4,6},{5,7},{6,4},{7,5},{8,10},{9,11},{10,... | collective-permute-start | bytes 835592 | tf_op jit(solution)/shard_map/ppermute | solution.py:179
  31.9 8.4 %collective-permute-start.9 = (bf16[2,32,2048]{2,1,0:T(8,128)(2,1)S(1)}, bf16[2,32,2048]{2,1,0:T(8,128)(2,1)S(1)}, u32[]{:S(2)}, u32[]{:S(2)}) collective-permute-start(bf16[2,32,2048]{2,1,0:T(8,128)(2,1)S(1)} %fusion.1), channel_id=1, source_target_pairs={{0,2},{1,3},{2,0},{3,1},{4,6},{5,7},{6,4},{7,5},{8,10},{9,11},{10,... | collective-permute-start | bytes 786440 | tf_op jit(solution)/shard_map/ppermute | solution.py:179
  45.2 13.3 %collective-permute-start.13 = (bf16[1,32,2048]{2,1,0:T(8,128)(2,1)S(1)}, bf16[1,32,2048]{2,1,0:T(8,128)(2,1)S(1)}, u32[]{:S(2)}, u32[]{:S(2)}) collective-permute-start(bf16[1,32,2048]{2,1,0:T(8,128)(2,1)S(1)} %get-tuple-element.41), channel_id=1, source_target_pairs={{0,4},{4,0},{8,12},{12,8},{16,20},{20,16},{24,28},{28,24},{1,5},{5... | collective-permute-start | bytes 393224 | tf_op jit(solution)/shard_map/ppermute | solution.py:179
  45.7 14.8 %collective-permute-start.15 = (bf16[1,32,2048]{2,1,0:T(8,128)(2,1)S(1)}, bf16[1,32,2048]{2,1,0:T(8,128)(2,1)S(1)}, u32[]{:S(2)}, u32[]{:S(2)}) collective-permute-start(bf16[1,32,2048]{2,1,0:T(8,128)(2,1)S(1)} %get-tuple-element.42), channel_id=1, source_target_pairs={{0,4},{4,0},{8,12},{12,8},{16,20},{20,16},{24,28},{28,24},{1,5},{5... | collective-permute-start | bytes 393224 | tf_op jit(solution)/shard_map/ppermute | solution.py:179
  47.2 13.2 %collective-permute-start.16 = (bf16[1,32,2048]{2,1,0:T(8,128)(2,1)S(1)}, bf16[1,32,2048]{2,1,0:T(8,128)(2,1)S(1)}, u32[]{:S(2)}, u32[]{:S(2)}) collective-permute-start(bf16[1,32,2048]{2,1,0:T(8,128)(2,1)S(1)} %get-tuple-element.43), channel_id=1, source_target_pairs={{0,8},{4,12},{8,0},{12,4},{16,24},{20,28},{24,16},{28,20},{1,9},{5... | collective-permute-start | bytes 393224 | tf_op jit(solution)/shard_map/ppermute | solution.py:179
  48.6 11.9 %collective-permute-start.17 = (bf16[1,32,2048]{2,1,0:T(8,128)(2,1)S(1)}, bf16[1,32,2048]{2,1,0:T(8,128)(2,1)S(1)}, u32[]{:S(2)}, u32[]{:S(2)}) collective-permute-start(bf16[1,32,2048]{2,1,0:T(8,128)(2,1)S(1)} %get-tuple-element.44), channel_id=1, source_target_pairs={{0,12},{4,8},{8,4},{12,0},{16,28},{20,24},{24,20},{28,16},{1,13},{... | collective-permute-start | bytes 393224 | tf_op jit(solution)/shard_map/ppermute | solution.py:179
  50.0 13.6 %collective-permute-start.12 = (bf16[1,32,2048]{2,1,0:T(8,128)(2,1)S(1)}, bf16[1,32,2048]{2,1,0:T(8,128)(2,1)S(1)}, u32[]{:S(2)}, u32[]{:S(2)}) collective-permute-start(bf16[1,32,2048]{2,1,0:T(8,128)(2,1)S(1)} %add_convert_fusion.3), channel_id=1, source_target_pairs={{0,16},{4,20},{8,24},{12,28},{16,0},{20,4},{24,8},{28,12},{1,17},{... | collective-permute-start | bytes 393224 | tf_op jit(solution)/shard_map/ppermute | solution.py:179
  58.6 7.6 %collective-permute-start.14 = (bf16[1,32,2048]{2,1,0:T(8,128)(2,1)S(1)}, bf16[1,32,2048]{2,1,0:T(8,128)(2,1)S(1)}, u32[]{:S(2)}, u32[]{:S(2)}) collective-permute-start(bf16[1,32,2048]{2,1,0:T(8,128)(2,1)S(1)} %add_convert_fusion.2), channel_id=1, source_target_pairs={{0,24},{4,28},{8,16},{12,20},{16,8},{20,12},{24,0},{28,4},{1,25},{... | collective-permute-start | bytes 393224 | tf_op jit(solution)/shard_map/ppermute | solution.py:179
  70.7 8.7 %collective-permute-start.18 = (bf16[1,32,2048]{2,1,0:T(8,128)(2,1)S(1)}, bf16[1,32,2048]{2,1,0:T(8,128)(2,1)S(1)}, u32[]{:S(2)}, u32[]{:S(2)}) collective-permute-start(bf16[1,32,2048]{2,1,0:T(8,128)(2,1)S(1)} %get-tuple-element.46.refs_0_), channel_id=1, source_target_pairs={{0,16},{4,20},{8,24},{12,28},{16,0},{20,4},{24,8},{28,12},{1,17},{... | collective-permute-start | bytes 393224 | tf_op jit(solution)/shard_map/ppermute | solution.py:179
  71.7 7.6 %collective-permute-start.20 = (bf16[1,32,2048]{2,1,0:T(8,128)(2,1)S(1)}, bf16[1,32,2048]{2,1,0:T(8,128)(2,1)S(1)}, u32[]{:S(2)}, u32[]{:S(2)}) collective-permute-start(bf16[1,32,2048]{2,1,0:T(8,128)(2,1)S(1)} %get-tuple-element.46.refs_0_), channel_id=1, source_target_pairs={{0,24},{4,28},{8,16},{12,20},{16,8},{20,12},{24,0},{28,4},{1,25},{... | collective-permute-start | bytes 393224 | tf_op jit(solution)/shard_map/ppermute | solution.py:179
  73.1 8.3 %collective-permute-start.22 = (bf16[1,32,2048]{2,1,0:T(8,128)(2,1)S(1)}, bf16[1,32,2048]{2,1,0:T(8,128)(2,1)S(1)}, u32[]{:S(2)}, u32[]{:S(2)}) collective-permute-start(bf16[1,32,2048]{2,1,0:T(8,128)(2,1)S(1)} %get-tuple-element.46.refs_0_), channel_id=1, source_target_pairs={{0,4},{4,0},{8,12},{12,8},{16,20},{20,16},{24,28},{28,24},{1,5},{5... | collective-permute-start | bytes 393224 | tf_op jit(solution)/shard_map/ppermute | solution.py:179
  73.6 7.8 %collective-permute-start.24 = (bf16[1,32,2048]{2,1,0:T(8,128)(2,1)S(1)}, bf16[1,32,2048]{2,1,0:T(8,128)(2,1)S(1)}, u32[]{:S(2)}, u32[]{:S(2)}) collective-permute-start(bf16[1,32,2048]{2,1,0:T(8,128)(2,1)S(1)} %collective-permute-done.23.refs_2_), channel_id=1, source_target_pairs={{0,4},{4,0},{8,12},{12,8},{16,20},{20,16},{24,28},{28,24},{1,5},{5... | collective-permute-start | bytes 393224 | tf_op jit(solution)/shard_map/ppermute | solution.py:179
  88.7 8.4 %collective-permute-start.26 = (bf16[2,32,2048]{2,1,0:T(8,128)(2,1)S(1)}, bf16[2,32,2048]{2,1,0:T(8,128)(2,1)S(1)}, u32[]{:S(2)}, u32[]{:S(2)}) collective-permute-start(bf16[2,32,2048]{2,1,0:T(8,128)(2,1)S(1)} %fusion.2), channel_id=1, source_target_pairs={{0,2},{1,3},{2,0},{3,1},{4,6},{5,7},{6,4},{7,5},{8,10},{9,11},{10,... | collective-permute-start | bytes 786440 | tf_op jit(solution)/shard_map/ppermute | solution.py:179
  100.9 10.8 %collective-permute-start.30 = (bf16[1,32,2048]{2,1,0:T(8,128)(2,1)S(1)}, bf16[1,32,2048]{2,1,0:T(8,128)(2,1)S(1)}, u32[]{:S(2)}, u32[]{:S(2)}) collective-permute-start(bf16[1,32,2048]{2,1,0:T(8,128)(2,1)S(1)} %get-tuple-element.56), channel_id=1, source_target_pairs={{0,4},{4,0},{8,12},{12,8},{16,20},{20,16},{24,28},{28,24},{1,5},{5... | collective-permute-start | bytes 393224 | tf_op jit(solution)/shard_map/ppermute | solution.py:179
  102.5 12.4 %collective-permute-start.32 = (bf16[1,32,2048]{2,1,0:T(8,128)(2,1)S(1)}, bf16[1,32,2048]{2,1,0:T(8,128)(2,1)S(1)}, u32[]{:S(2)}, u32[]{:S(2)}) collective-permute-start(bf16[1,32,2048]{2,1,0:T(8,128)(2,1)S(1)} %get-tuple-element.57), channel_id=1, source_target_pairs={{0,4},{4,0},{8,12},{12,8},{16,20},{20,16},{24,28},{28,24},{1,5},{5... | collective-permute-start | bytes 393224 | tf_op jit(solution)/shard_map/ppermute | solution.py:179
  102.9 12.0 %collective-permute-start.33 = (bf16[1,32,2048]{2,1,0:T(8,128)(2,1)S(1)}, bf16[1,32,2048]{2,1,0:T(8,128)(2,1)S(1)}, u32[]{:S(2)}, u32[]{:S(2)}) collective-permute-start(bf16[1,32,2048]{2,1,0:T(8,128)(2,1)S(1)} %get-tuple-element.58), channel_id=1, source_target_pairs={{0,8},{4,12},{8,0},{12,4},{16,24},{20,28},{24,16},{28,20},{1,9},{5... | collective-permute-start | bytes 393224 | tf_op jit(solution)/shard_map/ppermute | solution.py:179
  102.9 12.0 %collective-permute-start.34 = (bf16[1,32,2048]{2,1,0:T(8,128)(2,1)S(1)}, bf16[1,32,2048]{2,1,0:T(8,128)(2,1)S(1)}, u32[]{:S(2)}, u32[]{:S(2)}) collective-permute-start(bf16[1,32,2048]{2,1,0:T(8,128)(2,1)S(1)} %get-tuple-element.59), channel_id=1, source_target_pairs={{0,12},{4,8},{8,4},{12,0},{16,28},{20,24},{24,20},{28,16},{1,13},{... | collective-permute-start | bytes 393224 | tf_op jit(solution)/shard_map/ppermute | solution.py:179
  106.9 12.3 %collective-permute-start.29 = (bf16[1,32,2048]{2,1,0:T(8,128)(2,1)S(1)}, bf16[1,32,2048]{2,1,0:T(8,128)(2,1)S(1)}, u32[]{:S(2)}, u32[]{:S(2)}) collective-permute-start(bf16[1,32,2048]{2,1,0:T(8,128)(2,1)S(1)} %add_convert_fusion.1), channel_id=1, source_target_pairs={{0,16},{4,20},{8,24},{12,28},{16,0},{20,4},{24,8},{28,12},{1,17},{... | collective-permute-start | bytes 393224 | tf_op jit(solution)/shard_map/ppermute | solution.py:179
  (17 other events, 124.7 us)

commit v8 on v7

--- a/solution.py
+++ b/solution.py
@@ -179,12 +179,16 @@
     return lax.ppermute(value, axis, [(i, i ^ k) for i in range(size)])
 
 
+def strides(size):
+    return sorted(range(2, size, 2), key=lambda k: (k % 4 == 0, -k))
+
+
 def gather_pairs(own, axis, size):
     parts = [None] * size
     parts[0] = own
-    for k in range(size - 2, 0, -2):
+    for k in strides(size):
         parts[k] = swap(own, axis, size, k)
-    for k in range(size - 2, -1, -2):
+    for k in [0] + strides(size):
         parts[k + 1] = swap(parts[k], axis, size, 1)
     return parts
 
@@ -227,13 +231,11 @@
 
 
 def share_pairs(kept, sent, axis, size):
-    shares = {}
-    for k in range(4, size, 2):
+    shares = []
+    for k in strides(size)[::-1]:
         pair = kept[k] + swap(sent[k + 1], axis, size, 1).astype(jnp.float32)
-        shares[k] = swap(pair.astype(jnp.bfloat16), axis, size, k)
-    for k in range(1, min(size, 4)):
-        shares[k] = swap(sent[k], axis, size, k)
-    return list(shares.values())
+        shares.append(swap(pair.astype(jnp.bfloat16), axis, size, k))
+    return shares + [swap(sent[1], axis, size, 1)]
 
 
 def sum_halves(kept, sent, axis, size):
@@ -281,46 +283,33 @@
     share = weights[:, None]
     cost = share * states[:, width : width + 1] + (1.0 - share) * states[:, width + 1 :]
     whole, rounded = jnp.float32, jnp.bfloat16
-    late = [k for k in range(5, cols, 2)]
-    early = [k for k in range(cols) if k not in late]
+    order = [k for pair in strides(cols)[::-1] + [0] for k in (pair + 1, pair)]
     mine, other = (tuple(range(p, rows, 2)) for p in (0, 1))
-    keep = tuple(k for k in range(cols) if k % 2 == 0 and k != 2)
-    send = tuple(k for k in range(cols) if k not in keep)
+    keep, send = (tuple(range(p, cols, 2)) for p in (0, 1))
     for step in range(ITERS):
         dual_parts = gather_pairs(rounded_dual[0], "col", cols)
-        begun = sweep(
-            Plan(
-                False, step == 0, tuple((k,) for k in early),
-                (Out(mine, whole, True), Out(other, whole, True)), False,
-            ),
-            blocks, info, [dual_parts[k] for k in early], [], primal.shape[2],
-        )
-        kept, sent = sweep(
-            Plan(
-                False, False, tuple((k,) for k in late),
-                (Out(mine, whole, True), Out(other, rounded, True)), True,
-            ),
-            blocks, info, [dual_parts[k] for k in late], begun, primal.shape[2],
-        )
+        sent, kept = [
+            sweep(
+                Plan(
+                    False, step == 0, tuple((k,) for k in order),
+                    (Out(other, rounded, True) if sending else Out(mine, whole, True),), False,
+                ),
+                blocks, info, [dual_parts[k] for k in order], [], primal.shape[2],
+            )[0]
+            for sending in (True, False)
+        ]
         pull = sum_halves(kept, sent, "row", rows)
         fresh = jnp.maximum(primal - step_primal * (cost - pull), 0.0)
         extra = (2.0 * fresh - primal).astype(jnp.bfloat16)
         primal = fresh
-        kept, sent = sweep(
-            Plan(
-                True, False, (mine,),
-                (Out(keep, whole, True), Out(send, whole, True)), False,
-            ),
-            blocks, info_back, [extra], [], dual.shape[1],
-        )
-        extra = swap(extra, "row", rows, 1)
+        extra = [extra, swap(extra, "row", rows, 1)]
         (sent,) = sweep(
-            Plan(True, False, (other,), (Out(send, rounded, False),), True),
-            blocks, info_back, [extra], [sent], dual.shape[1],
+            Plan(True, False, (mine, other), (Out(send, rounded, False),), False),
+            blocks, info_back, extra, [], dual.shape[1],
         )
         (kept,) = sweep(
-            Plan(True, False, (other,), (Out(keep, whole, False),), True),
-            blocks, info_back, [extra], [kept], dual.shape[1],
+            Plan(True, False, (mine, other), (Out(keep, whole, False),), False),
+            blocks, info_back, extra, [], dual.shape[1],
         )
         shares = share_pairs(kept, sent, "col", cols)
         dual, *rounded_dual = update_dual(

time: 120 us -> 117 us (0.975); the launches traced: 120 us -> 114 us
  starting transfers between devices: 53.7 us -> 50.4 us
  Pallas kernels: 14.3 us -> 11.2 us
  waiting for transfers between devices: 44.2 us -> 45.5 us
    ppermute x35, starting transfers between devices: 53.7 us -> 50.4 us  [swap(): return lax.ppermute(value, axis, [(i, i ^ k) for i in range(size)])]
    pallas_call x10 -> x8, Pallas kernels: 13.2 us -> 10.2 us  [sweep(): pl.pallas_call(functools.partial(sweep_kernel, plan, parts[0].shape[2] //...]
    ppermute x35, waiting for transfers between devices: 44.2 us -> 45.5 us  [swap(): return lax.ppermute(value, axis, [(i, i ^ k) for i in range(size)])]
  transfers between devices with their start and end apart: 35 -> 35, of which waited for: 16 -> 20; matrix products, arithmetic and copies ran while one was open for 3% -> 4% of each run, Pallas kernels for 9% -> 6%
where the time goes in v8:
time: 117 us; the launch traced here: 114 us
  starting transfers between devices  50.4 us (43%)
  waiting for transfers between devices  45.5 us (39%)
  Pallas kernels  11.2 us (10%)
  local copies, waits for them, and re-layouts  4.07 us (3%)
  other arithmetic  1.73 us (1%)
  between operations  1.6 us (1%)
    ppermute x35, starting transfers between devices, swap(): return lax.ppermute(value, axis, [(i, i ^ k) for i in range(size)])  50.4 us
    ppermute x35, waiting for transfers between devices, swap(): return lax.ppermute(value, axis, [(i, i ^ k) for i in range(size)])  45.5 us
    pallas_call x8, Pallas kernels, sweep(): pl.pallas_call(functools.partial(sweep_kernel, plan, parts[0].shape[2] //...  10.2 us
    unnamed x18, local copies, waits for them, and re-layouts  3.93 us
  transfers between devices with their start and end apart: 35, of which 20 were waited for; matrix products, arithmetic and copies ran while one was open for 4% of the time, Pallas kernels for 6%

profile of v8, /device:TPU:0, one launch (start us, length us, event | category | flops | bytes accessed | tf_op | source)
XLA Modules:
  0.0 114.5 jit_solution(14716697301216772505)
XLA Ops:
  1.7 4.1 %collective-permute-start.1 = (bf16[1,32,2048]{2,1,0:T(8,128)(2,1)S(1)}, bf16[1,32,2048]{2,1,0:T(8,128)(2,1)S(1)}, u32[]{:S(2)}, u32[]{:S(2)}) collective-permute-start(bf16[1,32,2048]{2,1,0:T(8,128)(2,1)S(1)} %bitcast.35), channel_id=1, source_target_pairs={{0,16},{4,20},{8,24},{12,28},{16,0},{20,4},{24,8},{28,12},{1,17},{... | collective-permute-start | bytes 393224 | tf_op jit(solution)/shard_map/ppermute | solution.py:179
  5.8 1.6 %collective-permute-start.3 = (bf16[1,32,2048]{2,1,0:T(8,128)(2,1)S(1)}, bf16[1,32,2048]{2,1,0:T(8,128)(2,1)S(1)}, u32[]{:S(2)}, u32[]{:S(2)}) collective-permute-start(bf16[1,32,2048]{2,1,0:T(8,128)(2,1)S(1)} %bitcast.36), channel_id=1, source_target_pairs={{0,8},{4,12},{8,0},{12,4},{16,24},{20,28},{24,16},{28,20},{1,9},{5... | collective-permute-start | bytes 393224 | tf_op jit(solution)/shard_map/ppermute | solution.py:179
  7.4 1.7 %collective-permute-start.7 = (bf16[1,32,2048]{2,1,0:T(8,128)(2,1)S(1)}, bf16[1,32,2048]{2,1,0:T(8,128)(2,1)S(1)}, u32[]{:S(2)}, u32[]{:S(2)}) collective-permute-start(bf16[1,32,2048]{2,1,0:T(8,128)(2,1)S(1)} %bitcast.38), channel_id=1, source_target_pairs={{0,4},{4,0},{8,12},{12,8},{16,20},{20,16},{24,28},{28,24},{1,5},{5... | collective-permute-start | bytes 393224 | tf_op jit(solution)/shard_map/ppermute | solution.py:179
  10.1 3.6 %collective-permute-done.1.refs_1_ = bf16[1,32,2048]{2,1,0:T(8,128)(2,1)S(1)} collective-permute-done((bf16[1,32,2048]{2,1,0:T(8,128)(2,1)S(1)}, bf16[1,32,2048]{2,1,0:T(8,128)(2,1)S(1)}, u32[]{:S(2)}, u32[]{:S(2)}) %collective-permute-start.1) | collective-permute-done | bytes 131104 | tf_op jit(solution)/shard_map/ppermute | solution.py:179
  13.7 2.1 %collective-permute-start.2 = (bf16[1,32,2048]{2,1,0:T(8,128)(2,1)S(1)}, bf16[1,32,2048]{2,1,0:T(8,128)(2,1)S(1)}, u32[]{:S(2)}, u32[]{:S(2)}) collective-permute-start(bf16[1,32,2048]{2,1,0:T(8,128)(2,1)S(1)} %collective-permute-done.1.refs_1_), channel_id=1, source_target_pairs={{0,4},{4,0},{8,12},{12,8},{16,20},{20,16},{24,28},{28,24},{1,5},{5... | collective-permute-start | bytes 393224 | tf_op jit(solution)/shard_map/ppermute | solution.py:179
  16.1 1.8 %collective-permute-start.6 = (bf16[1,32,2048]{2,1,0:T(8,128)(2,1)S(1)}, bf16[1,32,2048]{2,1,0:T(8,128)(2,1)S(1)}, u32[]{:S(2)}, u32[]{:S(2)}) collective-permute-start(bf16[1,32,2048]{2,1,0:T(8,128)(2,1)S(1)} %collective-permute-done.5.refs_5_), channel_id=1, source_target_pairs={{0,4},{4,0},{8,12},{12,8},{16,20},{20,16},{24,28},{28,24},{1,5},{5... | collective-permute-start | bytes 393224 | tf_op jit(solution)/shard_map/ppermute | solution.py:179
  18.7 1.6 %collective-permute-start = (f32[34,2048]{1,0:T(8,128)S(1)}, f32[34,2048]{1,0:T(8,128)S(1)}, u32[]{:S(2)}, u32[]{:S(2)}) collective-permute-start(f32[34,2048]{1,0:T(8,128)S(1)} %get-tuple-element.49), channel_id=1, source_target_pairs={{0,2},{1,3},{2,0},{3,1},{4,6},{5,7},{6,4},{7,5},{8,10},{9,11},{10,... | collective-permute-start | bytes 835592 | tf_op jit(solution)/shard_map/ppermute | solution.py:179
  23.0 2.8 %transpose_sweep.5 = bf16[2,32,2048]{2,1,0:T(8,128)(2,1)S(1)} custom-call(s32[19]{0:T(128)S(1)} %get-tuple-element.55.info, bf16[8,1024,512]{2,1,0:T(8,128)(2,1)} %bitcast.25, bf16[1,32,2048]{2,1,0:T(8,128)(2,1)S(1)} %collective-permute-done.2.refs_0_, bf16[1,32,2048]{2,1,0:T(8,128)(2,1)S(1)} %collective-permute-done.1.refs_1_, ...), custom_call_target="tpu_custom_call" | custom-call | flops 134217728 | bytes 4194304 | tf_op jit(solution)/shard_map/transpose_sweep/pallas_call | solution.py:152
  27.5 2.9 %collective-permute-start.9 = (bf16[2,32,2048]{2,1,0:T(8,128)(2,1)S(1)}, bf16[2,32,2048]{2,1,0:T(8,128)(2,1)S(1)}, u32[]{:S(2)}, u32[]{:S(2)}) collective-permute-start(bf16[2,32,2048]{2,1,0:T(8,128)(2,1)S(1)} %fusion.1), channel_id=1, source_target_pairs={{0,2},{1,3},{2,0},{3,1},{4,6},{5,7},{6,4},{7,5},{8,10},{9,11},{10,... | collective-permute-start | bytes 786440 | tf_op jit(solution)/shard_map/ppermute | solution.py:179
  30.4 6.9 %collective-permute-done.9 = bf16[2,32,2048]{2,1,0:T(8,128)(2,1)S(1)} collective-permute-done((bf16[2,32,2048]{2,1,0:T(8,128)(2,1)S(1)}, bf16[2,32,2048]{2,1,0:T(8,128)(2,1)S(1)}, u32[]{:S(2)}, u32[]{:S(2)}) %collective-permute-start.9) | collective-permute-done | bytes 262176 | tf_op jit(solution)/shard_map/ppermute | solution.py:179
  46.8 1.7 %collective-permute-start.12 = (bf16[1,32,2048]{2,1,0:T(8,128)(2,1)S(1)}, bf16[1,32,2048]{2,1,0:T(8,128)(2,1)S(1)}, u32[]{:S(2)}, u32[]{:S(2)}) collective-permute-start(bf16[1,32,2048]{2,1,0:T(8,128)(2,1)S(1)} %add_convert_fusion.5), channel_id=1, source_target_pairs={{0,16},{4,20},{8,24},{12,28},{16,0},{20,4},{24,8},{28,12},{1,17},{... | collective-permute-start | bytes 393224 | tf_op jit(solution)/shard_map/ppermute | solution.py:179
  49.6 3.5 %collective-permute-start.14 = (bf16[1,32,2048]{2,1,0:T(8,128)(2,1)S(1)}, bf16[1,32,2048]{2,1,0:T(8,128)(2,1)S(1)}, u32[]{:S(2)}, u32[]{:S(2)}) collective-permute-start(bf16[1,32,2048]{2,1,0:T(8,128)(2,1)S(1)} %add_convert_fusion.4), channel_id=1, source_target_pairs={{0,8},{4,12},{8,0},{12,4},{16,24},{20,28},{24,16},{28,20},{1,9},{5... | collective-permute-start | bytes 393224 | tf_op jit(solution)/shard_map/ppermute | solution.py:179
  53.2 4.6 %collective-permute-start.16 = (bf16[1,32,2048]{2,1,0:T(8,128)(2,1)S(1)}, bf16[1,32,2048]{2,1,0:T(8,128)(2,1)S(1)}, u32[]{:S(2)}, u32[]{:S(2)}) collective-permute-start(bf16[1,32,2048]{2,1,0:T(8,128)(2,1)S(1)} %add_convert_fusion.3), channel_id=1, source_target_pairs={{0,24},{4,28},{8,16},{12,20},{16,8},{20,12},{24,0},{28,4},{1,25},{... | collective-permute-start | bytes 393224 | tf_op jit(solution)/shard_map/ppermute | solution.py:179
  57.9 2.9 %collective-permute-done.16.refs_2_ = bf16[1,32,2048]{2,1,0:T(8,128)(2,1)S(1)} collective-permute-done((bf16[1,32,2048]{2,1,0:T(8,128)(2,1)S(1)}, bf16[1,32,2048]{2,1,0:T(8,128)(2,1)S(1)}, u32[]{:S(2)}, u32[]{:S(2)}) %collective-permute-start.16) | collective-permute-done | bytes 131104 | tf_op jit(solution)/shard_map/ppermute | solution.py:179
  61.9 4.0 %collective-permute-start.20 = (bf16[1,32,2048]{2,1,0:T(8,128)(2,1)S(1)}, bf16[1,32,2048]{2,1,0:T(8,128)(2,1)S(1)}, u32[]{:S(2)}, u32[]{:S(2)}) collective-permute-start(bf16[1,32,2048]{2,1,0:T(8,128)(2,1)S(1)} %get-tuple-element.28.refs_7_), channel_id=1, source_target_pairs={{0,8},{4,12},{8,0},{12,4},{16,24},{20,28},{24,16},{28,20},{1,9},{5... | collective-permute-start | bytes 393224 | tf_op jit(solution)/shard_map/ppermute | solution.py:179
  66.8 3.4 %collective-permute-done.18.refs_1_ = bf16[1,32,2048]{2,1,0:T(8,128)(2,1)S(1)} collective-permute-done((bf16[1,32,2048]{2,1,0:T(8,128)(2,1)S(1)}, bf16[1,32,2048]{2,1,0:T(8,128)(2,1)S(1)}, u32[]{:S(2)}, u32[]{:S(2)}) %collective-permute-start.18) | collective-permute-done | bytes 131104 | tf_op jit(solution)/shard_map/ppermute | solution.py:179
  70.3 3.5 %collective-permute-start.19 = (bf16[1,32,2048]{2,1,0:T(8,128)(2,1)S(1)}, bf16[1,32,2048]{2,1,0:T(8,128)(2,1)S(1)}, u32[]{:S(2)}, u32[]{:S(2)}) collective-permute-start(bf16[1,32,2048]{2,1,0:T(8,128)(2,1)S(1)} %collective-permute-done.18.refs_1_), channel_id=1, source_target_pairs={{0,4},{4,0},{8,12},{12,8},{16,20},{20,16},{24,28},{28,24},{1,5},{5... | collective-permute-start | bytes 393224 | tf_op jit(solution)/shard_map/ppermute | solution.py:179
  73.8 2.0 %collective-permute-start.23 = (bf16[1,32,2048]{2,1,0:T(8,128)(2,1)S(1)}, bf16[1,32,2048]{2,1,0:T(8,128)(2,1)S(1)}, u32[]{:S(2)}, u32[]{:S(2)}) collective-permute-start(bf16[1,32,2048]{2,1,0:T(8,128)(2,1)S(1)} %collective-permute-done.22.refs_5_), channel_id=1, source_target_pairs={{0,4},{4,0},{8,12},{12,8},{16,20},{20,16},{24,28},{28,24},{1,5},{5... | collective-permute-start | bytes 393224 | tf_op jit(solution)/shard_map/ppermute | solution.py:179
  76.7 2.0 %collective-permute-done.21.refs_2_ = bf16[1,32,2048]{2,1,0:T(8,128)(2,1)S(1)} collective-permute-done((bf16[1,32,2048]{2,1,0:T(8,128)(2,1)S(1)}, bf16[1,32,2048]{2,1,0:T(8,128)(2,1)S(1)}, u32[]{:S(2)}, u32[]{:S(2)}) %collective-permute-start.21) | collective-permute-done | bytes 131104 | tf_op jit(solution)/shard_map/ppermute | solution.py:179
  84.7 6.8 %collective-permute-done.26 = bf16[2,32,2048]{2,1,0:T(8,128)(2,1)S(1)} collective-permute-done((bf16[2,32,2048]{2,1,0:T(8,128)(2,1)S(1)}, bf16[2,32,2048]{2,1,0:T(8,128)(2,1)S(1)}, u32[]{:S(2)}, u32[]{:S(2)}) %collective-permute-start.26) | collective-permute-done | bytes 262176 | tf_op jit(solution)/shard_map/ppermute | solution.py:179
  101.1 2.7 %collective-permute-done.30 = bf16[1,32,2048]{2,1,0:T(8,128)(2,1)S(1)} collective-permute-done((bf16[1,32,2048]{2,1,0:T(8,128)(2,1)S(1)}, bf16[1,32,2048]{2,1,0:T(8,128)(2,1)S(1)}, u32[]{:S(2)}, u32[]{:S(2)}) %collective-permute-start.30) | collective-permute-done | bytes 131104 | tf_op jit(solution)/shard_map/ppermute | solution.py:179
  104.6 2.0 %collective-permute-done.32 = bf16[1,32,2048]{2,1,0:T(8,128)(2,1)S(1)} collective-permute-done((bf16[1,32,2048]{2,1,0:T(8,128)(2,1)S(1)}, bf16[1,32,2048]{2,1,0:T(8,128)(2,1)S(1)}, u32[]{:S(2)}, u32[]{:S(2)}) %collective-permute-start.32) | collective-permute-done | bytes 131104 | tf_op jit(solution)/shard_map/ppermute | solution.py:179
  106.7 2.5 %collective-permute-start.33 = (bf16[1,32,2048]{2,1,0:T(8,128)(2,1)S(1)}, bf16[1,32,2048]{2,1,0:T(8,128)(2,1)S(1)}, u32[]{:S(2)}, u32[]{:S(2)}) collective-permute-start(bf16[1,32,2048]{2,1,0:T(8,128)(2,1)S(1)} %add_convert_fusion), channel_id=1, source_target_pairs={{0,24},{4,28},{8,16},{12,20},{16,8},{20,12},{24,0},{28,4},{1,25},{... | collective-permute-start | bytes 393224 | tf_op jit(solution)/shard_map/ppermute | solution.py:179
  110.1 3.5 %collective-permute-done.33.refs_2_ = bf16[1,32,2048]{2,1,0:T(8,128)(2,1)S(1)} collective-permute-done((bf16[1,32,2048]{2,1,0:T(8,128)(2,1)S(1)}, bf16[1,32,2048]{2,1,0:T(8,128)(2,1)S(1)}, u32[]{:S(2)}, u32[]{:S(2)}) %collective-permute-start.33) | collective-permute-done | bytes 131104 | tf_op jit(solution)/shard_map/ppermute | solution.py:179
  (93 shorter events, 38.6 us)
Async XLA Ops:
  1.7 12.1 %collective-permute-start.1 = (bf16[1,32,2048]{2,1,0:T(8,128)(2,1)S(1)}, bf16[1,32,2048]{2,1,0:T(8,128)(2,1)S(1)}, u32[]{:S(2)}, u32[]{:S(2)}) collective-permute-start(bf16[1,32,2048]{2,1,0:T(8,128)(2,1)S(1)} %bitcast.35), channel_id=1, source_target_pairs={{0,16},{4,20},{8,24},{12,28},{16,0},{20,4},{24,8},{28,12},{1,17},{... | collective-permute-start | bytes 393224 | tf_op jit(solution)/shard_map/ppermute | solution.py:179
  5.8 10.1 %collective-permute-start.3 = (bf16[1,32,2048]{2,1,0:T(8,128)(2,1)S(1)}, bf16[1,32,2048]{2,1,0:T(8,128)(2,1)S(1)}, u32[]{:S(2)}, u32[]{:S(2)}) collective-permute-start(bf16[1,32,2048]{2,1,0:T(8,128)(2,1)S(1)} %bitcast.36), channel_id=1, source_target_pairs={{0,8},{4,12},{8,0},{12,4},{16,24},{20,28},{24,16},{28,20},{1,9},{5... | collective-permute-start | bytes 393224 | tf_op jit(solution)/shard_map/ppermute | solution.py:179
  7.4 8.8 %collective-permute-start.5 = (bf16[1,32,2048]{2,1,0:T(8,128)(2,1)S(1)}, bf16[1,32,2048]{2,1,0:T(8,128)(2,1)S(1)}, u32[]{:S(2)}, u32[]{:S(2)}) collective-permute-start(bf16[1,32,2048]{2,1,0:T(8,128)(2,1)S(1)} %bitcast.37), channel_id=1, source_target_pairs={{0,24},{4,28},{8,16},{12,20},{16,8},{20,12},{24,0},{28,4},{1,25},{... | collective-permute-start | bytes 393224 | tf_op jit(solution)/shard_map/ppermute | solution.py:179
  7.4 14.5 %collective-permute-start.7 = (bf16[1,32,2048]{2,1,0:T(8,128)(2,1)S(1)}, bf16[1,32,2048]{2,1,0:T(8,128)(2,1)S(1)}, u32[]{:S(2)}, u32[]{:S(2)}) collective-permute-start(bf16[1,32,2048]{2,1,0:T(8,128)(2,1)S(1)} %bitcast.38), channel_id=1, source_target_pairs={{0,4},{4,0},{8,12},{12,8},{16,20},{20,16},{24,28},{28,24},{1,5},{5... | collective-permute-start | bytes 393224 | tf_op jit(solution)/shard_map/ppermute | solution.py:179
  13.7 8.1 %collective-permute-start.2 = (bf16[1,32,2048]{2,1,0:T(8,128)(2,1)S(1)}, bf16[1,32,2048]{2,1,0:T(8,128)(2,1)S(1)}, u32[]{:S(2)}, u32[]{:S(2)}) collective-permute-start(bf16[1,32,2048]{2,1,0:T(8,128)(2,1)S(1)} %collective-permute-done.1.refs_1_), channel_id=1, source_target_pairs={{0,4},{4,0},{8,12},{12,8},{16,20},{20,16},{24,28},{28,24},{1,5},{5... | collective-permute-start | bytes 393224 | tf_op jit(solution)/shard_map/ppermute | solution.py:179
  16.1 6.9 %collective-permute-start.6 = (bf16[1,32,2048]{2,1,0:T(8,128)(2,1)S(1)}, bf16[1,32,2048]{2,1,0:T(8,128)(2,1)S(1)}, u32[]{:S(2)}, u32[]{:S(2)}) collective-permute-start(bf16[1,32,2048]{2,1,0:T(8,128)(2,1)S(1)} %collective-permute-done.5.refs_5_), channel_id=1, source_target_pairs={{0,4},{4,0},{8,12},{12,8},{16,20},{20,16},{24,28},{28,24},{1,5},{5... | collective-permute-start | bytes 393224 | tf_op jit(solution)/shard_map/ppermute | solution.py:179
  18.7 8.1 %collective-permute-start = (f32[34,2048]{1,0:T(8,128)S(1)}, f32[34,2048]{1,0:T(8,128)S(1)}, u32[]{:S(2)}, u32[]{:S(2)}) collective-permute-start(f32[34,2048]{1,0:T(8,128)S(1)} %get-tuple-element.49), channel_id=1, source_target_pairs={{0,2},{1,3},{2,0},{3,1},{4,6},{5,7},{6,4},{7,5},{8,10},{9,11},{10,... | collective-permute-start | bytes 835592 | tf_op jit(solution)/shard_map/ppermute | solution.py:179
  27.5 9.8 %collective-permute-start.9 = (bf16[2,32,2048]{2,1,0:T(8,128)(2,1)S(1)}, bf16[2,32,2048]{2,1,0:T(8,128)(2,1)S(1)}, u32[]{:S(2)}, u32[]{:S(2)}) collective-permute-start(bf16[2,32,2048]{2,1,0:T(8,128)(2,1)S(1)} %fusion.1), channel_id=1, source_target_pairs={{0,2},{1,3},{2,0},{3,1},{4,6},{5,7},{6,4},{7,5},{8,10},{9,11},{10,... | collective-permute-start | bytes 786440 | tf_op jit(solution)/shard_map/ppermute | solution.py:179
  41.7 7.9 %collective-permute-start.13 = (bf16[1,32,2048]{2,1,0:T(8,128)(2,1)S(1)}, bf16[1,32,2048]{2,1,0:T(8,128)(2,1)S(1)}, u32[]{:S(2)}, u32[]{:S(2)}) collective-permute-start(bf16[1,32,2048]{2,1,0:T(8,128)(2,1)S(1)} %get-tuple-element.23), channel_id=1, source_target_pairs={{0,4},{4,0},{8,12},{12,8},{16,20},{20,16},{24,28},{28,24},{1,5},{5... | collective-permute-start | bytes 393224 | tf_op jit(solution)/shard_map/ppermute | solution.py:179
  42.5 10.7 %collective-permute-start.15 = (bf16[1,32,2048]{2,1,0:T(8,128)(2,1)S(1)}, bf16[1,32,2048]{2,1,0:T(8,128)(2,1)S(1)}, u32[]{:S(2)}, u32[]{:S(2)}) collective-permute-start(bf16[1,32,2048]{2,1,0:T(8,128)(2,1)S(1)} %get-tuple-element.25), channel_id=1, source_target_pairs={{0,4},{4,0},{8,12},{12,8},{16,20},{20,16},{24,28},{28,24},{1,5},{5... | collective-permute-start | bytes 393224 | tf_op jit(solution)/shard_map/ppermute | solution.py:179
  43.8 14.1 %collective-permute-start.17 = (bf16[1,32,2048]{2,1,0:T(8,128)(2,1)S(1)}, bf16[1,32,2048]{2,1,0:T(8,128)(2,1)S(1)}, u32[]{:S(2)}, u32[]{:S(2)}) collective-permute-start(bf16[1,32,2048]{2,1,0:T(8,128)(2,1)S(1)} %get-tuple-element.26), channel_id=1, source_target_pairs={{0,4},{4,0},{8,12},{12,8},{16,20},{20,16},{24,28},{28,24},{1,5},{5... | collective-permute-start | bytes 393224 | tf_op jit(solution)/shard_map/ppermute | solution.py:179
  46.8 11.1 %collective-permute-start.12 = (bf16[1,32,2048]{2,1,0:T(8,128)(2,1)S(1)}, bf16[1,32,2048]{2,1,0:T(8,128)(2,1)S(1)}, u32[]{:S(2)}, u32[]{:S(2)}) collective-permute-start(bf16[1,32,2048]{2,1,0:T(8,128)(2,1)S(1)} %add_convert_fusion.5), channel_id=1, source_target_pairs={{0,16},{4,20},{8,24},{12,28},{16,0},{20,4},{24,8},{28,12},{1,17},{... | collective-permute-start | bytes 393224 | tf_op jit(solution)/shard_map/ppermute | solution.py:179
  49.6 8.3 %collective-permute-start.14 = (bf16[1,32,2048]{2,1,0:T(8,128)(2,1)S(1)}, bf16[1,32,2048]{2,1,0:T(8,128)(2,1)S(1)}, u32[]{:S(2)}, u32[]{:S(2)}) collective-permute-start(bf16[1,32,2048]{2,1,0:T(8,128)(2,1)S(1)} %add_convert_fusion.4), channel_id=1, source_target_pairs={{0,8},{4,12},{8,0},{12,4},{16,24},{20,28},{24,16},{28,20},{1,9},{5... | collective-permute-start | bytes 393224 | tf_op jit(solution)/shard_map/ppermute | solution.py:179
  53.2 7.7 %collective-permute-start.16 = (bf16[1,32,2048]{2,1,0:T(8,128)(2,1)S(1)}, bf16[1,32,2048]{2,1,0:T(8,128)(2,1)S(1)}, u32[]{:S(2)}, u32[]{:S(2)}) collective-permute-start(bf16[1,32,2048]{2,1,0:T(8,128)(2,1)S(1)} %add_convert_fusion.3), channel_id=1, source_target_pairs={{0,24},{4,28},{8,16},{12,20},{16,8},{20,12},{24,0},{28,4},{1,25},{... | collective-permute-start | bytes 393224 | tf_op jit(solution)/shard_map/ppermute | solution.py:179
  61.0 9.3 %collective-permute-start.18 = (bf16[1,32,2048]{2,1,0:T(8,128)(2,1)S(1)}, bf16[1,32,2048]{2,1,0:T(8,128)(2,1)S(1)}, u32[]{:S(2)}, u32[]{:S(2)}) collective-permute-start(bf16[1,32,2048]{2,1,0:T(8,128)(2,1)S(1)} %get-tuple-element.28.refs_7_), channel_id=1, source_target_pairs={{0,16},{4,20},{8,24},{12,28},{16,0},{20,4},{24,8},{28,12},{1,17},{... | collective-permute-start | bytes 393224 | tf_op jit(solution)/shard_map/ppermute | solution.py:179
  61.9 11.8 %collective-permute-start.20 = (bf16[1,32,2048]{2,1,0:T(8,128)(2,1)S(1)}, bf16[1,32,2048]{2,1,0:T(8,128)(2,1)S(1)}, u32[]{:S(2)}, u32[]{:S(2)}) collective-permute-start(bf16[1,32,2048]{2,1,0:T(8,128)(2,1)S(1)} %get-tuple-element.28.refs_7_), channel_id=1, source_target_pairs={{0,8},{4,12},{8,0},{12,4},{16,24},{20,28},{24,16},{28,20},{1,9},{5... | collective-permute-start | bytes 393224 | tf_op jit(solution)/shard_map/ppermute | solution.py:179
  65.9 7.8 %collective-permute-start.22 = (bf16[1,32,2048]{2,1,0:T(8,128)(2,1)S(1)}, bf16[1,32,2048]{2,1,0:T(8,128)(2,1)S(1)}, u32[]{:S(2)}, u32[]{:S(2)}) collective-permute-start(bf16[1,32,2048]{2,1,0:T(8,128)(2,1)S(1)} %get-tuple-element.28.refs_7_), channel_id=1, source_target_pairs={{0,24},{4,28},{8,16},{12,20},{16,8},{20,12},{24,0},{28,4},{1,25},{... | collective-permute-start | bytes 393224 | tf_op jit(solution)/shard_map/ppermute | solution.py:179
  65.9 9.8 %collective-permute-start.24 = (bf16[1,32,2048]{2,1,0:T(8,128)(2,1)S(1)}, bf16[1,32,2048]{2,1,0:T(8,128)(2,1)S(1)}, u32[]{:S(2)}, u32[]{:S(2)}) collective-permute-start(bf16[1,32,2048]{2,1,0:T(8,128)(2,1)S(1)} %get-tuple-element.28.refs_7_), channel_id=1, source_target_pairs={{0,4},{4,0},{8,12},{12,8},{16,20},{20,16},{24,28},{28,24},{1,5},{5... | collective-permute-start | bytes 393224 | tf_op jit(solution)/shard_map/ppermute | solution.py:179
  83.1 8.4 %collective-permute-start.26 = (bf16[2,32,2048]{2,1,0:T(8,128)(2,1)S(1)}, bf16[2,32,2048]{2,1,0:T(8,128)(2,1)S(1)}, u32[]{:S(2)}, u32[]{:S(2)}) collective-permute-start(bf16[2,32,2048]{2,1,0:T(8,128)(2,1)S(1)} %fusion.2), channel_id=1, source_target_pairs={{0,2},{1,3},{2,0},{3,1},{4,6},{5,7},{6,4},{7,5},{8,10},{9,11},{10,... | collective-permute-start | bytes 786440 | tf_op jit(solution)/shard_map/ppermute | solution.py:179
  95.5 8.3 %collective-permute-start.30 = (bf16[1,32,2048]{2,1,0:T(8,128)(2,1)S(1)}, bf16[1,32,2048]{2,1,0:T(8,128)(2,1)S(1)}, u32[]{:S(2)}, u32[]{:S(2)}) collective-permute-start(bf16[1,32,2048]{2,1,0:T(8,128)(2,1)S(1)} %get-tuple-element.32), channel_id=1, source_target_pairs={{0,4},{4,0},{8,12},{12,8},{16,20},{20,16},{24,28},{28,24},{1,5},{5... | collective-permute-start | bytes 393224 | tf_op jit(solution)/shard_map/ppermute | solution.py:179
  96.7 9.9 %collective-permute-start.32 = (bf16[1,32,2048]{2,1,0:T(8,128)(2,1)S(1)}, bf16[1,32,2048]{2,1,0:T(8,128)(2,1)S(1)}, u32[]{:S(2)}, u32[]{:S(2)}) collective-permute-start(bf16[1,32,2048]{2,1,0:T(8,128)(2,1)S(1)} %get-tuple-element.34), channel_id=1, source_target_pairs={{0,4},{4,0},{8,12},{12,8},{16,20},{20,16},{24,28},{28,24},{1,5},{5... | collective-permute-start | bytes 393224 | tf_op jit(solution)/shard_map/ppermute | solution.py:179
  97.5 12.6 %collective-permute-start.34 = (bf16[1,32,2048]{2,1,0:T(8,128)(2,1)S(1)}, bf16[1,32,2048]{2,1,0:T(8,128)(2,1)S(1)}, u32[]{:S(2)}, u32[]{:S(2)}) collective-permute-start(bf16[1,32,2048]{2,1,0:T(8,128)(2,1)S(1)} %get-tuple-element.35), channel_id=1, source_target_pairs={{0,4},{4,0},{8,12},{12,8},{16,20},{20,16},{24,28},{28,24},{1,5},{5... | collective-permute-start | bytes 393224 | tf_op jit(solution)/shard_map/ppermute | solution.py:179
  101.0 9.1 %collective-permute-start.29 = (bf16[1,32,2048]{2,1,0:T(8,128)(2,1)S(1)}, bf16[1,32,2048]{2,1,0:T(8,128)(2,1)S(1)}, u32[]{:S(2)}, u32[]{:S(2)}) collective-permute-start(bf16[1,32,2048]{2,1,0:T(8,128)(2,1)S(1)} %add_convert_fusion.2), channel_id=1, source_target_pairs={{0,16},{4,20},{8,24},{12,28},{16,0},{20,4},{24,8},{28,12},{1,17},{... | collective-permute-start | bytes 393224 | tf_op jit(solution)/shard_map/ppermute | solution.py:179
  106.7 6.9 %collective-permute-start.33 = (bf16[1,32,2048]{2,1,0:T(8,128)(2,1)S(1)}, bf16[1,32,2048]{2,1,0:T(8,128)(2,1)S(1)}, u32[]{:S(2)}, u32[]{:S(2)}) collective-permute-start(bf16[1,32,2048]{2,1,0:T(8,128)(2,1)S(1)} %add_convert_fusion), channel_id=1, source_target_pairs={{0,24},{4,28},{8,16},{12,20},{16,8},{20,12},{24,0},{28,4},{1,25},{... | collective-permute-start | bytes 393224 | tf_op jit(solution)/shard_map/ppermute | solution.py:179
  (17 other events, 165.8 us)

commit v9 on v8

--- a/solution.py
+++ b/solution.py
@@ -285,7 +285,9 @@
     whole, rounded = jnp.float32, jnp.bfloat16
     order = [k for pair in strides(cols)[::-1] + [0] for k in (pair + 1, pair)]
     mine, other = (tuple(range(p, rows, 2)) for p in (0, 1))
-    keep, send = (tuple(range(p, cols, 2)) for p in (0, 1))
+    keep = tuple(range(0, cols, 2))
+    leave = [k + 1 for k in strides(cols)[::-1] + [0]]
+    first, then = tuple(leave[:2]), tuple(leave[2:])
     for step in range(ITERS):
         dual_parts = gather_pairs(rounded_dual[0], "col", cols)
         sent, kept = [
@@ -304,13 +306,17 @@
         primal = fresh
         extra = [extra, swap(extra, "row", rows, 1)]
         (sent,) = sweep(
-            Plan(True, False, (mine, other), (Out(send, rounded, False),), False),
+            Plan(True, False, (mine, other), (Out(first, rounded, False),), False),
             blocks, info_back, extra, [], dual.shape[1],
         )
-        (kept,) = sweep(
-            Plan(True, False, (mine, other), (Out(keep, whole, False),), False),
+        rest, kept = sweep(
+            Plan(
+                True, False, (mine, other),
+                (Out(then, rounded, False), Out(keep, whole, False)), False,
+            ),
             blocks, info_back, extra, [], dual.shape[1],
         )
+        sent |= rest
         shares = share_pairs(kept, sent, "col", cols)
         dual, *rounded_dual = update_dual(
             shares, kept[0], demand, row_kind, dual, step == ITERS - 1

time: 117 us -> 116 us (level); the launches traced: 114 us -> 115 us
  waiting for transfers between devices: 45.5 us -> 47.4 us
  Pallas kernels: 11.2 us -> 9.43 us
    ppermute x35, waiting for transfers between devices: 45.5 us -> 47.4 us  [swap(): return lax.ppermute(value, axis, [(i, i ^ k) for i in range(size)])]
    pallas_call x8, Pallas kernels: 10.2 us -> 8.42 us  [sweep(): pl.pallas_call(functools.partial(sweep_kernel, plan, parts[0].shape[2] //...]
  transfers between devices with their start and end apart: 35 -> 35, of which waited for: 20 -> 23; matrix products, arithmetic and copies ran while one was open for 4% -> 3% of each run, Pallas kernels for 6% -> 5%
where the time goes in v9:
time: 116 us; the launch traced here: 115 us
  starting transfers between devices  51 us (44%)
  waiting for transfers between devices  47.4 us (41%)
  Pallas kernels  9.43 us (8%)
  local copies, waits for them, and re-layouts  4.07 us (4%)
  other arithmetic  1.74 us (2%)
  between operations  1.56 us (1%)
    ppermute x35, starting transfers between devices, swap(): return lax.ppermute(value, axis, [(i, i ^ k) for i in range(size)])  51 us
    ppermute x35, waiting for transfers between devices, swap(): return lax.ppermute(value, axis, [(i, i ^ k) for i in range(size)])  47.4 us
    pallas_call x8, Pallas kernels, sweep(): pl.pallas_call(functools.partial(sweep_kernel, plan, parts[0].shape[2] //...  8.42 us
    unnamed x18, local copies, waits for them, and re-layouts  3.93 us
  transfers between devices with their start and end apart: 35, of which 23 were waited for; matrix products, arithmetic and copies ran while one was open for 3% of the time, Pallas kernels for 5%

profile of v9, /device:TPU:0, one launch (start us, length us, event | category | flops | bytes accessed | tf_op | source)
XLA Modules:
  0.0 115.2 jit_solution(10497420195292034862)
XLA Ops:
  1.7 4.1 %collective-permute-start.1 = (bf16[1,32,2048]{2,1,0:T(8,128)(2,1)S(1)}, bf16[1,32,2048]{2,1,0:T(8,128)(2,1)S(1)}, u32[]{:S(2)}, u32[]{:S(2)}) collective-permute-start(bf16[1,32,2048]{2,1,0:T(8,128)(2,1)S(1)} %bitcast.35), channel_id=1, source_target_pairs={{0,16},{4,20},{8,24},{12,28},{16,0},{20,4},{24,8},{28,12},{1,17},{... | collective-permute-start | bytes 393224 | tf_op jit(solution)/shard_map/ppermute | solution.py:179
  5.8 1.6 %collective-permute-start.3 = (bf16[1,32,2048]{2,1,0:T(8,128)(2,1)S(1)}, bf16[1,32,2048]{2,1,0:T(8,128)(2,1)S(1)}, u32[]{:S(2)}, u32[]{:S(2)}) collective-permute-start(bf16[1,32,2048]{2,1,0:T(8,128)(2,1)S(1)} %bitcast.36), channel_id=1, source_target_pairs={{0,8},{4,12},{8,0},{12,4},{16,24},{20,28},{24,16},{28,20},{1,9},{5... | collective-permute-start | bytes 393224 | tf_op jit(solution)/shard_map/ppermute | solution.py:179
  7.4 1.7 %collective-permute-start.7 = (bf16[1,32,2048]{2,1,0:T(8,128)(2,1)S(1)}, bf16[1,32,2048]{2,1,0:T(8,128)(2,1)S(1)}, u32[]{:S(2)}, u32[]{:S(2)}) collective-permute-start(bf16[1,32,2048]{2,1,0:T(8,128)(2,1)S(1)} %bitcast.38), channel_id=1, source_target_pairs={{0,4},{4,0},{8,12},{12,8},{16,20},{20,16},{24,28},{28,24},{1,5},{5... | collective-permute-start | bytes 393224 | tf_op jit(solution)/shard_map/ppermute | solution.py:179
  10.1 3.6 %collective-permute-done.1.refs_1_ = bf16[1,32,2048]{2,1,0:T(8,128)(2,1)S(1)} collective-permute-done((bf16[1,32,2048]{2,1,0:T(8,128)(2,1)S(1)}, bf16[1,32,2048]{2,1,0:T(8,128)(2,1)S(1)}, u32[]{:S(2)}, u32[]{:S(2)}) %collective-permute-start.1) | collective-permute-done | bytes 131104 | tf_op jit(solution)/shard_map/ppermute | solution.py:179
  13.7 2.1 %collective-permute-start.2 = (bf16[1,32,2048]{2,1,0:T(8,128)(2,1)S(1)}, bf16[1,32,2048]{2,1,0:T(8,128)(2,1)S(1)}, u32[]{:S(2)}, u32[]{:S(2)}) collective-permute-start(bf16[1,32,2048]{2,1,0:T(8,128)(2,1)S(1)} %collective-permute-done.1.refs_1_), channel_id=1, source_target_pairs={{0,4},{4,0},{8,12},{12,8},{16,20},{20,16},{24,28},{28,24},{1,5},{5... | collective-permute-start | bytes 393224 | tf_op jit(solution)/shard_map/ppermute | solution.py:179
  16.1 1.8 %collective-permute-start.6 = (bf16[1,32,2048]{2,1,0:T(8,128)(2,1)S(1)}, bf16[1,32,2048]{2,1,0:T(8,128)(2,1)S(1)}, u32[]{:S(2)}, u32[]{:S(2)}) collective-permute-start(bf16[1,32,2048]{2,1,0:T(8,128)(2,1)S(1)} %collective-permute-done.5.refs_5_), channel_id=1, source_target_pairs={{0,4},{4,0},{8,12},{12,8},{16,20},{20,16},{24,28},{28,24},{1,5},{5... | collective-permute-start | bytes 393224 | tf_op jit(solution)/shard_map/ppermute | solution.py:179
  18.7 1.6 %collective-permute-start = (f32[34,2048]{1,0:T(8,128)S(1)}, f32[34,2048]{1,0:T(8,128)S(1)}, u32[]{:S(2)}, u32[]{:S(2)}) collective-permute-start(f32[34,2048]{1,0:T(8,128)S(1)} %get-tuple-element.49), channel_id=1, source_target_pairs={{0,2},{1,3},{2,0},{3,1},{4,6},{5,7},{6,4},{7,5},{8,10},{9,11},{10,... | collective-permute-start | bytes 835592 | tf_op jit(solution)/shard_map/ppermute | solution.py:179
  23.0 2.5 %transpose_sweep.5 = bf16[2,32,2048]{2,1,0:T(8,128)(2,1)S(1)} custom-call(s32[19]{0:T(128)S(1)} %get-tuple-element.55.info, bf16[8,1024,512]{2,1,0:T(8,128)(2,1)} %bitcast.25, bf16[1,32,2048]{2,1,0:T(8,128)(2,1)S(1)} %collective-permute-done.2.refs_0_, bf16[1,32,2048]{2,1,0:T(8,128)(2,1)S(1)} %collective-permute-done.1.refs_1_, ...), custom_call_target="tpu_custom_call" | custom-call | flops 134217728 | bytes 4194304 | tf_op jit(solution)/shard_map/transpose_sweep/pallas_call | solution.py:152
  27.2 3.6 %collective-permute-start.9 = (bf16[2,32,2048]{2,1,0:T(8,128)(2,1)S(1)}, bf16[2,32,2048]{2,1,0:T(8,128)(2,1)S(1)}, u32[]{:S(2)}, u32[]{:S(2)}) collective-permute-start(bf16[2,32,2048]{2,1,0:T(8,128)(2,1)S(1)} %fusion.1), channel_id=1, source_target_pairs={{0,2},{1,3},{2,0},{3,1},{4,6},{5,7},{6,4},{7,5},{8,10},{9,11},{10,... | collective-permute-start | bytes 786440 | tf_op jit(solution)/shard_map/ppermute | solution.py:179
  30.7 6.6 %collective-permute-done.9 = bf16[2,32,2048]{2,1,0:T(8,128)(2,1)S(1)} collective-permute-done((bf16[2,32,2048]{2,1,0:T(8,128)(2,1)S(1)}, bf16[2,32,2048]{2,1,0:T(8,128)(2,1)S(1)}, u32[]{:S(2)}, u32[]{:S(2)}) %collective-permute-start.9) | collective-permute-done | bytes 262176 | tf_op jit(solution)/shard_map/ppermute | solution.py:179
  43.2 2.2 %collective-permute-start.15 = (bf16[1,32,2048]{2,1,0:T(8,128)(2,1)S(1)}, bf16[1,32,2048]{2,1,0:T(8,128)(2,1)S(1)}, u32[]{:S(2)}, u32[]{:S(2)}) collective-permute-start(bf16[1,32,2048]{2,1,0:T(8,128)(2,1)S(1)} %get-tuple-element.25), channel_id=1, source_target_pairs={{0,4},{4,0},{8,12},{12,8},{16,20},{20,16},{24,28},{28,24},{1,5},{5... | collective-permute-start | bytes 393224 | tf_op jit(solution)/shard_map/ppermute | solution.py:179
  46.8 3.6 %collective-permute-start.12 = (bf16[1,32,2048]{2,1,0:T(8,128)(2,1)S(1)}, bf16[1,32,2048]{2,1,0:T(8,128)(2,1)S(1)}, u32[]{:S(2)}, u32[]{:S(2)}) collective-permute-start(bf16[1,32,2048]{2,1,0:T(8,128)(2,1)S(1)} %add_convert_fusion.5), channel_id=1, source_target_pairs={{0,16},{4,20},{8,24},{12,28},{16,0},{20,4},{24,8},{28,12},{1,17},{... | collective-permute-start | bytes 393224 | tf_op jit(solution)/shard_map/ppermute | solution.py:179
  52.4 4.5 %collective-permute-start.16 = (bf16[1,32,2048]{2,1,0:T(8,128)(2,1)S(1)}, bf16[1,32,2048]{2,1,0:T(8,128)(2,1)S(1)}, u32[]{:S(2)}, u32[]{:S(2)}) collective-permute-start(bf16[1,32,2048]{2,1,0:T(8,128)(2,1)S(1)} %add_convert_fusion.3), channel_id=1, source_target_pairs={{0,24},{4,28},{8,16},{12,20},{16,8},{20,12},{24,0},{28,4},{1,25},{... | collective-permute-start | bytes 393224 | tf_op jit(solution)/shard_map/ppermute | solution.py:179
  57.3 4.1 %collective-permute-done.14.refs_1_ = bf16[1,32,2048]{2,1,0:T(8,128)(2,1)S(1)} collective-permute-done((bf16[1,32,2048]{2,1,0:T(8,128)(2,1)S(1)}, bf16[1,32,2048]{2,1,0:T(8,128)(2,1)S(1)}, u32[]{:S(2)}, u32[]{:S(2)}) %collective-permute-start.14) | collective-permute-done | bytes 131104 | tf_op jit(solution)/shard_map/ppermute | solution.py:179
  61.6 3.2 %collective-permute-start.18 = (bf16[1,32,2048]{2,1,0:T(8,128)(2,1)S(1)}, bf16[1,32,2048]{2,1,0:T(8,128)(2,1)S(1)}, u32[]{:S(2)}, u32[]{:S(2)}) collective-permute-start(bf16[1,32,2048]{2,1,0:T(8,128)(2,1)S(1)} %get-tuple-element.28.refs_7_), channel_id=1, source_target_pairs={{0,16},{4,20},{8,24},{12,28},{16,0},{20,4},{24,8},{28,12},{1,17},{... | collective-permute-start | bytes 393224 | tf_op jit(solution)/shard_map/ppermute | solution.py:179
  67.1 4.8 %collective-permute-done.18.refs_1_ = bf16[1,32,2048]{2,1,0:T(8,128)(2,1)S(1)} collective-permute-done((bf16[1,32,2048]{2,1,0:T(8,128)(2,1)S(1)}, bf16[1,32,2048]{2,1,0:T(8,128)(2,1)S(1)}, u32[]{:S(2)}, u32[]{:S(2)}) %collective-permute-start.18) | collective-permute-done | bytes 131104 | tf_op jit(solution)/shard_map/ppermute | solution.py:179
  76.9 2.8 %collective-permute-done.21.refs_2_ = bf16[1,32,2048]{2,1,0:T(8,128)(2,1)S(1)} collective-permute-done((bf16[1,32,2048]{2,1,0:T(8,128)(2,1)S(1)}, bf16[1,32,2048]{2,1,0:T(8,128)(2,1)S(1)}, u32[]{:S(2)}, u32[]{:S(2)}) %collective-permute-start.21) | collective-permute-done | bytes 131104 | tf_op jit(solution)/shard_map/ppermute | solution.py:179
  83.7 1.9 %collective-permute-start.26 = (bf16[2,32,2048]{2,1,0:T(8,128)(2,1)S(1)}, bf16[2,32,2048]{2,1,0:T(8,128)(2,1)S(1)}, u32[]{:S(2)}, u32[]{:S(2)}) collective-permute-start(bf16[2,32,2048]{2,1,0:T(8,128)(2,1)S(1)} %fusion.2), channel_id=1, source_target_pairs={{0,2},{1,3},{2,0},{3,1},{4,6},{5,7},{6,4},{7,5},{8,10},{9,11},{10,... | collective-permute-start | bytes 786440 | tf_op jit(solution)/shard_map/ppermute | solution.py:179
  85.6 6.6 %collective-permute-done.26 = bf16[2,32,2048]{2,1,0:T(8,128)(2,1)S(1)} collective-permute-done((bf16[2,32,2048]{2,1,0:T(8,128)(2,1)S(1)}, bf16[2,32,2048]{2,1,0:T(8,128)(2,1)S(1)}, u32[]{:S(2)}, u32[]{:S(2)}) %collective-permute-start.26) | collective-permute-done | bytes 262176 | tf_op jit(solution)/shard_map/ppermute | solution.py:179
  98.1 2.1 %collective-permute-start.32 = (bf16[1,32,2048]{2,1,0:T(8,128)(2,1)S(1)}, bf16[1,32,2048]{2,1,0:T(8,128)(2,1)S(1)}, u32[]{:S(2)}, u32[]{:S(2)}) collective-permute-start(bf16[1,32,2048]{2,1,0:T(8,128)(2,1)S(1)} %get-tuple-element.34), channel_id=1, source_target_pairs={{0,4},{4,0},{8,12},{12,8},{16,20},{20,16},{24,28},{28,24},{1,5},{5... | collective-permute-start | bytes 393224 | tf_op jit(solution)/shard_map/ppermute | solution.py:179
  101.6 2.0 %collective-permute-start.29 = (bf16[1,32,2048]{2,1,0:T(8,128)(2,1)S(1)}, bf16[1,32,2048]{2,1,0:T(8,128)(2,1)S(1)}, u32[]{:S(2)}, u32[]{:S(2)}) collective-permute-start(bf16[1,32,2048]{2,1,0:T(8,128)(2,1)S(1)} %add_convert_fusion.2), channel_id=1, source_target_pairs={{0,16},{4,20},{8,24},{12,28},{16,0},{20,4},{24,8},{28,12},{1,17},{... | collective-permute-start | bytes 393224 | tf_op jit(solution)/shard_map/ppermute | solution.py:179
  105.4 1.8 %collective-permute-done.32 = bf16[1,32,2048]{2,1,0:T(8,128)(2,1)S(1)} collective-permute-done((bf16[1,32,2048]{2,1,0:T(8,128)(2,1)S(1)}, bf16[1,32,2048]{2,1,0:T(8,128)(2,1)S(1)}, u32[]{:S(2)}, u32[]{:S(2)}) %collective-permute-start.32) | collective-permute-done | bytes 131104 | tf_op jit(solution)/shard_map/ppermute | solution.py:179
  107.3 2.6 %collective-permute-start.33 = (bf16[1,32,2048]{2,1,0:T(8,128)(2,1)S(1)}, bf16[1,32,2048]{2,1,0:T(8,128)(2,1)S(1)}, u32[]{:S(2)}, u32[]{:S(2)}) collective-permute-start(bf16[1,32,2048]{2,1,0:T(8,128)(2,1)S(1)} %add_convert_fusion), channel_id=1, source_target_pairs={{0,24},{4,28},{8,16},{12,20},{16,8},{20,12},{24,0},{28,4},{1,25},{... | collective-permute-start | bytes 393224 | tf_op jit(solution)/shard_map/ppermute | solution.py:179
  110.9 3.5 %collective-permute-done.31.refs_1_ = bf16[1,32,2048]{2,1,0:T(8,128)(2,1)S(1)} collective-permute-done((bf16[1,32,2048]{2,1,0:T(8,128)(2,1)S(1)}, bf16[1,32,2048]{2,1,0:T(8,128)(2,1)S(1)}, u32[]{:S(2)}, u32[]{:S(2)}) %collective-permute-start.31) | collective-permute-done | bytes 131104 | tf_op jit(solution)/shard_map/ppermute | solution.py:179
  (93 shorter events, 38.9 us)
Async XLA Ops:
  1.7 12.1 %collective-permute-start.1 = (bf16[1,32,2048]{2,1,0:T(8,128)(2,1)S(1)}, bf16[1,32,2048]{2,1,0:T(8,128)(2,1)S(1)}, u32[]{:S(2)}, u32[]{:S(2)}) collective-permute-start(bf16[1,32,2048]{2,1,0:T(8,128)(2,1)S(1)} %bitcast.35), channel_id=1, source_target_pairs={{0,16},{4,20},{8,24},{12,28},{16,0},{20,4},{24,8},{28,12},{1,17},{... | collective-permute-start | bytes 393224 | tf_op jit(solution)/shard_map/ppermute | solution.py:179
  5.8 10.1 %collective-permute-start.3 = (bf16[1,32,2048]{2,1,0:T(8,128)(2,1)S(1)}, bf16[1,32,2048]{2,1,0:T(8,128)(2,1)S(1)}, u32[]{:S(2)}, u32[]{:S(2)}) collective-permute-start(bf16[1,32,2048]{2,1,0:T(8,128)(2,1)S(1)} %bitcast.36), channel_id=1, source_target_pairs={{0,8},{4,12},{8,0},{12,4},{16,24},{20,28},{24,16},{28,20},{1,9},{5... | collective-permute-start | bytes 393224 | tf_op jit(solution)/shard_map/ppermute | solution.py:179
  7.4 8.8 %collective-permute-start.5 = (bf16[1,32,2048]{2,1,0:T(8,128)(2,1)S(1)}, bf16[1,32,2048]{2,1,0:T(8,128)(2,1)S(1)}, u32[]{:S(2)}, u32[]{:S(2)}) collective-permute-start(bf16[1,32,2048]{2,1,0:T(8,128)(2,1)S(1)} %bitcast.37), channel_id=1, source_target_pairs={{0,24},{4,28},{8,16},{12,20},{16,8},{20,12},{24,0},{28,4},{1,25},{... | collective-permute-start | bytes 393224 | tf_op jit(solution)/shard_map/ppermute | solution.py:179
  7.4 14.5 %collective-permute-start.7 = (bf16[1,32,2048]{2,1,0:T(8,128)(2,1)S(1)}, bf16[1,32,2048]{2,1,0:T(8,128)(2,1)S(1)}, u32[]{:S(2)}, u32[]{:S(2)}) collective-permute-start(bf16[1,32,2048]{2,1,0:T(8,128)(2,1)S(1)} %bitcast.38), channel_id=1, source_target_pairs={{0,4},{4,0},{8,12},{12,8},{16,20},{20,16},{24,28},{28,24},{1,5},{5... | collective-permute-start | bytes 393224 | tf_op jit(solution)/shard_map/ppermute | solution.py:179
  13.7 8.1 %collective-permute-start.2 = (bf16[1,32,2048]{2,1,0:T(8,128)(2,1)S(1)}, bf16[1,32,2048]{2,1,0:T(8,128)(2,1)S(1)}, u32[]{:S(2)}, u32[]{:S(2)}) collective-permute-start(bf16[1,32,2048]{2,1,0:T(8,128)(2,1)S(1)} %collective-permute-done.1.refs_1_), channel_id=1, source_target_pairs={{0,4},{4,0},{8,12},{12,8},{16,20},{20,16},{24,28},{28,24},{1,5},{5... | collective-permute-start | bytes 393224 | tf_op jit(solution)/shard_map/ppermute | solution.py:179
  18.7 8.0 %collective-permute-start = (f32[34,2048]{1,0:T(8,128)S(1)}, f32[34,2048]{1,0:T(8,128)S(1)}, u32[]{:S(2)}, u32[]{:S(2)}) collective-permute-start(f32[34,2048]{1,0:T(8,128)S(1)} %get-tuple-element.49), channel_id=1, source_target_pairs={{0,2},{1,3},{2,0},{3,1},{4,6},{5,7},{6,4},{7,5},{8,10},{9,11},{10,... | collective-permute-start | bytes 835592 | tf_op jit(solution)/shard_map/ppermute | solution.py:179
  27.2 10.2 %collective-permute-start.9 = (bf16[2,32,2048]{2,1,0:T(8,128)(2,1)S(1)}, bf16[2,32,2048]{2,1,0:T(8,128)(2,1)S(1)}, u32[]{:S(2)}, u32[]{:S(2)}) collective-permute-start(bf16[2,32,2048]{2,1,0:T(8,128)(2,1)S(1)} %fusion.1), channel_id=1, source_target_pairs={{0,2},{1,3},{2,0},{3,1},{4,6},{5,7},{6,4},{7,5},{8,10},{9,11},{10,... | collective-permute-start | bytes 786440 | tf_op jit(solution)/shard_map/ppermute | solution.py:179
  41.6 8.8 %collective-permute-start.13 = (bf16[1,32,2048]{2,1,0:T(8,128)(2,1)S(1)}, bf16[1,32,2048]{2,1,0:T(8,128)(2,1)S(1)}, u32[]{:S(2)}, u32[]{:S(2)}) collective-permute-start(bf16[1,32,2048]{2,1,0:T(8,128)(2,1)S(1)} %get-tuple-element.23), channel_id=1, source_target_pairs={{0,4},{4,0},{8,12},{12,8},{16,20},{20,16},{24,28},{28,24},{1,5},{5... | collective-permute-start | bytes 393224 | tf_op jit(solution)/shard_map/ppermute | solution.py:179
  43.2 9.2 %collective-permute-start.15 = (bf16[1,32,2048]{2,1,0:T(8,128)(2,1)S(1)}, bf16[1,32,2048]{2,1,0:T(8,128)(2,1)S(1)}, u32[]{:S(2)}, u32[]{:S(2)}) collective-permute-start(bf16[1,32,2048]{2,1,0:T(8,128)(2,1)S(1)} %get-tuple-element.25), channel_id=1, source_target_pairs={{0,4},{4,0},{8,12},{12,8},{16,20},{20,16},{24,28},{28,24},{1,5},{5... | collective-permute-start | bytes 393224 | tf_op jit(solution)/shard_map/ppermute | solution.py:179
  45.4 11.6 %collective-permute-start.17 = (bf16[1,32,2048]{2,1,0:T(8,128)(2,1)S(1)}, bf16[1,32,2048]{2,1,0:T(8,128)(2,1)S(1)}, u32[]{:S(2)}, u32[]{:S(2)}) collective-permute-start(bf16[1,32,2048]{2,1,0:T(8,128)(2,1)S(1)} %get-tuple-element.26), channel_id=1, source_target_pairs={{0,4},{4,0},{8,12},{12,8},{16,20},{20,16},{24,28},{28,24},{1,5},{5... | collective-permute-start | bytes 393224 | tf_op jit(solution)/shard_map/ppermute | solution.py:179
  46.8 10.6 %collective-permute-start.12 = (bf16[1,32,2048]{2,1,0:T(8,128)(2,1)S(1)}, bf16[1,32,2048]{2,1,0:T(8,128)(2,1)S(1)}, u32[]{:S(2)}, u32[]{:S(2)}) collective-permute-start(bf16[1,32,2048]{2,1,0:T(8,128)(2,1)S(1)} %add_convert_fusion.5), channel_id=1, source_target_pairs={{0,16},{4,20},{8,24},{12,28},{16,0},{20,4},{24,8},{28,12},{1,17},{... | collective-permute-start | bytes 393224 | tf_op jit(solution)/shard_map/ppermute | solution.py:179
  50.4 11.0 %collective-permute-start.14 = (bf16[1,32,2048]{2,1,0:T(8,128)(2,1)S(1)}, bf16[1,32,2048]{2,1,0:T(8,128)(2,1)S(1)}, u32[]{:S(2)}, u32[]{:S(2)}) collective-permute-start(bf16[1,32,2048]{2,1,0:T(8,128)(2,1)S(1)} %add_convert_fusion.4), channel_id=1, source_target_pairs={{0,8},{4,12},{8,0},{12,4},{16,24},{20,28},{24,16},{28,20},{1,9},{5... | collective-permute-start | bytes 393224 | tf_op jit(solution)/shard_map/ppermute | solution.py:179
  52.4 9.0 %collective-permute-start.16 = (bf16[1,32,2048]{2,1,0:T(8,128)(2,1)S(1)}, bf16[1,32,2048]{2,1,0:T(8,128)(2,1)S(1)}, u32[]{:S(2)}, u32[]{:S(2)}) collective-permute-start(bf16[1,32,2048]{2,1,0:T(8,128)(2,1)S(1)} %add_convert_fusion.3), channel_id=1, source_target_pairs={{0,24},{4,28},{8,16},{12,20},{16,8},{20,12},{24,0},{28,4},{1,25},{... | collective-permute-start | bytes 393224 | tf_op jit(solution)/shard_map/ppermute | solution.py:179
  61.6 10.3 %collective-permute-start.18 = (bf16[1,32,2048]{2,1,0:T(8,128)(2,1)S(1)}, bf16[1,32,2048]{2,1,0:T(8,128)(2,1)S(1)}, u32[]{:S(2)}, u32[]{:S(2)}) collective-permute-start(bf16[1,32,2048]{2,1,0:T(8,128)(2,1)S(1)} %get-tuple-element.28.refs_7_), channel_id=1, source_target_pairs={{0,16},{4,20},{8,24},{12,28},{16,0},{20,4},{24,8},{28,12},{1,17},{... | collective-permute-start | bytes 393224 | tf_op jit(solution)/shard_map/ppermute | solution.py:179
  64.7 8.4 %collective-permute-start.20 = (bf16[1,32,2048]{2,1,0:T(8,128)(2,1)S(1)}, bf16[1,32,2048]{2,1,0:T(8,128)(2,1)S(1)}, u32[]{:S(2)}, u32[]{:S(2)}) collective-permute-start(bf16[1,32,2048]{2,1,0:T(8,128)(2,1)S(1)} %get-tuple-element.28.refs_7_), channel_id=1, source_target_pairs={{0,8},{4,12},{8,0},{12,4},{16,24},{20,28},{24,16},{28,20},{1,9},{5... | collective-permute-start | bytes 393224 | tf_op jit(solution)/shard_map/ppermute | solution.py:179
  64.8 10.4 %collective-permute-start.22 = (bf16[1,32,2048]{2,1,0:T(8,128)(2,1)S(1)}, bf16[1,32,2048]{2,1,0:T(8,128)(2,1)S(1)}, u32[]{:S(2)}, u32[]{:S(2)}) collective-permute-start(bf16[1,32,2048]{2,1,0:T(8,128)(2,1)S(1)} %get-tuple-element.28.refs_7_), channel_id=1, source_target_pairs={{0,24},{4,28},{8,16},{12,20},{16,8},{20,12},{24,0},{28,4},{1,25},{... | collective-permute-start | bytes 393224 | tf_op jit(solution)/shard_map/ppermute | solution.py:179
  66.3 9.7 %collective-permute-start.24 = (bf16[1,32,2048]{2,1,0:T(8,128)(2,1)S(1)}, bf16[1,32,2048]{2,1,0:T(8,128)(2,1)S(1)}, u32[]{:S(2)}, u32[]{:S(2)}) collective-permute-start(bf16[1,32,2048]{2,1,0:T(8,128)(2,1)S(1)} %get-tuple-element.28.refs_7_), channel_id=1, source_target_pairs={{0,4},{4,0},{8,12},{12,8},{16,20},{20,16},{24,28},{28,24},{1,5},{5... | collective-permute-start | bytes 393224 | tf_op jit(solution)/shard_map/ppermute | solution.py:179
  83.7 8.5 %collective-permute-start.26 = (bf16[2,32,2048]{2,1,0:T(8,128)(2,1)S(1)}, bf16[2,32,2048]{2,1,0:T(8,128)(2,1)S(1)}, u32[]{:S(2)}, u32[]{:S(2)}) collective-permute-start(bf16[2,32,2048]{2,1,0:T(8,128)(2,1)S(1)} %fusion.2), channel_id=1, source_target_pairs={{0,2},{1,3},{2,0},{3,1},{4,6},{5,7},{6,4},{7,5},{8,10},{9,11},{10,... | collective-permute-start | bytes 786440 | tf_op jit(solution)/shard_map/ppermute | solution.py:179
  96.4 8.0 %collective-permute-start.30 = (bf16[1,32,2048]{2,1,0:T(8,128)(2,1)S(1)}, bf16[1,32,2048]{2,1,0:T(8,128)(2,1)S(1)}, u32[]{:S(2)}, u32[]{:S(2)}) collective-permute-start(bf16[1,32,2048]{2,1,0:T(8,128)(2,1)S(1)} %get-tuple-element.32), channel_id=1, source_target_pairs={{0,4},{4,0},{8,12},{12,8},{16,20},{20,16},{24,28},{28,24},{1,5},{5... | collective-permute-start | bytes 393224 | tf_op jit(solution)/shard_map/ppermute | solution.py:179
  98.1 9.2 %collective-permute-start.32 = (bf16[1,32,2048]{2,1,0:T(8,128)(2,1)S(1)}, bf16[1,32,2048]{2,1,0:T(8,128)(2,1)S(1)}, u32[]{:S(2)}, u32[]{:S(2)}) collective-permute-start(bf16[1,32,2048]{2,1,0:T(8,128)(2,1)S(1)} %get-tuple-element.34), channel_id=1, source_target_pairs={{0,4},{4,0},{8,12},{12,8},{16,20},{20,16},{24,28},{28,24},{1,5},{5... | collective-permute-start | bytes 393224 | tf_op jit(solution)/shard_map/ppermute | solution.py:179
  100.2 10.7 %collective-permute-start.34 = (bf16[1,32,2048]{2,1,0:T(8,128)(2,1)S(1)}, bf16[1,32,2048]{2,1,0:T(8,128)(2,1)S(1)}, u32[]{:S(2)}, u32[]{:S(2)}) collective-permute-start(bf16[1,32,2048]{2,1,0:T(8,128)(2,1)S(1)} %get-tuple-element.35), channel_id=1, source_target_pairs={{0,4},{4,0},{8,12},{12,8},{16,20},{20,16},{24,28},{28,24},{1,5},{5... | collective-permute-start | bytes 393224 | tf_op jit(solution)/shard_map/ppermute | solution.py:179
  101.6 9.2 %collective-permute-start.29 = (bf16[1,32,2048]{2,1,0:T(8,128)(2,1)S(1)}, bf16[1,32,2048]{2,1,0:T(8,128)(2,1)S(1)}, u32[]{:S(2)}, u32[]{:S(2)}) collective-permute-start(bf16[1,32,2048]{2,1,0:T(8,128)(2,1)S(1)} %add_convert_fusion.2), channel_id=1, source_target_pairs={{0,16},{4,20},{8,24},{12,28},{16,0},{20,4},{24,8},{28,12},{1,17},{... | collective-permute-start | bytes 393224 | tf_op jit(solution)/shard_map/ppermute | solution.py:179
  104.4 9.9 %collective-permute-start.31 = (bf16[1,32,2048]{2,1,0:T(8,128)(2,1)S(1)}, bf16[1,32,2048]{2,1,0:T(8,128)(2,1)S(1)}, u32[]{:S(2)}, u32[]{:S(2)}) collective-permute-start(bf16[1,32,2048]{2,1,0:T(8,128)(2,1)S(1)} %add_convert_fusion.1), channel_id=1, source_target_pairs={{0,8},{4,12},{8,0},{12,4},{16,24},{20,28},{24,16},{28,20},{1,9},{5... | collective-permute-start | bytes 393224 | tf_op jit(solution)/shard_map/ppermute | solution.py:179
  107.3 7.1 %collective-permute-start.33 = (bf16[1,32,2048]{2,1,0:T(8,128)(2,1)S(1)}, bf16[1,32,2048]{2,1,0:T(8,128)(2,1)S(1)}, u32[]{:S(2)}, u32[]{:S(2)}) collective-permute-start(bf16[1,32,2048]{2,1,0:T(8,128)(2,1)S(1)} %add_convert_fusion), channel_id=1, source_target_pairs={{0,24},{4,28},{8,16},{12,20},{16,8},{20,12},{24,0},{28,4},{1,25},{... | collective-permute-start | bytes 393224 | tf_op jit(solution)/shard_map/ppermute | solution.py:179
  (17 other events, 166.4 us)

commit v10 on v9

--- a/solution.py
+++ b/solution.py
@@ -18,6 +18,7 @@
 
 VMEM_LIMIT = 24 * 1024 * 1024
 FETCH_LIMIT = 46 * 1024 * 1024
+LOAD_LIMIT = 42 * 1024 * 1024
 
 
 def among(value, ks):
@@ -175,6 +176,39 @@
     ]
 
 
+def load_kernel(info, tiles, held, arrived):
+    live = info[2 * tiles.shape[0]]
+
+    def fetch(slot):
+        return pltpu.make_async_copy(tiles.at[slot], held.at[slot], arrived.at[slot])
+
+    def start(slot, carry):
+        fetch(slot).start()
+        return carry
+
+    def finish(slot, carry):
+        fetch(slot).wait()
+        return carry
+
+    lax.fori_loop(0, live, start, 0)
+    lax.fori_loop(0, live, finish, 0)
+
+
+def load_tiles(info, tiles):
+    return pl.pallas_call(
+        load_kernel,
+        out_shape=jax.ShapeDtypeStruct(tiles.shape, tiles.dtype),
+        in_specs=[pl.BlockSpec(memory_space=pltpu.SMEM), pl.BlockSpec(memory_space=pl.ANY)],
+        out_specs=pl.BlockSpec(memory_space=pltpu.VMEM),
+        scratch_shapes=[pltpu.SemaphoreType.DMA((tiles.shape[0],))],
+        compiler_params=pltpu.CompilerParams(vmem_limit_bytes=LOAD_LIMIT),
+        cost_estimate=pl.CostEstimate(
+            flops=0, bytes_accessed=4 * tiles.size, transcendentals=0
+        ),
+        name="load_tiles",
+    )(info, tiles)
+
+
 def swap(value, axis, size, k):
     return lax.ppermute(value, axis, [(i, i ^ k) for i in range(size)])
 
@@ -288,12 +322,13 @@
     keep = tuple(range(0, cols, 2))
     leave = [k + 1 for k in strides(cols)[::-1] + [0]]
     first, then = tuple(leave[:2]), tuple(leave[2:])
+    blocks = load_tiles(info, blocks)
     for step in range(ITERS):
         dual_parts = gather_pairs(rounded_dual[0], "col", cols)
         sent, kept = [
             sweep(
                 Plan(
-                    False, step == 0, tuple((k,) for k in order),
+                    False, False, tuple((k,) for k in order),
                     (Out(other, rounded, True) if sending else Out(mine, whole, True),), False,
                 ),
                 blocks, info, [dual_parts[k] for k in order], [], primal.shape[2],

time: 116 us -> 116 us (level)
  Pallas kernels: 9.43 us -> 13.8 us
  waiting for transfers between devices: 47.4 us -> 44.9 us
  starting transfers between devices: 51 us -> 48.8 us
    ppermute x35, waiting for transfers between devices: 47.4 us -> 44.9 us  [swap(): return lax.ppermute(value, axis, [(i, i ^ k) for i in range(size)])]
    pallas_call x0 -> x1, Pallas kernels: none -> 2.48 us  [load_tiles(): pl.pallas_call(load_kernel, out_shape=jax.ShapeDtypeStruct(tiles.shape, t...]
    ppermute x35, starting transfers between devices: 51 us -> 48.8 us  [swap(): return lax.ppermute(value, axis, [(i, i ^ k) for i in range(size)])]
    pallas_call x8, Pallas kernels: 8.42 us -> 10.3 us  [sweep(): pl.pallas_call(functools.partial(sweep_kernel, plan, parts[0].shape[2] //...]
    unnamed x18 -> x14, local copies, waits for them, and re-layouts: 3.93 us -> 3.91 us
  transfers between devices with their start and end apart: 35 -> 35, of which waited for: 23 -> 17; matrix products, arithmetic and copies ran while one was open for 3% -> 4% of each run, Pallas kernels for 5% -> 9%
where the time goes in v10:
time: 116 us; the launch traced here: 115 us
  starting transfers between devices  48.8 us (42%)
  waiting for transfers between devices  44.9 us (39%)
  Pallas kernels  13.8 us (12%)
  local copies, waits for them, and re-layouts  4.05 us (3%)
  other arithmetic  1.72 us (1%)
  between operations  1.59 us (1%)
    ppermute x35, starting transfers between devices, swap(): return lax.ppermute(value, axis, [(i, i ^ k) for i in range(size)])  48.8 us
    ppermute x35, waiting for transfers between devices, swap(): return lax.ppermute(value, axis, [(i, i ^ k) for i in range(size)])  44.9 us
    pallas_call x8, Pallas kernels, sweep(): pl.pallas_call(functools.partial(sweep_kernel, plan, parts[0].shape[2] //...  10.3 us
    unnamed x14, local copies, waits for them, and re-layouts  3.91 us
    pallas_call x1, Pallas kernels, load_tiles(): pl.pallas_call(load_kernel, out_shape=jax.ShapeDtypeStruct(tiles.shape, t...  2.48 us
  transfers between devices with their start and end apart: 35, of which 17 were waited for; matrix products, arithmetic and copies ran while one was open for 4% of the time, Pallas kernels for 9%

profile of v10, /device:TPU:0, one launch (start us, length us, event | category | flops | bytes accessed | tf_op | source)
XLA Modules:
  0.0 114.8 jit_solution(15188722245160071751)
XLA Ops:
  1.7 4.1 %collective-permute-start.1 = (bf16[1,32,2048]{2,1,0:T(8,128)(2,1)S(1)}, bf16[1,32,2048]{2,1,0:T(8,128)(2,1)S(1)}, u32[]{:S(2)}, u32[]{:S(2)}) collective-permute-start(bf16[1,32,2048]{2,1,0:T(8,128)(2,1)S(1)} %bitcast.25), channel_id=1, source_target_pairs={{0,16},{4,20},{8,24},{12,28},{16,0},{20,4},{24,8},{28,12},{1,17},{... | collective-permute-start | bytes 393224 | tf_op jit(solution)/shard_map/ppermute | solution.py:213
  7.3 1.7 %collective-permute-start.7 = (bf16[1,32,2048]{2,1,0:T(8,128)(2,1)S(1)}, bf16[1,32,2048]{2,1,0:T(8,128)(2,1)S(1)}, u32[]{:S(2)}, u32[]{:S(2)}) collective-permute-start(bf16[1,32,2048]{2,1,0:T(8,128)(2,1)S(1)} %bitcast.28), channel_id=1, source_target_pairs={{0,4},{4,0},{8,12},{12,8},{16,20},{20,16},{24,28},{28,24},{1,5},{5... | collective-permute-start | bytes 393224 | tf_op jit(solution)/shard_map/ppermute | solution.py:213
  10.1 3.6 %collective-permute-done.1.refs_1_ = bf16[1,32,2048]{2,1,0:T(8,128)(2,1)S(1)} collective-permute-done((bf16[1,32,2048]{2,1,0:T(8,128)(2,1)S(1)}, bf16[1,32,2048]{2,1,0:T(8,128)(2,1)S(1)}, u32[]{:S(2)}, u32[]{:S(2)}) %collective-permute-start.1) | collective-permute-done | bytes 131104 | tf_op jit(solution)/shard_map/ppermute | solution.py:213
  13.7 2.1 %collective-permute-start.2 = (bf16[1,32,2048]{2,1,0:T(8,128)(2,1)S(1)}, bf16[1,32,2048]{2,1,0:T(8,128)(2,1)S(1)}, u32[]{:S(2)}, u32[]{:S(2)}) collective-permute-start(bf16[1,32,2048]{2,1,0:T(8,128)(2,1)S(1)} %collective-permute-done.1.refs_1_), channel_id=1, source_target_pairs={{0,4},{4,0},{8,12},{12,8},{16,20},{20,16},{24,28},{28,24},{1,5},{5... | collective-permute-start | bytes 393224 | tf_op jit(solution)/shard_map/ppermute | solution.py:213
  16.1 1.8 %collective-permute-start.6 = (bf16[1,32,2048]{2,1,0:T(8,128)(2,1)S(1)}, bf16[1,32,2048]{2,1,0:T(8,128)(2,1)S(1)}, u32[]{:S(2)}, u32[]{:S(2)}) collective-permute-start(bf16[1,32,2048]{2,1,0:T(8,128)(2,1)S(1)} %collective-permute-done.5.refs_5_), channel_id=1, source_target_pairs={{0,4},{4,0},{8,12},{12,8},{16,20},{20,16},{24,28},{28,24},{1,5},{5... | collective-permute-start | bytes 393224 | tf_op jit(solution)/shard_map/ppermute | solution.py:213
  21.8 2.5 %load_tiles.1.tiles = bf16[8,1024,512]{2,1,0:T(8,128)(2,1)S(1)} custom-call(s32[19]{0:T(128)S(1)} %get-tuple-element.55.info, bf16[8,1024,512]{2,1,0:T(8,128)(2,1)} %bitcast.32), custom_call_target="tpu_custom_call" | custom-call | bytes 16777216 | tf_op jit(solution)/shard_map/load_tiles/pallas_call | solution.py:198
  28.4 7.0 %collective-permute-done.9 = bf16[2,32,2048]{2,1,0:T(8,128)(2,1)S(1)} collective-permute-done((bf16[2,32,2048]{2,1,0:T(8,128)(2,1)S(1)}, bf16[2,32,2048]{2,1,0:T(8,128)(2,1)S(1)}, u32[]{:S(2)}, u32[]{:S(2)}) %collective-permute-start.9) | collective-permute-done | bytes 262176 | tf_op jit(solution)/shard_map/ppermute | solution.py:213
  40.0 2.2 %forward_sweep.4 = (bf16[1,32,2048]{2,1,0:T(8,128)(2,1)S(1)}, bf16[1,32,2048]{2,1,0:T(8,128)(2,1)S(1)}, f32[1,32,2048]{2,1,0:T(8,128)S(1)}, f32[1,32,2048]{2,1,0...) custom-call(s32[19]{0:T(128)S(1)} %get-tuple-element.54.info, ...), custom_call_target="tpu_custom_call" | custom-call | flops 134217728 | bytes 4194304 | tf_op jit(solution)/shard_map/forward_sweep/pallas_call | solution.py:153
  44.3 4.0 %collective-permute-start.12 = (bf16[1,32,2048]{2,1,0:T(8,128)(2,1)S(1)}, bf16[1,32,2048]{2,1,0:T(8,128)(2,1)S(1)}, u32[]{:S(2)}, u32[]{:S(2)}) collective-permute-start(bf16[1,32,2048]{2,1,0:T(8,128)(2,1)S(1)} %add_convert_fusion.5), channel_id=1, source_target_pairs={{0,16},{4,20},{8,24},{12,28},{16,0},{20,4},{24,8},{28,12},{1,17},{... | collective-permute-start | bytes 393224 | tf_op jit(solution)/shard_map/ppermute | solution.py:213
  48.3 2.6 %collective-permute-start.14 = (bf16[1,32,2048]{2,1,0:T(8,128)(2,1)S(1)}, bf16[1,32,2048]{2,1,0:T(8,128)(2,1)S(1)}, u32[]{:S(2)}, u32[]{:S(2)}) collective-permute-start(bf16[1,32,2048]{2,1,0:T(8,128)(2,1)S(1)} %add_convert_fusion.4), channel_id=1, source_target_pairs={{0,8},{4,12},{8,0},{12,4},{16,24},{20,28},{24,16},{28,20},{1,9},{5... | collective-permute-start | bytes 393224 | tf_op jit(solution)/shard_map/ppermute | solution.py:213
  51.0 2.9 %collective-permute-start.16 = (bf16[1,32,2048]{2,1,0:T(8,128)(2,1)S(1)}, bf16[1,32,2048]{2,1,0:T(8,128)(2,1)S(1)}, u32[]{:S(2)}, u32[]{:S(2)}) collective-permute-start(bf16[1,32,2048]{2,1,0:T(8,128)(2,1)S(1)} %add_convert_fusion.3), channel_id=1, source_target_pairs={{0,24},{4,28},{8,16},{12,20},{16,8},{20,12},{24,0},{28,4},{1,25},{... | collective-permute-start | bytes 393224 | tf_op jit(solution)/shard_map/ppermute | solution.py:213
  54.9 4.3 %collective-permute-done.16.refs_2_ = bf16[1,32,2048]{2,1,0:T(8,128)(2,1)S(1)} collective-permute-done((bf16[1,32,2048]{2,1,0:T(8,128)(2,1)S(1)}, bf16[1,32,2048]{2,1,0:T(8,128)(2,1)S(1)}, u32[]{:S(2)}, u32[]{:S(2)}) %collective-permute-start.16) | collective-permute-done | bytes 131104 | tf_op jit(solution)/shard_map/ppermute | solution.py:213
  59.3 2.9 %collective-permute-start.18 = (bf16[1,32,2048]{2,1,0:T(8,128)(2,1)S(1)}, bf16[1,32,2048]{2,1,0:T(8,128)(2,1)S(1)}, u32[]{:S(2)}, u32[]{:S(2)}) collective-permute-start(bf16[1,32,2048]{2,1,0:T(8,128)(2,1)S(1)} %get-tuple-element.28.refs_7_), channel_id=1, source_target_pairs={{0,16},{4,20},{8,24},{12,28},{16,0},{20,4},{24,8},{28,12},{1,17},{... | collective-permute-start | bytes 393224 | tf_op jit(solution)/shard_map/ppermute | solution.py:213
  62.2 1.9 %collective-permute-start.22 = (bf16[1,32,2048]{2,1,0:T(8,128)(2,1)S(1)}, bf16[1,32,2048]{2,1,0:T(8,128)(2,1)S(1)}, u32[]{:S(2)}, u32[]{:S(2)}) collective-permute-start(bf16[1,32,2048]{2,1,0:T(8,128)(2,1)S(1)} %get-tuple-element.28.refs_7_), channel_id=1, source_target_pairs={{0,24},{4,28},{8,16},{12,20},{16,8},{20,12},{24,0},{28,4},{1,25},{... | collective-permute-start | bytes 393224 | tf_op jit(solution)/shard_map/ppermute | solution.py:213
  64.5 6.1 %collective-permute-done.18.refs_1_ = bf16[1,32,2048]{2,1,0:T(8,128)(2,1)S(1)} collective-permute-done((bf16[1,32,2048]{2,1,0:T(8,128)(2,1)S(1)}, bf16[1,32,2048]{2,1,0:T(8,128)(2,1)S(1)}, u32[]{:S(2)}, u32[]{:S(2)}) %collective-permute-start.18) | collective-permute-done | bytes 131104 | tf_op jit(solution)/shard_map/ppermute | solution.py:213
  73.1 2.8 %collective-permute-done.19.refs_0_ = bf16[1,32,2048]{2,1,0:T(8,128)(2,1)S(1)} collective-permute-done((bf16[1,32,2048]{2,1,0:T(8,128)(2,1)S(1)}, bf16[1,32,2048]{2,1,0:T(8,128)(2,1)S(1)}, u32[]{:S(2)}, u32[]{:S(2)}) %collective-permute-start.19) | collective-permute-done | bytes 131104 | tf_op jit(solution)/shard_map/ppermute | solution.py:213
  81.2 4.1 %collective-permute-start.26 = (bf16[2,32,2048]{2,1,0:T(8,128)(2,1)S(1)}, bf16[2,32,2048]{2,1,0:T(8,128)(2,1)S(1)}, u32[]{:S(2)}, u32[]{:S(2)}) collective-permute-start(bf16[2,32,2048]{2,1,0:T(8,128)(2,1)S(1)} %fusion.2), channel_id=1, source_target_pairs={{0,2},{1,3},{2,0},{3,1},{4,6},{5,7},{6,4},{7,5},{8,10},{9,11},{10,... | collective-permute-start | bytes 786440 | tf_op jit(solution)/shard_map/ppermute | solution.py:213
  85.3 7.1 %collective-permute-done.26 = bf16[2,32,2048]{2,1,0:T(8,128)(2,1)S(1)} collective-permute-done((bf16[2,32,2048]{2,1,0:T(8,128)(2,1)S(1)}, bf16[2,32,2048]{2,1,0:T(8,128)(2,1)S(1)}, u32[]{:S(2)}, u32[]{:S(2)}) %collective-permute-start.26) | collective-permute-done | bytes 262176 | tf_op jit(solution)/shard_map/ppermute | solution.py:213
  95.4 1.7 %collective-permute-start.30 = (bf16[1,32,2048]{2,1,0:T(8,128)(2,1)S(1)}, bf16[1,32,2048]{2,1,0:T(8,128)(2,1)S(1)}, u32[]{:S(2)}, u32[]{:S(2)}) collective-permute-start(bf16[1,32,2048]{2,1,0:T(8,128)(2,1)S(1)} %get-tuple-element.32), channel_id=1, source_target_pairs={{0,4},{4,0},{8,12},{12,8},{16,20},{20,16},{24,28},{28,24},{1,5},{5... | collective-permute-start | bytes 393224 | tf_op jit(solution)/shard_map/ppermute | solution.py:213
  97.1 2.2 %forward_sweep.6 = (bf16[1,32,2048]{2,1,0:T(8,128)(2,1)S(1)}, bf16[1,32,2048]{2,1,0:T(8,128)(2,1)S(1)}, f32[1,32,2048]{2,1,0:T(8,128)S(1)}, f32[1,32,2048]{2,1,0...) custom-call(s32[19]{0:T(128)S(1)} %get-tuple-element.54.info, ...), custom_call_target="tpu_custom_call" | custom-call | flops 134217728 | bytes 4194304 | tf_op jit(solution)/shard_map/forward_sweep/pallas_call | solution.py:153
  99.4 2.0 %collective-permute-start.34 = (bf16[1,32,2048]{2,1,0:T(8,128)(2,1)S(1)}, bf16[1,32,2048]{2,1,0:T(8,128)(2,1)S(1)}, u32[]{:S(2)}, u32[]{:S(2)}) collective-permute-start(bf16[1,32,2048]{2,1,0:T(8,128)(2,1)S(1)} %get-tuple-element.35), channel_id=1, source_target_pairs={{0,4},{4,0},{8,12},{12,8},{16,20},{20,16},{24,28},{28,24},{1,5},{5... | collective-permute-start | bytes 393224 | tf_op jit(solution)/shard_map/ppermute | solution.py:213
  102.1 2.0 %collective-permute-done.30 = bf16[1,32,2048]{2,1,0:T(8,128)(2,1)S(1)} collective-permute-done((bf16[1,32,2048]{2,1,0:T(8,128)(2,1)S(1)}, bf16[1,32,2048]{2,1,0:T(8,128)(2,1)S(1)}, u32[]{:S(2)}, u32[]{:S(2)}) %collective-permute-start.30) | collective-permute-done | bytes 131104 | tf_op jit(solution)/shard_map/ppermute | solution.py:213
  107.0 2.2 %collective-permute-start.33 = (bf16[1,32,2048]{2,1,0:T(8,128)(2,1)S(1)}, bf16[1,32,2048]{2,1,0:T(8,128)(2,1)S(1)}, u32[]{:S(2)}, u32[]{:S(2)}) collective-permute-start(bf16[1,32,2048]{2,1,0:T(8,128)(2,1)S(1)} %add_convert_fusion), channel_id=1, source_target_pairs={{0,24},{4,28},{8,16},{12,20},{16,8},{20,12},{24,0},{28,4},{1,25},{... | collective-permute-start | bytes 393224 | tf_op jit(solution)/shard_map/ppermute | solution.py:213
  111.0 2.9 %collective-permute-done.33.refs_2_ = bf16[1,32,2048]{2,1,0:T(8,128)(2,1)S(1)} collective-permute-done((bf16[1,32,2048]{2,1,0:T(8,128)(2,1)S(1)}, bf16[1,32,2048]{2,1,0:T(8,128)(2,1)S(1)}, u32[]{:S(2)}, u32[]{:S(2)}) %collective-permute-start.33) | collective-permute-done | bytes 131104 | tf_op jit(solution)/shard_map/ppermute | solution.py:213
  (89 shorter events, 36.7 us)
Async XLA Ops:
  1.7 12.1 %collective-permute-start.1 = (bf16[1,32,2048]{2,1,0:T(8,128)(2,1)S(1)}, bf16[1,32,2048]{2,1,0:T(8,128)(2,1)S(1)}, u32[]{:S(2)}, u32[]{:S(2)}) collective-permute-start(bf16[1,32,2048]{2,1,0:T(8,128)(2,1)S(1)} %bitcast.25), channel_id=1, source_target_pairs={{0,16},{4,20},{8,24},{12,28},{16,0},{20,4},{24,8},{28,12},{1,17},{... | collective-permute-start | bytes 393224 | tf_op jit(solution)/shard_map/ppermute | solution.py:213
  5.8 10.1 %collective-permute-start.3 = (bf16[1,32,2048]{2,1,0:T(8,128)(2,1)S(1)}, bf16[1,32,2048]{2,1,0:T(8,128)(2,1)S(1)}, u32[]{:S(2)}, u32[]{:S(2)}) collective-permute-start(bf16[1,32,2048]{2,1,0:T(8,128)(2,1)S(1)} %bitcast.26), channel_id=1, source_target_pairs={{0,8},{4,12},{8,0},{12,4},{16,24},{20,28},{24,16},{28,20},{1,9},{5... | collective-permute-start | bytes 393224 | tf_op jit(solution)/shard_map/ppermute | solution.py:213
  7.3 8.8 %collective-permute-start.5 = (bf16[1,32,2048]{2,1,0:T(8,128)(2,1)S(1)}, bf16[1,32,2048]{2,1,0:T(8,128)(2,1)S(1)}, u32[]{:S(2)}, u32[]{:S(2)}) collective-permute-start(bf16[1,32,2048]{2,1,0:T(8,128)(2,1)S(1)} %bitcast.27), channel_id=1, source_target_pairs={{0,24},{4,28},{8,16},{12,20},{16,8},{20,12},{24,0},{28,4},{1,25},{... | collective-permute-start | bytes 393224 | tf_op jit(solution)/shard_map/ppermute | solution.py:213
  7.3 17.0 %collective-permute-start.7 = (bf16[1,32,2048]{2,1,0:T(8,128)(2,1)S(1)}, bf16[1,32,2048]{2,1,0:T(8,128)(2,1)S(1)}, u32[]{:S(2)}, u32[]{:S(2)}) collective-permute-start(bf16[1,32,2048]{2,1,0:T(8,128)(2,1)S(1)} %bitcast.28), channel_id=1, source_target_pairs={{0,4},{4,0},{8,12},{12,8},{16,20},{20,16},{24,28},{28,24},{1,5},{5... | collective-permute-start | bytes 393224 | tf_op jit(solution)/shard_map/ppermute | solution.py:213
  13.7 10.6 %collective-permute-start.2 = (bf16[1,32,2048]{2,1,0:T(8,128)(2,1)S(1)}, bf16[1,32,2048]{2,1,0:T(8,128)(2,1)S(1)}, u32[]{:S(2)}, u32[]{:S(2)}) collective-permute-start(bf16[1,32,2048]{2,1,0:T(8,128)(2,1)S(1)} %collective-permute-done.1.refs_1_), channel_id=1, source_target_pairs={{0,4},{4,0},{8,12},{12,8},{16,20},{20,16},{24,28},{28,24},{1,5},{5... | collective-permute-start | bytes 393224 | tf_op jit(solution)/shard_map/ppermute | solution.py:213
  15.9 8.5 %collective-permute-start.4 = (bf16[1,32,2048]{2,1,0:T(8,128)(2,1)S(1)}, bf16[1,32,2048]{2,1,0:T(8,128)(2,1)S(1)}, u32[]{:S(2)}, u32[]{:S(2)}) collective-permute-start(bf16[1,32,2048]{2,1,0:T(8,128)(2,1)S(1)} %collective-permute-done.3.refs_3_), channel_id=1, source_target_pairs={{0,4},{4,0},{8,12},{12,8},{16,20},{20,16},{24,28},{28,24},{1,5},{5... | collective-permute-start | bytes 393224 | tf_op jit(solution)/shard_map/ppermute | solution.py:213
  16.1 8.2 %collective-permute-start.6 = (bf16[1,32,2048]{2,1,0:T(8,128)(2,1)S(1)}, bf16[1,32,2048]{2,1,0:T(8,128)(2,1)S(1)}, u32[]{:S(2)}, u32[]{:S(2)}) collective-permute-start(bf16[1,32,2048]{2,1,0:T(8,128)(2,1)S(1)} %collective-permute-done.5.refs_5_), channel_id=1, source_target_pairs={{0,4},{4,0},{8,12},{12,8},{16,20},{20,16},{24,28},{28,24},{1,5},{5... | collective-permute-start | bytes 393224 | tf_op jit(solution)/shard_map/ppermute | solution.py:213
  18.6 8.1 %collective-permute-start = (f32[34,2048]{1,0:T(8,128)S(1)}, f32[34,2048]{1,0:T(8,128)S(1)}, u32[]{:S(2)}, u32[]{:S(2)}) collective-permute-start(f32[34,2048]{1,0:T(8,128)S(1)} %get-tuple-element.49), channel_id=1, source_target_pairs={{0,2},{1,3},{2,0},{3,1},{4,6},{5,7},{6,4},{7,5},{8,10},{9,11},{10,... | collective-permute-start | bytes 835592 | tf_op jit(solution)/shard_map/ppermute | solution.py:213
  26.9 8.4 %collective-permute-start.9 = (bf16[2,32,2048]{2,1,0:T(8,128)(2,1)S(1)}, bf16[2,32,2048]{2,1,0:T(8,128)(2,1)S(1)}, u32[]{:S(2)}, u32[]{:S(2)}) collective-permute-start(bf16[2,32,2048]{2,1,0:T(8,128)(2,1)S(1)} %fusion.1), channel_id=1, source_target_pairs={{0,2},{1,3},{2,0},{3,1},{4,6},{5,7},{6,4},{7,5},{8,10},{9,11},{10,... | collective-permute-start | bytes 786440 | tf_op jit(solution)/shard_map/ppermute | solution.py:213
  39.4 8.9 %collective-permute-start.13 = (bf16[1,32,2048]{2,1,0:T(8,128)(2,1)S(1)}, bf16[1,32,2048]{2,1,0:T(8,128)(2,1)S(1)}, u32[]{:S(2)}, u32[]{:S(2)}) collective-permute-start(bf16[1,32,2048]{2,1,0:T(8,128)(2,1)S(1)} %get-tuple-element.23), channel_id=1, source_target_pairs={{0,4},{4,0},{8,12},{12,8},{16,20},{20,16},{24,28},{28,24},{1,5},{5... | collective-permute-start | bytes 393224 | tf_op jit(solution)/shard_map/ppermute | solution.py:213
  42.2 8.7 %collective-permute-start.15 = (bf16[1,32,2048]{2,1,0:T(8,128)(2,1)S(1)}, bf16[1,32,2048]{2,1,0:T(8,128)(2,1)S(1)}, u32[]{:S(2)}, u32[]{:S(2)}) collective-permute-start(bf16[1,32,2048]{2,1,0:T(8,128)(2,1)S(1)} %get-tuple-element.25), channel_id=1, source_target_pairs={{0,4},{4,0},{8,12},{12,8},{16,20},{20,16},{24,28},{28,24},{1,5},{5... | collective-permute-start | bytes 393224 | tf_op jit(solution)/shard_map/ppermute | solution.py:213
  43.2 10.7 %collective-permute-start.17 = (bf16[1,32,2048]{2,1,0:T(8,128)(2,1)S(1)}, bf16[1,32,2048]{2,1,0:T(8,128)(2,1)S(1)}, u32[]{:S(2)}, u32[]{:S(2)}) collective-permute-start(bf16[1,32,2048]{2,1,0:T(8,128)(2,1)S(1)} %get-tuple-element.26), channel_id=1, source_target_pairs={{0,4},{4,0},{8,12},{12,8},{16,20},{20,16},{24,28},{28,24},{1,5},{5... | collective-permute-start | bytes 393224 | tf_op jit(solution)/shard_map/ppermute | solution.py:213
  44.3 9.8 %collective-permute-start.12 = (bf16[1,32,2048]{2,1,0:T(8,128)(2,1)S(1)}, bf16[1,32,2048]{2,1,0:T(8,128)(2,1)S(1)}, u32[]{:S(2)}, u32[]{:S(2)}) collective-permute-start(bf16[1,32,2048]{2,1,0:T(8,128)(2,1)S(1)} %add_convert_fusion.5), channel_id=1, source_target_pairs={{0,16},{4,20},{8,24},{12,28},{16,0},{20,4},{24,8},{28,12},{1,17},{... | collective-permute-start | bytes 393224 | tf_op jit(solution)/shard_map/ppermute | solution.py:213
  51.0 8.2 %collective-permute-start.16 = (bf16[1,32,2048]{2,1,0:T(8,128)(2,1)S(1)}, bf16[1,32,2048]{2,1,0:T(8,128)(2,1)S(1)}, u32[]{:S(2)}, u32[]{:S(2)}) collective-permute-start(bf16[1,32,2048]{2,1,0:T(8,128)(2,1)S(1)} %add_convert_fusion.3), channel_id=1, source_target_pairs={{0,24},{4,28},{8,16},{12,20},{16,8},{20,12},{24,0},{28,4},{1,25},{... | collective-permute-start | bytes 393224 | tf_op jit(solution)/shard_map/ppermute | solution.py:213
  59.3 11.3 %collective-permute-start.18 = (bf16[1,32,2048]{2,1,0:T(8,128)(2,1)S(1)}, bf16[1,32,2048]{2,1,0:T(8,128)(2,1)S(1)}, u32[]{:S(2)}, u32[]{:S(2)}) collective-permute-start(bf16[1,32,2048]{2,1,0:T(8,128)(2,1)S(1)} %get-tuple-element.28.refs_7_), channel_id=1, source_target_pairs={{0,16},{4,20},{8,24},{12,28},{16,0},{20,4},{24,8},{28,12},{1,17},{... | collective-permute-start | bytes 393224 | tf_op jit(solution)/shard_map/ppermute | solution.py:213
  62.2 8.9 %collective-permute-start.20 = (bf16[1,32,2048]{2,1,0:T(8,128)(2,1)S(1)}, bf16[1,32,2048]{2,1,0:T(8,128)(2,1)S(1)}, u32[]{:S(2)}, u32[]{:S(2)}) collective-permute-start(bf16[1,32,2048]{2,1,0:T(8,128)(2,1)S(1)} %get-tuple-element.28.refs_7_), channel_id=1, source_target_pairs={{0,8},{4,12},{8,0},{12,4},{16,24},{20,28},{24,16},{28,20},{1,9},{5... | collective-permute-start | bytes 393224 | tf_op jit(solution)/shard_map/ppermute | solution.py:213
  62.2 10.5 %collective-permute-start.22 = (bf16[1,32,2048]{2,1,0:T(8,128)(2,1)S(1)}, bf16[1,32,2048]{2,1,0:T(8,128)(2,1)S(1)}, u32[]{:S(2)}, u32[]{:S(2)}) collective-permute-start(bf16[1,32,2048]{2,1,0:T(8,128)(2,1)S(1)} %get-tuple-element.28.refs_7_), channel_id=1, source_target_pairs={{0,24},{4,28},{8,16},{12,20},{16,8},{20,12},{24,0},{28,4},{1,25},{... | collective-permute-start | bytes 393224 | tf_op jit(solution)/shard_map/ppermute | solution.py:213
  64.1 9.1 %collective-permute-start.24 = (bf16[1,32,2048]{2,1,0:T(8,128)(2,1)S(1)}, bf16[1,32,2048]{2,1,0:T(8,128)(2,1)S(1)}, u32[]{:S(2)}, u32[]{:S(2)}) collective-permute-start(bf16[1,32,2048]{2,1,0:T(8,128)(2,1)S(1)} %get-tuple-element.28.refs_7_), channel_id=1, source_target_pairs={{0,4},{4,0},{8,12},{12,8},{16,20},{20,16},{24,28},{28,24},{1,5},{5... | collective-permute-start | bytes 393224 | tf_op jit(solution)/shard_map/ppermute | solution.py:213
  81.2 11.2 %collective-permute-start.26 = (bf16[2,32,2048]{2,1,0:T(8,128)(2,1)S(1)}, bf16[2,32,2048]{2,1,0:T(8,128)(2,1)S(1)}, u32[]{:S(2)}, u32[]{:S(2)}) collective-permute-start(bf16[2,32,2048]{2,1,0:T(8,128)(2,1)S(1)} %fusion.2), channel_id=1, source_target_pairs={{0,2},{1,3},{2,0},{3,1},{4,6},{5,7},{6,4},{7,5},{8,10},{9,11},{10,... | collective-permute-start | bytes 786440 | tf_op jit(solution)/shard_map/ppermute | solution.py:213
  95.4 8.8 %collective-permute-start.30 = (bf16[1,32,2048]{2,1,0:T(8,128)(2,1)S(1)}, bf16[1,32,2048]{2,1,0:T(8,128)(2,1)S(1)}, u32[]{:S(2)}, u32[]{:S(2)}) collective-permute-start(bf16[1,32,2048]{2,1,0:T(8,128)(2,1)S(1)} %get-tuple-element.32), channel_id=1, source_target_pairs={{0,4},{4,0},{8,12},{12,8},{16,20},{20,16},{24,28},{28,24},{1,5},{5... | collective-permute-start | bytes 393224 | tf_op jit(solution)/shard_map/ppermute | solution.py:213
  99.3 7.7 %collective-permute-start.32 = (bf16[1,32,2048]{2,1,0:T(8,128)(2,1)S(1)}, bf16[1,32,2048]{2,1,0:T(8,128)(2,1)S(1)}, u32[]{:S(2)}, u32[]{:S(2)}) collective-permute-start(bf16[1,32,2048]{2,1,0:T(8,128)(2,1)S(1)} %get-tuple-element.34), channel_id=1, source_target_pairs={{0,4},{4,0},{8,12},{12,8},{16,20},{20,16},{24,28},{28,24},{1,5},{5... | collective-permute-start | bytes 393224 | tf_op jit(solution)/shard_map/ppermute | solution.py:213
  99.4 10.8 %collective-permute-start.34 = (bf16[1,32,2048]{2,1,0:T(8,128)(2,1)S(1)}, bf16[1,32,2048]{2,1,0:T(8,128)(2,1)S(1)}, u32[]{:S(2)}, u32[]{:S(2)}) collective-permute-start(bf16[1,32,2048]{2,1,0:T(8,128)(2,1)S(1)} %get-tuple-element.35), channel_id=1, source_target_pairs={{0,4},{4,0},{8,12},{12,8},{16,20},{20,16},{24,28},{28,24},{1,5},{5... | collective-permute-start | bytes 393224 | tf_op jit(solution)/shard_map/ppermute | solution.py:213
  101.4 8.8 %collective-permute-start.29 = (bf16[1,32,2048]{2,1,0:T(8,128)(2,1)S(1)}, bf16[1,32,2048]{2,1,0:T(8,128)(2,1)S(1)}, u32[]{:S(2)}, u32[]{:S(2)}) collective-permute-start(bf16[1,32,2048]{2,1,0:T(8,128)(2,1)S(1)} %add_convert_fusion.2), channel_id=1, source_target_pairs={{0,16},{4,20},{8,24},{12,28},{16,0},{20,4},{24,8},{28,12},{1,17},{... | collective-permute-start | bytes 393224 | tf_op jit(solution)/shard_map/ppermute | solution.py:213
  107.0 6.9 %collective-permute-start.33 = (bf16[1,32,2048]{2,1,0:T(8,128)(2,1)S(1)}, bf16[1,32,2048]{2,1,0:T(8,128)(2,1)S(1)}, u32[]{:S(2)}, u32[]{:S(2)}) collective-permute-start(bf16[1,32,2048]{2,1,0:T(8,128)(2,1)S(1)} %add_convert_fusion), channel_id=1, source_target_pairs={{0,24},{4,28},{8,16},{12,20},{16,8},{20,12},{24,0},{28,4},{1,25},{... | collective-permute-start | bytes 393224 | tf_op jit(solution)/shard_map/ppermute | solution.py:213
  (15 other events, 111.7 us)

commit v11 on v10

--- a/solution.py
+++ b/solution.py
@@ -17,7 +17,6 @@
 step_dual = 0.4
 
 VMEM_LIMIT = 24 * 1024 * 1024
-FETCH_LIMIT = 46 * 1024 * 1024
 LOAD_LIMIT = 42 * 1024 * 1024
 
 
@@ -44,13 +43,12 @@
 
 class Plan(typing.NamedTuple):
     forward: bool
-    fetched: bool
     senders: tuple
     outs: tuple
     begun: bool
 
 
-def sweep_kernel(plan, per_in, info, tiles, *refs):
+def sweep_kernel(plan, per_in, places, live, tiles, *refs):
     refs = list(refs)
     parts = [refs.pop(0) for _ in plan.senders]
     begun = [refs.pop(0) for _ in plan.outs] if plan.begun else []
@@ -59,17 +57,14 @@
     sums = [
         result[0] if out.direct else refs.pop(0) for out, result in zip(plan.outs, results)
     ]
-    held, arrived = refs if plan.fetched else (tiles, None)
-    slots = tiles.shape[0]
-    live = info[2 * slots]
-    me_in = info[2 * slots + 1]
-    me_out = info[2 * slots + 2]
+    me_in = lax.axis_index("row" if plan.forward else "col")
+    me_out = lax.axis_index("col" if plan.forward else "row")
     span_in = operand.shape[1]
     span_out = tiles.shape[1] if plan.forward else tiles.shape[2]
     per_out = sums[0].shape[2] // span_out
 
     def ends(slot):
-        row, col = info[2 * slot], info[2 * slot + 1]
+        row, col = places[0, slot], places[1, slot]
         return (col, row) if plan.forward else (row, col)
 
     def accepted(slot):
@@ -80,19 +75,6 @@
             target, sum((out.ks for out in plan.outs), ())
         )
 
-    def fetch(slot):
-        return pltpu.make_async_copy(tiles.at[slot], held.at[slot], arrived.at[slot])
-
-    if plan.fetched:
-
-        def start(slot, carry):
-            @pl.when(accepted(slot))
-            def _():
-                fetch(slot).start()
-
-            return carry
-
-        lax.fori_loop(0, live, start, 0)
     for i, total in enumerate(sums):
         total[...] = begun[i][...] if begun else jnp.zeros_like(total)
 
@@ -109,11 +91,9 @@
                 def _():
                     operand[...] = part[position(source, ks), :, pl.ds(place, span_in)]
 
-            if plan.fetched:
-                fetch(slot).wait()
             contract = (((1,), (1,)), ((), ())) if plan.forward else (((1,), (0,)), ((), ()))
             term = lax.dot_general(
-                operand[...], held[slot], contract, preferred_element_type=jnp.float32
+                operand[...], tiles[slot], contract, preferred_element_type=jnp.float32
             )
             to = pl.multiple_of((block_out % per_out) * span_out, span_out)
             for total, out in zip(sums, plan.outs):
@@ -124,7 +104,7 @@
 
         return carry
 
-    lax.fori_loop(0, live, visit, 0)
+    lax.fori_loop(0, live[0, 0], visit, 0)
     for out, result, total in zip(plan.outs, results, sums):
         if not out.direct:
             each = len(out.ks) // len(result)
@@ -132,7 +112,7 @@
                 ref[...] = total[i * each : (i + 1) * each].astype(ref.dtype)
 
 
-def sweep(plan, tiles, info, parts, begun, wide):
+def sweep(plan, tiles, places, live, parts, begun, wide):
     slots, rows_tile, cols_tile = tiles.shape
     width = parts[0].shape[1]
     span_in = cols_tile if plan.forward else rows_tile
@@ -147,38 +127,29 @@
             out_shape += [jax.ShapeDtypeStruct((1, width, wide), out.kind)] * many
         if not out.direct:
             scratch += [pltpu.VMEM((many, width, wide), jnp.float32)]
-    if plan.fetched:
-        scratch += [pltpu.VMEM(tiles.shape, tiles.dtype), pltpu.SemaphoreType.DMA((slots,))]
     vmem = pl.BlockSpec(memory_space=pltpu.VMEM)
     flat = pl.pallas_call(
         functools.partial(sweep_kernel, plan, parts[0].shape[2] // span_in),
         out_shape=out_shape,
-        in_specs=[
-            pl.BlockSpec(memory_space=pltpu.SMEM),
-            pl.BlockSpec(memory_space=pl.ANY) if plan.fetched else vmem,
-        ]
-        + [vmem] * (len(parts) + len(begun)),
+        in_specs=[pl.BlockSpec(memory_space=pltpu.SMEM)] * 2
+        + [vmem] * (1 + len(parts) + len(begun)),
         out_specs=[vmem] * len(out_shape),
         scratch_shapes=scratch,
-        compiler_params=pltpu.CompilerParams(
-            vmem_limit_bytes=FETCH_LIMIT if plan.fetched else VMEM_LIMIT
-        ),
+        compiler_params=pltpu.CompilerParams(vmem_limit_bytes=VMEM_LIMIT),
         cost_estimate=pl.CostEstimate(
             flops=slots * width * rows_tile * cols_tile,
             bytes_accessed=tiles.size,
             transcendentals=0,
         ),
         name="forward_sweep" if plan.forward else "transpose_sweep",
-    )(info, tiles, *parts, *begun)
+    )(places, live, tiles, *parts, *begun)
     flat = list(flat)
     return [
         flat.pop(0) if out.stacked else {k: flat.pop(0) for k in out.ks} for out in plan.outs
     ]
 
 
-def load_kernel(info, tiles, held, arrived):
-    live = info[2 * tiles.shape[0]]
-
+def load_kernel(live, tiles, held, arrived):
     def fetch(slot):
         return pltpu.make_async_copy(tiles.at[slot], held.at[slot], arrived.at[slot])
 
@@ -190,11 +161,11 @@
         fetch(slot).wait()
         return carry
 
-    lax.fori_loop(0, live, start, 0)
-    lax.fori_loop(0, live, finish, 0)
-
-
-def load_tiles(info, tiles):
+    lax.fori_loop(0, live[0, 0], start, 0)
+    lax.fori_loop(0, live[0, 0], finish, 0)
+
+
+def load_tiles(live, tiles):
     return pl.pallas_call(
         load_kernel,
         out_shape=jax.ShapeDtypeStruct(tiles.shape, tiles.dtype),
@@ -206,7 +177,7 @@
             flops=0, bytes_accessed=4 * tiles.size, transcendentals=0
         ),
         name="load_tiles",
-    )(info, tiles)
+    )(live, tiles)
 
 
 def swap(value, axis, size, k):
@@ -214,7 +185,7 @@
 
 
 def strides(size):
-    return sorted(range(2, size, 2), key=lambda k: (k % 4 == 0, -k))
+    return sorted(range(2, size, 2), key=lambda k: (k % 4 != 0, k))
 
 
 def gather_pairs(own, axis, size):
@@ -266,7 +237,7 @@
 
 def share_pairs(kept, sent, axis, size):
     shares = []
-    for k in strides(size)[::-1]:
+    for k in strides(size):
         pair = kept[k] + swap(sent[k + 1], axis, size, 1).astype(jnp.float32)
         shares.append(swap(pair.astype(jnp.bfloat16), axis, size, k))
     return shares + [swap(sent[1], axis, size, 1)]
@@ -297,16 +268,7 @@
     primal_start,
     dual_start,
 ):
-    blocks = tiles[0, 0]
-    info = jnp.concatenate(
-        [
-            tile_index.reshape(-1),
-            tile_count.reshape(-1),
-            lax.axis_index("col")[None],
-            lax.axis_index("row")[None],
-        ]
-    ).astype(jnp.int32)
-    info_back = jnp.concatenate([info[:-2], info[-1:], info[-2:-1]])
+    places = tile_index[0, 0].T
     dual = dual_start[:, 0, :]
     rounded_dual = [dual.astype(jnp.bfloat16)[None]]
     state = jnp.concatenate([primal_start[:, 0, :], carbon, completion])
@@ -319,19 +281,19 @@
     whole, rounded = jnp.float32, jnp.bfloat16
     order = [k for pair in strides(cols)[::-1] + [0] for k in (pair + 1, pair)]
     mine, other = (tuple(range(p, rows, 2)) for p in (0, 1))
+    blocks = load_tiles(tile_count, tiles[0, 0])
     keep = tuple(range(0, cols, 2))
-    leave = [k + 1 for k in strides(cols)[::-1] + [0]]
+    leave = [k + 1 for k in strides(cols) + [0]]
     first, then = tuple(leave[:2]), tuple(leave[2:])
-    blocks = load_tiles(info, blocks)
     for step in range(ITERS):
         dual_parts = gather_pairs(rounded_dual[0], "col", cols)
         sent, kept = [
             sweep(
                 Plan(
-                    False, False, tuple((k,) for k in order),
+                    False, tuple((k,) for k in order),
                     (Out(other, rounded, True) if sending else Out(mine, whole, True),), False,
                 ),
-                blocks, info, [dual_parts[k] for k in order], [], primal.shape[2],
+                blocks, places, tile_count, [dual_parts[k] for k in order], [], primal.shape[2],
             )[0]
             for sending in (True, False)
         ]
@@ -341,15 +303,15 @@
         primal = fresh
         extra = [extra, swap(extra, "row", rows, 1)]
         (sent,) = sweep(
-            Plan(True, False, (mine, other), (Out(first, rounded, False),), False),
-            blocks, info_back, extra, [], dual.shape[1],
+            Plan(True, (mine, other), (Out(first, rounded, False),), False),
+            blocks, places, tile_count, extra, [], dual.shape[1],
         )
         rest, kept = sweep(
             Plan(
-                True, False, (mine, other),
+                True, (mine, other),
                 (Out(then, rounded, False), Out(keep, whole, False)), False,
             ),
-            blocks, info_back, extra, [], dual.shape[1],
+            blocks, places, tile_count, extra, [], dual.shape[1],
         )
         sent |= rest
         shares = share_pairs(kept, sent, "col", cols)

time: 116 us -> 112 us (0.966); the launches traced: 115 us -> 112 us
  waiting for transfers between devices: 44.9 us -> 51.2 us
  Pallas kernels: 13.8 us -> 9.21 us
  starting transfers between devices: 48.8 us -> 45.4 us
    ppermute x35, waiting for transfers between devices: 44.9 us -> 51.2 us  [swap(): return lax.ppermute(value, axis, [(i, i ^ k) for i in range(size)])]
    ppermute x35, starting transfers between devices: 48.8 us -> 45.4 us  [swap(): return lax.ppermute(value, axis, [(i, i ^ k) for i in range(size)])]
    pallas_call x8, Pallas kernels: 10.3 us -> 6.9 us  [sweep(): pl.pallas_call(functools.partial(sweep_kernel, plan, parts[0].shape[2] //...]
    pallas_call x1, Pallas kernels: 2.48 us -> 1.3 us  [load_tiles(): pl.pallas_call(load_kernel, out_shape=jax.ShapeDtypeStruct(tiles.shape, t...]
    unnamed x14 -> x15, local copies, waits for them, and re-layouts: 3.91 us -> 3.17 us
  transfers between devices with their start and end apart: 35 -> 35, of which waited for: 17 -> 20; matrix products, arithmetic and copies ran while one was open for 4% -> 3% of each run, Pallas kernels for 9% -> 5%
where the time goes in v11:
time: 112 us
  waiting for transfers between devices  51.2 us (46%)
  starting transfers between devices  45.4 us (41%)
  Pallas kernels  9.21 us (8%)
  local copies, waits for them, and re-layouts  3.22 us (3%)
  other arithmetic  1.64 us (1%)
  between operations  1.62 us (1%)
    ppermute x35, waiting for transfers between devices, swap(): return lax.ppermute(value, axis, [(i, i ^ k) for i in range(size)])  51.2 us
    ppermute x35, starting transfers between devices, swap(): return lax.ppermute(value, axis, [(i, i ^ k) for i in range(size)])  45.4 us
    pallas_call x8, Pallas kernels, sweep(): pl.pallas_call(functools.partial(sweep_kernel, plan, parts[0].shape[2] //...  6.9 us
    unnamed x15, local copies, waits for them, and re-layouts  3.17 us
  transfers between devices with their start and end apart: 35, of which 20 were waited for; matrix products, arithmetic and copies ran while one was open for 3% of the time, Pallas kernels for 5%

profile of v11, /device:TPU:0, one launch (start us, length us, event | category | flops | bytes accessed | tf_op | source)
XLA Modules:
  0.0 112.3 jit_solution(6950178162015873108)
XLA Ops:
  1.7 5.1 %collective-permute-start.1 = (bf16[1,32,2048]{2,1,0:T(8,128)(2,1)S(1)}, bf16[1,32,2048]{2,1,0:T(8,128)(2,1)S(1)}, u32[]{:S(2)}, u32[]{:S(2)}) collective-permute-start(bf16[1,32,2048]{2,1,0:T(8,128)(2,1)S(1)} %bitcast.22), channel_id=1, source_target_pairs={{0,24},{4,28},{8,16},{12,20},{16,8},{20,12},{24,0},{28,4},{1,25},{... | collective-permute-start | bytes 393224 | tf_op jit(solution)/shard_map/ppermute | solution.py:184
  7.4 1.6 %collective-permute-start.7 = (bf16[1,32,2048]{2,1,0:T(8,128)(2,1)S(1)}, bf16[1,32,2048]{2,1,0:T(8,128)(2,1)S(1)}, u32[]{:S(2)}, u32[]{:S(2)}) collective-permute-start(bf16[1,32,2048]{2,1,0:T(8,128)(2,1)S(1)} %bitcast.25), channel_id=1, source_target_pairs={{0,4},{4,0},{8,12},{12,8},{16,20},{20,16},{24,28},{28,24},{1,5},{5... | collective-permute-start | bytes 393224 | tf_op jit(solution)/shard_map/ppermute | solution.py:184
  11.1 1.7 %collective-permute-start.2 = (bf16[1,32,2048]{2,1,0:T(8,128)(2,1)S(1)}, bf16[1,32,2048]{2,1,0:T(8,128)(2,1)S(1)}, u32[]{:S(2)}, u32[]{:S(2)}) collective-permute-start(bf16[1,32,2048]{2,1,0:T(8,128)(2,1)S(1)} %collective-permute-done.1.refs_1_), channel_id=1, source_target_pairs={{0,4},{4,0},{8,12},{12,8},{16,20},{20,16},{24,28},{28,24},{1,5},{5... | collective-permute-start | bytes 393224 | tf_op jit(solution)/shard_map/ppermute | solution.py:184
  15.6 2.3 %collective-permute-done.5.refs_5_ = bf16[1,32,2048]{2,1,0:T(8,128)(2,1)S(1)} collective-permute-done((bf16[1,32,2048]{2,1,0:T(8,128)(2,1)S(1)}, bf16[1,32,2048]{2,1,0:T(8,128)(2,1)S(1)}, u32[]{:S(2)}, u32[]{:S(2)}) %collective-permute-start.5) | collective-permute-done | bytes 131104 | tf_op jit(solution)/shard_map/ppermute | solution.py:184
  25.4 3.2 %collective-permute-done = f32[34,2048]{1,0:T(8,128)S(1)} collective-permute-done((f32[34,2048]{1,0:T(8,128)S(1)}, f32[34,2048]{1,0:T(8,128)S(1)}, u32[]{:S(2)}, u32[]{:S(2)}) %collective-permute-start) | collective-permute-done | bytes 278560 | tf_op jit(solution)/shard_map/ppermute | solution.py:184
  30.4 4.8 %collective-permute-done.9 = bf16[2,32,2048]{2,1,0:T(8,128)(2,1)S(1)} collective-permute-done((bf16[2,32,2048]{2,1,0:T(8,128)(2,1)S(1)}, bf16[2,32,2048]{2,1,0:T(8,128)(2,1)S(1)}, u32[]{:S(2)}, u32[]{:S(2)}) %collective-permute-start.9) | collective-permute-done | bytes 262176 | tf_op jit(solution)/shard_map/ppermute | solution.py:184
  37.8 2.5 %collective-permute-start.11 = (bf16[1,32,2048]{2,1,0:T(8,128)(2,1)S(1)}, bf16[1,32,2048]{2,1,0:T(8,128)(2,1)S(1)}, u32[]{:S(2)}, u32[]{:S(2)}) collective-permute-start(bf16[1,32,2048]{2,1,0:T(8,128)(2,1)S(1)} %get-tuple-element.21), channel_id=1, source_target_pairs={{0,4},{4,0},{8,12},{12,8},{16,20},{20,16},{24,28},{28,24},{1,5},{5... | collective-permute-start | bytes 393224 | tf_op jit(solution)/shard_map/ppermute | solution.py:184
  41.6 2.5 %collective-permute-start.15 = (bf16[1,32,2048]{2,1,0:T(8,128)(2,1)S(1)}, bf16[1,32,2048]{2,1,0:T(8,128)(2,1)S(1)}, u32[]{:S(2)}, u32[]{:S(2)}) collective-permute-start(bf16[1,32,2048]{2,1,0:T(8,128)(2,1)S(1)} %get-tuple-element.25), channel_id=1, source_target_pairs={{0,4},{4,0},{8,12},{12,8},{16,20},{20,16},{24,28},{28,24},{1,5},{5... | collective-permute-start | bytes 393224 | tf_op jit(solution)/shard_map/ppermute | solution.py:184
  45.5 1.9 %collective-permute-done.13 = bf16[1,32,2048]{2,1,0:T(8,128)(2,1)S(1)} collective-permute-done((bf16[1,32,2048]{2,1,0:T(8,128)(2,1)S(1)}, bf16[1,32,2048]{2,1,0:T(8,128)(2,1)S(1)}, u32[]{:S(2)}, u32[]{:S(2)}) %collective-permute-start.13) | collective-permute-done | bytes 131104 | tf_op jit(solution)/shard_map/ppermute | solution.py:184
  48.4 1.8 %collective-permute-done.15 = bf16[1,32,2048]{2,1,0:T(8,128)(2,1)S(1)} collective-permute-done((bf16[1,32,2048]{2,1,0:T(8,128)(2,1)S(1)}, bf16[1,32,2048]{2,1,0:T(8,128)(2,1)S(1)}, u32[]{:S(2)}, u32[]{:S(2)}) %collective-permute-start.15) | collective-permute-done | bytes 131104 | tf_op jit(solution)/shard_map/ppermute | solution.py:184
  50.3 3.1 %collective-permute-start.16 = (bf16[1,32,2048]{2,1,0:T(8,128)(2,1)S(1)}, bf16[1,32,2048]{2,1,0:T(8,128)(2,1)S(1)}, u32[]{:S(2)}, u32[]{:S(2)}) collective-permute-start(bf16[1,32,2048]{2,1,0:T(8,128)(2,1)S(1)} %add_convert_fusion.3), channel_id=1, source_target_pairs={{0,24},{4,28},{8,16},{12,20},{16,8},{20,12},{24,0},{28,4},{1,25},{... | collective-permute-start | bytes 393224 | tf_op jit(solution)/shard_map/ppermute | solution.py:184
  53.5 4.4 %collective-permute-done.14.refs_1_ = bf16[1,32,2048]{2,1,0:T(8,128)(2,1)S(1)} collective-permute-done((bf16[1,32,2048]{2,1,0:T(8,128)(2,1)S(1)}, bf16[1,32,2048]{2,1,0:T(8,128)(2,1)S(1)}, u32[]{:S(2)}, u32[]{:S(2)}) %collective-permute-start.14) | collective-permute-done | bytes 131104 | tf_op jit(solution)/shard_map/ppermute | solution.py:184
  58.0 2.4 %collective-permute-start.18 = (bf16[1,32,2048]{2,1,0:T(8,128)(2,1)S(1)}, bf16[1,32,2048]{2,1,0:T(8,128)(2,1)S(1)}, u32[]{:S(2)}, u32[]{:S(2)}) collective-permute-start(bf16[1,32,2048]{2,1,0:T(8,128)(2,1)S(1)} %get-tuple-element.28.refs_7_), channel_id=1, source_target_pairs={{0,24},{4,28},{8,16},{12,20},{16,8},{20,12},{24,0},{28,4},{1,25},{... | collective-permute-start | bytes 393224 | tf_op jit(solution)/shard_map/ppermute | solution.py:184
  64.0 2.2 %collective-permute-done.18.refs_1_ = bf16[1,32,2048]{2,1,0:T(8,128)(2,1)S(1)} collective-permute-done((bf16[1,32,2048]{2,1,0:T(8,128)(2,1)S(1)}, bf16[1,32,2048]{2,1,0:T(8,128)(2,1)S(1)}, u32[]{:S(2)}, u32[]{:S(2)}) %collective-permute-start.18) | collective-permute-done | bytes 131104 | tf_op jit(solution)/shard_map/ppermute | solution.py:184
  66.2 1.7 %collective-permute-start.19 = (bf16[1,32,2048]{2,1,0:T(8,128)(2,1)S(1)}, bf16[1,32,2048]{2,1,0:T(8,128)(2,1)S(1)}, u32[]{:S(2)}, u32[]{:S(2)}) collective-permute-start(bf16[1,32,2048]{2,1,0:T(8,128)(2,1)S(1)} %collective-permute-done.18.refs_1_), channel_id=1, source_target_pairs={{0,4},{4,0},{8,12},{12,8},{16,20},{20,16},{24,28},{28,24},{1,5},{5... | collective-permute-start | bytes 393224 | tf_op jit(solution)/shard_map/ppermute | solution.py:184
  68.7 3.1 %collective-permute-done.22.refs_5_ = bf16[1,32,2048]{2,1,0:T(8,128)(2,1)S(1)} collective-permute-done((bf16[1,32,2048]{2,1,0:T(8,128)(2,1)S(1)}, bf16[1,32,2048]{2,1,0:T(8,128)(2,1)S(1)}, u32[]{:S(2)}, u32[]{:S(2)}) %collective-permute-start.22) | collective-permute-done | bytes 131104 | tf_op jit(solution)/shard_map/ppermute | solution.py:184
  73.1 3.6 %collective-permute-done.23.refs_4_ = bf16[1,32,2048]{2,1,0:T(8,128)(2,1)S(1)} collective-permute-done((bf16[1,32,2048]{2,1,0:T(8,128)(2,1)S(1)}, bf16[1,32,2048]{2,1,0:T(8,128)(2,1)S(1)}, u32[]{:S(2)}, u32[]{:S(2)}) %collective-permute-start.23) | collective-permute-done | bytes 131104 | tf_op jit(solution)/shard_map/ppermute | solution.py:184
  79.4 8.5 %collective-permute-done.26 = bf16[2,32,2048]{2,1,0:T(8,128)(2,1)S(1)} collective-permute-done((bf16[2,32,2048]{2,1,0:T(8,128)(2,1)S(1)}, bf16[2,32,2048]{2,1,0:T(8,128)(2,1)S(1)}, u32[]{:S(2)}, u32[]{:S(2)}) %collective-permute-start.26) | collective-permute-done | bytes 262176 | tf_op jit(solution)/shard_map/ppermute | solution.py:184
  90.5 2.6 %collective-permute-start.28 = (bf16[1,32,2048]{2,1,0:T(8,128)(2,1)S(1)}, bf16[1,32,2048]{2,1,0:T(8,128)(2,1)S(1)}, u32[]{:S(2)}, u32[]{:S(2)}) collective-permute-start(bf16[1,32,2048]{2,1,0:T(8,128)(2,1)S(1)} %get-tuple-element.30), channel_id=1, source_target_pairs={{0,4},{4,0},{8,12},{12,8},{16,20},{20,16},{24,28},{28,24},{1,5},{5... | collective-permute-start | bytes 393224 | tf_op jit(solution)/shard_map/ppermute | solution.py:184
  94.4 2.5 %collective-permute-start.32 = (bf16[1,32,2048]{2,1,0:T(8,128)(2,1)S(1)}, bf16[1,32,2048]{2,1,0:T(8,128)(2,1)S(1)}, u32[]{:S(2)}, u32[]{:S(2)}) collective-permute-start(bf16[1,32,2048]{2,1,0:T(8,128)(2,1)S(1)} %get-tuple-element.34), channel_id=1, source_target_pairs={{0,4},{4,0},{8,12},{12,8},{16,20},{20,16},{24,28},{28,24},{1,5},{5... | collective-permute-start | bytes 393224 | tf_op jit(solution)/shard_map/ppermute | solution.py:184
  97.4 2.3 %collective-permute-start.29 = (bf16[1,32,2048]{2,1,0:T(8,128)(2,1)S(1)}, bf16[1,32,2048]{2,1,0:T(8,128)(2,1)S(1)}, u32[]{:S(2)}, u32[]{:S(2)}) collective-permute-start(bf16[1,32,2048]{2,1,0:T(8,128)(2,1)S(1)} %add_convert_fusion.2), channel_id=1, source_target_pairs={{0,16},{4,20},{8,24},{12,28},{16,0},{20,4},{24,8},{28,12},{1,17},{... | collective-permute-start | bytes 393224 | tf_op jit(solution)/shard_map/ppermute | solution.py:184
  100.5 2.5 %collective-permute-done.32 = bf16[1,32,2048]{2,1,0:T(8,128)(2,1)S(1)} collective-permute-done((bf16[1,32,2048]{2,1,0:T(8,128)(2,1)S(1)}, bf16[1,32,2048]{2,1,0:T(8,128)(2,1)S(1)}, u32[]{:S(2)}, u32[]{:S(2)}) %collective-permute-start.32) | collective-permute-done | bytes 131104 | tf_op jit(solution)/shard_map/ppermute | solution.py:184
  103.0 2.1 %collective-permute-start.33 = (bf16[1,32,2048]{2,1,0:T(8,128)(2,1)S(1)}, bf16[1,32,2048]{2,1,0:T(8,128)(2,1)S(1)}, u32[]{:S(2)}, u32[]{:S(2)}) collective-permute-start(bf16[1,32,2048]{2,1,0:T(8,128)(2,1)S(1)} %add_convert_fusion), channel_id=1, source_target_pairs={{0,24},{4,28},{8,16},{12,20},{16,8},{20,12},{24,0},{28,4},{1,25},{... | collective-permute-start | bytes 393224 | tf_op jit(solution)/shard_map/ppermute | solution.py:184
  106.2 5.2 %collective-permute-done.31.refs_1_ = bf16[1,32,2048]{2,1,0:T(8,128)(2,1)S(1)} collective-permute-done((bf16[1,32,2048]{2,1,0:T(8,128)(2,1)S(1)}, bf16[1,32,2048]{2,1,0:T(8,128)(2,1)S(1)}, u32[]{:S(2)}, u32[]{:S(2)}) %collective-permute-start.31) | collective-permute-done | bytes 131104 | tf_op jit(solution)/shard_map/ppermute | solution.py:184
  (88 shorter events, 36.8 us)
Async XLA Ops:
  1.7 9.5 %collective-permute-start.1 = (bf16[1,32,2048]{2,1,0:T(8,128)(2,1)S(1)}, bf16[1,32,2048]{2,1,0:T(8,128)(2,1)S(1)}, u32[]{:S(2)}, u32[]{:S(2)}) collective-permute-start(bf16[1,32,2048]{2,1,0:T(8,128)(2,1)S(1)} %bitcast.22), channel_id=1, source_target_pairs={{0,24},{4,28},{8,16},{12,20},{16,8},{20,12},{24,0},{28,4},{1,25},{... | collective-permute-start | bytes 393224 | tf_op jit(solution)/shard_map/ppermute | solution.py:184
  6.8 7.4 %collective-permute-start.3 = (bf16[1,32,2048]{2,1,0:T(8,128)(2,1)S(1)}, bf16[1,32,2048]{2,1,0:T(8,128)(2,1)S(1)}, u32[]{:S(2)}, u32[]{:S(2)}) collective-permute-start(bf16[1,32,2048]{2,1,0:T(8,128)(2,1)S(1)} %bitcast.23), channel_id=1, source_target_pairs={{0,8},{4,12},{8,0},{12,4},{16,24},{20,28},{24,16},{28,20},{1,9},{5... | collective-permute-start | bytes 393224 | tf_op jit(solution)/shard_map/ppermute | solution.py:184
  6.8 11.1 %collective-permute-start.5 = (bf16[1,32,2048]{2,1,0:T(8,128)(2,1)S(1)}, bf16[1,32,2048]{2,1,0:T(8,128)(2,1)S(1)}, u32[]{:S(2)}, u32[]{:S(2)}) collective-permute-start(bf16[1,32,2048]{2,1,0:T(8,128)(2,1)S(1)} %bitcast.24), channel_id=1, source_target_pairs={{0,16},{4,20},{8,24},{12,28},{16,0},{20,4},{24,8},{28,12},{1,17},{... | collective-permute-start | bytes 393224 | tf_op jit(solution)/shard_map/ppermute | solution.py:184
  7.4 16.3 %collective-permute-start.7 = (bf16[1,32,2048]{2,1,0:T(8,128)(2,1)S(1)}, bf16[1,32,2048]{2,1,0:T(8,128)(2,1)S(1)}, u32[]{:S(2)}, u32[]{:S(2)}) collective-permute-start(bf16[1,32,2048]{2,1,0:T(8,128)(2,1)S(1)} %bitcast.25), channel_id=1, source_target_pairs={{0,4},{4,0},{8,12},{12,8},{16,20},{20,16},{24,28},{28,24},{1,5},{5... | collective-permute-start | bytes 393224 | tf_op jit(solution)/shard_map/ppermute | solution.py:184
  11.1 12.5 %collective-permute-start.2 = (bf16[1,32,2048]{2,1,0:T(8,128)(2,1)S(1)}, bf16[1,32,2048]{2,1,0:T(8,128)(2,1)S(1)}, u32[]{:S(2)}, u32[]{:S(2)}) collective-permute-start(bf16[1,32,2048]{2,1,0:T(8,128)(2,1)S(1)} %collective-permute-done.1.refs_1_), channel_id=1, source_target_pairs={{0,4},{4,0},{8,12},{12,8},{16,20},{20,16},{24,28},{28,24},{1,5},{5... | collective-permute-start | bytes 393224 | tf_op jit(solution)/shard_map/ppermute | solution.py:184
  14.2 9.5 %collective-permute-start.4 = (bf16[1,32,2048]{2,1,0:T(8,128)(2,1)S(1)}, bf16[1,32,2048]{2,1,0:T(8,128)(2,1)S(1)}, u32[]{:S(2)}, u32[]{:S(2)}) collective-permute-start(bf16[1,32,2048]{2,1,0:T(8,128)(2,1)S(1)} %collective-permute-done.3.refs_3_), channel_id=1, source_target_pairs={{0,4},{4,0},{8,12},{12,8},{16,20},{20,16},{24,28},{28,24},{1,5},{5... | collective-permute-start | bytes 393224 | tf_op jit(solution)/shard_map/ppermute | solution.py:184
  20.1 8.6 %collective-permute-start = (f32[34,2048]{1,0:T(8,128)S(1)}, f32[34,2048]{1,0:T(8,128)S(1)}, u32[]{:S(2)}, u32[]{:S(2)}) collective-permute-start(f32[34,2048]{1,0:T(8,128)S(1)} %get-tuple-element.47), channel_id=1, source_target_pairs={{0,2},{1,3},{2,0},{3,1},{4,6},{5,7},{6,4},{7,5},{8,10},{9,11},{10,... | collective-permute-start | bytes 835592 | tf_op jit(solution)/shard_map/ppermute | solution.py:184
  40.3 7.2 %collective-permute-start.13 = (bf16[1,32,2048]{2,1,0:T(8,128)(2,1)S(1)}, bf16[1,32,2048]{2,1,0:T(8,128)(2,1)S(1)}, u32[]{:S(2)}, u32[]{:S(2)}) collective-permute-start(bf16[1,32,2048]{2,1,0:T(8,128)(2,1)S(1)} %get-tuple-element.23), channel_id=1, source_target_pairs={{0,4},{4,0},{8,12},{12,8},{16,20},{20,16},{24,28},{28,24},{1,5},{5... | collective-permute-start | bytes 393224 | tf_op jit(solution)/shard_map/ppermute | solution.py:184
  41.6 8.6 %collective-permute-start.15 = (bf16[1,32,2048]{2,1,0:T(8,128)(2,1)S(1)}, bf16[1,32,2048]{2,1,0:T(8,128)(2,1)S(1)}, u32[]{:S(2)}, u32[]{:S(2)}) collective-permute-start(bf16[1,32,2048]{2,1,0:T(8,128)(2,1)S(1)} %get-tuple-element.25), channel_id=1, source_target_pairs={{0,4},{4,0},{8,12},{12,8},{16,20},{20,16},{24,28},{28,24},{1,5},{5... | collective-permute-start | bytes 393224 | tf_op jit(solution)/shard_map/ppermute | solution.py:184
  44.1 9.3 %collective-permute-start.17 = (bf16[1,32,2048]{2,1,0:T(8,128)(2,1)S(1)}, bf16[1,32,2048]{2,1,0:T(8,128)(2,1)S(1)}, u32[]{:S(2)}, u32[]{:S(2)}) collective-permute-start(bf16[1,32,2048]{2,1,0:T(8,128)(2,1)S(1)} %get-tuple-element.26), channel_id=1, source_target_pairs={{0,4},{4,0},{8,12},{12,8},{16,20},{20,16},{24,28},{28,24},{1,5},{5... | collective-permute-start | bytes 393224 | tf_op jit(solution)/shard_map/ppermute | solution.py:184
  44.6 8.8 %collective-permute-start.12 = (bf16[1,32,2048]{2,1,0:T(8,128)(2,1)S(1)}, bf16[1,32,2048]{2,1,0:T(8,128)(2,1)S(1)}, u32[]{:S(2)}, u32[]{:S(2)}) collective-permute-start(bf16[1,32,2048]{2,1,0:T(8,128)(2,1)S(1)} %add_convert_fusion.5), channel_id=1, source_target_pairs={{0,16},{4,20},{8,24},{12,28},{16,0},{20,4},{24,8},{28,12},{1,17},{... | collective-permute-start | bytes 393224 | tf_op jit(solution)/shard_map/ppermute | solution.py:184
  47.5 10.4 %collective-permute-start.14 = (bf16[1,32,2048]{2,1,0:T(8,128)(2,1)S(1)}, bf16[1,32,2048]{2,1,0:T(8,128)(2,1)S(1)}, u32[]{:S(2)}, u32[]{:S(2)}) collective-permute-start(bf16[1,32,2048]{2,1,0:T(8,128)(2,1)S(1)} %add_convert_fusion.4), channel_id=1, source_target_pairs={{0,8},{4,12},{8,0},{12,4},{16,24},{20,28},{24,16},{28,20},{1,9},{5... | collective-permute-start | bytes 393224 | tf_op jit(solution)/shard_map/ppermute | solution.py:184
  50.3 7.6 %collective-permute-start.16 = (bf16[1,32,2048]{2,1,0:T(8,128)(2,1)S(1)}, bf16[1,32,2048]{2,1,0:T(8,128)(2,1)S(1)}, u32[]{:S(2)}, u32[]{:S(2)}) collective-permute-start(bf16[1,32,2048]{2,1,0:T(8,128)(2,1)S(1)} %add_convert_fusion.3), channel_id=1, source_target_pairs={{0,24},{4,28},{8,16},{12,20},{16,8},{20,12},{24,0},{28,4},{1,25},{... | collective-permute-start | bytes 393224 | tf_op jit(solution)/shard_map/ppermute | solution.py:184
  58.0 8.2 %collective-permute-start.18 = (bf16[1,32,2048]{2,1,0:T(8,128)(2,1)S(1)}, bf16[1,32,2048]{2,1,0:T(8,128)(2,1)S(1)}, u32[]{:S(2)}, u32[]{:S(2)}) collective-permute-start(bf16[1,32,2048]{2,1,0:T(8,128)(2,1)S(1)} %get-tuple-element.28.refs_7_), channel_id=1, source_target_pairs={{0,24},{4,28},{8,16},{12,20},{16,8},{20,12},{24,0},{28,4},{1,25},{... | collective-permute-start | bytes 393224 | tf_op jit(solution)/shard_map/ppermute | solution.py:184
  60.4 7.5 %collective-permute-start.20 = (bf16[1,32,2048]{2,1,0:T(8,128)(2,1)S(1)}, bf16[1,32,2048]{2,1,0:T(8,128)(2,1)S(1)}, u32[]{:S(2)}, u32[]{:S(2)}) collective-permute-start(bf16[1,32,2048]{2,1,0:T(8,128)(2,1)S(1)} %get-tuple-element.28.refs_7_), channel_id=1, source_target_pairs={{0,8},{4,12},{8,0},{12,4},{16,24},{20,28},{24,16},{28,20},{1,9},{5... | collective-permute-start | bytes 393224 | tf_op jit(solution)/shard_map/ppermute | solution.py:184
  61.3 10.5 %collective-permute-start.22 = (bf16[1,32,2048]{2,1,0:T(8,128)(2,1)S(1)}, bf16[1,32,2048]{2,1,0:T(8,128)(2,1)S(1)}, u32[]{:S(2)}, u32[]{:S(2)}) collective-permute-start(bf16[1,32,2048]{2,1,0:T(8,128)(2,1)S(1)} %get-tuple-element.28.refs_7_), channel_id=1, source_target_pairs={{0,16},{4,20},{8,24},{12,28},{16,0},{20,4},{24,8},{28,12},{1,17},{... | collective-permute-start | bytes 393224 | tf_op jit(solution)/shard_map/ppermute | solution.py:184
  62.4 10.6 %collective-permute-start.24 = (bf16[1,32,2048]{2,1,0:T(8,128)(2,1)S(1)}, bf16[1,32,2048]{2,1,0:T(8,128)(2,1)S(1)}, u32[]{:S(2)}, u32[]{:S(2)}) collective-permute-start(bf16[1,32,2048]{2,1,0:T(8,128)(2,1)S(1)} %get-tuple-element.28.refs_7_), channel_id=1, source_target_pairs={{0,4},{4,0},{8,12},{12,8},{16,20},{20,16},{24,28},{28,24},{1,5},{5... | collective-permute-start | bytes 393224 | tf_op jit(solution)/shard_map/ppermute | solution.py:184
  79.4 8.6 %collective-permute-start.26 = (bf16[2,32,2048]{2,1,0:T(8,128)(2,1)S(1)}, bf16[2,32,2048]{2,1,0:T(8,128)(2,1)S(1)}, u32[]{:S(2)}, u32[]{:S(2)}) collective-permute-start(bf16[2,32,2048]{2,1,0:T(8,128)(2,1)S(1)} %fusion.2), channel_id=1, source_target_pairs={{0,2},{1,3},{2,0},{3,1},{4,6},{5,7},{6,4},{7,5},{8,10},{9,11},{10,... | collective-permute-start | bytes 786440 | tf_op jit(solution)/shard_map/ppermute | solution.py:184
  93.1 7.1 %collective-permute-start.30 = (bf16[1,32,2048]{2,1,0:T(8,128)(2,1)S(1)}, bf16[1,32,2048]{2,1,0:T(8,128)(2,1)S(1)}, u32[]{:S(2)}, u32[]{:S(2)}) collective-permute-start(bf16[1,32,2048]{2,1,0:T(8,128)(2,1)S(1)} %get-tuple-element.32), channel_id=1, source_target_pairs={{0,4},{4,0},{8,12},{12,8},{16,20},{20,16},{24,28},{28,24},{1,5},{5... | collective-permute-start | bytes 393224 | tf_op jit(solution)/shard_map/ppermute | solution.py:184
  94.4 8.7 %collective-permute-start.32 = (bf16[1,32,2048]{2,1,0:T(8,128)(2,1)S(1)}, bf16[1,32,2048]{2,1,0:T(8,128)(2,1)S(1)}, u32[]{:S(2)}, u32[]{:S(2)}) collective-permute-start(bf16[1,32,2048]{2,1,0:T(8,128)(2,1)S(1)} %get-tuple-element.34), channel_id=1, source_target_pairs={{0,4},{4,0},{8,12},{12,8},{16,20},{20,16},{24,28},{28,24},{1,5},{5... | collective-permute-start | bytes 393224 | tf_op jit(solution)/shard_map/ppermute | solution.py:184
  96.9 9.3 %collective-permute-start.34 = (bf16[1,32,2048]{2,1,0:T(8,128)(2,1)S(1)}, bf16[1,32,2048]{2,1,0:T(8,128)(2,1)S(1)}, u32[]{:S(2)}, u32[]{:S(2)}) collective-permute-start(bf16[1,32,2048]{2,1,0:T(8,128)(2,1)S(1)} %get-tuple-element.35), channel_id=1, source_target_pairs={{0,4},{4,0},{8,12},{12,8},{16,20},{20,16},{24,28},{28,24},{1,5},{5... | collective-permute-start | bytes 393224 | tf_op jit(solution)/shard_map/ppermute | solution.py:184
  97.4 8.8 %collective-permute-start.29 = (bf16[1,32,2048]{2,1,0:T(8,128)(2,1)S(1)}, bf16[1,32,2048]{2,1,0:T(8,128)(2,1)S(1)}, u32[]{:S(2)}, u32[]{:S(2)}) collective-permute-start(bf16[1,32,2048]{2,1,0:T(8,128)(2,1)S(1)} %add_convert_fusion.2), channel_id=1, source_target_pairs={{0,16},{4,20},{8,24},{12,28},{16,0},{20,4},{24,8},{28,12},{1,17},{... | collective-permute-start | bytes 393224 | tf_op jit(solution)/shard_map/ppermute | solution.py:184
  100.2 11.2 %collective-permute-start.31 = (bf16[1,32,2048]{2,1,0:T(8,128)(2,1)S(1)}, bf16[1,32,2048]{2,1,0:T(8,128)(2,1)S(1)}, u32[]{:S(2)}, u32[]{:S(2)}) collective-permute-start(bf16[1,32,2048]{2,1,0:T(8,128)(2,1)S(1)} %add_convert_fusion.1), channel_id=1, source_target_pairs={{0,8},{4,12},{8,0},{12,4},{16,24},{20,28},{24,16},{28,20},{1,9},{5... | collective-permute-start | bytes 393224 | tf_op jit(solution)/shard_map/ppermute | solution.py:184
  103.0 8.4 %collective-permute-start.33 = (bf16[1,32,2048]{2,1,0:T(8,128)(2,1)S(1)}, bf16[1,32,2048]{2,1,0:T(8,128)(2,1)S(1)}, u32[]{:S(2)}, u32[]{:S(2)}) collective-permute-start(bf16[1,32,2048]{2,1,0:T(8,128)(2,1)S(1)} %add_convert_fusion), channel_id=1, source_target_pairs={{0,24},{4,28},{8,16},{12,20},{16,8},{20,12},{24,0},{28,4},{1,25},{... | collective-permute-start | bytes 393224 | tf_op jit(solution)/shard_map/ppermute | solution.py:184
  (16 other events, 116.8 us)

commit v12 on v11

--- a/solution.py
+++ b/solution.py
@@ -21,7 +21,7 @@
 
 
 def among(value, ks):
-    return functools.reduce(jnp.logical_or, [value == k for k in ks])
+    return ((sum(1 << k for k in ks) >> value) & 1) == 1
 
 
 def position(value, ks):
@@ -38,52 +38,43 @@
 
     @property
     def direct(self):
-        return self.kind == jnp.float32 and self.stacked
+        return self.kind == jnp.float32
 
 
 class Plan(typing.NamedTuple):
     forward: bool
     senders: tuple
     outs: tuple
-    begun: bool
 
 
 def sweep_kernel(plan, per_in, places, live, tiles, *refs):
     refs = list(refs)
     parts = [refs.pop(0) for _ in plan.senders]
-    begun = [refs.pop(0) for _ in plan.outs] if plan.begun else []
     results = [[refs.pop(0) for _ in (out.ks[:1] if out.stacked else out.ks)] for out in plan.outs]
     operand = refs.pop(0)
-    sums = [
-        result[0] if out.direct else refs.pop(0) for out, result in zip(plan.outs, results)
-    ]
+    sums = [result if out.direct else [refs.pop(0)] for out, result in zip(plan.outs, results)]
     me_in = lax.axis_index("row" if plan.forward else "col")
     me_out = lax.axis_index("col" if plan.forward else "row")
     span_in = operand.shape[1]
     span_out = tiles.shape[1] if plan.forward else tiles.shape[2]
-    per_out = sums[0].shape[2] // span_out
+    per_out = sums[0][0].shape[2] // span_out
 
     def ends(slot):
         row, col = places[0, slot], places[1, slot]
         return (col, row) if plan.forward else (row, col)
 
-    def accepted(slot):
+    receivers = sum((out.ks for out in plan.outs), ())
+
+    for total in sum(sums, []):
+        total[...] = jnp.zeros_like(total)
+
+    def visit(slot, carry):
         block_in, block_out = ends(slot)
-        source = (block_in // per_in) ^ me_in
         target = (block_out // per_out) ^ me_out
-        return among(source, sum(plan.senders, ())) & among(
-            target, sum((out.ks for out in plan.outs), ())
-        )
-
-    for i, total in enumerate(sums):
-        total[...] = begun[i][...] if begun else jnp.zeros_like(total)
-
-    def visit(slot, carry):
-        @pl.when(accepted(slot))
+
+        @pl.when(among(target, receivers))
         def _():
-            block_in, block_out = ends(slot)
             source = (block_in // per_in) ^ me_in
-            target = (block_out // per_out) ^ me_out
             place = pl.multiple_of((block_in % per_in) * span_in, span_in)
             for part, ks in zip(parts, plan.senders):
 
@@ -96,27 +87,27 @@
                 operand[...], tiles[slot], contract, preferred_element_type=jnp.float32
             )
             to = pl.multiple_of((block_out % per_out) * span_out, span_out)
-            for total, out in zip(sums, plan.outs):
-
-                @pl.when(among(target, out.ks))
-                def _():
-                    total[position(target, out.ks), :, pl.ds(to, span_out)] += term
+            for totals, out in zip(sums, plan.outs):
+                for total, ks in zip(totals, [out.ks] if len(totals) == 1 else [(k,) for k in out.ks]):
+
+                    @pl.when(among(target, ks) if ks != receivers else True)
+                    def _():
+                        total[position(target, ks), :, pl.ds(to, span_out)] += term
 
         return carry
 
     lax.fori_loop(0, live[0, 0], visit, 0)
-    for out, result, total in zip(plan.outs, results, sums):
+    for out, result, (total, *_) in zip(plan.outs, results, sums):
         if not out.direct:
             each = len(out.ks) // len(result)
             for i, ref in enumerate(result):
                 ref[...] = total[i * each : (i + 1) * each].astype(ref.dtype)
 
 
-def sweep(plan, tiles, places, live, parts, begun, wide):
+def sweep(plan, tiles, places, live, parts, wide):
     slots, rows_tile, cols_tile = tiles.shape
     width = parts[0].shape[1]
     span_in = cols_tile if plan.forward else rows_tile
-    plan = plan._replace(begun=bool(begun))
     out_shape = []
     scratch = [pltpu.VMEM((width, span_in), jnp.bfloat16)]
     for out in plan.outs:
@@ -132,7 +123,7 @@
         functools.partial(sweep_kernel, plan, parts[0].shape[2] // span_in),
         out_shape=out_shape,
         in_specs=[pl.BlockSpec(memory_space=pltpu.SMEM)] * 2
-        + [vmem] * (1 + len(parts) + len(begun)),
+        + [vmem] * (1 + len(parts)),
         out_specs=[vmem] * len(out_shape),
         scratch_shapes=scratch,
         compiler_params=pltpu.CompilerParams(vmem_limit_bytes=VMEM_LIMIT),
@@ -142,7 +133,7 @@
             transcendentals=0,
         ),
         name="forward_sweep" if plan.forward else "transpose_sweep",
-    )(places, live, tiles, *parts, *begun)
+    )(places, live, tiles, *parts)
     flat = list(flat)
     return [
         flat.pop(0) if out.stacked else {k: flat.pop(0) for k in out.ks} for out in plan.outs
@@ -291,9 +282,9 @@
             sweep(
                 Plan(
                     False, tuple((k,) for k in order),
-                    (Out(other, rounded, True) if sending else Out(mine, whole, True),), False,
+                    (Out(other, rounded, True) if sending else Out(mine, whole, True),),
                 ),
-                blocks, places, tile_count, [dual_parts[k] for k in order], [], primal.shape[2],
+                blocks, places, tile_count, [dual_parts[k] for k in order], primal.shape[2],
             )[0]
             for sending in (True, False)
         ]
@@ -303,15 +294,15 @@
         primal = fresh
         extra = [extra, swap(extra, "row", rows, 1)]
         (sent,) = sweep(
-            Plan(True, (mine, other), (Out(first, rounded, False),), False),
-            blocks, places, tile_count, extra, [], dual.shape[1],
+            Plan(True, (mine, other), (Out(first, rounded, False),)),
+            blocks, places, tile_count, extra, dual.shape[1],
         )
         rest, kept = sweep(
             Plan(
                 True, (mine, other),
-                (Out(then, rounded, False), Out(keep, whole, False)), False,
+                (Out(then, rounded, False), Out(keep, whole, False)),
             ),
-            blocks, places, tile_count, extra, [], dual.shape[1],
+            blocks, places, tile_count, extra, dual.shape[1],
         )
         sent |= rest
         shares = share_pairs(kept, sent, "col", cols)

time: 112 us -> 113 us (level); the launches traced: 112 us -> 112 us
  Pallas kernels: 9.21 us -> 14.8 us
  waiting for transfers between devices: 51.2 us -> 47.6 us
  starting transfers between devices: 45.4 us -> 43.1 us
    pallas_call x8, Pallas kernels: 6.9 us -> 11.5 us  [sweep(): pl.pallas_call(functools.partial(sweep_kernel, plan, parts[0].shape[2] //...]
    ppermute x35, waiting for transfers between devices: 51.2 us -> 47.6 us  [swap(): return lax.ppermute(value, axis, [(i, i ^ k) for i in range(size)])]
    ppermute x35, starting transfers between devices: 45.4 us -> 43.1 us  [swap(): return lax.ppermute(value, axis, [(i, i ^ k) for i in range(size)])]
  transfers between devices with their start and end apart: 35 -> 35, of which waited for: 20 -> 23; matrix products, arithmetic and copies ran while one was open for 3% -> 3% of each run, Pallas kernels for 5% -> 8%
where the time goes in v12:
time: 113 us; the launch traced here: 112 us
  waiting for transfers between devices  47.6 us (42%)
  starting transfers between devices  43.1 us (38%)
  Pallas kernels  14.8 us (13%)
  local copies, waits for them, and re-layouts  3.22 us (3%)
  other arithmetic  1.64 us (1%)
  between operations  1.62 us (1%)
    ppermute x35, waiting for transfers between devices, swap(): return lax.ppermute(value, axis, [(i, i ^ k) for i in range(size)])  47.6 us
    ppermute x35, starting transfers between devices, swap(): return lax.ppermute(value, axis, [(i, i ^ k) for i in range(size)])  43.1 us
    pallas_call x8, Pallas kernels, sweep(): pl.pallas_call(functools.partial(sweep_kernel, plan, parts[0].shape[2] //...  11.5 us
    unnamed x15, local copies, waits for them, and re-layouts  3.17 us
  transfers between devices with their start and end apart: 35, of which 23 were waited for; matrix products, arithmetic and copies ran while one was open for 3% of the time, Pallas kernels for 8%

profile of v12, /device:TPU:0, one launch (start us, length us, event | category | flops | bytes accessed | tf_op | source)
XLA Modules:
  0.0 111.9 jit_solution(17962050942987194427)
XLA Ops:
  1.7 5.1 %collective-permute-start.1 = (bf16[1,32,2048]{2,1,0:T(8,128)(2,1)S(1)}, bf16[1,32,2048]{2,1,0:T(8,128)(2,1)S(1)}, u32[]{:S(2)}, u32[]{:S(2)}) collective-permute-start(bf16[1,32,2048]{2,1,0:T(8,128)(2,1)S(1)} %bitcast.22), channel_id=1, source_target_pairs={{0,24},{4,28},{8,16},{12,20},{16,8},{20,12},{24,0},{28,4},{1,25},{... | collective-permute-start | bytes 393224 | tf_op jit(solution)/shard_map/ppermute | solution.py:175
  11.1 1.7 %collective-permute-start.2 = (bf16[1,32,2048]{2,1,0:T(8,128)(2,1)S(1)}, bf16[1,32,2048]{2,1,0:T(8,128)(2,1)S(1)}, u32[]{:S(2)}, u32[]{:S(2)}) collective-permute-start(bf16[1,32,2048]{2,1,0:T(8,128)(2,1)S(1)} %collective-permute-done.1.refs_1_), channel_id=1, source_target_pairs={{0,4},{4,0},{8,12},{12,8},{16,20},{20,16},{24,28},{28,24},{1,5},{5... | collective-permute-start | bytes 393224 | tf_op jit(solution)/shard_map/ppermute | solution.py:175
  15.6 2.3 %collective-permute-done.5.refs_5_ = bf16[1,32,2048]{2,1,0:T(8,128)(2,1)S(1)} collective-permute-done((bf16[1,32,2048]{2,1,0:T(8,128)(2,1)S(1)}, bf16[1,32,2048]{2,1,0:T(8,128)(2,1)S(1)}, u32[]{:S(2)}, u32[]{:S(2)}) %collective-permute-start.5) | collective-permute-done | bytes 131104 | tf_op jit(solution)/shard_map/ppermute | solution.py:175
  22.4 2.3 %load_tiles.1.tiles = bf16[8,1024,512]{2,1,0:T(8,128)(2,1)S(1)} custom-call(s32[1,1]{1,0:T(1,128)S(6)} %copy.28.live, bf16[8,1024,512]{2,1,0:T(8,128)(2,1)} %bitcast.37), custom_call_target="tpu_custom_call" | custom-call | bytes 16777216 | tf_op jit(solution)/shard_map/load_tiles/pallas_call | solution.py:160
  30.4 6.0 %collective-permute-done.9 = bf16[2,32,2048]{2,1,0:T(8,128)(2,1)S(1)} collective-permute-done((bf16[2,32,2048]{2,1,0:T(8,128)(2,1)S(1)}, bf16[2,32,2048]{2,1,0:T(8,128)(2,1)S(1)}, u32[]{:S(2)}, u32[]{:S(2)}) %collective-permute-start.9) | collective-permute-done | bytes 262176 | tf_op jit(solution)/shard_map/ppermute | solution.py:175
  39.9 2.0 %collective-permute-start.13 = (bf16[1,32,2048]{2,1,0:T(8,128)(2,1)S(1)}, bf16[1,32,2048]{2,1,0:T(8,128)(2,1)S(1)}, u32[]{:S(2)}, u32[]{:S(2)}) collective-permute-start(bf16[1,32,2048]{2,1,0:T(8,128)(2,1)S(1)} %get-tuple-element.23), channel_id=1, source_target_pairs={{0,4},{4,0},{8,12},{12,8},{16,20},{20,16},{24,28},{28,24},{1,5},{5... | collective-permute-start | bytes 393224 | tf_op jit(solution)/shard_map/ppermute | solution.py:175
  41.9 1.7 %forward_sweep.4 = (bf16[1,32,2048]{2,1,0:T(8,128)(2,1)S(1)}, bf16[1,32,2048]{2,1,0:T(8,128)(2,1)S(1)}, f32[1,32,2048]{2,1,0:T(8,128)S(1)}, f32[1,32,2048]{2,1,0...) custom-call(s32[2,8]{1,0:T(2,128)S(1)} %bitcast.32, s32[1,1]{1,0:T(1,128)S(6)} %copy.28.live, ...), custom_call_target="tpu_custom_call" | custom-call | flops 134217728 | bytes 4194304 | tf_op jit(solution)/shard_map/forward_sweep/pallas_call | solution.py:122
  43.7 2.0 %collective-permute-start.17 = (bf16[1,32,2048]{2,1,0:T(8,128)(2,1)S(1)}, bf16[1,32,2048]{2,1,0:T(8,128)(2,1)S(1)}, u32[]{:S(2)}, u32[]{:S(2)}) collective-permute-start(bf16[1,32,2048]{2,1,0:T(8,128)(2,1)S(1)} %get-tuple-element.26), channel_id=1, source_target_pairs={{0,4},{4,0},{8,12},{12,8},{16,20},{20,16},{24,28},{28,24},{1,5},{5... | collective-permute-start | bytes 393224 | tf_op jit(solution)/shard_map/ppermute | solution.py:175
  46.4 2.7 %collective-permute-done.13 = bf16[1,32,2048]{2,1,0:T(8,128)(2,1)S(1)} collective-permute-done((bf16[1,32,2048]{2,1,0:T(8,128)(2,1)S(1)}, bf16[1,32,2048]{2,1,0:T(8,128)(2,1)S(1)}, u32[]{:S(2)}, u32[]{:S(2)}) %collective-permute-start.13) | collective-permute-done | bytes 131104 | tf_op jit(solution)/shard_map/ppermute | solution.py:175
  49.1 3.5 %collective-permute-start.14 = (bf16[1,32,2048]{2,1,0:T(8,128)(2,1)S(1)}, bf16[1,32,2048]{2,1,0:T(8,128)(2,1)S(1)}, u32[]{:S(2)}, u32[]{:S(2)}) collective-permute-start(bf16[1,32,2048]{2,1,0:T(8,128)(2,1)S(1)} %add_convert_fusion.4), channel_id=1, source_target_pairs={{0,8},{4,12},{8,0},{12,4},{16,24},{20,28},{24,16},{28,20},{1,9},{5... | collective-permute-start | bytes 393224 | tf_op jit(solution)/shard_map/ppermute | solution.py:175
  52.6 3.5 %collective-permute-start.16 = (bf16[1,32,2048]{2,1,0:T(8,128)(2,1)S(1)}, bf16[1,32,2048]{2,1,0:T(8,128)(2,1)S(1)}, u32[]{:S(2)}, u32[]{:S(2)}) collective-permute-start(bf16[1,32,2048]{2,1,0:T(8,128)(2,1)S(1)} %add_convert_fusion.3), channel_id=1, source_target_pairs={{0,24},{4,28},{8,16},{12,20},{16,8},{20,12},{24,0},{28,4},{1,25},{... | collective-permute-start | bytes 393224 | tf_op jit(solution)/shard_map/ppermute | solution.py:175
  56.9 2.5 %collective-permute-done.16.refs_2_ = bf16[1,32,2048]{2,1,0:T(8,128)(2,1)S(1)} collective-permute-done((bf16[1,32,2048]{2,1,0:T(8,128)(2,1)S(1)}, bf16[1,32,2048]{2,1,0:T(8,128)(2,1)S(1)}, u32[]{:S(2)}, u32[]{:S(2)}) %collective-permute-start.16) | collective-permute-done | bytes 131104 | tf_op jit(solution)/shard_map/ppermute | solution.py:175
  59.6 3.6 %collective-permute-start.18 = (bf16[1,32,2048]{2,1,0:T(8,128)(2,1)S(1)}, bf16[1,32,2048]{2,1,0:T(8,128)(2,1)S(1)}, u32[]{:S(2)}, u32[]{:S(2)}) collective-permute-start(bf16[1,32,2048]{2,1,0:T(8,128)(2,1)S(1)} %get-tuple-element.28.refs_7_), channel_id=1, source_target_pairs={{0,24},{4,28},{8,16},{12,20},{16,8},{20,12},{24,0},{28,4},{1,25},{... | collective-permute-start | bytes 393224 | tf_op jit(solution)/shard_map/ppermute | solution.py:175
  64.3 3.2 %collective-permute-done.18.refs_1_ = bf16[1,32,2048]{2,1,0:T(8,128)(2,1)S(1)} collective-permute-done((bf16[1,32,2048]{2,1,0:T(8,128)(2,1)S(1)}, bf16[1,32,2048]{2,1,0:T(8,128)(2,1)S(1)}, u32[]{:S(2)}, u32[]{:S(2)}) %collective-permute-start.18) | collective-permute-done | bytes 131104 | tf_op jit(solution)/shard_map/ppermute | solution.py:175
  68.1 2.4 %collective-permute-done.20.refs_3_ = bf16[1,32,2048]{2,1,0:T(8,128)(2,1)S(1)} collective-permute-done((bf16[1,32,2048]{2,1,0:T(8,128)(2,1)S(1)}, bf16[1,32,2048]{2,1,0:T(8,128)(2,1)S(1)}, u32[]{:S(2)}, u32[]{:S(2)}) %collective-permute-start.20) | collective-permute-done | bytes 131104 | tf_op jit(solution)/shard_map/ppermute | solution.py:175
  72.8 2.6 %collective-permute-done.21.refs_2_ = bf16[1,32,2048]{2,1,0:T(8,128)(2,1)S(1)} collective-permute-done((bf16[1,32,2048]{2,1,0:T(8,128)(2,1)S(1)}, bf16[1,32,2048]{2,1,0:T(8,128)(2,1)S(1)}, u32[]{:S(2)}, u32[]{:S(2)}) %collective-permute-start.21) | collective-permute-done | bytes 131104 | tf_op jit(solution)/shard_map/ppermute | solution.py:175
  80.2 8.3 %collective-permute-done.26 = bf16[2,32,2048]{2,1,0:T(8,128)(2,1)S(1)} collective-permute-done((bf16[2,32,2048]{2,1,0:T(8,128)(2,1)S(1)}, bf16[2,32,2048]{2,1,0:T(8,128)(2,1)S(1)}, u32[]{:S(2)}, u32[]{:S(2)}) %collective-permute-start.26) | collective-permute-done | bytes 262176 | tf_op jit(solution)/shard_map/ppermute | solution.py:175
  92.4 1.6 %collective-permute-start.30 = (bf16[1,32,2048]{2,1,0:T(8,128)(2,1)S(1)}, bf16[1,32,2048]{2,1,0:T(8,128)(2,1)S(1)}, u32[]{:S(2)}, u32[]{:S(2)}) collective-permute-start(bf16[1,32,2048]{2,1,0:T(8,128)(2,1)S(1)} %get-tuple-element.32), channel_id=1, source_target_pairs={{0,4},{4,0},{8,12},{12,8},{16,20},{20,16},{24,28},{28,24},{1,5},{5... | collective-permute-start | bytes 393224 | tf_op jit(solution)/shard_map/ppermute | solution.py:175
  94.1 1.7 %forward_sweep.6 = (bf16[1,32,2048]{2,1,0:T(8,128)(2,1)S(1)}, bf16[1,32,2048]{2,1,0:T(8,128)(2,1)S(1)}, f32[1,32,2048]{2,1,0:T(8,128)S(1)}, f32[1,32,2048]{2,1,0...) custom-call(s32[2,8]{1,0:T(2,128)S(1)} %bitcast.36, s32[1,1]{1,0:T(1,128)S(6)} %copy.28.live, ...), custom_call_target="tpu_custom_call" | custom-call | flops 134217728 | bytes 4194304 | tf_op jit(solution)/shard_map/forward_sweep/pallas_call | solution.py:122
  96.2 1.7 %collective-permute-start.34 = (bf16[1,32,2048]{2,1,0:T(8,128)(2,1)S(1)}, bf16[1,32,2048]{2,1,0:T(8,128)(2,1)S(1)}, u32[]{:S(2)}, u32[]{:S(2)}) collective-permute-start(bf16[1,32,2048]{2,1,0:T(8,128)(2,1)S(1)} %get-tuple-element.35), channel_id=1, source_target_pairs={{0,4},{4,0},{8,12},{12,8},{16,20},{20,16},{24,28},{28,24},{1,5},{5... | collective-permute-start | bytes 393224 | tf_op jit(solution)/shard_map/ppermute | solution.py:175
  98.5 2.7 %collective-permute-done.30 = bf16[1,32,2048]{2,1,0:T(8,128)(2,1)S(1)} collective-permute-done((bf16[1,32,2048]{2,1,0:T(8,128)(2,1)S(1)}, bf16[1,32,2048]{2,1,0:T(8,128)(2,1)S(1)}, u32[]{:S(2)}, u32[]{:S(2)}) %collective-permute-start.30) | collective-permute-done | bytes 131104 | tf_op jit(solution)/shard_map/ppermute | solution.py:175
  101.3 2.3 %collective-permute-start.31 = (bf16[1,32,2048]{2,1,0:T(8,128)(2,1)S(1)}, bf16[1,32,2048]{2,1,0:T(8,128)(2,1)S(1)}, u32[]{:S(2)}, u32[]{:S(2)}) collective-permute-start(bf16[1,32,2048]{2,1,0:T(8,128)(2,1)S(1)} %add_convert_fusion.1), channel_id=1, source_target_pairs={{0,8},{4,12},{8,0},{12,4},{16,24},{20,28},{24,16},{28,20},{1,9},{5... | collective-permute-start | bytes 393224 | tf_op jit(solution)/shard_map/ppermute | solution.py:175
  104.1 3.0 %collective-permute-start.33 = (bf16[1,32,2048]{2,1,0:T(8,128)(2,1)S(1)}, bf16[1,32,2048]{2,1,0:T(8,128)(2,1)S(1)}, u32[]{:S(2)}, u32[]{:S(2)}) collective-permute-start(bf16[1,32,2048]{2,1,0:T(8,128)(2,1)S(1)} %add_convert_fusion), channel_id=1, source_target_pairs={{0,24},{4,28},{8,16},{12,20},{16,8},{20,12},{24,0},{28,4},{1,25},{... | collective-permute-start | bytes 393224 | tf_op jit(solution)/shard_map/ppermute | solution.py:175
  108.1 2.9 %collective-permute-done.33.refs_2_ = bf16[1,32,2048]{2,1,0:T(8,128)(2,1)S(1)} collective-permute-done((bf16[1,32,2048]{2,1,0:T(8,128)(2,1)S(1)}, bf16[1,32,2048]{2,1,0:T(8,128)(2,1)S(1)}, u32[]{:S(2)}, u32[]{:S(2)}) %collective-permute-start.33) | collective-permute-done | bytes 131104 | tf_op jit(solution)/shard_map/ppermute | solution.py:175
  (88 shorter events, 39.0 us)
Async XLA Ops:
  1.7 9.5 %collective-permute-start.1 = (bf16[1,32,2048]{2,1,0:T(8,128)(2,1)S(1)}, bf16[1,32,2048]{2,1,0:T(8,128)(2,1)S(1)}, u32[]{:S(2)}, u32[]{:S(2)}) collective-permute-start(bf16[1,32,2048]{2,1,0:T(8,128)(2,1)S(1)} %bitcast.22), channel_id=1, source_target_pairs={{0,24},{4,28},{8,16},{12,20},{16,8},{20,12},{24,0},{28,4},{1,25},{... | collective-permute-start | bytes 393224 | tf_op jit(solution)/shard_map/ppermute | solution.py:175
  6.8 7.4 %collective-permute-start.3 = (bf16[1,32,2048]{2,1,0:T(8,128)(2,1)S(1)}, bf16[1,32,2048]{2,1,0:T(8,128)(2,1)S(1)}, u32[]{:S(2)}, u32[]{:S(2)}) collective-permute-start(bf16[1,32,2048]{2,1,0:T(8,128)(2,1)S(1)} %bitcast.23), channel_id=1, source_target_pairs={{0,8},{4,12},{8,0},{12,4},{16,24},{20,28},{24,16},{28,20},{1,9},{5... | collective-permute-start | bytes 393224 | tf_op jit(solution)/shard_map/ppermute | solution.py:175
  6.8 11.1 %collective-permute-start.5 = (bf16[1,32,2048]{2,1,0:T(8,128)(2,1)S(1)}, bf16[1,32,2048]{2,1,0:T(8,128)(2,1)S(1)}, u32[]{:S(2)}, u32[]{:S(2)}) collective-permute-start(bf16[1,32,2048]{2,1,0:T(8,128)(2,1)S(1)} %bitcast.24), channel_id=1, source_target_pairs={{0,16},{4,20},{8,24},{12,28},{16,0},{20,4},{24,8},{28,12},{1,17},{... | collective-permute-start | bytes 393224 | tf_op jit(solution)/shard_map/ppermute | solution.py:175
  7.4 17.2 %collective-permute-start.7 = (bf16[1,32,2048]{2,1,0:T(8,128)(2,1)S(1)}, bf16[1,32,2048]{2,1,0:T(8,128)(2,1)S(1)}, u32[]{:S(2)}, u32[]{:S(2)}) collective-permute-start(bf16[1,32,2048]{2,1,0:T(8,128)(2,1)S(1)} %bitcast.25), channel_id=1, source_target_pairs={{0,4},{4,0},{8,12},{12,8},{16,20},{20,16},{24,28},{28,24},{1,5},{5... | collective-permute-start | bytes 393224 | tf_op jit(solution)/shard_map/ppermute | solution.py:175
  11.1 13.5 %collective-permute-start.2 = (bf16[1,32,2048]{2,1,0:T(8,128)(2,1)S(1)}, bf16[1,32,2048]{2,1,0:T(8,128)(2,1)S(1)}, u32[]{:S(2)}, u32[]{:S(2)}) collective-permute-start(bf16[1,32,2048]{2,1,0:T(8,128)(2,1)S(1)} %collective-permute-done.1.refs_1_), channel_id=1, source_target_pairs={{0,4},{4,0},{8,12},{12,8},{16,20},{20,16},{24,28},{28,24},{1,5},{5... | collective-permute-start | bytes 393224 | tf_op jit(solution)/shard_map/ppermute | solution.py:175
  14.2 10.5 %collective-permute-start.4 = (bf16[1,32,2048]{2,1,0:T(8,128)(2,1)S(1)}, bf16[1,32,2048]{2,1,0:T(8,128)(2,1)S(1)}, u32[]{:S(2)}, u32[]{:S(2)}) collective-permute-start(bf16[1,32,2048]{2,1,0:T(8,128)(2,1)S(1)} %collective-permute-done.3.refs_3_), channel_id=1, source_target_pairs={{0,4},{4,0},{8,12},{12,8},{16,20},{20,16},{24,28},{28,24},{1,5},{5... | collective-permute-start | bytes 393224 | tf_op jit(solution)/shard_map/ppermute | solution.py:175
  20.1 8.6 %collective-permute-start = (f32[34,2048]{1,0:T(8,128)S(1)}, f32[34,2048]{1,0:T(8,128)S(1)}, u32[]{:S(2)}, u32[]{:S(2)}) collective-permute-start(f32[34,2048]{1,0:T(8,128)S(1)} %get-tuple-element.47), channel_id=1, source_target_pairs={{0,2},{1,3},{2,0},{3,1},{4,6},{5,7},{6,4},{7,5},{8,10},{9,11},{10,... | collective-permute-start | bytes 835592 | tf_op jit(solution)/shard_map/ppermute | solution.py:175
  28.8 7.6 %collective-permute-start.9 = (bf16[2,32,2048]{2,1,0:T(8,128)(2,1)S(1)}, bf16[2,32,2048]{2,1,0:T(8,128)(2,1)S(1)}, u32[]{:S(2)}, u32[]{:S(2)}) collective-permute-start(bf16[2,32,2048]{2,1,0:T(8,128)(2,1)S(1)} %fusion.1), channel_id=1, source_target_pairs={{0,2},{1,3},{2,0},{3,1},{4,6},{5,7},{6,4},{7,5},{8,10},{9,11},{10,... | collective-permute-start | bytes 786440 | tf_op jit(solution)/shard_map/ppermute | solution.py:175
  39.9 9.2 %collective-permute-start.13 = (bf16[1,32,2048]{2,1,0:T(8,128)(2,1)S(1)}, bf16[1,32,2048]{2,1,0:T(8,128)(2,1)S(1)}, u32[]{:S(2)}, u32[]{:S(2)}) collective-permute-start(bf16[1,32,2048]{2,1,0:T(8,128)(2,1)S(1)} %get-tuple-element.23), channel_id=1, source_target_pairs={{0,4},{4,0},{8,12},{12,8},{16,20},{20,16},{24,28},{28,24},{1,5},{5... | collective-permute-start | bytes 393224 | tf_op jit(solution)/shard_map/ppermute | solution.py:175
  43.6 9.0 %collective-permute-start.15 = (bf16[1,32,2048]{2,1,0:T(8,128)(2,1)S(1)}, bf16[1,32,2048]{2,1,0:T(8,128)(2,1)S(1)}, u32[]{:S(2)}, u32[]{:S(2)}) collective-permute-start(bf16[1,32,2048]{2,1,0:T(8,128)(2,1)S(1)} %get-tuple-element.25), channel_id=1, source_target_pairs={{0,4},{4,0},{8,12},{12,8},{16,20},{20,16},{24,28},{28,24},{1,5},{5... | collective-permute-start | bytes 393224 | tf_op jit(solution)/shard_map/ppermute | solution.py:175
  43.7 12.5 %collective-permute-start.17 = (bf16[1,32,2048]{2,1,0:T(8,128)(2,1)S(1)}, bf16[1,32,2048]{2,1,0:T(8,128)(2,1)S(1)}, u32[]{:S(2)}, u32[]{:S(2)}) collective-permute-start(bf16[1,32,2048]{2,1,0:T(8,128)(2,1)S(1)} %get-tuple-element.26), channel_id=1, source_target_pairs={{0,4},{4,0},{8,12},{12,8},{16,20},{20,16},{24,28},{28,24},{1,5},{5... | collective-permute-start | bytes 393224 | tf_op jit(solution)/shard_map/ppermute | solution.py:175
  46.3 9.9 %collective-permute-start.12 = (bf16[1,32,2048]{2,1,0:T(8,128)(2,1)S(1)}, bf16[1,32,2048]{2,1,0:T(8,128)(2,1)S(1)}, u32[]{:S(2)}, u32[]{:S(2)}) collective-permute-start(bf16[1,32,2048]{2,1,0:T(8,128)(2,1)S(1)} %add_convert_fusion.5), channel_id=1, source_target_pairs={{0,16},{4,20},{8,24},{12,28},{16,0},{20,4},{24,8},{28,12},{1,17},{... | collective-permute-start | bytes 393224 | tf_op jit(solution)/shard_map/ppermute | solution.py:175
  49.1 7.8 %collective-permute-start.14 = (bf16[1,32,2048]{2,1,0:T(8,128)(2,1)S(1)}, bf16[1,32,2048]{2,1,0:T(8,128)(2,1)S(1)}, u32[]{:S(2)}, u32[]{:S(2)}) collective-permute-start(bf16[1,32,2048]{2,1,0:T(8,128)(2,1)S(1)} %add_convert_fusion.4), channel_id=1, source_target_pairs={{0,8},{4,12},{8,0},{12,4},{16,24},{20,28},{24,16},{28,20},{1,9},{5... | collective-permute-start | bytes 393224 | tf_op jit(solution)/shard_map/ppermute | solution.py:175
  59.6 7.9 %collective-permute-start.18 = (bf16[1,32,2048]{2,1,0:T(8,128)(2,1)S(1)}, bf16[1,32,2048]{2,1,0:T(8,128)(2,1)S(1)}, u32[]{:S(2)}, u32[]{:S(2)}) collective-permute-start(bf16[1,32,2048]{2,1,0:T(8,128)(2,1)S(1)} %get-tuple-element.28.refs_7_), channel_id=1, source_target_pairs={{0,24},{4,28},{8,16},{12,20},{16,8},{20,12},{24,0},{28,4},{1,25},{... | collective-permute-start | bytes 393224 | tf_op jit(solution)/shard_map/ppermute | solution.py:175
  63.2 7.3 %collective-permute-start.20 = (bf16[1,32,2048]{2,1,0:T(8,128)(2,1)S(1)}, bf16[1,32,2048]{2,1,0:T(8,128)(2,1)S(1)}, u32[]{:S(2)}, u32[]{:S(2)}) collective-permute-start(bf16[1,32,2048]{2,1,0:T(8,128)(2,1)S(1)} %get-tuple-element.28.refs_7_), channel_id=1, source_target_pairs={{0,8},{4,12},{8,0},{12,4},{16,24},{20,28},{24,16},{28,20},{1,9},{5... | collective-permute-start | bytes 393224 | tf_op jit(solution)/shard_map/ppermute | solution.py:175
  63.2 7.8 %collective-permute-start.22 = (bf16[1,32,2048]{2,1,0:T(8,128)(2,1)S(1)}, bf16[1,32,2048]{2,1,0:T(8,128)(2,1)S(1)}, u32[]{:S(2)}, u32[]{:S(2)}) collective-permute-start(bf16[1,32,2048]{2,1,0:T(8,128)(2,1)S(1)} %get-tuple-element.28.refs_7_), channel_id=1, source_target_pairs={{0,16},{4,20},{8,24},{12,28},{16,0},{20,4},{24,8},{28,12},{1,17},{... | collective-permute-start | bytes 393224 | tf_op jit(solution)/shard_map/ppermute | solution.py:175
  64.1 8.5 %collective-permute-start.24 = (bf16[1,32,2048]{2,1,0:T(8,128)(2,1)S(1)}, bf16[1,32,2048]{2,1,0:T(8,128)(2,1)S(1)}, u32[]{:S(2)}, u32[]{:S(2)}) collective-permute-start(bf16[1,32,2048]{2,1,0:T(8,128)(2,1)S(1)} %get-tuple-element.28.refs_7_), channel_id=1, source_target_pairs={{0,4},{4,0},{8,12},{12,8},{16,20},{20,16},{24,28},{28,24},{1,5},{5... | collective-permute-start | bytes 393224 | tf_op jit(solution)/shard_map/ppermute | solution.py:175
  80.2 8.4 %collective-permute-start.26 = (bf16[2,32,2048]{2,1,0:T(8,128)(2,1)S(1)}, bf16[2,32,2048]{2,1,0:T(8,128)(2,1)S(1)}, u32[]{:S(2)}, u32[]{:S(2)}) collective-permute-start(bf16[2,32,2048]{2,1,0:T(8,128)(2,1)S(1)} %fusion.2), channel_id=1, source_target_pairs={{0,2},{1,3},{2,0},{3,1},{4,6},{5,7},{6,4},{7,5},{8,10},{9,11},{10,... | collective-permute-start | bytes 786440 | tf_op jit(solution)/shard_map/ppermute | solution.py:175
  92.4 8.8 %collective-permute-start.30 = (bf16[1,32,2048]{2,1,0:T(8,128)(2,1)S(1)}, bf16[1,32,2048]{2,1,0:T(8,128)(2,1)S(1)}, u32[]{:S(2)}, u32[]{:S(2)}) collective-permute-start(bf16[1,32,2048]{2,1,0:T(8,128)(2,1)S(1)} %get-tuple-element.32), channel_id=1, source_target_pairs={{0,4},{4,0},{8,12},{12,8},{16,20},{20,16},{24,28},{28,24},{1,5},{5... | collective-permute-start | bytes 393224 | tf_op jit(solution)/shard_map/ppermute | solution.py:175
  95.7 8.3 %collective-permute-start.32 = (bf16[1,32,2048]{2,1,0:T(8,128)(2,1)S(1)}, bf16[1,32,2048]{2,1,0:T(8,128)(2,1)S(1)}, u32[]{:S(2)}, u32[]{:S(2)}) collective-permute-start(bf16[1,32,2048]{2,1,0:T(8,128)(2,1)S(1)} %get-tuple-element.34), channel_id=1, source_target_pairs={{0,4},{4,0},{8,12},{12,8},{16,20},{20,16},{24,28},{28,24},{1,5},{5... | collective-permute-start | bytes 393224 | tf_op jit(solution)/shard_map/ppermute | solution.py:175
  96.2 12.0 %collective-permute-start.34 = (bf16[1,32,2048]{2,1,0:T(8,128)(2,1)S(1)}, bf16[1,32,2048]{2,1,0:T(8,128)(2,1)S(1)}, u32[]{:S(2)}, u32[]{:S(2)}) collective-permute-start(bf16[1,32,2048]{2,1,0:T(8,128)(2,1)S(1)} %get-tuple-element.35), channel_id=1, source_target_pairs={{0,4},{4,0},{8,12},{12,8},{16,20},{20,16},{24,28},{28,24},{1,5},{5... | collective-permute-start | bytes 393224 | tf_op jit(solution)/shard_map/ppermute | solution.py:175
  98.5 9.7 %collective-permute-start.29 = (bf16[1,32,2048]{2,1,0:T(8,128)(2,1)S(1)}, bf16[1,32,2048]{2,1,0:T(8,128)(2,1)S(1)}, u32[]{:S(2)}, u32[]{:S(2)}) collective-permute-start(bf16[1,32,2048]{2,1,0:T(8,128)(2,1)S(1)} %add_convert_fusion.2), channel_id=1, source_target_pairs={{0,16},{4,20},{8,24},{12,28},{16,0},{20,4},{24,8},{28,12},{1,17},{... | collective-permute-start | bytes 393224 | tf_op jit(solution)/shard_map/ppermute | solution.py:175
  101.3 6.9 %collective-permute-start.31 = (bf16[1,32,2048]{2,1,0:T(8,128)(2,1)S(1)}, bf16[1,32,2048]{2,1,0:T(8,128)(2,1)S(1)}, u32[]{:S(2)}, u32[]{:S(2)}) collective-permute-start(bf16[1,32,2048]{2,1,0:T(8,128)(2,1)S(1)} %add_convert_fusion.1), channel_id=1, source_target_pairs={{0,8},{4,12},{8,0},{12,4},{16,24},{20,28},{24,16},{28,20},{1,9},{5... | collective-permute-start | bytes 393224 | tf_op jit(solution)/shard_map/ppermute | solution.py:175
  104.1 6.9 %collective-permute-start.33 = (bf16[1,32,2048]{2,1,0:T(8,128)(2,1)S(1)}, bf16[1,32,2048]{2,1,0:T(8,128)(2,1)S(1)}, u32[]{:S(2)}, u32[]{:S(2)}) collective-permute-start(bf16[1,32,2048]{2,1,0:T(8,128)(2,1)S(1)} %add_convert_fusion), channel_id=1, source_target_pairs={{0,24},{4,28},{8,16},{12,20},{16,8},{20,12},{24,0},{28,4},{1,25},{... | collective-permute-start | bytes 393224 | tf_op jit(solution)/shard_map/ppermute | solution.py:175
  (16 other events, 118.9 us)

commit v13 on v12

--- a/solution.py
+++ b/solution.py
@@ -47,7 +47,7 @@
     outs: tuple
 
 
-def sweep_kernel(plan, per_in, places, live, tiles, *refs):
+def sweep_kernel(plan, per_in, block_rows, block_cols, live, tiles, *refs):
     refs = list(refs)
     parts = [refs.pop(0) for _ in plan.senders]
     results = [[refs.pop(0) for _ in (out.ks[:1] if out.stacked else out.ks)] for out in plan.outs]
@@ -60,7 +60,8 @@
     per_out = sums[0][0].shape[2] // span_out
 
     def ends(slot):
-        row, col = places[0, slot], places[1, slot]
+        row = (block_rows[0, 0] >> (4 * slot)) & 15
+        col = (block_cols[0, 0] >> (4 * slot)) & 15
         return (col, row) if plan.forward else (row, col)
 
     receivers = sum((out.ks for out in plan.outs), ())
@@ -104,7 +105,7 @@
                 ref[...] = total[i * each : (i + 1) * each].astype(ref.dtype)
 
 
-def sweep(plan, tiles, places, live, parts, wide):
+def sweep(plan, tiles, places, parts, wide):
     slots, rows_tile, cols_tile = tiles.shape
     width = parts[0].shape[1]
     span_in = cols_tile if plan.forward else rows_tile
@@ -122,7 +123,7 @@
     flat = pl.pallas_call(
         functools.partial(sweep_kernel, plan, parts[0].shape[2] // span_in),
         out_shape=out_shape,
-        in_specs=[pl.BlockSpec(memory_space=pltpu.SMEM)] * 2
+        in_specs=[pl.BlockSpec(memory_space=pltpu.SMEM)] * 3
         + [vmem] * (1 + len(parts)),
         out_specs=[vmem] * len(out_shape),
         scratch_shapes=scratch,
@@ -133,7 +134,7 @@
             transcendentals=0,
         ),
         name="forward_sweep" if plan.forward else "transpose_sweep",
-    )(places, live, tiles, *parts)
+    )(*places, tiles, *parts)
     flat = list(flat)
     return [
         flat.pop(0) if out.stacked else {k: flat.pop(0) for k in out.ks} for out in plan.outs
@@ -259,7 +260,10 @@
     primal_start,
     dual_start,
 ):
-    places = tile_index[0, 0].T
+    shifts = 4 * jnp.arange(tile_index.shape[2], dtype=jnp.int32)
+    packed = jnp.sum(tile_index[0, 0] << shifts[:, None], axis=0, dtype=jnp.int32)
+    none = lax.axis_index("col") // cols
+    places = ((packed[0] | none).reshape(1, 1), (packed[1] | none).reshape(1, 1), tile_count)
     dual = dual_start[:, 0, :]
     rounded_dual = [dual.astype(jnp.bfloat16)[None]]
     state = jnp.concatenate([primal_start[:, 0, :], carbon, completion])
@@ -284,7 +288,7 @@
                     False, tuple((k,) for k in order),
                     (Out(other, rounded, True) if sending else Out(mine, whole, True),),
                 ),
-                blocks, places, tile_count, [dual_parts[k] for k in order], primal.shape[2],
+                blocks, places, [dual_parts[k] for k in order], primal.shape[2],
             )[0]
             for sending in (True, False)
         ]
@@ -295,14 +299,14 @@
         extra = [extra, swap(extra, "row", rows, 1)]
         (sent,) = sweep(
             Plan(True, (mine, other), (Out(first, rounded, False),)),
-            blocks, places, tile_count, extra, dual.shape[1],
+            blocks, places, extra, dual.shape[1],
         )
         rest, kept = sweep(
             Plan(
                 True, (mine, other),
                 (Out(then, rounded, False), Out(keep, whole, False)),
             ),
-            blocks, places, tile_count, extra, dual.shape[1],
+            blocks, places, extra, dual.shape[1],
         )
         sent |= rest
         shares = share_pairs(kept, sent, "col", cols)

time: 113 us -> 110 us (0.973); the launches traced: 112 us -> 111 us
  Pallas kernels: 14.8 us -> 4.54 us
  starting transfers between devices: 43.1 us -> 49.7 us
  between operations: 1.62 us -> 2.87 us
    pallas_call x8, Pallas kernels: 11.5 us -> 2.24 us  [sweep(): pl.pallas_call(functools.partial(sweep_kernel, plan, parts[0].shape[2] //...]
    ppermute x35, starting transfers between devices: 43.1 us -> 49.7 us  [swap(): return lax.ppermute(value, axis, [(i, i ^ k) for i in range(size)])]
    unnamed x15 -> x13, local copies, waits for them, and re-layouts: 3.17 us -> 3.59 us
  transfers between devices with their start and end apart: 35 -> 35, of which waited for: 23 -> 20; matrix products, arithmetic and copies ran while one was open for 3% -> 4% of each run, Pallas kernels for 8% -> 3%
where the time goes in v13:
time: 110 us; the launch traced here: 111 us
  starting transfers between devices  49.7 us (45%)
  waiting for transfers between devices  46.8 us (43%)
  Pallas kernels  4.54 us (4%)
  local copies, waits for them, and re-layouts  4.24 us (4%)
  between operations  2.87 us (3%)
  other arithmetic  2.42 us (2%)
    ppermute x35, starting transfers between devices, swap(): return lax.ppermute(value, axis, [(i, i ^ k) for i in range(size)])  49.7 us
    ppermute x35, waiting for transfers between devices, swap(): return lax.ppermute(value, axis, [(i, i ^ k) for i in range(size)])  46.8 us
    unnamed x13, local copies, waits for them, and re-layouts  3.59 us
    pallas_call x8, Pallas kernels, sweep(): pl.pallas_call(functools.partial(sweep_kernel, plan, parts[0].shape[2] //...  2.24 us
  transfers between devices with their start and end apart: 35, of which 20 were waited for; matrix products, arithmetic and copies ran while one was open for 4% of the time, Pallas kernels for 3%

profile of v13, /device:TPU:0, one launch (start us, length us, event | category | flops | bytes accessed | tf_op | source)
XLA Modules:
  0.0 110.6 jit_solution(3719405071683516025)
XLA Ops:
  1.7 5.1 %collective-permute-start.1 = (bf16[1,32,2048]{2,1,0:T(8,128)(2,1)S(1)}, bf16[1,32,2048]{2,1,0:T(8,128)(2,1)S(1)}, u32[]{:S(2)}, u32[]{:S(2)}) collective-permute-start(bf16[1,32,2048]{2,1,0:T(8,128)(2,1)S(1)} %bitcast.27), channel_id=1, source_target_pairs={{0,24},{4,28},{8,16},{12,20},{16,8},{20,12},{24,0},{28,4},{1,25},{... | collective-permute-start | bytes 393224 | tf_op jit(solution)/shard_map/ppermute | solution.py:176
  7.4 1.6 %collective-permute-start.7 = (bf16[1,32,2048]{2,1,0:T(8,128)(2,1)S(1)}, bf16[1,32,2048]{2,1,0:T(8,128)(2,1)S(1)}, u32[]{:S(2)}, u32[]{:S(2)}) collective-permute-start(bf16[1,32,2048]{2,1,0:T(8,128)(2,1)S(1)} %bitcast.30), channel_id=1, source_target_pairs={{0,4},{4,0},{8,12},{12,8},{16,20},{20,16},{24,28},{28,24},{1,5},{5... | collective-permute-start | bytes 393224 | tf_op jit(solution)/shard_map/ppermute | solution.py:176
  15.6 2.3 %collective-permute-done.5.refs_5_ = bf16[1,32,2048]{2,1,0:T(8,128)(2,1)S(1)} collective-permute-done((bf16[1,32,2048]{2,1,0:T(8,128)(2,1)S(1)}, bf16[1,32,2048]{2,1,0:T(8,128)(2,1)S(1)}, u32[]{:S(2)}, u32[]{:S(2)}) %collective-permute-start.5) | collective-permute-done | bytes 131104 | tf_op jit(solution)/shard_map/ppermute | solution.py:176
  25.8 2.6 %collective-permute-start.9 = (bf16[2,32,2048]{2,1,0:T(8,128)(2,1)S(1)}, bf16[2,32,2048]{2,1,0:T(8,128)(2,1)S(1)}, u32[]{:S(2)}, u32[]{:S(2)}) collective-permute-start(bf16[2,32,2048]{2,1,0:T(8,128)(2,1)S(1)} %fusion.1), channel_id=1, source_target_pairs={{0,2},{1,3},{2,0},{3,1},{4,6},{5,7},{6,4},{7,5},{8,10},{9,11},{10,... | collective-permute-start | bytes 786440 | tf_op jit(solution)/shard_map/ppermute | solution.py:176
  28.4 6.6 %collective-permute-done.9 = bf16[2,32,2048]{2,1,0:T(8,128)(2,1)S(1)} collective-permute-done((bf16[2,32,2048]{2,1,0:T(8,128)(2,1)S(1)}, bf16[2,32,2048]{2,1,0:T(8,128)(2,1)S(1)}, u32[]{:S(2)}, u32[]{:S(2)}) %collective-permute-start.9) | collective-permute-done | bytes 262176 | tf_op jit(solution)/shard_map/ppermute | solution.py:176
  37.2 1.9 %collective-permute-start.13 = (bf16[1,32,2048]{2,1,0:T(8,128)(2,1)S(1)}, bf16[1,32,2048]{2,1,0:T(8,128)(2,1)S(1)}, u32[]{:S(2)}, u32[]{:S(2)}) collective-permute-start(bf16[1,32,2048]{2,1,0:T(8,128)(2,1)S(1)} %get-tuple-element.23), channel_id=1, source_target_pairs={{0,4},{4,0},{8,12},{12,8},{16,20},{20,16},{24,28},{28,24},{1,5},{5... | collective-permute-start | bytes 393224 | tf_op jit(solution)/shard_map/ppermute | solution.py:176
  39.9 1.9 %collective-permute-start.17 = (bf16[1,32,2048]{2,1,0:T(8,128)(2,1)S(1)}, bf16[1,32,2048]{2,1,0:T(8,128)(2,1)S(1)}, u32[]{:S(2)}, u32[]{:S(2)}) collective-permute-start(bf16[1,32,2048]{2,1,0:T(8,128)(2,1)S(1)} %get-tuple-element.26), channel_id=1, source_target_pairs={{0,4},{4,0},{8,12},{12,8},{16,20},{20,16},{24,28},{28,24},{1,5},{5... | collective-permute-start | bytes 393224 | tf_op jit(solution)/shard_map/ppermute | solution.py:176
  41.7 1.6 %collective-permute-done.11 = bf16[1,32,2048]{2,1,0:T(8,128)(2,1)S(1)} collective-permute-done((bf16[1,32,2048]{2,1,0:T(8,128)(2,1)S(1)}, bf16[1,32,2048]{2,1,0:T(8,128)(2,1)S(1)}, u32[]{:S(2)}, u32[]{:S(2)}) %collective-permute-start.11) | collective-permute-done | bytes 131104 | tf_op jit(solution)/shard_map/ppermute | solution.py:176
  43.4 2.3 %collective-permute-start.12 = (bf16[1,32,2048]{2,1,0:T(8,128)(2,1)S(1)}, bf16[1,32,2048]{2,1,0:T(8,128)(2,1)S(1)}, u32[]{:S(2)}, u32[]{:S(2)}) collective-permute-start(bf16[1,32,2048]{2,1,0:T(8,128)(2,1)S(1)} %add_convert_fusion.5), channel_id=1, source_target_pairs={{0,16},{4,20},{8,24},{12,28},{16,0},{20,4},{24,8},{28,12},{1,17},{... | collective-permute-start | bytes 393224 | tf_op jit(solution)/shard_map/ppermute | solution.py:176
  49.0 3.7 %collective-permute-start.16 = (bf16[1,32,2048]{2,1,0:T(8,128)(2,1)S(1)}, bf16[1,32,2048]{2,1,0:T(8,128)(2,1)S(1)}, u32[]{:S(2)}, u32[]{:S(2)}) collective-permute-start(bf16[1,32,2048]{2,1,0:T(8,128)(2,1)S(1)} %add_convert_fusion.3), channel_id=1, source_target_pairs={{0,24},{4,28},{8,16},{12,20},{16,8},{20,12},{24,0},{28,4},{1,25},{... | collective-permute-start | bytes 393224 | tf_op jit(solution)/shard_map/ppermute | solution.py:176
  53.2 3.8 %collective-permute-done.16.refs_2_ = bf16[1,32,2048]{2,1,0:T(8,128)(2,1)S(1)} collective-permute-done((bf16[1,32,2048]{2,1,0:T(8,128)(2,1)S(1)}, bf16[1,32,2048]{2,1,0:T(8,128)(2,1)S(1)}, u32[]{:S(2)}, u32[]{:S(2)}) %collective-permute-start.16) | collective-permute-done | bytes 131104 | tf_op jit(solution)/shard_map/ppermute | solution.py:176
  57.1 2.7 %collective-permute-start.18 = (bf16[1,32,2048]{2,1,0:T(8,128)(2,1)S(1)}, bf16[1,32,2048]{2,1,0:T(8,128)(2,1)S(1)}, u32[]{:S(2)}, u32[]{:S(2)}) collective-permute-start(bf16[1,32,2048]{2,1,0:T(8,128)(2,1)S(1)} %get-tuple-element.28.refs_7_), channel_id=1, source_target_pairs={{0,24},{4,28},{8,16},{12,20},{16,8},{20,12},{24,0},{28,4},{1,25},{... | collective-permute-start | bytes 393224 | tf_op jit(solution)/shard_map/ppermute | solution.py:176
  61.6 1.7 %collective-permute-start.24 = (bf16[1,32,2048]{2,1,0:T(8,128)(2,1)S(1)}, bf16[1,32,2048]{2,1,0:T(8,128)(2,1)S(1)}, u32[]{:S(2)}, u32[]{:S(2)}) collective-permute-start(bf16[1,32,2048]{2,1,0:T(8,128)(2,1)S(1)} %get-tuple-element.28.refs_7_), channel_id=1, source_target_pairs={{0,4},{4,0},{8,12},{12,8},{16,20},{20,16},{24,28},{28,24},{1,5},{5... | collective-permute-start | bytes 393224 | tf_op jit(solution)/shard_map/ppermute | solution.py:176
  63.3 2.1 %collective-permute-done.18.refs_1_ = bf16[1,32,2048]{2,1,0:T(8,128)(2,1)S(1)} collective-permute-done((bf16[1,32,2048]{2,1,0:T(8,128)(2,1)S(1)}, bf16[1,32,2048]{2,1,0:T(8,128)(2,1)S(1)}, u32[]{:S(2)}, u32[]{:S(2)}) %collective-permute-start.18) | collective-permute-done | bytes 131104 | tf_op jit(solution)/shard_map/ppermute | solution.py:176
  65.4 1.8 %collective-permute-start.19 = (bf16[1,32,2048]{2,1,0:T(8,128)(2,1)S(1)}, bf16[1,32,2048]{2,1,0:T(8,128)(2,1)S(1)}, u32[]{:S(2)}, u32[]{:S(2)}) collective-permute-start(bf16[1,32,2048]{2,1,0:T(8,128)(2,1)S(1)} %collective-permute-done.18.refs_1_), channel_id=1, source_target_pairs={{0,4},{4,0},{8,12},{12,8},{16,20},{20,16},{24,28},{28,24},{1,5},{5... | collective-permute-start | bytes 393224 | tf_op jit(solution)/shard_map/ppermute | solution.py:176
  68.2 4.2 %collective-permute-done.22.refs_5_ = bf16[1,32,2048]{2,1,0:T(8,128)(2,1)S(1)} collective-permute-done((bf16[1,32,2048]{2,1,0:T(8,128)(2,1)S(1)}, bf16[1,32,2048]{2,1,0:T(8,128)(2,1)S(1)}, u32[]{:S(2)}, u32[]{:S(2)}) %collective-permute-start.22) | collective-permute-done | bytes 131104 | tf_op jit(solution)/shard_map/ppermute | solution.py:176
  73.8 4.0 %collective-permute-done.23.refs_4_ = bf16[1,32,2048]{2,1,0:T(8,128)(2,1)S(1)} collective-permute-done((bf16[1,32,2048]{2,1,0:T(8,128)(2,1)S(1)}, bf16[1,32,2048]{2,1,0:T(8,128)(2,1)S(1)}, u32[]{:S(2)}, u32[]{:S(2)}) %collective-permute-start.23) | collective-permute-done | bytes 131104 | tf_op jit(solution)/shard_map/ppermute | solution.py:176
  79.6 8.3 %collective-permute-done.26 = bf16[2,32,2048]{2,1,0:T(8,128)(2,1)S(1)} collective-permute-done((bf16[2,32,2048]{2,1,0:T(8,128)(2,1)S(1)}, bf16[2,32,2048]{2,1,0:T(8,128)(2,1)S(1)}, u32[]{:S(2)}, u32[]{:S(2)}) %collective-permute-start.26) | collective-permute-done | bytes 262176 | tf_op jit(solution)/shard_map/ppermute | solution.py:176
  89.9 1.8 %collective-permute-start.28 = (bf16[1,32,2048]{2,1,0:T(8,128)(2,1)S(1)}, bf16[1,32,2048]{2,1,0:T(8,128)(2,1)S(1)}, u32[]{:S(2)}, u32[]{:S(2)}) collective-permute-start(bf16[1,32,2048]{2,1,0:T(8,128)(2,1)S(1)} %get-tuple-element.30), channel_id=1, source_target_pairs={{0,4},{4,0},{8,12},{12,8},{16,20},{20,16},{24,28},{28,24},{1,5},{5... | collective-permute-start | bytes 393224 | tf_op jit(solution)/shard_map/ppermute | solution.py:176
  92.6 1.8 %collective-permute-start.32 = (bf16[1,32,2048]{2,1,0:T(8,128)(2,1)S(1)}, bf16[1,32,2048]{2,1,0:T(8,128)(2,1)S(1)}, u32[]{:S(2)}, u32[]{:S(2)}) collective-permute-start(bf16[1,32,2048]{2,1,0:T(8,128)(2,1)S(1)} %get-tuple-element.34), channel_id=1, source_target_pairs={{0,4},{4,0},{8,12},{12,8},{16,20},{20,16},{24,28},{28,24},{1,5},{5... | collective-permute-start | bytes 393224 | tf_op jit(solution)/shard_map/ppermute | solution.py:176
  96.4 2.6 %collective-permute-start.29 = (bf16[1,32,2048]{2,1,0:T(8,128)(2,1)S(1)}, bf16[1,32,2048]{2,1,0:T(8,128)(2,1)S(1)}, u32[]{:S(2)}, u32[]{:S(2)}) collective-permute-start(bf16[1,32,2048]{2,1,0:T(8,128)(2,1)S(1)} %add_convert_fusion.2), channel_id=1, source_target_pairs={{0,16},{4,20},{8,24},{12,28},{16,0},{20,4},{24,8},{28,12},{1,17},{... | collective-permute-start | bytes 393224 | tf_op jit(solution)/shard_map/ppermute | solution.py:176
  99.2 2.3 %collective-permute-start.31 = (bf16[1,32,2048]{2,1,0:T(8,128)(2,1)S(1)}, bf16[1,32,2048]{2,1,0:T(8,128)(2,1)S(1)}, u32[]{:S(2)}, u32[]{:S(2)}) collective-permute-start(bf16[1,32,2048]{2,1,0:T(8,128)(2,1)S(1)} %add_convert_fusion.1), channel_id=1, source_target_pairs={{0,8},{4,12},{8,0},{12,4},{16,24},{20,28},{24,16},{28,20},{1,9},{5... | collective-permute-start | bytes 393224 | tf_op jit(solution)/shard_map/ppermute | solution.py:176
  102.0 3.1 %collective-permute-start.33 = (bf16[1,32,2048]{2,1,0:T(8,128)(2,1)S(1)}, bf16[1,32,2048]{2,1,0:T(8,128)(2,1)S(1)}, u32[]{:S(2)}, u32[]{:S(2)}) collective-permute-start(bf16[1,32,2048]{2,1,0:T(8,128)(2,1)S(1)} %add_convert_fusion), channel_id=1, source_target_pairs={{0,24},{4,28},{8,16},{12,20},{16,8},{20,12},{24,0},{28,4},{1,25},{... | collective-permute-start | bytes 393224 | tf_op jit(solution)/shard_map/ppermute | solution.py:176
  106.1 3.6 %collective-permute-done.33.refs_2_ = bf16[1,32,2048]{2,1,0:T(8,128)(2,1)S(1)} collective-permute-done((bf16[1,32,2048]{2,1,0:T(8,128)(2,1)S(1)}, bf16[1,32,2048]{2,1,0:T(8,128)(2,1)S(1)}, u32[]{:S(2)}, u32[]{:S(2)}) %collective-permute-start.33) | collective-permute-done | bytes 131104 | tf_op jit(solution)/shard_map/ppermute | solution.py:176
  (89 shorter events, 34.3 us)
Async XLA Ops:
  1.7 10.8 %collective-permute-start.1 = (bf16[1,32,2048]{2,1,0:T(8,128)(2,1)S(1)}, bf16[1,32,2048]{2,1,0:T(8,128)(2,1)S(1)}, u32[]{:S(2)}, u32[]{:S(2)}) collective-permute-start(bf16[1,32,2048]{2,1,0:T(8,128)(2,1)S(1)} %bitcast.27), channel_id=1, source_target_pairs={{0,24},{4,28},{8,16},{12,20},{16,8},{20,12},{24,0},{28,4},{1,25},{... | collective-permute-start | bytes 393224 | tf_op jit(solution)/shard_map/ppermute | solution.py:176
  6.8 7.4 %collective-permute-start.3 = (bf16[1,32,2048]{2,1,0:T(8,128)(2,1)S(1)}, bf16[1,32,2048]{2,1,0:T(8,128)(2,1)S(1)}, u32[]{:S(2)}, u32[]{:S(2)}) collective-permute-start(bf16[1,32,2048]{2,1,0:T(8,128)(2,1)S(1)} %bitcast.28), channel_id=1, source_target_pairs={{0,8},{4,12},{8,0},{12,4},{16,24},{20,28},{24,16},{28,20},{1,9},{5... | collective-permute-start | bytes 393224 | tf_op jit(solution)/shard_map/ppermute | solution.py:176
  6.8 11.1 %collective-permute-start.5 = (bf16[1,32,2048]{2,1,0:T(8,128)(2,1)S(1)}, bf16[1,32,2048]{2,1,0:T(8,128)(2,1)S(1)}, u32[]{:S(2)}, u32[]{:S(2)}) collective-permute-start(bf16[1,32,2048]{2,1,0:T(8,128)(2,1)S(1)} %bitcast.29), channel_id=1, source_target_pairs={{0,16},{4,20},{8,24},{12,28},{16,0},{20,4},{24,8},{28,12},{1,17},{... | collective-permute-start | bytes 393224 | tf_op jit(solution)/shard_map/ppermute | solution.py:176
  7.4 16.6 %collective-permute-start.7 = (bf16[1,32,2048]{2,1,0:T(8,128)(2,1)S(1)}, bf16[1,32,2048]{2,1,0:T(8,128)(2,1)S(1)}, u32[]{:S(2)}, u32[]{:S(2)}) collective-permute-start(bf16[1,32,2048]{2,1,0:T(8,128)(2,1)S(1)} %bitcast.30), channel_id=1, source_target_pairs={{0,4},{4,0},{8,12},{12,8},{16,20},{20,16},{24,28},{28,24},{1,5},{5... | collective-permute-start | bytes 393224 | tf_op jit(solution)/shard_map/ppermute | solution.py:176
  10.9 14.2 %collective-permute-start = (f32[34,2048]{1,0:T(8,128)S(1)}, f32[34,2048]{1,0:T(8,128)S(1)}, u32[]{:S(2)}, u32[]{:S(2)}) collective-permute-start(f32[34,2048]{1,0:T(8,128)S(1)} %get-tuple-element.47), channel_id=1, source_target_pairs={{0,2},{1,3},{2,0},{3,1},{4,6},{5,7},{6,4},{7,5},{8,10},{9,11},{10,... | collective-permute-start | bytes 835592 | tf_op jit(solution)/shard_map/ppermute | solution.py:176
  12.5 11.6 %collective-permute-start.2 = (bf16[1,32,2048]{2,1,0:T(8,128)(2,1)S(1)}, bf16[1,32,2048]{2,1,0:T(8,128)(2,1)S(1)}, u32[]{:S(2)}, u32[]{:S(2)}) collective-permute-start(bf16[1,32,2048]{2,1,0:T(8,128)(2,1)S(1)} %collective-permute-done.1.refs_1_), channel_id=1, source_target_pairs={{0,4},{4,0},{8,12},{12,8},{16,20},{20,16},{24,28},{28,24},{1,5},{5... | collective-permute-start | bytes 393224 | tf_op jit(solution)/shard_map/ppermute | solution.py:176
  14.2 9.8 %collective-permute-start.4 = (bf16[1,32,2048]{2,1,0:T(8,128)(2,1)S(1)}, bf16[1,32,2048]{2,1,0:T(8,128)(2,1)S(1)}, u32[]{:S(2)}, u32[]{:S(2)}) collective-permute-start(bf16[1,32,2048]{2,1,0:T(8,128)(2,1)S(1)} %collective-permute-done.3.refs_3_), channel_id=1, source_target_pairs={{0,4},{4,0},{8,12},{12,8},{16,20},{20,16},{24,28},{28,24},{1,5},{5... | collective-permute-start | bytes 393224 | tf_op jit(solution)/shard_map/ppermute | solution.py:176
  25.8 9.2 %collective-permute-start.9 = (bf16[2,32,2048]{2,1,0:T(8,128)(2,1)S(1)}, bf16[2,32,2048]{2,1,0:T(8,128)(2,1)S(1)}, u32[]{:S(2)}, u32[]{:S(2)}) collective-permute-start(bf16[2,32,2048]{2,1,0:T(8,128)(2,1)S(1)} %fusion.1), channel_id=1, source_target_pairs={{0,2},{1,3},{2,0},{3,1},{4,6},{5,7},{6,4},{7,5},{8,10},{9,11},{10,... | collective-permute-start | bytes 786440 | tf_op jit(solution)/shard_map/ppermute | solution.py:176
  37.2 9.0 %collective-permute-start.13 = (bf16[1,32,2048]{2,1,0:T(8,128)(2,1)S(1)}, bf16[1,32,2048]{2,1,0:T(8,128)(2,1)S(1)}, u32[]{:S(2)}, u32[]{:S(2)}) collective-permute-start(bf16[1,32,2048]{2,1,0:T(8,128)(2,1)S(1)} %get-tuple-element.23), channel_id=1, source_target_pairs={{0,4},{4,0},{8,12},{12,8},{16,20},{20,16},{24,28},{28,24},{1,5},{5... | collective-permute-start | bytes 393224 | tf_op jit(solution)/shard_map/ppermute | solution.py:176
  39.6 9.3 %collective-permute-start.15 = (bf16[1,32,2048]{2,1,0:T(8,128)(2,1)S(1)}, bf16[1,32,2048]{2,1,0:T(8,128)(2,1)S(1)}, u32[]{:S(2)}, u32[]{:S(2)}) collective-permute-start(bf16[1,32,2048]{2,1,0:T(8,128)(2,1)S(1)} %get-tuple-element.25), channel_id=1, source_target_pairs={{0,4},{4,0},{8,12},{12,8},{16,20},{20,16},{24,28},{28,24},{1,5},{5... | collective-permute-start | bytes 393224 | tf_op jit(solution)/shard_map/ppermute | solution.py:176
  39.9 12.9 %collective-permute-start.17 = (bf16[1,32,2048]{2,1,0:T(8,128)(2,1)S(1)}, bf16[1,32,2048]{2,1,0:T(8,128)(2,1)S(1)}, u32[]{:S(2)}, u32[]{:S(2)}) collective-permute-start(bf16[1,32,2048]{2,1,0:T(8,128)(2,1)S(1)} %get-tuple-element.26), channel_id=1, source_target_pairs={{0,4},{4,0},{8,12},{12,8},{16,20},{20,16},{24,28},{28,24},{1,5},{5... | collective-permute-start | bytes 393224 | tf_op jit(solution)/shard_map/ppermute | solution.py:176
  43.4 9.4 %collective-permute-start.12 = (bf16[1,32,2048]{2,1,0:T(8,128)(2,1)S(1)}, bf16[1,32,2048]{2,1,0:T(8,128)(2,1)S(1)}, u32[]{:S(2)}, u32[]{:S(2)}) collective-permute-start(bf16[1,32,2048]{2,1,0:T(8,128)(2,1)S(1)} %add_convert_fusion.5), channel_id=1, source_target_pairs={{0,16},{4,20},{8,24},{12,28},{16,0},{20,4},{24,8},{28,12},{1,17},{... | collective-permute-start | bytes 393224 | tf_op jit(solution)/shard_map/ppermute | solution.py:176
  49.0 7.9 %collective-permute-start.16 = (bf16[1,32,2048]{2,1,0:T(8,128)(2,1)S(1)}, bf16[1,32,2048]{2,1,0:T(8,128)(2,1)S(1)}, u32[]{:S(2)}, u32[]{:S(2)}) collective-permute-start(bf16[1,32,2048]{2,1,0:T(8,128)(2,1)S(1)} %add_convert_fusion.3), channel_id=1, source_target_pairs={{0,24},{4,28},{8,16},{12,20},{16,8},{20,12},{24,0},{28,4},{1,25},{... | collective-permute-start | bytes 393224 | tf_op jit(solution)/shard_map/ppermute | solution.py:176
  57.1 8.3 %collective-permute-start.18 = (bf16[1,32,2048]{2,1,0:T(8,128)(2,1)S(1)}, bf16[1,32,2048]{2,1,0:T(8,128)(2,1)S(1)}, u32[]{:S(2)}, u32[]{:S(2)}) collective-permute-start(bf16[1,32,2048]{2,1,0:T(8,128)(2,1)S(1)} %get-tuple-element.28.refs_7_), channel_id=1, source_target_pairs={{0,24},{4,28},{8,16},{12,20},{16,8},{20,12},{24,0},{28,4},{1,25},{... | collective-permute-start | bytes 393224 | tf_op jit(solution)/shard_map/ppermute | solution.py:176
  59.8 7.4 %collective-permute-start.20 = (bf16[1,32,2048]{2,1,0:T(8,128)(2,1)S(1)}, bf16[1,32,2048]{2,1,0:T(8,128)(2,1)S(1)}, u32[]{:S(2)}, u32[]{:S(2)}) collective-permute-start(bf16[1,32,2048]{2,1,0:T(8,128)(2,1)S(1)} %get-tuple-element.28.refs_7_), channel_id=1, source_target_pairs={{0,8},{4,12},{8,0},{12,4},{16,24},{20,28},{24,16},{28,20},{1,9},{5... | collective-permute-start | bytes 393224 | tf_op jit(solution)/shard_map/ppermute | solution.py:176
  61.0 11.4 %collective-permute-start.22 = (bf16[1,32,2048]{2,1,0:T(8,128)(2,1)S(1)}, bf16[1,32,2048]{2,1,0:T(8,128)(2,1)S(1)}, u32[]{:S(2)}, u32[]{:S(2)}) collective-permute-start(bf16[1,32,2048]{2,1,0:T(8,128)(2,1)S(1)} %get-tuple-element.28.refs_7_), channel_id=1, source_target_pairs={{0,16},{4,20},{8,24},{12,28},{16,0},{20,4},{24,8},{28,12},{1,17},{... | collective-permute-start | bytes 393224 | tf_op jit(solution)/shard_map/ppermute | solution.py:176
  61.6 12.2 %collective-permute-start.24 = (bf16[1,32,2048]{2,1,0:T(8,128)(2,1)S(1)}, bf16[1,32,2048]{2,1,0:T(8,128)(2,1)S(1)}, u32[]{:S(2)}, u32[]{:S(2)}) collective-permute-start(bf16[1,32,2048]{2,1,0:T(8,128)(2,1)S(1)} %get-tuple-element.28.refs_7_), channel_id=1, source_target_pairs={{0,4},{4,0},{8,12},{12,8},{16,20},{20,16},{24,28},{28,24},{1,5},{5... | collective-permute-start | bytes 393224 | tf_op jit(solution)/shard_map/ppermute | solution.py:176
  65.4 8.4 %collective-permute-start.19 = (bf16[1,32,2048]{2,1,0:T(8,128)(2,1)S(1)}, bf16[1,32,2048]{2,1,0:T(8,128)(2,1)S(1)}, u32[]{:S(2)}, u32[]{:S(2)}) collective-permute-start(bf16[1,32,2048]{2,1,0:T(8,128)(2,1)S(1)} %collective-permute-done.18.refs_1_), channel_id=1, source_target_pairs={{0,4},{4,0},{8,12},{12,8},{16,20},{20,16},{24,28},{28,24},{1,5},{5... | collective-permute-start | bytes 393224 | tf_op jit(solution)/shard_map/ppermute | solution.py:176
  79.5 8.4 %collective-permute-start.26 = (bf16[2,32,2048]{2,1,0:T(8,128)(2,1)S(1)}, bf16[2,32,2048]{2,1,0:T(8,128)(2,1)S(1)}, u32[]{:S(2)}, u32[]{:S(2)}) collective-permute-start(bf16[2,32,2048]{2,1,0:T(8,128)(2,1)S(1)} %fusion.2), channel_id=1, source_target_pairs={{0,2},{1,3},{2,0},{3,1},{4,6},{5,7},{6,4},{7,5},{8,10},{9,11},{10,... | collective-permute-start | bytes 786440 | tf_op jit(solution)/shard_map/ppermute | solution.py:176
  91.8 7.4 %collective-permute-start.30 = (bf16[1,32,2048]{2,1,0:T(8,128)(2,1)S(1)}, bf16[1,32,2048]{2,1,0:T(8,128)(2,1)S(1)}, u32[]{:S(2)}, u32[]{:S(2)}) collective-permute-start(bf16[1,32,2048]{2,1,0:T(8,128)(2,1)S(1)} %get-tuple-element.32), channel_id=1, source_target_pairs={{0,4},{4,0},{8,12},{12,8},{16,20},{20,16},{24,28},{28,24},{1,5},{5... | collective-permute-start | bytes 393224 | tf_op jit(solution)/shard_map/ppermute | solution.py:176
  92.6 9.3 %collective-permute-start.32 = (bf16[1,32,2048]{2,1,0:T(8,128)(2,1)S(1)}, bf16[1,32,2048]{2,1,0:T(8,128)(2,1)S(1)}, u32[]{:S(2)}, u32[]{:S(2)}) collective-permute-start(bf16[1,32,2048]{2,1,0:T(8,128)(2,1)S(1)} %get-tuple-element.34), channel_id=1, source_target_pairs={{0,4},{4,0},{8,12},{12,8},{16,20},{20,16},{24,28},{28,24},{1,5},{5... | collective-permute-start | bytes 393224 | tf_op jit(solution)/shard_map/ppermute | solution.py:176
  94.5 11.7 %collective-permute-start.34 = (bf16[1,32,2048]{2,1,0:T(8,128)(2,1)S(1)}, bf16[1,32,2048]{2,1,0:T(8,128)(2,1)S(1)}, u32[]{:S(2)}, u32[]{:S(2)}) collective-permute-start(bf16[1,32,2048]{2,1,0:T(8,128)(2,1)S(1)} %get-tuple-element.35), channel_id=1, source_target_pairs={{0,4},{4,0},{8,12},{12,8},{16,20},{20,16},{24,28},{28,24},{1,5},{5... | collective-permute-start | bytes 393224 | tf_op jit(solution)/shard_map/ppermute | solution.py:176
  96.4 9.8 %collective-permute-start.29 = (bf16[1,32,2048]{2,1,0:T(8,128)(2,1)S(1)}, bf16[1,32,2048]{2,1,0:T(8,128)(2,1)S(1)}, u32[]{:S(2)}, u32[]{:S(2)}) collective-permute-start(bf16[1,32,2048]{2,1,0:T(8,128)(2,1)S(1)} %add_convert_fusion.2), channel_id=1, source_target_pairs={{0,16},{4,20},{8,24},{12,28},{16,0},{20,4},{24,8},{28,12},{1,17},{... | collective-permute-start | bytes 393224 | tf_op jit(solution)/shard_map/ppermute | solution.py:176
  102.0 7.7 %collective-permute-start.33 = (bf16[1,32,2048]{2,1,0:T(8,128)(2,1)S(1)}, bf16[1,32,2048]{2,1,0:T(8,128)(2,1)S(1)}, u32[]{:S(2)}, u32[]{:S(2)}) collective-permute-start(bf16[1,32,2048]{2,1,0:T(8,128)(2,1)S(1)} %add_convert_fusion), channel_id=1, source_target_pairs={{0,24},{4,28},{8,16},{12,20},{16,8},{20,12},{24,0},{28,4},{1,25},{... | collective-permute-start | bytes 393224 | tf_op jit(solution)/shard_map/ppermute | solution.py:176
  (15 other events, 112.9 us)

commit v14 on v13

--- a/solution.py
+++ b/solution.py
@@ -278,6 +278,8 @@
     mine, other = (tuple(range(p, rows, 2)) for p in (0, 1))
     blocks = load_tiles(tile_count, tiles[0, 0])
     keep = tuple(range(0, cols, 2))
+    soon = tuple(strides(cols)[:2])
+    later = tuple(k for k in keep if k not in soon)
     leave = [k + 1 for k in strides(cols) + [0]]
     first, then = tuple(leave[:2]), tuple(leave[2:])
     for step in range(ITERS):
@@ -304,11 +306,16 @@
         rest, kept = sweep(
             Plan(
                 True, (mine, other),
-                (Out(then, rounded, False), Out(keep, whole, False)),
+                (Out(then, rounded, False), Out(soon, whole, False)),
             ),
             blocks, places, extra, dual.shape[1],
         )
+        (last,) = sweep(
+            Plan(True, (mine, other), (Out(later, whole, False),)),
+            blocks, places, extra, dual.shape[1],
+        )
         sent |= rest
+        kept |= last
         shares = share_pairs(kept, sent, "col", cols)
         dual, *rounded_dual = update_dual(
             shares, kept[0], demand, row_kind, dual, step == ITERS - 1

time: 110 us -> 111 us (level)
  starting transfers between devices: 49.7 us -> 45.7 us
  waiting for transfers between devices: 46.8 us -> 49.7 us
  Pallas kernels: 4.54 us -> 6.54 us
    ppermute x35, starting transfers between devices: 49.7 us -> 45.7 us  [swap(): return lax.ppermute(value, axis, [(i, i ^ k) for i in range(size)])]
    ppermute x35, waiting for transfers between devices: 46.8 us -> 49.7 us  [swap(): return lax.ppermute(value, axis, [(i, i ^ k) for i in range(size)])]
    pallas_call x8 -> x10, Pallas kernels: 2.24 us -> 3.93 us  [sweep(): pl.pallas_call(functools.partial(sweep_kernel, plan, parts[0].shape[2] //...]
  transfers between devices with their start and end apart: 35 -> 35, of which waited for: 20 -> 22; matrix products, arithmetic and copies ran while one was open for 4% -> 4% of each run, Pallas kernels for 3% -> 4%
where the time goes in v14:
time: 111 us
  waiting for transfers between devices  49.7 us (45%)
  starting transfers between devices  45.7 us (41%)
  Pallas kernels  6.54 us (6%)
  local copies, waits for them, and re-layouts  3.9 us (4%)
  between operations  2.92 us (3%)
  other arithmetic  2.41 us (2%)
    ppermute x35, waiting for transfers between devices, swap(): return lax.ppermute(value, axis, [(i, i ^ k) for i in range(size)])  49.7 us
    ppermute x35, starting transfers between devices, swap(): return lax.ppermute(value, axis, [(i, i ^ k) for i in range(size)])  45.7 us
    pallas_call x10, Pallas kernels, sweep(): pl.pallas_call(functools.partial(sweep_kernel, plan, parts[0].shape[2] //...  3.93 us
    unnamed x13, local copies, waits for them, and re-layouts  3.25 us
  transfers between devices with their start and end apart: 35, of which 22 were waited for; matrix products, arithmetic and copies ran while one was open for 4% of the time, Pallas kernels for 4%

profile of v14, /device:TPU:0, one launch (start us, length us, event | category | flops | bytes accessed | tf_op | source)
XLA Modules:
  0.0 111.2 jit_solution(8348102075614607104)
XLA Ops:
  1.7 5.1 %collective-permute-start.1 = (bf16[1,32,2048]{2,1,0:T(8,128)(2,1)S(1)}, bf16[1,32,2048]{2,1,0:T(8,128)(2,1)S(1)}, u32[]{:S(2)}, u32[]{:S(2)}) collective-permute-start(bf16[1,32,2048]{2,1,0:T(8,128)(2,1)S(1)} %bitcast.27), channel_id=1, source_target_pairs={{0,24},{4,28},{8,16},{12,20},{16,8},{20,12},{24,0},{28,4},{1,25},{... | collective-permute-start | bytes 393224 | tf_op jit(solution)/shard_map/ppermute | solution.py:176
  7.4 1.6 %collective-permute-start.7 = (bf16[1,32,2048]{2,1,0:T(8,128)(2,1)S(1)}, bf16[1,32,2048]{2,1,0:T(8,128)(2,1)S(1)}, u32[]{:S(2)}, u32[]{:S(2)}) collective-permute-start(bf16[1,32,2048]{2,1,0:T(8,128)(2,1)S(1)} %bitcast.30), channel_id=1, source_target_pairs={{0,4},{4,0},{8,12},{12,8},{16,20},{20,16},{24,28},{28,24},{1,5},{5... | collective-permute-start | bytes 393224 | tf_op jit(solution)/shard_map/ppermute | solution.py:176
  15.6 2.3 %collective-permute-done.5.refs_5_ = bf16[1,32,2048]{2,1,0:T(8,128)(2,1)S(1)} collective-permute-done((bf16[1,32,2048]{2,1,0:T(8,128)(2,1)S(1)}, bf16[1,32,2048]{2,1,0:T(8,128)(2,1)S(1)}, u32[]{:S(2)}, u32[]{:S(2)}) %collective-permute-start.5) | collective-permute-done | bytes 131104 | tf_op jit(solution)/shard_map/ppermute | solution.py:176
  22.7 1.6 %load_tiles.1.tiles = bf16[8,1024,512]{2,1,0:T(8,128)(2,1)S(1)} custom-call(s32[1,1]{1,0:T(1,128)S(6)} %copy.28.live, bf16[8,1024,512]{2,1,0:T(8,128)(2,1)} %bitcast.34), custom_call_target="tpu_custom_call" | custom-call | bytes 16777216 | tf_op jit(solution)/shard_map/load_tiles/pallas_call | solution.py:161
  26.4 2.8 %collective-permute-start.9 = (bf16[2,32,2048]{2,1,0:T(8,128)(2,1)S(1)}, bf16[2,32,2048]{2,1,0:T(8,128)(2,1)S(1)}, u32[]{:S(2)}, u32[]{:S(2)}) collective-permute-start(bf16[2,32,2048]{2,1,0:T(8,128)(2,1)S(1)} %fusion.1), channel_id=1, source_target_pairs={{0,2},{1,3},{2,0},{3,1},{4,6},{5,7},{6,4},{7,5},{8,10},{9,11},{10,... | collective-permute-start | bytes 786440 | tf_op jit(solution)/shard_map/ppermute | solution.py:176
  29.3 6.6 %collective-permute-done.9 = bf16[2,32,2048]{2,1,0:T(8,128)(2,1)S(1)} collective-permute-done((bf16[2,32,2048]{2,1,0:T(8,128)(2,1)S(1)}, bf16[2,32,2048]{2,1,0:T(8,128)(2,1)S(1)}, u32[]{:S(2)}, u32[]{:S(2)}) %collective-permute-start.9) | collective-permute-done | bytes 262176 | tf_op jit(solution)/shard_map/ppermute | solution.py:176
  38.4 2.0 %collective-permute-start.13 = (bf16[1,32,2048]{2,1,0:T(8,128)(2,1)S(1)}, bf16[1,32,2048]{2,1,0:T(8,128)(2,1)S(1)}, u32[]{:S(2)}, u32[]{:S(2)}) collective-permute-start(bf16[1,32,2048]{2,1,0:T(8,128)(2,1)S(1)} %get-tuple-element.23), channel_id=1, source_target_pairs={{0,4},{4,0},{8,12},{12,8},{16,20},{20,16},{24,28},{28,24},{1,5},{5... | collective-permute-start | bytes 393224 | tf_op jit(solution)/shard_map/ppermute | solution.py:176
  43.2 1.6 %collective-permute-done.11 = bf16[1,32,2048]{2,1,0:T(8,128)(2,1)S(1)} collective-permute-done((bf16[1,32,2048]{2,1,0:T(8,128)(2,1)S(1)}, bf16[1,32,2048]{2,1,0:T(8,128)(2,1)S(1)}, u32[]{:S(2)}, u32[]{:S(2)}) %collective-permute-start.11) | collective-permute-done | bytes 131104 | tf_op jit(solution)/shard_map/ppermute | solution.py:176
  44.9 2.7 %collective-permute-done.13 = bf16[1,32,2048]{2,1,0:T(8,128)(2,1)S(1)} collective-permute-done((bf16[1,32,2048]{2,1,0:T(8,128)(2,1)S(1)}, bf16[1,32,2048]{2,1,0:T(8,128)(2,1)S(1)}, u32[]{:S(2)}, u32[]{:S(2)}) %collective-permute-start.13) | collective-permute-done | bytes 131104 | tf_op jit(solution)/shard_map/ppermute | solution.py:176
  47.6 2.4 %collective-permute-start.14 = (bf16[1,32,2048]{2,1,0:T(8,128)(2,1)S(1)}, bf16[1,32,2048]{2,1,0:T(8,128)(2,1)S(1)}, u32[]{:S(2)}, u32[]{:S(2)}) collective-permute-start(bf16[1,32,2048]{2,1,0:T(8,128)(2,1)S(1)} %add_convert_fusion.4), channel_id=1, source_target_pairs={{0,8},{4,12},{8,0},{12,4},{16,24},{20,28},{24,16},{28,20},{1,9},{5... | collective-permute-start | bytes 393224 | tf_op jit(solution)/shard_map/ppermute | solution.py:176
  50.4 4.5 %collective-permute-start.16 = (bf16[1,32,2048]{2,1,0:T(8,128)(2,1)S(1)}, bf16[1,32,2048]{2,1,0:T(8,128)(2,1)S(1)}, u32[]{:S(2)}, u32[]{:S(2)}) collective-permute-start(bf16[1,32,2048]{2,1,0:T(8,128)(2,1)S(1)} %add_convert_fusion.3), channel_id=1, source_target_pairs={{0,24},{4,28},{8,16},{12,20},{16,8},{20,12},{24,0},{28,4},{1,25},{... | collective-permute-start | bytes 393224 | tf_op jit(solution)/shard_map/ppermute | solution.py:176
  55.0 2.9 %collective-permute-done.16.refs_2_ = bf16[1,32,2048]{2,1,0:T(8,128)(2,1)S(1)} collective-permute-done((bf16[1,32,2048]{2,1,0:T(8,128)(2,1)S(1)}, bf16[1,32,2048]{2,1,0:T(8,128)(2,1)S(1)}, u32[]{:S(2)}, u32[]{:S(2)}) %collective-permute-start.16) | collective-permute-done | bytes 131104 | tf_op jit(solution)/shard_map/ppermute | solution.py:176
  58.1 3.9 %collective-permute-start.18 = (bf16[1,32,2048]{2,1,0:T(8,128)(2,1)S(1)}, bf16[1,32,2048]{2,1,0:T(8,128)(2,1)S(1)}, u32[]{:S(2)}, u32[]{:S(2)}) collective-permute-start(bf16[1,32,2048]{2,1,0:T(8,128)(2,1)S(1)} %get-tuple-element.28.refs_7_), channel_id=1, source_target_pairs={{0,24},{4,28},{8,16},{12,20},{16,8},{20,12},{24,0},{28,4},{1,25},{... | collective-permute-start | bytes 393224 | tf_op jit(solution)/shard_map/ppermute | solution.py:176
  62.6 3.1 %collective-permute-done.18.refs_1_ = bf16[1,32,2048]{2,1,0:T(8,128)(2,1)S(1)} collective-permute-done((bf16[1,32,2048]{2,1,0:T(8,128)(2,1)S(1)}, bf16[1,32,2048]{2,1,0:T(8,128)(2,1)S(1)}, u32[]{:S(2)}, u32[]{:S(2)}) %collective-permute-start.18) | collective-permute-done | bytes 131104 | tf_op jit(solution)/shard_map/ppermute | solution.py:176
  66.5 2.4 %collective-permute-done.20.refs_3_ = bf16[1,32,2048]{2,1,0:T(8,128)(2,1)S(1)} collective-permute-done((bf16[1,32,2048]{2,1,0:T(8,128)(2,1)S(1)}, bf16[1,32,2048]{2,1,0:T(8,128)(2,1)S(1)}, u32[]{:S(2)}, u32[]{:S(2)}) %collective-permute-start.20) | collective-permute-done | bytes 131104 | tf_op jit(solution)/shard_map/ppermute | solution.py:176
  71.5 2.3 %collective-permute-done.21.refs_2_ = bf16[1,32,2048]{2,1,0:T(8,128)(2,1)S(1)} collective-permute-done((bf16[1,32,2048]{2,1,0:T(8,128)(2,1)S(1)}, bf16[1,32,2048]{2,1,0:T(8,128)(2,1)S(1)}, u32[]{:S(2)}, u32[]{:S(2)}) %collective-permute-start.21) | collective-permute-done | bytes 131104 | tf_op jit(solution)/shard_map/ppermute | solution.py:176
  77.3 4.9 %collective-permute-start.26 = (bf16[2,32,2048]{2,1,0:T(8,128)(2,1)S(1)}, bf16[2,32,2048]{2,1,0:T(8,128)(2,1)S(1)}, u32[]{:S(2)}, u32[]{:S(2)}) collective-permute-start(bf16[2,32,2048]{2,1,0:T(8,128)(2,1)S(1)} %fusion.2), channel_id=1, source_target_pairs={{0,2},{1,3},{2,0},{3,1},{4,6},{5,7},{6,4},{7,5},{8,10},{9,11},{10,... | collective-permute-start | bytes 786440 | tf_op jit(solution)/shard_map/ppermute | solution.py:176
  82.2 6.6 %collective-permute-done.26 = bf16[2,32,2048]{2,1,0:T(8,128)(2,1)S(1)} collective-permute-done((bf16[2,32,2048]{2,1,0:T(8,128)(2,1)S(1)}, bf16[2,32,2048]{2,1,0:T(8,128)(2,1)S(1)}, u32[]{:S(2)}, u32[]{:S(2)}) %collective-permute-start.26) | collective-permute-done | bytes 262176 | tf_op jit(solution)/shard_map/ppermute | solution.py:176
  91.3 2.0 %collective-permute-start.30 = (bf16[1,32,2048]{2,1,0:T(8,128)(2,1)S(1)}, bf16[1,32,2048]{2,1,0:T(8,128)(2,1)S(1)}, u32[]{:S(2)}, u32[]{:S(2)}) collective-permute-start(bf16[1,32,2048]{2,1,0:T(8,128)(2,1)S(1)} %get-tuple-element.32), channel_id=1, source_target_pairs={{0,4},{4,0},{8,12},{12,8},{16,20},{20,16},{24,28},{28,24},{1,5},{5... | collective-permute-start | bytes 393224 | tf_op jit(solution)/shard_map/ppermute | solution.py:176
  96.1 1.6 %collective-permute-done.28 = bf16[1,32,2048]{2,1,0:T(8,128)(2,1)S(1)} collective-permute-done((bf16[1,32,2048]{2,1,0:T(8,128)(2,1)S(1)}, bf16[1,32,2048]{2,1,0:T(8,128)(2,1)S(1)}, u32[]{:S(2)}, u32[]{:S(2)}) %collective-permute-start.28) | collective-permute-done | bytes 131104 | tf_op jit(solution)/shard_map/ppermute | solution.py:176
  97.8 2.7 %collective-permute-done.30 = bf16[1,32,2048]{2,1,0:T(8,128)(2,1)S(1)} collective-permute-done((bf16[1,32,2048]{2,1,0:T(8,128)(2,1)S(1)}, bf16[1,32,2048]{2,1,0:T(8,128)(2,1)S(1)}, u32[]{:S(2)}, u32[]{:S(2)}) %collective-permute-start.30) | collective-permute-done | bytes 131104 | tf_op jit(solution)/shard_map/ppermute | solution.py:176
  101.2 2.1 %collective-permute-done.32 = bf16[1,32,2048]{2,1,0:T(8,128)(2,1)S(1)} collective-permute-done((bf16[1,32,2048]{2,1,0:T(8,128)(2,1)S(1)}, bf16[1,32,2048]{2,1,0:T(8,128)(2,1)S(1)}, u32[]{:S(2)}, u32[]{:S(2)}) %collective-permute-start.32) | collective-permute-done | bytes 131104 | tf_op jit(solution)/shard_map/ppermute | solution.py:176
  103.4 2.8 %collective-permute-start.33 = (bf16[1,32,2048]{2,1,0:T(8,128)(2,1)S(1)}, bf16[1,32,2048]{2,1,0:T(8,128)(2,1)S(1)}, u32[]{:S(2)}, u32[]{:S(2)}) collective-permute-start(bf16[1,32,2048]{2,1,0:T(8,128)(2,1)S(1)} %add_convert_fusion), channel_id=1, source_target_pairs={{0,24},{4,28},{8,16},{12,20},{16,8},{20,12},{24,0},{28,4},{1,25},{... | collective-permute-start | bytes 393224 | tf_op jit(solution)/shard_map/ppermute | solution.py:176
  107.2 3.1 %collective-permute-done.33.refs_2_ = bf16[1,32,2048]{2,1,0:T(8,128)(2,1)S(1)} collective-permute-done((bf16[1,32,2048]{2,1,0:T(8,128)(2,1)S(1)}, bf16[1,32,2048]{2,1,0:T(8,128)(2,1)S(1)}, u32[]{:S(2)}, u32[]{:S(2)}) %collective-permute-start.33) | collective-permute-done | bytes 131104 | tf_op jit(solution)/shard_map/ppermute | solution.py:176
  (91 shorter events, 34.6 us)
Async XLA Ops:
  1.7 10.8 %collective-permute-start.1 = (bf16[1,32,2048]{2,1,0:T(8,128)(2,1)S(1)}, bf16[1,32,2048]{2,1,0:T(8,128)(2,1)S(1)}, u32[]{:S(2)}, u32[]{:S(2)}) collective-permute-start(bf16[1,32,2048]{2,1,0:T(8,128)(2,1)S(1)} %bitcast.27), channel_id=1, source_target_pairs={{0,24},{4,28},{8,16},{12,20},{16,8},{20,12},{24,0},{28,4},{1,25},{... | collective-permute-start | bytes 393224 | tf_op jit(solution)/shard_map/ppermute | solution.py:176
  6.8 7.4 %collective-permute-start.3 = (bf16[1,32,2048]{2,1,0:T(8,128)(2,1)S(1)}, bf16[1,32,2048]{2,1,0:T(8,128)(2,1)S(1)}, u32[]{:S(2)}, u32[]{:S(2)}) collective-permute-start(bf16[1,32,2048]{2,1,0:T(8,128)(2,1)S(1)} %bitcast.28), channel_id=1, source_target_pairs={{0,8},{4,12},{8,0},{12,4},{16,24},{20,28},{24,16},{28,20},{1,9},{5... | collective-permute-start | bytes 393224 | tf_op jit(solution)/shard_map/ppermute | solution.py:176
  6.8 11.1 %collective-permute-start.5 = (bf16[1,32,2048]{2,1,0:T(8,128)(2,1)S(1)}, bf16[1,32,2048]{2,1,0:T(8,128)(2,1)S(1)}, u32[]{:S(2)}, u32[]{:S(2)}) collective-permute-start(bf16[1,32,2048]{2,1,0:T(8,128)(2,1)S(1)} %bitcast.29), channel_id=1, source_target_pairs={{0,16},{4,20},{8,24},{12,28},{16,0},{20,4},{24,8},{28,12},{1,17},{... | collective-permute-start | bytes 393224 | tf_op jit(solution)/shard_map/ppermute | solution.py:176
  7.4 16.9 %collective-permute-start.7 = (bf16[1,32,2048]{2,1,0:T(8,128)(2,1)S(1)}, bf16[1,32,2048]{2,1,0:T(8,128)(2,1)S(1)}, u32[]{:S(2)}, u32[]{:S(2)}) collective-permute-start(bf16[1,32,2048]{2,1,0:T(8,128)(2,1)S(1)} %bitcast.30), channel_id=1, source_target_pairs={{0,4},{4,0},{8,12},{12,8},{16,20},{20,16},{24,28},{28,24},{1,5},{5... | collective-permute-start | bytes 393224 | tf_op jit(solution)/shard_map/ppermute | solution.py:176
  10.9 14.5 %collective-permute-start = (f32[34,2048]{1,0:T(8,128)S(1)}, f32[34,2048]{1,0:T(8,128)S(1)}, u32[]{:S(2)}, u32[]{:S(2)}) collective-permute-start(f32[34,2048]{1,0:T(8,128)S(1)} %get-tuple-element.47), channel_id=1, source_target_pairs={{0,2},{1,3},{2,0},{3,1},{4,6},{5,7},{6,4},{7,5},{8,10},{9,11},{10,... | collective-permute-start | bytes 835592 | tf_op jit(solution)/shard_map/ppermute | solution.py:176
  12.5 11.9 %collective-permute-start.2 = (bf16[1,32,2048]{2,1,0:T(8,128)(2,1)S(1)}, bf16[1,32,2048]{2,1,0:T(8,128)(2,1)S(1)}, u32[]{:S(2)}, u32[]{:S(2)}) collective-permute-start(bf16[1,32,2048]{2,1,0:T(8,128)(2,1)S(1)} %collective-permute-done.1.refs_1_), channel_id=1, source_target_pairs={{0,4},{4,0},{8,12},{12,8},{16,20},{20,16},{24,28},{28,24},{1,5},{5... | collective-permute-start | bytes 393224 | tf_op jit(solution)/shard_map/ppermute | solution.py:176
  14.2 10.2 %collective-permute-start.4 = (bf16[1,32,2048]{2,1,0:T(8,128)(2,1)S(1)}, bf16[1,32,2048]{2,1,0:T(8,128)(2,1)S(1)}, u32[]{:S(2)}, u32[]{:S(2)}) collective-permute-start(bf16[1,32,2048]{2,1,0:T(8,128)(2,1)S(1)} %collective-permute-done.3.refs_3_), channel_id=1, source_target_pairs={{0,4},{4,0},{8,12},{12,8},{16,20},{20,16},{24,28},{28,24},{1,5},{5... | collective-permute-start | bytes 393224 | tf_op jit(solution)/shard_map/ppermute | solution.py:176
  26.4 9.4 %collective-permute-start.9 = (bf16[2,32,2048]{2,1,0:T(8,128)(2,1)S(1)}, bf16[2,32,2048]{2,1,0:T(8,128)(2,1)S(1)}, u32[]{:S(2)}, u32[]{:S(2)}) collective-permute-start(bf16[2,32,2048]{2,1,0:T(8,128)(2,1)S(1)} %fusion.1), channel_id=1, source_target_pairs={{0,2},{1,3},{2,0},{3,1},{4,6},{5,7},{6,4},{7,5},{8,10},{9,11},{10,... | collective-permute-start | bytes 786440 | tf_op jit(solution)/shard_map/ppermute | solution.py:176
  38.4 9.2 %collective-permute-start.13 = (bf16[1,32,2048]{2,1,0:T(8,128)(2,1)S(1)}, bf16[1,32,2048]{2,1,0:T(8,128)(2,1)S(1)}, u32[]{:S(2)}, u32[]{:S(2)}) collective-permute-start(bf16[1,32,2048]{2,1,0:T(8,128)(2,1)S(1)} %get-tuple-element.23), channel_id=1, source_target_pairs={{0,4},{4,0},{8,12},{12,8},{16,20},{20,16},{24,28},{28,24},{1,5},{5... | collective-permute-start | bytes 393224 | tf_op jit(solution)/shard_map/ppermute | solution.py:176
  40.5 9.9 %collective-permute-start.15 = (bf16[1,32,2048]{2,1,0:T(8,128)(2,1)S(1)}, bf16[1,32,2048]{2,1,0:T(8,128)(2,1)S(1)}, u32[]{:S(2)}, u32[]{:S(2)}) collective-permute-start(bf16[1,32,2048]{2,1,0:T(8,128)(2,1)S(1)} %get-tuple-element.25), channel_id=1, source_target_pairs={{0,4},{4,0},{8,12},{12,8},{16,20},{20,16},{24,28},{28,24},{1,5},{5... | collective-permute-start | bytes 393224 | tf_op jit(solution)/shard_map/ppermute | solution.py:176
  41.1 13.9 %collective-permute-start.17 = (bf16[1,32,2048]{2,1,0:T(8,128)(2,1)S(1)}, bf16[1,32,2048]{2,1,0:T(8,128)(2,1)S(1)}, u32[]{:S(2)}, u32[]{:S(2)}) collective-permute-start(bf16[1,32,2048]{2,1,0:T(8,128)(2,1)S(1)} %get-tuple-element.26), channel_id=1, source_target_pairs={{0,4},{4,0},{8,12},{12,8},{16,20},{20,16},{24,28},{28,24},{1,5},{5... | collective-permute-start | bytes 393224 | tf_op jit(solution)/shard_map/ppermute | solution.py:176
  44.8 10.2 %collective-permute-start.12 = (bf16[1,32,2048]{2,1,0:T(8,128)(2,1)S(1)}, bf16[1,32,2048]{2,1,0:T(8,128)(2,1)S(1)}, u32[]{:S(2)}, u32[]{:S(2)}) collective-permute-start(bf16[1,32,2048]{2,1,0:T(8,128)(2,1)S(1)} %add_convert_fusion.5), channel_id=1, source_target_pairs={{0,16},{4,20},{8,24},{12,28},{16,0},{20,4},{24,8},{28,12},{1,17},{... | collective-permute-start | bytes 393224 | tf_op jit(solution)/shard_map/ppermute | solution.py:176
  47.6 7.4 %collective-permute-start.14 = (bf16[1,32,2048]{2,1,0:T(8,128)(2,1)S(1)}, bf16[1,32,2048]{2,1,0:T(8,128)(2,1)S(1)}, u32[]{:S(2)}, u32[]{:S(2)}) collective-permute-start(bf16[1,32,2048]{2,1,0:T(8,128)(2,1)S(1)} %add_convert_fusion.4), channel_id=1, source_target_pairs={{0,8},{4,12},{8,0},{12,4},{16,24},{20,28},{24,16},{28,20},{1,9},{5... | collective-permute-start | bytes 393224 | tf_op jit(solution)/shard_map/ppermute | solution.py:176
  50.4 7.5 %collective-permute-start.16 = (bf16[1,32,2048]{2,1,0:T(8,128)(2,1)S(1)}, bf16[1,32,2048]{2,1,0:T(8,128)(2,1)S(1)}, u32[]{:S(2)}, u32[]{:S(2)}) collective-permute-start(bf16[1,32,2048]{2,1,0:T(8,128)(2,1)S(1)} %add_convert_fusion.3), channel_id=1, source_target_pairs={{0,24},{4,28},{8,16},{12,20},{16,8},{20,12},{24,0},{28,4},{1,25},{... | collective-permute-start | bytes 393224 | tf_op jit(solution)/shard_map/ppermute | solution.py:176
  58.1 7.6 %collective-permute-start.18 = (bf16[1,32,2048]{2,1,0:T(8,128)(2,1)S(1)}, bf16[1,32,2048]{2,1,0:T(8,128)(2,1)S(1)}, u32[]{:S(2)}, u32[]{:S(2)}) collective-permute-start(bf16[1,32,2048]{2,1,0:T(8,128)(2,1)S(1)} %get-tuple-element.28.refs_7_), channel_id=1, source_target_pairs={{0,24},{4,28},{8,16},{12,20},{16,8},{20,12},{24,0},{28,4},{1,25},{... | collective-permute-start | bytes 393224 | tf_op jit(solution)/shard_map/ppermute | solution.py:176
  62.0 6.9 %collective-permute-start.20 = (bf16[1,32,2048]{2,1,0:T(8,128)(2,1)S(1)}, bf16[1,32,2048]{2,1,0:T(8,128)(2,1)S(1)}, u32[]{:S(2)}, u32[]{:S(2)}) collective-permute-start(bf16[1,32,2048]{2,1,0:T(8,128)(2,1)S(1)} %get-tuple-element.28.refs_7_), channel_id=1, source_target_pairs={{0,8},{4,12},{8,0},{12,4},{16,24},{20,28},{24,16},{28,20},{1,9},{5... | collective-permute-start | bytes 393224 | tf_op jit(solution)/shard_map/ppermute | solution.py:176
  62.0 7.8 %collective-permute-start.22 = (bf16[1,32,2048]{2,1,0:T(8,128)(2,1)S(1)}, bf16[1,32,2048]{2,1,0:T(8,128)(2,1)S(1)}, u32[]{:S(2)}, u32[]{:S(2)}) collective-permute-start(bf16[1,32,2048]{2,1,0:T(8,128)(2,1)S(1)} %get-tuple-element.28.refs_7_), channel_id=1, source_target_pairs={{0,16},{4,20},{8,24},{12,28},{16,0},{20,4},{24,8},{28,12},{1,17},{... | collective-permute-start | bytes 393224 | tf_op jit(solution)/shard_map/ppermute | solution.py:176
  62.6 8.2 %collective-permute-start.24 = (bf16[1,32,2048]{2,1,0:T(8,128)(2,1)S(1)}, bf16[1,32,2048]{2,1,0:T(8,128)(2,1)S(1)}, u32[]{:S(2)}, u32[]{:S(2)}) collective-permute-start(bf16[1,32,2048]{2,1,0:T(8,128)(2,1)S(1)} %get-tuple-element.28.refs_7_), channel_id=1, source_target_pairs={{0,4},{4,0},{8,12},{12,8},{16,20},{20,16},{24,28},{28,24},{1,5},{5... | collective-permute-start | bytes 393224 | tf_op jit(solution)/shard_map/ppermute | solution.py:176
  77.3 11.5 %collective-permute-start.26 = (bf16[2,32,2048]{2,1,0:T(8,128)(2,1)S(1)}, bf16[2,32,2048]{2,1,0:T(8,128)(2,1)S(1)}, u32[]{:S(2)}, u32[]{:S(2)}) collective-permute-start(bf16[2,32,2048]{2,1,0:T(8,128)(2,1)S(1)} %fusion.2), channel_id=1, source_target_pairs={{0,2},{1,3},{2,0},{3,1},{4,6},{5,7},{6,4},{7,5},{8,10},{9,11},{10,... | collective-permute-start | bytes 786440 | tf_op jit(solution)/shard_map/ppermute | solution.py:176
  91.3 9.2 %collective-permute-start.30 = (bf16[1,32,2048]{2,1,0:T(8,128)(2,1)S(1)}, bf16[1,32,2048]{2,1,0:T(8,128)(2,1)S(1)}, u32[]{:S(2)}, u32[]{:S(2)}) collective-permute-start(bf16[1,32,2048]{2,1,0:T(8,128)(2,1)S(1)} %get-tuple-element.32), channel_id=1, source_target_pairs={{0,4},{4,0},{8,12},{12,8},{16,20},{20,16},{24,28},{28,24},{1,5},{5... | collective-permute-start | bytes 393224 | tf_op jit(solution)/shard_map/ppermute | solution.py:176
  93.5 9.9 %collective-permute-start.32 = (bf16[1,32,2048]{2,1,0:T(8,128)(2,1)S(1)}, bf16[1,32,2048]{2,1,0:T(8,128)(2,1)S(1)}, u32[]{:S(2)}, u32[]{:S(2)}) collective-permute-start(bf16[1,32,2048]{2,1,0:T(8,128)(2,1)S(1)} %get-tuple-element.34), channel_id=1, source_target_pairs={{0,4},{4,0},{8,12},{12,8},{16,20},{20,16},{24,28},{28,24},{1,5},{5... | collective-permute-start | bytes 393224 | tf_op jit(solution)/shard_map/ppermute | solution.py:176
  94.1 13.1 %collective-permute-start.34 = (bf16[1,32,2048]{2,1,0:T(8,128)(2,1)S(1)}, bf16[1,32,2048]{2,1,0:T(8,128)(2,1)S(1)}, u32[]{:S(2)}, u32[]{:S(2)}) collective-permute-start(bf16[1,32,2048]{2,1,0:T(8,128)(2,1)S(1)} %get-tuple-element.35), channel_id=1, source_target_pairs={{0,4},{4,0},{8,12},{12,8},{16,20},{20,16},{24,28},{28,24},{1,5},{5... | collective-permute-start | bytes 393224 | tf_op jit(solution)/shard_map/ppermute | solution.py:176
  97.8 9.4 %collective-permute-start.29 = (bf16[1,32,2048]{2,1,0:T(8,128)(2,1)S(1)}, bf16[1,32,2048]{2,1,0:T(8,128)(2,1)S(1)}, u32[]{:S(2)}, u32[]{:S(2)}) collective-permute-start(bf16[1,32,2048]{2,1,0:T(8,128)(2,1)S(1)} %add_convert_fusion.2), channel_id=1, source_target_pairs={{0,16},{4,20},{8,24},{12,28},{16,0},{20,4},{24,8},{28,12},{1,17},{... | collective-permute-start | bytes 393224 | tf_op jit(solution)/shard_map/ppermute | solution.py:176
  103.4 6.9 %collective-permute-start.33 = (bf16[1,32,2048]{2,1,0:T(8,128)(2,1)S(1)}, bf16[1,32,2048]{2,1,0:T(8,128)(2,1)S(1)}, u32[]{:S(2)}, u32[]{:S(2)}) collective-permute-start(bf16[1,32,2048]{2,1,0:T(8,128)(2,1)S(1)} %add_convert_fusion), channel_id=1, source_target_pairs={{0,24},{4,28},{8,16},{12,20},{16,8},{20,12},{24,0},{28,4},{1,25},{... | collective-permute-start | bytes 393224 | tf_op jit(solution)/shard_map/ppermute | solution.py:176
  (15 other events, 105.0 us)
